TPU v7x, 32 devices: a whole 2x2x4 slice. The times are simulated.
32 devices in a mesh: rack: 8 (over y, x, core), expert: 4 (over z).
Axes of the slice: x: 2, y: 2, z: 4, core: 2. Of those that a mesh axis runs over, the one named last changes fastest.
Arguments:
- hidden_in: bfloat16 [32, 3584], P(('rack', 'expert')), may hold values from -6 to 6
- norm_gain: float32 [3584], replicated, may hold values from 0.1 to 1.9
- expert_ids: int32 [4, 32, 8], P(None, ('rack', 'expert')), may hold values from 0 to 7, all different within a row; in each aligned block of 4 rows (0 to 3, 4 to 7, ..., all dimensions but the last counted through in order) at most 4 rows name the same one
- gate_levels: int32 [4, 32, 8], P(None, ('rack', 'expert')), may hold values from 1 to 255
- w_gate_up: bfloat16 [8, 4, 1792, 2, 1024], P('rack', 'expert'), may hold values from -0.09375 to 0.09375
- w_down: bfloat16 [8, 4, 1024, 1792], P('rack', 'expert'), may hold values from -0.125 to 0.125
Outputs:
- hidden_out: float32 [32, 3584], P(('rack', 'expert'))
Inputs may be any that keep to these rules, and one draw needn't show every extreme that they name: `expert_ids`: each token names 8 different experts in each step; in each step at most 4 of the 4 tokens of one index of rack (an aligned block of the token order) name the same expert, and that many do in some blocks.
All inputs are finite; a program needn't handle non-finite values.
Results may differ from a plain program's by a relative error of at most 0.015.
Values may be sent and summed in bfloat16 or wider, within the bound.
No kernel may reach another device: no remote copies, remote signals or barrier semaphores. Data moves between devices by JAX's collectives and lax.ppermute only.
A program may use at most 64 MiB of HBM per device.

v0:
```python
import jax
import jax.numpy as jnp
from jax import lax
from jax.sharding import PartitionSpec as P

TOP = 8
STEPS = 4


def swapped(shard, axis, bit):
    return lax.ppermute(shard, axis, [(i, i ^ 1 << bit) for i in range(lax.axis_size(axis))])


def per_device(hidden_in, norm_gain, expert_ids, gate_levels, w_gate_up, w_down):
    rack_count = lax.axis_size("rack")
    group_count = lax.axis_size("expert")
    group_index = lax.axis_index("expert")
    half_index = group_index % 2
    tok_rows = hidden_in.shape[0]
    rack_rows = tok_rows * group_count
    slot_count = min(rack_rows, 3 * rack_rows * TOP // (2 * rack_count))
    model_width = hidden_in.shape[1]
    half_width = model_width // 2
    part_width = w_down.shape[2]
    gate_up_weight = w_gate_up[0, 0].reshape(half_width, 2 * part_width)
    down_weight = w_down[0, 0]
    all_ids, all_levels = (
        lax.all_gather(expert_ids, "expert", axis=1, tiled=True),
        lax.all_gather(gate_levels, "expert", axis=1, tiled=True),
    )
    expert_range = jnp.arange(rack_count, dtype=jnp.int32)
    slot_ids = jnp.arange(slot_count, dtype=jnp.int32)
    residual = hidden_in.astype(jnp.float32)
    for step_index in range(STEPS):
        mean_square = jnp.mean(residual * residual, axis=-1, keepdims=True)
        normed = (residual * lax.rsqrt(mean_square + 1e-06) * norm_gain).astype(jnp.bfloat16)
        rack_normed = lax.all_gather(normed, "expert", axis=0, tiled=True)
        picked = all_ids[step_index]
        level_vals = all_levels[step_index].astype(jnp.float32)
        shares = level_vals / jnp.sum(level_vals, axis=-1, keepdims=True)
        matches = picked[:, :, None] == expert_range[None, None, :]
        chosen = jnp.sum(matches.astype(jnp.int32), axis=1)
        mixing = jnp.sum(jnp.where(matches, shares[:, :, None], jnp.float32(0.0)), axis=1).astype(
            jnp.bfloat16
        )
        slot_rank = jnp.cumsum(chosen, axis=0) - chosen
        placement = chosen[:, :, None] * (slot_rank[:, :, None] == slot_ids).astype(jnp.int32)
        dispatch_map = (
            jnp.transpose(placement, (1, 2, 0))
            .reshape(rack_count * slot_count, rack_rows)
            .astype(jnp.bfloat16)
        )
        outgoing = jnp.dot(dispatch_map, rack_normed, preferred_element_type=jnp.float32).astype(
            jnp.bfloat16
        )
        outgoing = outgoing.reshape(rack_count, slot_count, model_width)
        combine_map = (placement.astype(jnp.bfloat16) * mixing[:, :, None]).reshape(
            rack_rows, rack_count * slot_count
        )
        half_rows = lax.dynamic_slice_in_dim(outgoing, half_index * half_width, half_width, 2)
        slot_rows = lax.all_to_all(half_rows, "rack", split_axis=0, concat_axis=0, tiled=True)
        layout = slot_rows.shape
        flat_rows = slot_rows.reshape(-1, half_width)
        gate_up = jnp.dot(flat_rows, gate_up_weight, preferred_element_type=jnp.float32)
        gate_up = gate_up + swapped(gate_up.astype(jnp.bfloat16), "expert", 0).astype(gate_up.dtype)
        activated = (jax.nn.silu(gate_up[:, :part_width]) * gate_up[:, part_width:]).astype(
            jnp.bfloat16
        )
        partial_value = jnp.dot(activated, down_weight, preferred_element_type=jnp.float32).astype(
            jnp.bfloat16
        )
        partial_value = partial_value.reshape(layout)
        finished = lax.all_to_all(partial_value, "rack", split_axis=0, concat_axis=0, tiled=True)
        partial_sum = jnp.dot(
            combine_map, finished.reshape(-1, half_width), preferred_element_type=jnp.float32
        )
        full_sum = jnp.zeros((rack_rows, model_width), jnp.float32)
        full_sum = lax.dynamic_update_slice_in_dim(
            full_sum, partial_sum, half_index * half_width, 1
        )
        update = lax.psum_scatter(
            full_sum.astype(jnp.bfloat16), "expert", scatter_dimension=0, tiled=True
        ).astype(jnp.float32)
        residual = residual + update
    return residual


def solution(mesh):
    in_specs = (
        P(("rack", "expert"), None),
        P(),
        P(None, ("rack", "expert"), None),
        P(None, ("rack", "expert"), None),
        P("rack", "expert", None, None, None),
        P("rack", "expert", None, None),
    )
    out_specs = P(("rack", "expert"), None)
    return jax.shard_map(
        per_device, mesh=mesh, in_specs=in_specs, out_specs=out_specs, check_vma=False
    )
```

profile of v0, /device:TPU:0, one launch (start us, length us, event | category | flops | bytes accessed | tf_op | source)
XLA Modules:
  0.0 281.0 jit_solution(8665986093362209282)
XLA Ops:
  0.0 13.7 %all_gather.18 = s32[4,4,8]{2,0,1:T(4,128)S(1)} all-gather(s32[4,1,8]{2,0,1:T(4,128)} %bitcast.128), channel_id=1, replica_groups=mesh['rack'=8,'expert'=4] {'expert'}, dimensions={1}, use_global_device_ids=true | all-gather | bytes 640 | tf_op jit(solution)/shard_map/all_gather | solution.py:28
  14.2 1.4 multiply_reduce_fusion.3
  16.3 0.8 convert_bitcast_fusion.3
  17.0 13.1 %all-gather = bf16[4,1,3584]{2,1,0:T(2,128)(2,1)S(1)} all-gather(bf16[1,1,3584]{2,1,0:T(2,128)(2,1)S(1)} %convert_bitcast_fusion.3), channel_id=1, replica_groups=mesh['rack'=8,'expert'=4] {'expert'}, dimensions={0}, use_global_device_ids=true | all-gather | bytes 35840 | tf_op jit(solution)/shard_map/all_gather | solution.py:37
  30.1 0.3 convolution_convert_fusion.3
  30.5 0.7 constant_dynamic-slice_fusion.3
  31.2 3.7 %all-to-all-start = ((bf16[8,4,1792]{2,1,0:T(4,128)(2,1)}), bf16[8,4,1792]{2,1,0:T(4,128)(2,1)S(1)}, u32[]{:S(2)}, u32[]{:S(2)}) async-start(bf16[8,4,1792]{2,1,0:T(4,128)(2,1)} %constant_dynamic-slice_fusion.3), calls=%async_computation | async-start | bytes 229376 | tf_op jit(solution)/shard_map/all_to_all | solution.py:61
  35.1 9.1 %copy.31 = bf16[224,8,2,1024]{3,1,2,0:T(8,128)(2,1)} copy(bf16[224,8,2,1024]{3,2,1,0:T(2,128)(2,1)} %bitcast.111) | data formatting | bytes 14680064
  44.2 12.0 %all_gather.19 = s32[4,4,8]{2,0,1:T(4,128)S(1)} all-gather(s32[4,1,8]{2,0,1:T(4,128)S(1)} %bitcast.129), channel_id=1, replica_groups=mesh['rack'=8,'expert'=4] {'expert'}, dimensions={1}, use_global_device_ids=true | all-gather | bytes 640 | tf_op jit(solution)/shard_map/all_gather | solution.py:29
  57.0 0.6 dynamic-slice
  57.6 0.1 fusion.95
  57.8 4.6 %fusion.100 = (bf16[32,2048]{1,0:T(8,128)(2,1)S(1)}, f32[32,2048]{1,0:T(8,128)S(1)}) fusion(bf16[32,1792]{1,0:T(8,128)(2,1)S(1)} %reshape.245, bf16[1792,2048]{1,0:T(8,128)(2,1)} %bitcast.107), kind=kOutput, calls=%fused_computation.149 | convolution fusion | flops 234946560 | bytes 7847936 | tf_op jit(solution)/shard_map/dot_general | solution.py:64
  62.4 0.4 collective-permute-start
  62.8 4.6 %collective-permute-done = bf16[32,2048]{1,0:T(8,128)(2,1)S(1)} collective-permute-done((bf16[32,2048]{1,0:T(8,128)(2,1)S(1)}, bf16[32,2048]{1,0:T(8,128)(2,1)S(1)}, u32[]{:S(2)}, u32[]{:S(2)}) %collective-permute-start) | collective-permute-done | bytes 131104 | tf_op jit(solution)/shard_map/ppermute | solution.py:11
  67.4 0.7 fusion.8
  68.2 0.7 reshape.246
  68.8 4.2 %all-to-all-start.1 = ((bf16[8,4,1792]{2,1,0:T(4,128)(2,1)}), bf16[8,4,1792]{2,1,0:T(4,128)(2,1)S(1)}, u32[]{:S(2)}, u32[]{:S(2)}) async-start(bf16[8,4,1792]{2,1,0:T(4,128)(2,1)} %reshape.246), calls=%async_computation.1 | async-start | bytes 229376 | tf_op jit(solution)/shard_map/all_to_all | solution.py:73
  73.1 5.3 %all-to-all-done.1 = bf16[8,4,1792]{2,1,0:T(4,128)(2,1)S(1)} async-done(((bf16[8,4,1792]{2,1,0:T(4,128)(2,1)}), bf16[8,4,1792]{2,1,0:T(4,128)(2,1)S(1)}, u32[]{:S(2)}, u32[]{:S(2)}) %all-to-all-start.1) | async-done | bytes 114720 | tf_op jit(solution)/shard_map/all_to_all | solution.py:73
  78.4 0.2 fusion.23
  78.6 16.5 %all-reduce = bf16[4,3584]{1,0:T(4,128)(2,1)S(1)} all-reduce(bf16[4,3584]{1,0:T(4,128)(2,1)S(1)} %fusion.23), channel_id=2, replica_groups=mesh['rack'=8,'expert'=4] {'expert'}, use_global_device_ids=true, to_apply=%region_5.6.clone | all-reduce | flops 14336 | bytes 57344
  95.2 1.3 multiply_reduce_fusion.2
  97.1 13.1 %all-gather.1 = bf16[4,1,3584]{2,1,0:T(2,128)(2,1)S(1)} all-gather(bf16[1,1,3584]{2,1,0:T(2,128)(2,1)S(1)} %convert_bitcast_fusion.2), channel_id=1, replica_groups=mesh['rack'=8,'expert'=4] {'expert'}, dimensions={0}, use_global_device_ids=true | all-gather | bytes 35840 | tf_op jit(solution)/shard_map/all_gather | solution.py:37
  110.2 0.3 convolution_convert_fusion.2
  110.6 0.7 constant_dynamic-slice_fusion.2
  111.3 3.4 %all-to-all-start.2 = ((bf16[8,4,1792]{2,1,0:T(4,128)(2,1)}), bf16[8,4,1792]{2,1,0:T(4,128)(2,1)S(1)}, u32[]{:S(2)}, u32[]{:S(2)}) async-start(bf16[8,4,1792]{2,1,0:T(4,128)(2,1)} %constant_dynamic-slice_fusion.2), calls=%async_computation.2 | async-start | bytes 229376 | tf_op jit(solution)/shard_map/all_to_all | solution.py:61
  114.8 5.2 %all-to-all-done.2 = bf16[8,4,1792]{2,1,0:T(4,128)(2,1)S(1)} async-done(((bf16[8,4,1792]{2,1,0:T(4,128)(2,1)}), bf16[8,4,1792]{2,1,0:T(4,128)(2,1)S(1)}, u32[]{:S(2)}, u32[]{:S(2)}) %all-to-all-start.2) | async-done | bytes 114720 | tf_op jit(solution)/shard_map/all_to_all | solution.py:61
  120.0 4.6 %fusion.101 = (bf16[32,2048]{1,0:T(8,128)(2,1)S(1)}, f32[32,2048]{1,0:T(8,128)S(1)}) fusion(bf16[32,1792]{1,0:T(8,128)(2,1)S(1)} %reshape.248, bf16[1792,2048]{1,0:T(8,128)(2,1)} %bitcast.108), kind=kOutput, calls=%fused_computation.150 | convolution fusion | flops 234946560 | bytes 7847936 | tf_op jit(solution)/shard_map/dot_general | solution.py:64
  124.7 5.0 %collective-permute-done.1 = bf16[32,2048]{1,0:T(8,128)(2,1)S(1)} collective-permute-done((bf16[32,2048]{1,0:T(8,128)(2,1)S(1)}, bf16[32,2048]{1,0:T(8,128)(2,1)S(1)}, u32[]{:S(2)}, u32[]{:S(2)}) %collective-permute-start.1) | collective-permute-done | bytes 131104 | tf_op jit(solution)/shard_map/ppermute | solution.py:11
  129.7 0.7 fusion.11
  130.4 0.7 reshape.249
  131.1 3.4 %all-to-all-start.3 = ((bf16[8,4,1792]{2,1,0:T(4,128)(2,1)}), bf16[8,4,1792]{2,1,0:T(4,128)(2,1)S(1)}, u32[]{:S(2)}, u32[]{:S(2)}) async-start(bf16[8,4,1792]{2,1,0:T(4,128)(2,1)} %reshape.249), calls=%async_computation.3 | async-start | bytes 229376 | tf_op jit(solution)/shard_map/all_to_all | solution.py:73
  134.6 5.2 %all-to-all-done.3 = bf16[8,4,1792]{2,1,0:T(4,128)(2,1)S(1)} async-done(((bf16[8,4,1792]{2,1,0:T(4,128)(2,1)}), bf16[8,4,1792]{2,1,0:T(4,128)(2,1)S(1)}, u32[]{:S(2)}, u32[]{:S(2)}) %all-to-all-start.3) | async-done | bytes 114720 | tf_op jit(solution)/shard_map/all_to_all | solution.py:73
  139.8 0.2 fusion.22
  140.0 16.8 %all-reduce.1 = bf16[4,3584]{1,0:T(4,128)(2,1)S(1)} all-reduce(bf16[4,3584]{1,0:T(4,128)(2,1)S(1)} %fusion.22), channel_id=3, replica_groups=mesh['rack'=8,'expert'=4] {'expert'}, use_global_device_ids=true, to_apply=%region_11.12.clone | all-reduce | flops 14336 | bytes 57344
  156.8 1.3 multiply_reduce_fusion.1
  158.8 13.1 %all-gather.2 = bf16[4,1,3584]{2,1,0:T(2,128)(2,1)S(1)} all-gather(bf16[1,1,3584]{2,1,0:T(2,128)(2,1)S(1)} %convert_bitcast_fusion.1), channel_id=1, replica_groups=mesh['rack'=8,'expert'=4] {'expert'}, dimensions={0}, use_global_device_ids=true | all-gather | bytes 35840 | tf_op jit(solution)/shard_map/all_gather | solution.py:37
  171.9 0.3 convolution_convert_fusion.1
  172.2 0.7 constant_dynamic-slice_fusion.1
  172.9 3.5 %all-to-all-start.4 = ((bf16[8,4,1792]{2,1,0:T(4,128)(2,1)}), bf16[8,4,1792]{2,1,0:T(4,128)(2,1)S(1)}, u32[]{:S(2)}, u32[]{:S(2)}) async-start(bf16[8,4,1792]{2,1,0:T(4,128)(2,1)} %constant_dynamic-slice_fusion.1), calls=%async_computation.4 | async-start | bytes 229376 | tf_op jit(solution)/shard_map/all_to_all | solution.py:61
  176.8 4.8 %all-to-all-done.4 = bf16[8,4,1792]{2,1,0:T(4,128)(2,1)S(1)} async-done(((bf16[8,4,1792]{2,1,0:T(4,128)(2,1)}), bf16[8,4,1792]{2,1,0:T(4,128)(2,1)S(1)}, u32[]{:S(2)}, u32[]{:S(2)}) %all-to-all-start.4) | async-done | bytes 114720 | tf_op jit(solution)/shard_map/all_to_all | solution.py:61
  181.6 4.6 %fusion.102 = (bf16[32,2048]{1,0:T(8,128)(2,1)S(1)}, f32[32,2048]{1,0:T(8,128)S(1)}) fusion(bf16[32,1792]{1,0:T(8,128)(2,1)S(1)} %reshape.251, bf16[1792,2048]{1,0:T(8,128)(2,1)} %bitcast.109), kind=kOutput, calls=%fused_computation.151 | convolution fusion | flops 234946560 | bytes 7847936 | tf_op jit(solution)/shard_map/dot_general | solution.py:64
  186.3 5.0 %collective-permute-done.2 = bf16[32,2048]{1,0:T(8,128)(2,1)S(1)} collective-permute-done((bf16[32,2048]{1,0:T(8,128)(2,1)S(1)}, bf16[32,2048]{1,0:T(8,128)(2,1)S(1)}, u32[]{:S(2)}, u32[]{:S(2)}) %collective-permute-start.2) | collective-permute-done | bytes 131104 | tf_op jit(solution)/shard_map/ppermute | solution.py:11
  191.3 0.7 fusion.14
  192.1 0.7 reshape.252
  192.7 3.4 %all-to-all-start.5 = ((bf16[8,4,1792]{2,1,0:T(4,128)(2,1)}), bf16[8,4,1792]{2,1,0:T(4,128)(2,1)S(1)}, u32[]{:S(2)}, u32[]{:S(2)}) async-start(bf16[8,4,1792]{2,1,0:T(4,128)(2,1)} %reshape.252), calls=%async_computation.5 | async-start | bytes 229376 | tf_op jit(solution)/shard_map/all_to_all | solution.py:73
  196.1 0.1 select_reduce_fusion.1
  196.2 5.2 %all-to-all-done.5 = bf16[8,4,1792]{2,1,0:T(4,128)(2,1)S(1)} async-done(((bf16[8,4,1792]{2,1,0:T(4,128)(2,1)}), bf16[8,4,1792]{2,1,0:T(4,128)(2,1)S(1)}, u32[]{:S(2)}, u32[]{:S(2)}) %all-to-all-start.5) | async-done | bytes 114720 | tf_op jit(solution)/shard_map/all_to_all | solution.py:73
  201.4 0.2 fusion.21
  201.6 16.5 %all-reduce.2 = bf16[4,3584]{1,0:T(4,128)(2,1)S(1)} all-reduce(bf16[4,3584]{1,0:T(4,128)(2,1)S(1)} %fusion.21), channel_id=4, replica_groups=mesh['rack'=8,'expert'=4] {'expert'}, use_global_device_ids=true, to_apply=%region_17.18.clone | all-reduce | flops 14336 | bytes 57344
  218.2 1.3 multiply_reduce_fusion
  220.1 13.1 %all-gather.3 = bf16[4,1,3584]{2,1,0:T(2,128)(2,1)S(1)} all-gather(bf16[1,1,3584]{2,1,0:T(2,128)(2,1)S(1)} %convert_bitcast_fusion), channel_id=1, replica_groups=mesh['rack'=8,'expert'=4] {'expert'}, dimensions={0}, use_global_device_ids=true | all-gather | bytes 35840 | tf_op jit(solution)/shard_map/all_gather | solution.py:37
  233.2 0.3 convolution_convert_fusion
  233.6 0.7 constant_dynamic-slice_fusion
  234.3 3.4 %all-to-all-start.6 = ((bf16[8,4,1792]{2,1,0:T(4,128)(2,1)}), bf16[8,4,1792]{2,1,0:T(4,128)(2,1)S(1)}, u32[]{:S(2)}, u32[]{:S(2)}) async-start(bf16[8,4,1792]{2,1,0:T(4,128)(2,1)} %constant_dynamic-slice_fusion), calls=%async_computation.6 | async-start | bytes 229376 | tf_op jit(solution)/shard_map/all_to_all | solution.py:61
  237.7 5.3 %all-to-all-done.6 = bf16[8,4,1792]{2,1,0:T(4,128)(2,1)S(1)} async-done(((bf16[8,4,1792]{2,1,0:T(4,128)(2,1)}), bf16[8,4,1792]{2,1,0:T(4,128)(2,1)S(1)}, u32[]{:S(2)}, u32[]{:S(2)}) %all-to-all-start.6) | async-done | bytes 114720 | tf_op jit(solution)/shard_map/all_to_all | solution.py:61
  243.0 4.6 %fusion.103 = (bf16[32,2048]{1,0:T(8,128)(2,1)S(1)}, f32[32,2048]{1,0:T(8,128)S(1)}) fusion(bf16[32,1792]{1,0:T(8,128)(2,1)S(1)} %reshape.254, bf16[1792,2048]{1,0:T(8,128)(2,1)} %bitcast.110), kind=kOutput, calls=%fused_computation.152 | convolution fusion | flops 234946560 | bytes 7847936 | tf_op jit(solution)/shard_map/dot_general | solution.py:64
  247.7 5.0 %collective-permute-done.3 = bf16[32,2048]{1,0:T(8,128)(2,1)S(1)} collective-permute-done((bf16[32,2048]{1,0:T(8,128)(2,1)S(1)}, bf16[32,2048]{1,0:T(8,128)(2,1)S(1)}, u32[]{:S(2)}, u32[]{:S(2)}) %collective-permute-start.3) | collective-permute-done | bytes 131104 | tf_op jit(solution)/shard_map/ppermute | solution.py:11
  252.7 0.7 fusion.17
  253.4 0.7 reshape.255
  254.1 3.4 %all-to-all-start.7 = ((bf16[8,4,1792]{2,1,0:T(4,128)(2,1)}), bf16[8,4,1792]{2,1,0:T(4,128)(2,1)S(1)}, u32[]{:S(2)}, u32[]{:S(2)}) async-start(bf16[8,4,1792]{2,1,0:T(4,128)(2,1)} %reshape.255), calls=%async_computation.7 | async-start | bytes 229376 | tf_op jit(solution)/shard_map/all_to_all | solution.py:73
  257.6 5.2 %all-to-all-done.7 = bf16[8,4,1792]{2,1,0:T(4,128)(2,1)S(1)} async-done(((bf16[8,4,1792]{2,1,0:T(4,128)(2,1)}), bf16[8,4,1792]{2,1,0:T(4,128)(2,1)S(1)}, u32[]{:S(2)}, u32[]{:S(2)}) %all-to-all-start.7) | async-done | bytes 114720 | tf_op jit(solution)/shard_map/all_to_all | solution.py:73
  262.8 0.2 fusion.20
  263.0 16.8 %all-reduce.3 = bf16[4,3584]{1,0:T(4,128)(2,1)S(1)} all-reduce(bf16[4,3584]{1,0:T(4,128)(2,1)S(1)} %fusion.20), channel_id=5, replica_groups=mesh['rack'=8,'expert'=4] {'expert'}, use_global_device_ids=true, to_apply=%region_23.24.clone | all-reduce | flops 14336 | bytes 57344
  279.8 1.2 fusion.48
  (82 shorter events, 3.2 us)
Async XLA Ops:
  31.2 26.6 %all-to-all-start = ((bf16[8,4,1792]{2,1,0:T(4,128)(2,1)}), bf16[8,4,1792]{2,1,0:T(4,128)(2,1)S(1)}, u32[]{:S(2)}, u32[]{:S(2)}) async-start(bf16[8,4,1792]{2,1,0:T(4,128)(2,1)} %constant_dynamic-slice_fusion.3), calls=%async_computation | async-start | bytes 229376 | tf_op jit(solution)/shard_map/all_to_all | solution.py:61
  35.0 9.2 %copy-start.6 = (s32[4,1,8]{2,1,0:T(1,128)S(1)}, s32[4,1,8]{2,1,0:T(1,128)}, u32[]{:S(2)}) copy-start(s32[4,1,8]{2,1,0:T(1,128)} %param.9) | copy-start | bytes 388
  35.0 21.9 %copy-start.7 = (u32[32]{0:T(128)S(1)}, u32[32]{0:T(128)}, u32[]{:S(2)}) copy-start(u32[32]{0:T(128)} %constant.64) | copy-start | bytes 388
  44.2 51.0 %copy-start.5 = (bf16[1,3584]{1,0:T(2,128)(2,1)S(1)}, bf16[1,3584]{1,0:T(2,128)(2,1)}, u32[]{:S(2)}) copy-start(bf16[1,3584]{1,0:T(2,128)(2,1)} %param.6) | copy-start | bytes 21508
  44.2 52.9 %copy-start.4 = (f32[3584]{0:T(1024)S(1)}, f32[3584]{0:T(1024)}, u32[]{:S(2)}) copy-start(f32[3584]{0:T(1024)} %param.7) | copy-start | bytes 43012
  57.8 9.7 %copy-start = (bf16[1,1,1024,1792]{3,2,1,0:T(8,128)(2,1)S(1)}, bf16[1,1,1024,1792]{3,2,1,0:T(8,128)(2,1)}, u32[]{:S(2)}) copy-start(bf16[1,1,1024,1792]{3,2,1,0:T(8,128)(2,1)} %param.11) | copy-start | bytes 11010052
  62.4 5.0 %collective-permute-start = (bf16[32,2048]{1,0:T(8,128)(2,1)S(1)}, bf16[32,2048]{1,0:T(8,128)(2,1)S(1)}, u32[]{:S(2)}, u32[]{:S(2)}) collective-permute-start(bf16[32,2048]{1,0:T(8,128)(2,1)S(1)} %get-tuple-element.23), channel_id=1, source_target_pairs={{0,1},{1,0},{2,3},{3,2},{4,5},{5,4},{6,7},{7,6},{8,9},{9,8},{10,11... | collective-permute-start | bytes 393224 | tf_op jit(solution)/shard_map/ppermute | solution.py:11
  68.8 9.5 %all-to-all-start.1 = ((bf16[8,4,1792]{2,1,0:T(4,128)(2,1)}), bf16[8,4,1792]{2,1,0:T(4,128)(2,1)S(1)}, u32[]{:S(2)}, u32[]{:S(2)}) async-start(bf16[8,4,1792]{2,1,0:T(4,128)(2,1)} %reshape.246), calls=%async_computation.1 | async-start | bytes 229376 | tf_op jit(solution)/shard_map/all_to_all | solution.py:73
  111.3 8.7 %all-to-all-start.2 = ((bf16[8,4,1792]{2,1,0:T(4,128)(2,1)}), bf16[8,4,1792]{2,1,0:T(4,128)(2,1)S(1)}, u32[]{:S(2)}, u32[]{:S(2)}) async-start(bf16[8,4,1792]{2,1,0:T(4,128)(2,1)} %constant_dynamic-slice_fusion.2), calls=%async_computation.2 | async-start | bytes 229376 | tf_op jit(solution)/shard_map/all_to_all | solution.py:61
  120.0 9.7 %copy-start.1 = (bf16[1,1,1024,1792]{3,2,1,0:T(8,128)(2,1)S(1)}, bf16[1,1,1024,1792]{3,2,1,0:T(8,128)(2,1)}, u32[]{:S(2)}) copy-start(bf16[1,1,1024,1792]{3,2,1,0:T(8,128)(2,1)} %param.11) | copy-start | bytes 11010052
  124.6 5.1 %collective-permute-start.1 = (bf16[32,2048]{1,0:T(8,128)(2,1)S(1)}, bf16[32,2048]{1,0:T(8,128)(2,1)S(1)}, u32[]{:S(2)}, u32[]{:S(2)}) collective-permute-start(bf16[32,2048]{1,0:T(8,128)(2,1)S(1)} %get-tuple-element.25), channel_id=1, source_target_pairs={{0,1},{1,0},{2,3},{3,2},{4,5},{5,4},{6,7},{7,6},{8,9},{9,8},{10,11... | collective-permute-start | bytes 393224 | tf_op jit(solution)/shard_map/ppermute | solution.py:11
  131.1 8.7 %all-to-all-start.3 = ((bf16[8,4,1792]{2,1,0:T(4,128)(2,1)}), bf16[8,4,1792]{2,1,0:T(4,128)(2,1)S(1)}, u32[]{:S(2)}, u32[]{:S(2)}) async-start(bf16[8,4,1792]{2,1,0:T(4,128)(2,1)} %reshape.249), calls=%async_computation.3 | async-start | bytes 229376 | tf_op jit(solution)/shard_map/all_to_all | solution.py:73
  172.9 8.7 %all-to-all-start.4 = ((bf16[8,4,1792]{2,1,0:T(4,128)(2,1)}), bf16[8,4,1792]{2,1,0:T(4,128)(2,1)S(1)}, u32[]{:S(2)}, u32[]{:S(2)}) async-start(bf16[8,4,1792]{2,1,0:T(4,128)(2,1)} %constant_dynamic-slice_fusion.1), calls=%async_computation.4 | async-start | bytes 229376 | tf_op jit(solution)/shard_map/all_to_all | solution.py:61
  181.6 9.7 %copy-start.2 = (bf16[1,1,1024,1792]{3,2,1,0:T(8,128)(2,1)S(1)}, bf16[1,1,1024,1792]{3,2,1,0:T(8,128)(2,1)}, u32[]{:S(2)}) copy-start(bf16[1,1,1024,1792]{3,2,1,0:T(8,128)(2,1)} %param.11) | copy-start | bytes 11010052
  186.2 5.1 %collective-permute-start.2 = (bf16[32,2048]{1,0:T(8,128)(2,1)S(1)}, bf16[32,2048]{1,0:T(8,128)(2,1)S(1)}, u32[]{:S(2)}, u32[]{:S(2)}) collective-permute-start(bf16[32,2048]{1,0:T(8,128)(2,1)S(1)} %get-tuple-element.27), channel_id=1, source_target_pairs={{0,1},{1,0},{2,3},{3,2},{4,5},{5,4},{6,7},{7,6},{8,9},{9,8},{10,11... | collective-permute-start | bytes 393224 | tf_op jit(solution)/shard_map/ppermute | solution.py:11
  192.7 8.7 %all-to-all-start.5 = ((bf16[8,4,1792]{2,1,0:T(4,128)(2,1)}), bf16[8,4,1792]{2,1,0:T(4,128)(2,1)S(1)}, u32[]{:S(2)}, u32[]{:S(2)}) async-start(bf16[8,4,1792]{2,1,0:T(4,128)(2,1)} %reshape.252), calls=%async_computation.5 | async-start | bytes 229376 | tf_op jit(solution)/shard_map/all_to_all | solution.py:73
  234.3 8.7 %all-to-all-start.6 = ((bf16[8,4,1792]{2,1,0:T(4,128)(2,1)}), bf16[8,4,1792]{2,1,0:T(4,128)(2,1)S(1)}, u32[]{:S(2)}, u32[]{:S(2)}) async-start(bf16[8,4,1792]{2,1,0:T(4,128)(2,1)} %constant_dynamic-slice_fusion), calls=%async_computation.6 | async-start | bytes 229376 | tf_op jit(solution)/shard_map/all_to_all | solution.py:61
  243.0 9.7 %copy-start.3 = (bf16[1,1,1024,1792]{3,2,1,0:T(8,128)(2,1)S(1)}, bf16[1,1,1024,1792]{3,2,1,0:T(8,128)(2,1)}, u32[]{:S(2)}) copy-start(bf16[1,1,1024,1792]{3,2,1,0:T(8,128)(2,1)} %param.11) | copy-start | bytes 11010052
  247.6 5.1 %collective-permute-start.3 = (bf16[32,2048]{1,0:T(8,128)(2,1)S(1)}, bf16[32,2048]{1,0:T(8,128)(2,1)S(1)}, u32[]{:S(2)}, u32[]{:S(2)}) collective-permute-start(bf16[32,2048]{1,0:T(8,128)(2,1)S(1)} %get-tuple-element.29), channel_id=1, source_target_pairs={{0,1},{1,0},{2,3},{3,2},{4,5},{5,4},{6,7},{7,6},{8,9},{9,8},{10,11... | collective-permute-start | bytes 393224 | tf_op jit(solution)/shard_map/ppermute | solution.py:11
  254.1 8.7 %all-to-all-start.7 = ((bf16[8,4,1792]{2,1,0:T(4,128)(2,1)}), bf16[8,4,1792]{2,1,0:T(4,128)(2,1)S(1)}, u32[]{:S(2)}, u32[]{:S(2)}) async-start(bf16[8,4,1792]{2,1,0:T(4,128)(2,1)} %reshape.255), calls=%async_computation.7 | async-start | bytes 229376 | tf_op jit(solution)/shard_map/all_to_all | solution.py:73
where the time goes:
time: 283 us; the launch traced here: 281 us
  blocking collectives  145 us (51%)
  waiting for transfers between devices  55.5 us (20%)
  starting transfers between devices  28.8 us (10%)
  matrix products  23.2 us (8%)
  local copies, waits for them, and re-layouts  17.1 us (6%)
  other arithmetic  8.63 us (3%)
  between operations  3.16 us (1%)
    unnamed x4, blocking collectives  66.6 us
    all_gather x4, blocking collectives, per_device(): rack_normed = lax.all_gather(normed, 'expert', axis=0, tiled=True)  52.4 us
    all_to_all x4, waiting for transfers between devices, per_device(): lax.all_to_all(partial_value, 'rack', split_axis=0, concat_axis=0, tiled=...  20.8 us
    ppermute x4, waiting for transfers between devices, swapped(): lax.ppermute(shard, axis, [(i, i ^ 1 << bit) for i in range(lax.axis_size...  19.4 us
    dot_general x4, matrix products, per_device(): jnp.dot(flat_rows, gate_up_weight, preferred_element_type=jnp.float32)  18.4 us
    all_to_all x4, waiting for transfers between devices, per_device(): lax.all_to_all(half_rows, 'rack', split_axis=0, concat_axis=0, tiled=True)  15.2 us
    all_to_all x4, starting transfers between devices, per_device(): lax.all_to_all(partial_value, 'rack', split_axis=0, concat_axis=0, tiled=...  14.3 us
    all_to_all x4, starting transfers between devices, per_device(): lax.all_to_all(half_rows, 'rack', split_axis=0, concat_axis=0, tiled=True)  14 us
  transfers between devices with their start and end apart: 12, of which 11 were waited for; matrix products, arithmetic and copies ran while one was open for 4% of the time, Pallas kernels for 0%

commit v1 on v0

--- a/solution.py
+++ b/solution.py
@@ -9,6 +9,136 @@
 
 def swapped(shard, axis, bit):
     return lax.ppermute(shard, axis, [(i, i ^ 1 << bit) for i in range(lax.axis_size(axis))])
+
+
+def exchanged(shard, axis, mask):
+    return lax.ppermute(shard, axis, [(i, i ^ mask) for i in range(lax.axis_size(axis))])
+
+
+def widened(values):
+    return values.astype(jnp.float32)
+
+
+def rounded(values):
+    return values.astype(jnp.bfloat16)
+
+
+def dense_steps(hidden_in, norm_gain, expert_ids, gate_levels, w_gate_up, w_down):
+    rack_count = lax.axis_size("rack")
+    group_count = lax.axis_size("expert")
+    rack_index = lax.axis_index("rack")
+    group_index = lax.axis_index("expert")
+    chip_count = rack_count // 2
+    core_rows = chip_count * group_count
+    token_count = 2 * core_rows
+    model_width = hidden_in.shape[1]
+    half_width = model_width // 2
+    part_width = w_down.shape[2]
+    first_half = group_index % 2 == 0
+    gate_up_weight = w_gate_up[0, 0].reshape(half_width, 2 * part_width)
+    down_weight = w_down[0, 0]
+
+    def half_of(rows, own):
+        return jnp.where(first_half == own, rows[:, :half_width], rows[:, half_width:])
+
+    gain_half = half_of(norm_gain[None, :], True)
+
+    level_vals = gate_levels[:, 0, :].astype(jnp.float32)
+    shares = level_vals / jnp.sum(level_vals, axis=-1, keepdims=True)
+    matches = expert_ids[:, 0, :, None] == jnp.arange(rack_count, dtype=jnp.int32)
+    own_mixing = rounded(jnp.sum(jnp.where(matches, shares[:, :, None], jnp.float32(0.0)), axis=1))
+    own_mixing = own_mixing.reshape(1, STEPS * rack_count)
+    mixing_width = -(-STEPS * rack_count // 128) * 128
+    own_mixing = jnp.pad(own_mixing, ((0, 0), (0, mixing_width - STEPS * rack_count)))
+
+    rows = jnp.concatenate([half_of(hidden_in, True), own_mixing], axis=1)
+    other = jnp.concatenate([half_of(hidden_in, False), own_mixing], axis=1)
+    rows = jnp.concatenate([rows, exchanged(other, "expert", 1)], axis=0)
+    rows = jnp.concatenate(
+        [rows] + [exchanged(rows, "expert", mask) for mask in range(2, group_count, 2)], axis=0
+    )
+    rows = jnp.concatenate(
+        [rows] + [exchanged(rows, "rack", mask) for mask in range(2, rack_count, 2)], axis=0
+    )
+    rows = jnp.concatenate([rows, exchanged(rows, "rack", 1)], axis=0)
+    own_place = rack_index // 2 * group_count + group_index
+    places = jnp.arange(token_count, dtype=jnp.int32)
+    to_absolute = rounded(places[:, None] == (places[None, :] ^ own_place))
+    rows = jnp.dot(to_absolute, rows, preferred_element_type=jnp.float32)
+    residual = rows[:, :half_width]
+    all_mixing = rows[:, half_width : half_width + STEPS * rack_count]
+    own_expert = jnp.arange(rack_count, dtype=jnp.int32) == rack_index
+    mixing = jnp.sum(
+        jnp.where(own_expert, all_mixing.reshape(token_count, STEPS, rack_count), 0.0), axis=2
+    )
+
+    for step_index in range(STEPS):
+        last = step_index == STEPS - 1
+        square_sum = jnp.sum(residual * residual, axis=1, keepdims=True)
+        scaled = rounded(residual * gain_half)
+        gate_up = jnp.dot(scaled, gate_up_weight, preferred_element_type=jnp.float32)
+        square_high = rounded(lax.reduce_precision(square_sum, 8, 7))
+        square_low = rounded(square_sum - lax.reduce_precision(square_sum, 8, 7))
+        lane = lax.broadcasted_iota(jnp.int32, (token_count, 128), 1)
+        tail = jnp.where(lane == 0, square_high, square_low)
+        swapped_rows = exchanged(
+            jnp.concatenate([rounded(gate_up), tail], axis=1), "expert", 1
+        )
+        gate_up = gate_up + widened(swapped_rows[:, : 2 * part_width])
+        other_sum = widened(swapped_rows[:, 2 * part_width : 2 * part_width + 1]) + widened(
+            swapped_rows[:, 2 * part_width + 1 : 2 * part_width + 2]
+        )
+        gate_up = gate_up * lax.rsqrt((square_sum + other_sum) / model_width + 1e-06)
+        activated = rounded(jax.nn.silu(gate_up[:, :part_width]) * gate_up[:, part_width:])
+        term = rounded(jnp.dot(activated, down_weight, preferred_element_type=jnp.float32))
+        update = widened(term) * mixing[:, step_index : step_index + 1]
+        if last:
+            break
+        update = update[:core_rows] + widened(exchanged(rounded(update[core_rows:]), "rack", 1))
+        sent = rounded(update)
+        update = widened(sent)
+        for mask in range(2, rack_count, 2):
+            update = update + widened(exchanged(sent, "rack", mask))
+        sent = rounded(update)
+        update = widened(sent)
+        for mask in range(2, group_count, 2):
+            update = update + widened(exchanged(sent, "expert", mask))
+        sent = rounded(update)
+        update = jnp.concatenate([sent, exchanged(sent, "rack", 1)], axis=0)
+        residual = residual + widened(update)
+
+    token_ids = jnp.arange(token_count, dtype=jnp.int32)
+    token_rack = token_ids // group_count
+    place_of_token = (
+        (token_rack % 2 ^ rack_index % 2) * core_rows
+        + token_rack // 2 * group_count
+        + token_ids % group_count
+    )
+    to_tokens = rounded(place_of_token[:, None] == places[None, :])
+    outgoing = rounded(
+        jnp.dot(to_tokens, rounded(update), preferred_element_type=jnp.float32)
+    )
+    arrived = lax.all_to_all(outgoing, ("rack", "expert"), split_axis=0, concat_axis=0, tiled=True)
+    arrived = widened(arrived)
+    is_first = token_ids[:, None] % 2 == 0
+    update = jnp.concatenate(
+        [
+            jnp.sum(jnp.where(is_first, arrived, 0.0), axis=0, keepdims=True),
+            jnp.sum(jnp.where(is_first, 0.0, arrived), axis=0, keepdims=True),
+        ],
+        axis=1,
+    )
+    own_row = jnp.sum(jnp.where(places[:, None] == own_place, residual, 0.0), axis=0, keepdims=True)
+    other_row = jnp.sum(
+        jnp.where(places[:, None] == (own_place ^ 1), residual, 0.0), axis=0, keepdims=True
+    )
+    other_row = exchanged(other_row, "expert", 1)
+    own_residual = jnp.where(
+        first_half,
+        jnp.concatenate([own_row, other_row], axis=1),
+        jnp.concatenate([other_row, own_row], axis=1),
+    )
+    return own_residual + update
 
 
 def per_device(hidden_in, norm_gain, expert_ids, gate_levels, w_gate_up, w_down):
@@ -95,6 +225,7 @@
         P("rack", "expert", None, None),
     )
     out_specs = P(("rack", "expert"), None)
+    dense = mesh.shape["rack"] <= TOP
     return jax.shard_map(
-        per_device, mesh=mesh, in_specs=in_specs, out_specs=out_specs, check_vma=False
-    )
+        dense_steps if dense else per_device, mesh=mesh, in_specs=in_specs, out_specs=out_specs, check_vma=False
+    )

time: 283 us -> 145 us (0.51)
  blocking collectives: 145 us -> 0 us
  starting transfers between devices: 28.8 us -> 44.6 us
  matrix products: 23.2 us -> 29.1 us
  local copies, waits for them, and re-layouts: 17.1 us -> 12.6 us
  waiting for transfers between devices: 55.5 us -> 51.3 us
    all_gather x6 -> x0, blocking collectives: 78.1 us -> none  [the longest x4 52.4 us: per_device(): rack_normed = lax.all_gather(normed, 'expert', axis=0, tiled=True)]
    unnamed x4 -> x0, blocking collectives: 66.6 us -> none
    ppermute x4 -> x29, starting transfers between devices: 0.52 us -> 38.9 us  [exchanged(): lax.ppermute(shard, axis, [(i, i ^ mask) for i in range(lax.axis_size(axi...]
    all_to_all x8 -> x1, waiting for transfers between devices: 36.1 us -> 6.38 us  [dense_steps(): lax.all_to_all(outgoing, ('rack', 'expert'), split_axis=0, concat_axis=0,...]
    ppermute x4 -> x29, waiting for transfers between devices: 19.4 us -> 44.9 us  [exchanged(): lax.ppermute(shard, axis, [(i, i ^ mask) for i in range(lax.axis_size(axi...]
    all_to_all x8 -> x1, starting transfers between devices: 28.3 us -> 5.72 us  [dense_steps(): lax.all_to_all(outgoing, ('rack', 'expert'), split_axis=0, concat_axis=0,...]
    dot_general x16 -> x9, matrix products: 23.2 us -> 29.1 us  [the longest x4 17.8 us: dense_steps(): jnp.dot(scaled, gate_up_weight, preferred_element_type=jnp.float32)]
    reduce_sum x13 -> x8, other arithmetic: 5.95 us -> 2.43 us  [the longest x1 0.79 us: dense_steps(): shares = level_vals / jnp.sum(level_vals, axis=-1, keepdims=True)]
  transfers between devices with their start and end apart: 12 -> 30, of which waited for: 11 -> 26; matrix products, arithmetic and copies ran while one was open for 4% -> 7% of each run, Pallas kernels for 0% -> 0%
where the time goes in v1:
time: 145 us; the launch traced here: 144 us
  waiting for transfers between devices  51.3 us (35%)
  starting transfers between devices  44.6 us (31%)
  matrix products  29.1 us (20%)
  local copies, waits for them, and re-layouts  12.6 us (9%)
  other arithmetic  6.43 us (4%)
    ppermute x29, waiting for transfers between devices, exchanged(): lax.ppermute(shard, axis, [(i, i ^ mask) for i in range(lax.axis_size(axi...  44.9 us
    ppermute x29, starting transfers between devices, exchanged(): lax.ppermute(shard, axis, [(i, i ^ mask) for i in range(lax.axis_size(axi...  38.9 us
    dot_general x4, matrix products, dense_steps(): jnp.dot(scaled, gate_up_weight, preferred_element_type=jnp.float32)  17.8 us
    unnamed x11, local copies, waits for them, and re-layouts  10.6 us
    dot_general x3, matrix products, dense_steps(): jnp.dot(activated, down_weight, preferred_element_type=jnp.float32)  8.26 us
    all_to_all x1, waiting for transfers between devices, dense_steps(): lax.all_to_all(outgoing, ('rack', 'expert'), split_axis=0, concat_axis=0,...  6.38 us
    all_to_all x1, starting transfers between devices, dense_steps(): lax.all_to_all(outgoing, ('rack', 'expert'), split_axis=0, concat_axis=0,...  5.72 us
  transfers between devices with their start and end apart: 30, of which 26 were waited for; matrix products, arithmetic and copies ran while one was open for 7% of the time, Pallas kernels for 0%

profile of v1, /device:TPU:0, one launch (start us, length us, event | category | flops | bytes accessed | tf_op | source)
XLA Modules:
  0.0 144.3 jit_solution(6515229626825078792)
XLA Ops:
  0.0 0.7 convert_element_type.301
  0.7 0.8 convert_reduce_fusion
  1.6 0.8 select_reduce_fusion.2
  2.4 0.7 broadcast_select_fusion.1
  3.2 3.1 %collective-permute-start = (bf16[1,1920]{1,0:T(2,128)(2,1)S(1)}, bf16[1,1920]{1,0:T(2,128)(2,1)S(1)}, u32[]{:S(2)}, u32[]{:S(2)}) collective-permute-start(bf16[1,1920]{1,0:T(2,128)(2,1)S(1)} %get-tuple-element.33), channel_id=1, source_target_pairs={{0,1},{1,0},{2,3},{3,2},{4,5},{5,4},{6,7},{7,6},{8,9},{9,8},{10,11... | collective-permute-start | bytes 11528 | tf_op jit(solution)/shard_map/ppermute | solution.py:15
  6.3 0.7 broadcast_in_dim.126
  7.1 0.9 collective-permute-done
  7.9 3.1 %collective-permute-start.1 = (bf16[2,1920]{1,0:T(2,128)(2,1)S(1)}, bf16[2,1920]{1,0:T(2,128)(2,1)S(1)}, u32[]{:S(2)}, u32[]{:S(2)}) collective-permute-start(bf16[2,1920]{1,0:T(2,128)(2,1)S(1)} %pad_maximum_fusion.7), channel_id=1, source_target_pairs={{0,2},{1,3},{2,0},{3,1},{4,6},{5,7},{6,4},{7,5},{8,10},{9,11},{10,... | collective-permute-start | bytes 23048 | tf_op jit(solution)/shard_map/ppermute | solution.py:15
  11.0 1.6 %collective-permute-done.1 = bf16[2,1920]{1,0:T(2,128)(2,1)S(1)} collective-permute-done((bf16[2,1920]{1,0:T(2,128)(2,1)S(1)}, bf16[2,1920]{1,0:T(2,128)(2,1)S(1)}, u32[]{:S(2)}, u32[]{:S(2)}) %collective-permute-start.1) | collective-permute-done | bytes 7712 | tf_op jit(solution)/shard_map/ppermute | solution.py:15
  12.7 1.9 %collective-permute-start.2 = (bf16[4,1920]{1,0:T(4,128)(2,1)S(1)}, bf16[4,1920]{1,0:T(4,128)(2,1)S(1)}, u32[]{:S(2)}, u32[]{:S(2)}) collective-permute-start(bf16[4,1920]{1,0:T(4,128)(2,1)S(1)} %pad_maximum_fusion.4), channel_id=1, source_target_pairs={{0,8},{4,12},{8,0},{12,4},{16,24},{20,28},{24,16},{28,20},{1,9},{5... | collective-permute-start | bytes 46088 | tf_op jit(solution)/shard_map/ppermute | solution.py:15
  14.6 1.5 %collective-permute-start.3 = (bf16[4,1920]{1,0:T(4,128)(2,1)S(1)}, bf16[4,1920]{1,0:T(4,128)(2,1)S(1)}, u32[]{:S(2)}, u32[]{:S(2)}) collective-permute-start(bf16[4,1920]{1,0:T(4,128)(2,1)S(1)} %pad_maximum_fusion.4), channel_id=1, source_target_pairs={{0,16},{4,20},{8,24},{12,28},{16,0},{20,4},{24,8},{28,12},{1,17},{... | collective-permute-start | bytes 46088 | tf_op jit(solution)/shard_map/ppermute | solution.py:15
  16.3 9.1 %copy.60 = bf16[224,8,2,1024]{3,1,2,0:T(8,128)(2,1)} copy(bf16[224,8,2,1024]{3,2,1,0:T(2,128)(2,1)} %bitcast.109) | data formatting | bytes 14680064
  25.5 1.2 collective-permute-done.5
  27.2 4.4 %fusion.111 = (bf16[32,2048]{1,0:T(8,128)(2,1)S(1)}, f32[32,2048]{1,0:T(8,128)S(1)}) fusion(bf16[1792,2048]{1,0:T(8,128)(2,1)} %bitcast.105, f32[32,1920]{1,0:T(8,128)S(1)} %fusion.79, f32[1792]{0:T(1024)S(1)} %fusion.83), kind=kOutput, calls=%fused_computation.171 | convolution fusion | flops 235061248 | bytes 7970816 | tf_op jit(solution)/shard_map/dot_general | solution.py:79
  31.8 2.0 %collective-permute-start.6 = (bf16[32,2176]{1,0:T(8,128)(2,1)S(1)}, bf16[32,2176]{1,0:T(8,128)(2,1)S(1)}, u32[]{:S(2)}, u32[]{:S(2)}) collective-permute-start(bf16[32,2176]{1,0:T(8,128)(2,1)S(1)} %pad_maximum_fusion), channel_id=1, source_target_pairs={{0,1},{1,0},{2,3},{3,2},{4,5},{5,4},{6,7},{7,6},{8,9},{9,8},{10,11... | collective-permute-start | bytes 417800 | tf_op jit(solution)/shard_map/ppermute | solution.py:15
  33.9 3.8 %collective-permute-done.6 = bf16[32,2176]{1,0:T(8,128)(2,1)S(1)} collective-permute-done((bf16[32,2176]{1,0:T(8,128)(2,1)S(1)}, bf16[32,2176]{1,0:T(8,128)(2,1)S(1)}, u32[]{:S(2)}, u32[]{:S(2)}) %collective-permute-start.6) | collective-permute-done | bytes 139296 | tf_op jit(solution)/shard_map/ppermute | solution.py:15
  38.1 2.8 %fusion.14 = f32[32,1792]{1,0:T(8,128)S(1)} fusion(bf16[1,1,1024,1792]{3,2,1,0:T(8,128)(2,1)} %param.11, f32[32]{0:T(128)S(1)} %get-tuple-element.24, f32[32,2048]{1,0:T(8,128)S(1)} %add_multiply_fusion.3), kind=kOutput, calls=%fused_computation.10 | convolution fusion | flops 117809152 | bytes 4161664 | tf_op jit(solution)/shard_map/dot_general | solution.py:93
  40.9 1.2 collective-permute-done.7
  42.2 2.7 %collective-permute-start.10 = (bf16[16,1792]{1,0:T(8,128)(2,1)S(1)}, bf16[16,1792]{1,0:T(8,128)(2,1)S(1)}, u32[]{:S(2)}, u32[]{:S(2)}) collective-permute-start(bf16[16,1792]{1,0:T(8,128)(2,1)S(1)} %fusion.62), channel_id=1, source_target_pairs={{0,24},{4,28},{8,16},{12,20},{16,8},{20,12},{24,0},{28,4},{1,25},{... | collective-permute-start | bytes 172040 | tf_op jit(solution)/shard_map/ppermute | solution.py:15
  44.9 0.5 collective-permute-start.8
  45.8 1.7 %collective-permute-done.10 = bf16[16,1792]{1,0:T(8,128)(2,1)S(1)} collective-permute-done((bf16[16,1792]{1,0:T(8,128)(2,1)S(1)}, bf16[16,1792]{1,0:T(8,128)(2,1)S(1)}, u32[]{:S(2)}, u32[]{:S(2)}) %collective-permute-start.10) | collective-permute-done | bytes 57376 | tf_op jit(solution)/shard_map/ppermute | solution.py:15
  47.5 1.6 %collective-permute-done.8 = bf16[16,1792]{1,0:T(8,128)(2,1)S(1)} collective-permute-done((bf16[16,1792]{1,0:T(8,128)(2,1)S(1)}, bf16[16,1792]{1,0:T(8,128)(2,1)S(1)}, u32[]{:S(2)}, u32[]{:S(2)}) %collective-permute-start.8) | collective-permute-done | bytes 57376 | tf_op jit(solution)/shard_map/ppermute | solution.py:15
  49.0 0.5 collective-permute-done.9
  49.6 2.7 %collective-permute-start.11 = (bf16[16,1792]{1,0:T(8,128)(2,1)S(1)}, bf16[16,1792]{1,0:T(8,128)(2,1)S(1)}, u32[]{:S(2)}, u32[]{:S(2)}) collective-permute-start(bf16[16,1792]{1,0:T(8,128)(2,1)S(1)} %add_convert_fusion.5), channel_id=1, source_target_pairs={{0,2},{1,3},{2,0},{3,1},{4,6},{5,7},{6,4},{7,5},{8,10},{9,11},{10,... | collective-permute-start | bytes 172040 | tf_op jit(solution)/shard_map/ppermute | solution.py:15
  52.3 2.5 %collective-permute-done.11 = bf16[16,1792]{1,0:T(8,128)(2,1)S(1)} collective-permute-done((bf16[16,1792]{1,0:T(8,128)(2,1)S(1)}, bf16[16,1792]{1,0:T(8,128)(2,1)S(1)}, u32[]{:S(2)}, u32[]{:S(2)}) %collective-permute-start.11) | collective-permute-done | bytes 57376 | tf_op jit(solution)/shard_map/ppermute | solution.py:15
  54.9 1.2 collective-permute-done.12
  56.3 4.4 %fusion.112 = (bf16[32,2048]{1,0:T(8,128)(2,1)S(1)}, f32[32,2048]{1,0:T(8,128)S(1)}) fusion(bf16[1792,2048]{1,0:T(8,128)(2,1)} %bitcast.106, f32[1792]{0:T(1024)S(1)} %fusion.83, bf16[16,1792]{1,0:T(8,128)(2,1)S(1)} %collective-permute-done.12, bf16[16,1792]{1,0:T(8,128)(2,1)S(1)} %add_convert_fusion.4, f32[32,1920]{1,0:T(8,128)S(1)} %fusion.79), kind=kOutput, calls=%fused_computation.172 | convolution fusion | flops 235347968 | bytes 8085504 | tf_op jit(solution)/shard_map/dot_general | solution.py:79
  60.8 1.6 %collective-permute-start.13 = (bf16[32,2176]{1,0:T(8,128)(2,1)S(1)}, bf16[32,2176]{1,0:T(8,128)(2,1)S(1)}, u32[]{:S(2)}, u32[]{:S(2)}) collective-permute-start(bf16[32,2176]{1,0:T(8,128)(2,1)S(1)} %pad_maximum_fusion.1), channel_id=1, source_target_pairs={{0,1},{1,0},{2,3},{3,2},{4,5},{5,4},{6,7},{7,6},{8,9},{9,8},{10,11... | collective-permute-start | bytes 417800 | tf_op jit(solution)/shard_map/ppermute | solution.py:15
  62.4 4.2 %collective-permute-done.13 = bf16[32,2176]{1,0:T(8,128)(2,1)S(1)} collective-permute-done((bf16[32,2176]{1,0:T(8,128)(2,1)S(1)}, bf16[32,2176]{1,0:T(8,128)(2,1)S(1)}, u32[]{:S(2)}, u32[]{:S(2)}) %collective-permute-start.13) | collective-permute-done | bytes 139296 | tf_op jit(solution)/shard_map/ppermute | solution.py:15
  67.0 2.8 %fusion.23 = f32[32,1792]{1,0:T(8,128)S(1)} fusion(bf16[1,1,1024,1792]{3,2,1,0:T(8,128)(2,1)} %param.11, f32[32]{0:T(128)S(1)} %get-tuple-element.23, f32[32,2048]{1,0:T(8,128)S(1)} %add_multiply_fusion.2), kind=kOutput, calls=%fused_computation.13 | convolution fusion | flops 117809152 | bytes 4161664 | tf_op jit(solution)/shard_map/dot_general | solution.py:93
  69.8 1.2 collective-permute-done.14
  71.1 1.6 %collective-permute-start.15 = (bf16[16,1792]{1,0:T(8,128)(2,1)S(1)}, bf16[16,1792]{1,0:T(8,128)(2,1)S(1)}, u32[]{:S(2)}, u32[]{:S(2)}) collective-permute-start(bf16[16,1792]{1,0:T(8,128)(2,1)S(1)} %fusion.61), channel_id=1, source_target_pairs={{0,8},{4,12},{8,0},{12,4},{16,24},{20,28},{24,16},{28,20},{1,9},{5... | collective-permute-start | bytes 172040 | tf_op jit(solution)/shard_map/ppermute | solution.py:15
  73.1 1.5 %collective-permute-start.17 = (bf16[16,1792]{1,0:T(8,128)(2,1)S(1)}, bf16[16,1792]{1,0:T(8,128)(2,1)S(1)}, u32[]{:S(2)}, u32[]{:S(2)}) collective-permute-start(bf16[16,1792]{1,0:T(8,128)(2,1)S(1)} %fusion.61), channel_id=1, source_target_pairs={{0,24},{4,28},{8,16},{12,20},{16,8},{20,12},{24,0},{28,4},{1,25},{... | collective-permute-start | bytes 172040 | tf_op jit(solution)/shard_map/ppermute | solution.py:15
  74.6 0.7 collective-permute-done.15
  75.3 2.1 %collective-permute-done.16 = bf16[16,1792]{1,0:T(8,128)(2,1)S(1)} collective-permute-done((bf16[16,1792]{1,0:T(8,128)(2,1)S(1)}, bf16[16,1792]{1,0:T(8,128)(2,1)S(1)}, u32[]{:S(2)}, u32[]{:S(2)}) %collective-permute-start.16) | collective-permute-done | bytes 57376 | tf_op jit(solution)/shard_map/ppermute | solution.py:15
  77.4 0.8 collective-permute-done.17
  78.2 3.0 %collective-permute-start.18 = (bf16[16,1792]{1,0:T(8,128)(2,1)S(1)}, bf16[16,1792]{1,0:T(8,128)(2,1)S(1)}, u32[]{:S(2)}, u32[]{:S(2)}) collective-permute-start(bf16[16,1792]{1,0:T(8,128)(2,1)S(1)} %add_convert_fusion.3), channel_id=1, source_target_pairs={{0,2},{1,3},{2,0},{3,1},{4,6},{5,7},{6,4},{7,5},{8,10},{9,11},{10,... | collective-permute-start | bytes 172040 | tf_op jit(solution)/shard_map/ppermute | solution.py:15
  81.2 2.2 %collective-permute-done.18 = bf16[16,1792]{1,0:T(8,128)(2,1)S(1)} collective-permute-done((bf16[16,1792]{1,0:T(8,128)(2,1)S(1)}, bf16[16,1792]{1,0:T(8,128)(2,1)S(1)}, u32[]{:S(2)}, u32[]{:S(2)}) %collective-permute-start.18) | collective-permute-done | bytes 57376 | tf_op jit(solution)/shard_map/ppermute | solution.py:15
  83.5 1.2 collective-permute-done.19
  85.0 4.4 %fusion.113 = (bf16[32,2048]{1,0:T(8,128)(2,1)S(1)}, f32[32,2048]{1,0:T(8,128)S(1)}) fusion(bf16[1792,2048]{1,0:T(8,128)(2,1)} %bitcast.107, f32[1792]{0:T(1024)S(1)} %fusion.83, bf16[16,1792]{1,0:T(8,128)(2,1)S(1)} %collective-permute-done.19, bf16[16,1792]{1,0:T(8,128)(2,1)S(1)} %add_convert_fusion.2, bf16[16,1792]{1,0:T(8,128)(2,1)S(1)} %collective-permute-done.12, ...), kind=kOutput, calls=%fused_computation.173 | convolution fusion | flops 235634688 | bytes 8200192 | tf_op jit(solution)/shard_map/dot_general | solution.py:79
  89.4 1.8 %collective-permute-start.20 = (bf16[32,2176]{1,0:T(8,128)(2,1)S(1)}, bf16[32,2176]{1,0:T(8,128)(2,1)S(1)}, u32[]{:S(2)}, u32[]{:S(2)}) collective-permute-start(bf16[32,2176]{1,0:T(8,128)(2,1)S(1)} %pad_maximum_fusion.2), channel_id=1, source_target_pairs={{0,1},{1,0},{2,3},{3,2},{4,5},{5,4},{6,7},{7,6},{8,9},{9,8},{10,11... | collective-permute-start | bytes 417800 | tf_op jit(solution)/shard_map/ppermute | solution.py:15
  91.2 4.0 %collective-permute-done.20 = bf16[32,2176]{1,0:T(8,128)(2,1)S(1)} collective-permute-done((bf16[32,2176]{1,0:T(8,128)(2,1)S(1)}, bf16[32,2176]{1,0:T(8,128)(2,1)S(1)}, u32[]{:S(2)}, u32[]{:S(2)}) %collective-permute-start.20) | collective-permute-done | bytes 139296 | tf_op jit(solution)/shard_map/ppermute | solution.py:15
  95.6 2.8 %fusion.32 = f32[32,1792]{1,0:T(8,128)S(1)} fusion(bf16[1,1,1024,1792]{3,2,1,0:T(8,128)(2,1)} %param.11, f32[32]{0:T(128)S(1)} %get-tuple-element.22, f32[32,2048]{1,0:T(8,128)S(1)} %add_multiply_fusion.1), kind=kOutput, calls=%fused_computation.16 | convolution fusion | flops 117809152 | bytes 4161664 | tf_op jit(solution)/shard_map/dot_general | solution.py:93
  98.5 1.2 collective-permute-done.21
  99.7 0.7 collective-permute-start.22
  100.4 1.4 collective-permute-start.23
  101.8 1.4 collective-permute-start.24
  103.3 0.7 collective-permute-done.22
  104.0 0.6 collective-permute-done.23
  104.6 2.3 %collective-permute-done.24 = bf16[16,1792]{1,0:T(8,128)(2,1)S(1)} collective-permute-done((bf16[16,1792]{1,0:T(8,128)(2,1)S(1)}, bf16[16,1792]{1,0:T(8,128)(2,1)S(1)}, u32[]{:S(2)}, u32[]{:S(2)}) %collective-permute-start.24) | collective-permute-done | bytes 57376 | tf_op jit(solution)/shard_map/ppermute | solution.py:15
  107.0 3.3 %collective-permute-start.25 = (bf16[16,1792]{1,0:T(8,128)(2,1)S(1)}, bf16[16,1792]{1,0:T(8,128)(2,1)S(1)}, u32[]{:S(2)}, u32[]{:S(2)}) collective-permute-start(bf16[16,1792]{1,0:T(8,128)(2,1)S(1)} %add_convert_fusion.1), channel_id=1, source_target_pairs={{0,2},{1,3},{2,0},{3,1},{4,6},{5,7},{6,4},{7,5},{8,10},{9,11},{10,... | collective-permute-start | bytes 172040 | tf_op jit(solution)/shard_map/ppermute | solution.py:15
  110.3 2.2 %collective-permute-done.25 = bf16[16,1792]{1,0:T(8,128)(2,1)S(1)} collective-permute-done((bf16[16,1792]{1,0:T(8,128)(2,1)S(1)}, bf16[16,1792]{1,0:T(8,128)(2,1)S(1)}, u32[]{:S(2)}, u32[]{:S(2)}) %collective-permute-start.25) | collective-permute-done | bytes 57376 | tf_op jit(solution)/shard_map/ppermute | solution.py:15
  112.6 1.2 collective-permute-done.26
  114.0 4.4 %fusion.114 = (bf16[32,2048]{1,0:T(8,128)(2,1)S(1)}, f32[32,2048]{1,0:T(8,128)S(1)}) fusion(bf16[1792,2048]{1,0:T(8,128)(2,1)} %bitcast.108, f32[32,1792]{1,0:T(8,128)S(1)} %get-tuple-element.10, f32[1792]{0:T(1024)S(1)} %fusion.83), kind=kOutput, calls=%fused_computation.174 | convolution fusion | flops 235061248 | bytes 7969792 | tf_op jit(solution)/shard_map/dot_general | solution.py:79
  118.5 1.8 %collective-permute-start.28 = (bf16[32,2176]{1,0:T(8,128)(2,1)S(1)}, bf16[32,2176]{1,0:T(8,128)(2,1)S(1)}, u32[]{:S(2)}, u32[]{:S(2)}) collective-permute-start(bf16[32,2176]{1,0:T(8,128)(2,1)S(1)} %pad_maximum_fusion.3), channel_id=1, source_target_pairs={{0,1},{1,0},{2,3},{3,2},{4,5},{5,4},{6,7},{7,6},{8,9},{9,8},{10,11... | collective-permute-start | bytes 417800 | tf_op jit(solution)/shard_map/ppermute | solution.py:15
  120.4 4.0 %collective-permute-done.28 = bf16[32,2176]{1,0:T(8,128)(2,1)S(1)} collective-permute-done((bf16[32,2176]{1,0:T(8,128)(2,1)S(1)}, bf16[32,2176]{1,0:T(8,128)(2,1)S(1)}, u32[]{:S(2)}, u32[]{:S(2)}) %collective-permute-start.28) | collective-permute-done | bytes 139296 | tf_op jit(solution)/shard_map/ppermute | solution.py:15
  124.7 2.9 %fusion.47 = bf16[32,1,1792]{2,0,1:T(8,128)(2,1)S(1)} fusion(bf16[1,1,1024,1792]{3,2,1,0:T(8,128)(2,1)} %param.11, f32[32]{0:T(128)S(1)} %get-tuple-element.21, f32[32,2048]{1,0:T(8,128)S(1)} %add_multiply_fusion, s32[32]{0:T(128)S(1)} %fusion.84), kind=kOutput, calls=%fused_computation.22 | convolution fusion | flops 121594880 | bytes 4047104 | tf_op jit(solution)/shard_map/dot_general | solution.py:119
  127.6 0.5 broadcast.221
  128.1 0.7 reduce.3
  128.8 0.7 reshape.272
  129.5 5.7 %all-to-all-start = ((bf16[32,2,896]{2,1,0:T(2,128)(2,1)}), bf16[32,2,896]{2,1,0:T(2,128)(2,1)S(1)}, u32[]{:S(2)}, u32[]{:S(2)}) async-start(bf16[32,2,896]{2,1,0:T(2,128)(2,1)} %reshape.272), calls=%async_computation | async-start | bytes 229376 | tf_op jit(solution)/shard_map/all_to_all | solution.py:121
  135.2 1.8 %collective-permute-start.27 = (f32[1,1792]{1,0:T(1,128)S(1)}, f32[1,1792]{1,0:T(1,128)S(1)}, u32[]{:S(2)}, u32[]{:S(2)}) collective-permute-start(f32[1,1792]{1,0:T(1,128)S(1)} %broadcast_in_dim.137), channel_id=1, source_target_pairs={{0,1},{1,0},{2,3},{3,2},{4,5},{5,4},{6,7},{7,6},{8,9},{9,8},{10,11... | collective-permute-start | bytes 21512 | tf_op jit(solution)/shard_map/ppermute | solution.py:15
  137.1 6.4 %all-to-all-done = bf16[32,2,896]{2,1,0:T(2,128)(2,1)S(1)} async-done(((bf16[32,2,896]{2,1,0:T(2,128)(2,1)}), bf16[32,2,896]{2,1,0:T(2,128)(2,1)S(1)}, u32[]{:S(2)}, u32[]{:S(2)}) %all-to-all-start) | async-done | bytes 114720 | tf_op jit(solution)/shard_map/all_to_all | solution.py:121
  143.7 0.6 fusion.80
  (88 shorter events, 5.4 us)
Async XLA Ops:
  3.2 4.7 %collective-permute-start = (bf16[1,1920]{1,0:T(2,128)(2,1)S(1)}, bf16[1,1920]{1,0:T(2,128)(2,1)S(1)}, u32[]{:S(2)}, u32[]{:S(2)}) collective-permute-start(bf16[1,1920]{1,0:T(2,128)(2,1)S(1)} %get-tuple-element.33), channel_id=1, source_target_pairs={{0,1},{1,0},{2,3},{3,2},{4,5},{5,4},{6,7},{7,6},{8,9},{9,8},{10,11... | collective-permute-start | bytes 11528 | tf_op jit(solution)/shard_map/ppermute | solution.py:15
  7.9 4.7 %collective-permute-start.1 = (bf16[2,1920]{1,0:T(2,128)(2,1)S(1)}, bf16[2,1920]{1,0:T(2,128)(2,1)S(1)}, u32[]{:S(2)}, u32[]{:S(2)}) collective-permute-start(bf16[2,1920]{1,0:T(2,128)(2,1)S(1)} %pad_maximum_fusion.7), channel_id=1, source_target_pairs={{0,2},{1,3},{2,0},{3,1},{4,6},{5,7},{6,4},{7,5},{8,10},{9,11},{10,... | collective-permute-start | bytes 23048 | tf_op jit(solution)/shard_map/ppermute | solution.py:15
  12.7 12.7 %collective-permute-start.2 = (bf16[4,1920]{1,0:T(4,128)(2,1)S(1)}, bf16[4,1920]{1,0:T(4,128)(2,1)S(1)}, u32[]{:S(2)}, u32[]{:S(2)}) collective-permute-start(bf16[4,1920]{1,0:T(4,128)(2,1)S(1)} %pad_maximum_fusion.4), channel_id=1, source_target_pairs={{0,8},{4,12},{8,0},{12,4},{16,24},{20,28},{24,16},{28,20},{1,9},{5... | collective-permute-start | bytes 46088 | tf_op jit(solution)/shard_map/ppermute | solution.py:15
  14.6 10.8 %collective-permute-start.3 = (bf16[4,1920]{1,0:T(4,128)(2,1)S(1)}, bf16[4,1920]{1,0:T(4,128)(2,1)S(1)}, u32[]{:S(2)}, u32[]{:S(2)}) collective-permute-start(bf16[4,1920]{1,0:T(4,128)(2,1)S(1)} %pad_maximum_fusion.4), channel_id=1, source_target_pairs={{0,16},{4,20},{8,24},{12,28},{16,0},{20,4},{24,8},{28,12},{1,17},{... | collective-permute-start | bytes 46088 | tf_op jit(solution)/shard_map/ppermute | solution.py:15
  16.1 9.3 %collective-permute-start.4 = (bf16[4,1920]{1,0:T(4,128)(2,1)S(1)}, bf16[4,1920]{1,0:T(4,128)(2,1)S(1)}, u32[]{:S(2)}, u32[]{:S(2)}) collective-permute-start(bf16[4,1920]{1,0:T(4,128)(2,1)S(1)} %pad_maximum_fusion.4), channel_id=1, source_target_pairs={{0,24},{4,28},{8,16},{12,20},{16,8},{20,12},{24,0},{28,4},{1,25},{... | collective-permute-start | bytes 46088 | tf_op jit(solution)/shard_map/ppermute | solution.py:15
  25.5 1.3 collective-permute-start.5
  31.8 6.0 %collective-permute-start.6 = (bf16[32,2176]{1,0:T(8,128)(2,1)S(1)}, bf16[32,2176]{1,0:T(8,128)(2,1)S(1)}, u32[]{:S(2)}, u32[]{:S(2)}) collective-permute-start(bf16[32,2176]{1,0:T(8,128)(2,1)S(1)} %pad_maximum_fusion), channel_id=1, source_target_pairs={{0,1},{1,0},{2,3},{3,2},{4,5},{5,4},{6,7},{7,6},{8,9},{9,8},{10,11... | collective-permute-start | bytes 417800 | tf_op jit(solution)/shard_map/ppermute | solution.py:15
  40.9 1.3 collective-permute-start.7
  42.2 5.3 %collective-permute-start.10 = (bf16[16,1792]{1,0:T(8,128)(2,1)S(1)}, bf16[16,1792]{1,0:T(8,128)(2,1)S(1)}, u32[]{:S(2)}, u32[]{:S(2)}) collective-permute-start(bf16[16,1792]{1,0:T(8,128)(2,1)S(1)} %fusion.62), channel_id=1, source_target_pairs={{0,24},{4,28},{8,16},{12,20},{16,8},{20,12},{24,0},{28,4},{1,25},{... | collective-permute-start | bytes 172040 | tf_op jit(solution)/shard_map/ppermute | solution.py:15
  44.9 4.2 %collective-permute-start.8 = (bf16[16,1792]{1,0:T(8,128)(2,1)S(1)}, bf16[16,1792]{1,0:T(8,128)(2,1)S(1)}, u32[]{:S(2)}, u32[]{:S(2)}) collective-permute-start(bf16[16,1792]{1,0:T(8,128)(2,1)S(1)} %fusion.62), channel_id=1, source_target_pairs={{0,8},{4,12},{8,0},{12,4},{16,24},{20,28},{24,16},{28,20},{1,9},{5... | collective-permute-start | bytes 172040 | tf_op jit(solution)/shard_map/ppermute | solution.py:15
  45.4 4.2 %collective-permute-start.9 = (bf16[16,1792]{1,0:T(8,128)(2,1)S(1)}, bf16[16,1792]{1,0:T(8,128)(2,1)S(1)}, u32[]{:S(2)}, u32[]{:S(2)}) collective-permute-start(bf16[16,1792]{1,0:T(8,128)(2,1)S(1)} %fusion.62), channel_id=1, source_target_pairs={{0,16},{4,20},{8,24},{12,28},{16,0},{20,4},{24,8},{28,12},{1,17},{... | collective-permute-start | bytes 172040 | tf_op jit(solution)/shard_map/ppermute | solution.py:15
  49.6 5.1 %collective-permute-start.11 = (bf16[16,1792]{1,0:T(8,128)(2,1)S(1)}, bf16[16,1792]{1,0:T(8,128)(2,1)S(1)}, u32[]{:S(2)}, u32[]{:S(2)}) collective-permute-start(bf16[16,1792]{1,0:T(8,128)(2,1)S(1)} %add_convert_fusion.5), channel_id=1, source_target_pairs={{0,2},{1,3},{2,0},{3,1},{4,6},{5,7},{6,4},{7,5},{8,10},{9,11},{10,... | collective-permute-start | bytes 172040 | tf_op jit(solution)/shard_map/ppermute | solution.py:15
  54.8 1.3 collective-permute-start.12
  60.8 5.8 %collective-permute-start.13 = (bf16[32,2176]{1,0:T(8,128)(2,1)S(1)}, bf16[32,2176]{1,0:T(8,128)(2,1)S(1)}, u32[]{:S(2)}, u32[]{:S(2)}) collective-permute-start(bf16[32,2176]{1,0:T(8,128)(2,1)S(1)} %pad_maximum_fusion.1), channel_id=1, source_target_pairs={{0,1},{1,0},{2,3},{3,2},{4,5},{5,4},{6,7},{7,6},{8,9},{9,8},{10,11... | collective-permute-start | bytes 417800 | tf_op jit(solution)/shard_map/ppermute | solution.py:15
  69.7 1.3 collective-permute-start.14
  71.1 4.2 %collective-permute-start.15 = (bf16[16,1792]{1,0:T(8,128)(2,1)S(1)}, bf16[16,1792]{1,0:T(8,128)(2,1)S(1)}, u32[]{:S(2)}, u32[]{:S(2)}) collective-permute-start(bf16[16,1792]{1,0:T(8,128)(2,1)S(1)} %fusion.61), channel_id=1, source_target_pairs={{0,8},{4,12},{8,0},{12,4},{16,24},{20,28},{24,16},{28,20},{1,9},{5... | collective-permute-start | bytes 172040 | tf_op jit(solution)/shard_map/ppermute | solution.py:15
  72.6 4.8 %collective-permute-start.16 = (bf16[16,1792]{1,0:T(8,128)(2,1)S(1)}, bf16[16,1792]{1,0:T(8,128)(2,1)S(1)}, u32[]{:S(2)}, u32[]{:S(2)}) collective-permute-start(bf16[16,1792]{1,0:T(8,128)(2,1)S(1)} %fusion.61), channel_id=1, source_target_pairs={{0,16},{4,20},{8,24},{12,28},{16,0},{20,4},{24,8},{28,12},{1,17},{... | collective-permute-start | bytes 172040 | tf_op jit(solution)/shard_map/ppermute | solution.py:15
  73.1 5.1 %collective-permute-start.17 = (bf16[16,1792]{1,0:T(8,128)(2,1)S(1)}, bf16[16,1792]{1,0:T(8,128)(2,1)S(1)}, u32[]{:S(2)}, u32[]{:S(2)}) collective-permute-start(bf16[16,1792]{1,0:T(8,128)(2,1)S(1)} %fusion.61), channel_id=1, source_target_pairs={{0,24},{4,28},{8,16},{12,20},{16,8},{20,12},{24,0},{28,4},{1,25},{... | collective-permute-start | bytes 172040 | tf_op jit(solution)/shard_map/ppermute | solution.py:15
  78.2 5.2 %collective-permute-start.18 = (bf16[16,1792]{1,0:T(8,128)(2,1)S(1)}, bf16[16,1792]{1,0:T(8,128)(2,1)S(1)}, u32[]{:S(2)}, u32[]{:S(2)}) collective-permute-start(bf16[16,1792]{1,0:T(8,128)(2,1)S(1)} %add_convert_fusion.3), channel_id=1, source_target_pairs={{0,2},{1,3},{2,0},{3,1},{4,6},{5,7},{6,4},{7,5},{8,10},{9,11},{10,... | collective-permute-start | bytes 172040 | tf_op jit(solution)/shard_map/ppermute | solution.py:15
  83.4 1.3 collective-permute-start.19
  89.4 5.8 %collective-permute-start.20 = (bf16[32,2176]{1,0:T(8,128)(2,1)S(1)}, bf16[32,2176]{1,0:T(8,128)(2,1)S(1)}, u32[]{:S(2)}, u32[]{:S(2)}) collective-permute-start(bf16[32,2176]{1,0:T(8,128)(2,1)S(1)} %pad_maximum_fusion.2), channel_id=1, source_target_pairs={{0,1},{1,0},{2,3},{3,2},{4,5},{5,4},{6,7},{7,6},{8,9},{9,8},{10,11... | collective-permute-start | bytes 417800 | tf_op jit(solution)/shard_map/ppermute | solution.py:15
  98.4 1.3 collective-permute-start.21
  99.7 4.2 %collective-permute-start.22 = (bf16[16,1792]{1,0:T(8,128)(2,1)S(1)}, bf16[16,1792]{1,0:T(8,128)(2,1)S(1)}, u32[]{:S(2)}, u32[]{:S(2)}) collective-permute-start(bf16[16,1792]{1,0:T(8,128)(2,1)S(1)} %fusion.60), channel_id=1, source_target_pairs={{0,8},{4,12},{8,0},{12,4},{16,24},{20,28},{24,16},{28,20},{1,9},{5... | collective-permute-start | bytes 172040 | tf_op jit(solution)/shard_map/ppermute | solution.py:15
  100.4 4.2 %collective-permute-start.23 = (bf16[16,1792]{1,0:T(8,128)(2,1)S(1)}, bf16[16,1792]{1,0:T(8,128)(2,1)S(1)}, u32[]{:S(2)}, u32[]{:S(2)}) collective-permute-start(bf16[16,1792]{1,0:T(8,128)(2,1)S(1)} %fusion.60), channel_id=1, source_target_pairs={{0,16},{4,20},{8,24},{12,28},{16,0},{20,4},{24,8},{28,12},{1,17},{... | collective-permute-start | bytes 172040 | tf_op jit(solution)/shard_map/ppermute | solution.py:15
  101.8 5.1 %collective-permute-start.24 = (bf16[16,1792]{1,0:T(8,128)(2,1)S(1)}, bf16[16,1792]{1,0:T(8,128)(2,1)S(1)}, u32[]{:S(2)}, u32[]{:S(2)}) collective-permute-start(bf16[16,1792]{1,0:T(8,128)(2,1)S(1)} %fusion.60), channel_id=1, source_target_pairs={{0,24},{4,28},{8,16},{12,20},{16,8},{20,12},{24,0},{28,4},{1,25},{... | collective-permute-start | bytes 172040 | tf_op jit(solution)/shard_map/ppermute | solution.py:15
  107.0 5.5 %collective-permute-start.25 = (bf16[16,1792]{1,0:T(8,128)(2,1)S(1)}, bf16[16,1792]{1,0:T(8,128)(2,1)S(1)}, u32[]{:S(2)}, u32[]{:S(2)}) collective-permute-start(bf16[16,1792]{1,0:T(8,128)(2,1)S(1)} %add_convert_fusion.1), channel_id=1, source_target_pairs={{0,2},{1,3},{2,0},{3,1},{4,6},{5,7},{6,4},{7,5},{8,10},{9,11},{10,... | collective-permute-start | bytes 172040 | tf_op jit(solution)/shard_map/ppermute | solution.py:15
  112.5 1.3 collective-permute-start.26
  118.5 5.8 %collective-permute-start.28 = (bf16[32,2176]{1,0:T(8,128)(2,1)S(1)}, bf16[32,2176]{1,0:T(8,128)(2,1)S(1)}, u32[]{:S(2)}, u32[]{:S(2)}) collective-permute-start(bf16[32,2176]{1,0:T(8,128)(2,1)S(1)} %pad_maximum_fusion.3), channel_id=1, source_target_pairs={{0,1},{1,0},{2,3},{3,2},{4,5},{5,4},{6,7},{7,6},{8,9},{9,8},{10,11... | collective-permute-start | bytes 417800 | tf_op jit(solution)/shard_map/ppermute | solution.py:15
  129.5 14.0 %all-to-all-start = ((bf16[32,2,896]{2,1,0:T(2,128)(2,1)}), bf16[32,2,896]{2,1,0:T(2,128)(2,1)S(1)}, u32[]{:S(2)}, u32[]{:S(2)}) async-start(bf16[32,2,896]{2,1,0:T(2,128)(2,1)} %reshape.272), calls=%async_computation | async-start | bytes 229376 | tf_op jit(solution)/shard_map/all_to_all | solution.py:121
  135.2 8.5 %collective-permute-start.27 = (f32[1,1792]{1,0:T(1,128)S(1)}, f32[1,1792]{1,0:T(1,128)S(1)}, u32[]{:S(2)}, u32[]{:S(2)}) collective-permute-start(f32[1,1792]{1,0:T(1,128)S(1)} %broadcast_in_dim.137), channel_id=1, source_target_pairs={{0,1},{1,0},{2,3},{3,2},{4,5},{5,4},{6,7},{7,6},{8,9},{9,8},{10,11... | collective-permute-start | bytes 21512 | tf_op jit(solution)/shard_map/ppermute | solution.py:15

commit v2 on v1

--- a/solution.py
+++ b/solution.py
@@ -1,6 +1,10 @@
+import functools
+
 import jax
 import jax.numpy as jnp
 from jax import lax
+from jax.experimental import pallas as pl
+from jax.experimental.pallas import tpu as pltpu
 from jax.sharding import PartitionSpec as P
 
 TOP = 8
@@ -21,6 +25,76 @@
 
 def rounded(values):
     return values.astype(jnp.bfloat16)
+
+
+WHOLE = pl.BlockSpec(memory_space=pltpu.VMEM)
+LANES = 128
+
+
+def in_vmem(shape, dtype):
+    return pltpu.VMEM(shape, dtype)
+
+
+def kernel_call(body, out_shape, operands, flops):
+    operands = [pltpu.with_memory_space_constraint(o, pltpu.VMEM) for o in operands]
+    read = sum(o.size * o.dtype.itemsize for o in operands)
+    return pl.pallas_call(
+        body,
+        out_shape=out_shape,
+        in_specs=[WHOLE] * len(operands),
+        out_specs=jax.tree.map(lambda _: WHOLE, out_shape),
+        compiler_params=pltpu.CompilerParams(vmem_limit_bytes=24 * 2**20),
+        cost_estimate=pl.CostEstimate(flops=flops, bytes_accessed=read, transcendentals=0),
+    )(*operands)
+
+
+def column_blocks(width):
+    block = next(b for b in (512, 256, 128, width) if width % b == 0)
+    return [slice(start, start + block) for start in range(0, width, block)]
+
+
+def gate_up_body(has_update, *refs):
+    if has_update:
+        residual_ref, own_ref, other_ref, gain_ref, weight_ref, kept_ref, product_ref, message_ref = refs
+        update = jnp.concatenate([own_ref[...], other_ref[...]], axis=0)
+        residual = residual_ref[...] + widened(update)
+        kept_ref[...] = residual
+    else:
+        residual_ref, gain_ref, weight_ref, product_ref, message_ref = refs
+        residual = residual_ref[...]
+    scaled = rounded(residual * gain_ref[...])
+    width = weight_ref.shape[1]
+    for columns in column_blocks(width):
+        product = jnp.dot(scaled, weight_ref[:, columns], preferred_element_type=jnp.float32)
+        product_ref[:, columns] = product
+        message_ref[:, columns] = rounded(product)
+    square_sum = jnp.sum(residual * residual, axis=1, keepdims=True)
+    square_high = widened(rounded(square_sum))
+    lane = lax.broadcasted_iota(jnp.int32, (residual.shape[0], LANES), 1)
+    tail = jnp.where(lane == 0, square_high, square_sum - square_high)
+    message_ref[:, width:] = rounded(tail)
+
+
+def down_body(model_width, last, product_ref, message_ref, swapped_ref, weight_ref, mixing_ref, *out_refs):
+    width = product_ref.shape[1]
+    part = width // 2
+    tails = widened(message_ref[:, width:]) + widened(swapped_ref[:, width:])
+    square_sum = tails[:, 0:1] + tails[:, 1:2]
+    scale = lax.rsqrt(square_sum / model_width + 1e-06)
+    whole = product_ref[...] + widened(swapped_ref[:, :width])
+    gate = whole[:, :part] * scale
+    up = whole[:, part:] * scale
+    activated = rounded(gate / (1.0 + jnp.exp(-gate)) * up)
+    mixing = mixing_ref[...]
+    half = mixing.shape[0] // 2
+    for columns in column_blocks(weight_ref.shape[1]):
+        term = jnp.dot(activated, weight_ref[:, columns], preferred_element_type=jnp.float32)
+        update = widened(rounded(term)) * mixing
+        if last:
+            out_refs[0][:, columns] = rounded(update)
+        else:
+            out_refs[0][:, columns] = update[:half]
+            out_refs[1][:, columns] = rounded(update[half:])
 
 
 def dense_steps(hidden_in, norm_gain, expert_ids, gate_levels, w_gate_up, w_down):
@@ -43,58 +117,74 @@
 
     gain_half = half_of(norm_gain[None, :], True)
 
-    level_vals = gate_levels[:, 0, :].astype(jnp.float32)
-    shares = level_vals / jnp.sum(level_vals, axis=-1, keepdims=True)
-    matches = expert_ids[:, 0, :, None] == jnp.arange(rack_count, dtype=jnp.int32)
-    own_mixing = rounded(jnp.sum(jnp.where(matches, shares[:, :, None], jnp.float32(0.0)), axis=1))
-    own_mixing = own_mixing.reshape(1, STEPS * rack_count)
-    mixing_width = -(-STEPS * rack_count // 128) * 128
-    own_mixing = jnp.pad(own_mixing, ((0, 0), (0, mixing_width - STEPS * rack_count)))
-
-    rows = jnp.concatenate([half_of(hidden_in, True), own_mixing], axis=1)
-    other = jnp.concatenate([half_of(hidden_in, False), own_mixing], axis=1)
-    rows = jnp.concatenate([rows, exchanged(other, "expert", 1)], axis=0)
-    rows = jnp.concatenate(
-        [rows] + [exchanged(rows, "expert", mask) for mask in range(2, group_count, 2)], axis=0
-    )
-    rows = jnp.concatenate(
-        [rows] + [exchanged(rows, "rack", mask) for mask in range(2, rack_count, 2)], axis=0
-    )
-    rows = jnp.concatenate([rows, exchanged(rows, "rack", 1)], axis=0)
+    routing = rounded(jnp.concatenate([expert_ids.reshape(1, -1), gate_levels.reshape(1, -1)], axis=1))
+    route_width = STEPS * TOP
+    message_width = -(-(half_width + 2 * route_width) // 2048) * 2048
+    routing = jnp.pad(routing, ((0, 0), (0, message_width - half_width - 2 * route_width)))
+    messages = jnp.concatenate([hidden_in.reshape(2, half_width), jnp.tile(routing, (2, 1))], axis=1)
+    messages = messages.reshape(1, 2, message_width // 128, 128)
+    messages = jnp.broadcast_to(messages, (token_count // 2,) + messages.shape[1:])
+    messages = messages.reshape(token_count, message_width // 128, 128)
+    messages = lax.all_to_all(messages, ("rack", "expert"), split_axis=0, concat_axis=0, tiled=True)
+    messages = messages.reshape(token_count, message_width)
+    token_ids = jnp.arange(token_count, dtype=jnp.int32)
+    token_rack = token_ids // group_count
+    place_of_token = (
+        (token_rack % 2 ^ rack_index % 2) * core_rows
+        + token_rack // 2 * group_count
+        + token_ids % group_count
+    )
     own_place = rack_index // 2 * group_count + group_index
     places = jnp.arange(token_count, dtype=jnp.int32)
-    to_absolute = rounded(places[:, None] == (places[None, :] ^ own_place))
-    rows = jnp.dot(to_absolute, rows, preferred_element_type=jnp.float32)
+    to_places = rounded(places[:, None] == place_of_token[None, :])
+    rows = jnp.dot(to_places, messages, preferred_element_type=jnp.float32)
     residual = rows[:, :half_width]
-    all_mixing = rows[:, half_width : half_width + STEPS * rack_count]
-    own_expert = jnp.arange(rack_count, dtype=jnp.int32) == rack_index
-    mixing = jnp.sum(
-        jnp.where(own_expert, all_mixing.reshape(token_count, STEPS, rack_count), 0.0), axis=2
-    )
-
+    all_ids = rows[:, half_width : half_width + route_width].reshape(token_count, STEPS, TOP)
+    all_levels = rows[:, half_width + route_width : half_width + 2 * route_width].reshape(
+        token_count, STEPS, TOP
+    )
+    shares = all_levels / jnp.sum(all_levels, axis=-1, keepdims=True)
+    mixing = jnp.sum(jnp.where(all_ids == rack_index.astype(jnp.float32), shares, 0.0), axis=2)
+    mixing = widened(rounded(mixing))
+
+    product_width = 2 * part_width
+    product_flops = 2 * token_count * half_width * product_width
+    sent = received = None
     for step_index in range(STEPS):
         last = step_index == STEPS - 1
-        square_sum = jnp.sum(residual * residual, axis=1, keepdims=True)
-        scaled = rounded(residual * gain_half)
-        gate_up = jnp.dot(scaled, gate_up_weight, preferred_element_type=jnp.float32)
-        square_high = rounded(lax.reduce_precision(square_sum, 8, 7))
-        square_low = rounded(square_sum - lax.reduce_precision(square_sum, 8, 7))
-        lane = lax.broadcasted_iota(jnp.int32, (token_count, 128), 1)
-        tail = jnp.where(lane == 0, square_high, square_low)
-        swapped_rows = exchanged(
-            jnp.concatenate([rounded(gate_up), tail], axis=1), "expert", 1
-        )
-        gate_up = gate_up + widened(swapped_rows[:, : 2 * part_width])
-        other_sum = widened(swapped_rows[:, 2 * part_width : 2 * part_width + 1]) + widened(
-            swapped_rows[:, 2 * part_width + 1 : 2 * part_width + 2]
-        )
-        gate_up = gate_up * lax.rsqrt((square_sum + other_sum) / model_width + 1e-06)
-        activated = rounded(jax.nn.silu(gate_up[:, :part_width]) * gate_up[:, part_width:])
-        term = rounded(jnp.dot(activated, down_weight, preferred_element_type=jnp.float32))
-        update = widened(term) * mixing[:, step_index : step_index + 1]
+        has_update = step_index > 0
+        update_rows = [sent, received] if has_update else []
+        kept = [in_vmem((token_count, half_width), jnp.float32)] if has_update else []
+        *kept, product, message = kernel_call(
+            functools.partial(gate_up_body, has_update),
+            kept
+            + [
+                in_vmem((token_count, product_width), jnp.float32),
+                in_vmem((token_count, product_width + LANES), jnp.bfloat16),
+            ],
+            [residual] + update_rows + [gain_half, gate_up_weight],
+            product_flops,
+        )
+        if has_update:
+            residual = kept[0]
+        swapped_rows = exchanged(message, "expert", 1)
         if last:
+            out_shape = [in_vmem((token_count, half_width), jnp.bfloat16)]
+        else:
+            out_shape = [
+                in_vmem((core_rows, half_width), jnp.float32),
+                in_vmem((core_rows, half_width), jnp.bfloat16),
+            ]
+        outs = kernel_call(
+            functools.partial(down_body, model_width, last),
+            out_shape,
+            [product, message, swapped_rows, down_weight, mixing[:, step_index : step_index + 1]],
+            product_flops // 2,
+        )
+        if last:
+            update = outs[0]
             break
-        update = update[:core_rows] + widened(exchanged(rounded(update[core_rows:]), "rack", 1))
+        update = outs[0] + widened(exchanged(outs[1], "rack", 1))
         sent = rounded(update)
         update = widened(sent)
         for mask in range(2, rack_count, 2):
@@ -104,21 +194,16 @@
         for mask in range(2, group_count, 2):
             update = update + widened(exchanged(sent, "expert", mask))
         sent = rounded(update)
-        update = jnp.concatenate([sent, exchanged(sent, "rack", 1)], axis=0)
-        residual = residual + widened(update)
-
-    token_ids = jnp.arange(token_count, dtype=jnp.int32)
-    token_rack = token_ids // group_count
-    place_of_token = (
-        (token_rack % 2 ^ rack_index % 2) * core_rows
-        + token_rack // 2 * group_count
-        + token_ids % group_count
-    )
+        received = exchanged(sent, "rack", 1)
+
     to_tokens = rounded(place_of_token[:, None] == places[None, :])
     outgoing = rounded(
-        jnp.dot(to_tokens, rounded(update), preferred_element_type=jnp.float32)
-    )
-    arrived = lax.all_to_all(outgoing, ("rack", "expert"), split_axis=0, concat_axis=0, tiled=True)
+        jnp.dot(to_tokens, update, preferred_element_type=jnp.float32)
+    )
+    arrived = lax.all_to_all(
+        outgoing.reshape(token_count, half_width // 128, 128),
+        ("rack", "expert"), split_axis=0, concat_axis=0, tiled=True,
+    ).reshape(token_count, half_width)
     arrived = widened(arrived)
     is_first = token_ids[:, None] % 2 == 0
     update = jnp.concatenate(

time: 145 us -> 121 us (0.83)
  matrix products: 29.1 us -> 0.39 us
  Pallas kernels: 0 us -> 8.93 us
  local copies, waits for them, and re-layouts: 12.6 us -> 19.1 us
  starting transfers between devices: 44.6 us -> 38.9 us
  other arithmetic: 6.43 us -> 3.43 us
  waiting for transfers between devices: 51.3 us -> 49.7 us
    dot_general x9 -> x2, matrix products: 29.1 us -> 0.39 us  [the longest x1 0.22 us: dense_steps(): jnp.dot(to_tokens, update, preferred_element_type=jnp.float32)]
    ppermute x29 -> x23, starting transfers between devices: 38.9 us -> 26 us  [exchanged(): lax.ppermute(shard, axis, [(i, i ^ mask) for i in range(lax.axis_size(axi...]
    pallas_call x0 -> x8, Pallas kernels: none -> 8.93 us  [kernel_call(): pl.pallas_call(body, out_shape=out_shape, in_specs=[WHOLE] * len(operands...]
    all_to_all x1 -> x2, starting transfers between devices: 5.72 us -> 12.9 us  [the longest x1 7.3 us: dense_steps(): lax.all_to_all(messages, ('rack', 'expert'), split_axis=0, concat_axis=0,...]
    unnamed x11 -> x12, local copies, waits for them, and re-layouts: 10.6 us -> 16.3 us
    reduce_sum x7 -> x1, other arithmetic: 2.29 us -> 0.13 us  [dense_steps(): jnp.sum(jnp.where(places[:, None] == own_place, residual, 0.0), axis=0, k...]
    ppermute x29 -> x23, waiting for transfers between devices: 44.9 us -> 43.2 us  [exchanged(): lax.ppermute(shard, axis, [(i, i ^ mask) for i in range(lax.axis_size(axi...]
    all_to_all x1 -> x2, waiting for transfers between devices: 6.38 us -> 6.47 us  [the longest x1 6.47 us: dense_steps(): lax.all_to_all(outgoing.reshape(token_count, half_width // 128, 128), ('r...]
  transfers between devices with their start and end apart: 30 -> 25, of which waited for: 26 -> 22; matrix products, arithmetic and copies ran while one was open for 7% -> 8% of each run, Pallas kernels for 0% -> 0%
where the time goes in v2:
time: 121 us
  waiting for transfers between devices  49.7 us (41%)
  starting transfers between devices  38.9 us (32%)
  local copies, waits for them, and re-layouts  19.1 us (16%)
  Pallas kernels  8.93 us (7%)
  other arithmetic  3.43 us (3%)
    ppermute x23, waiting for transfers between devices, exchanged(): lax.ppermute(shard, axis, [(i, i ^ mask) for i in range(lax.axis_size(axi...  43.2 us
    ppermute x23, starting transfers between devices, exchanged(): lax.ppermute(shard, axis, [(i, i ^ mask) for i in range(lax.axis_size(axi...  26 us
    unnamed x12, local copies, waits for them, and re-layouts  16.3 us
    pallas_call x8, Pallas kernels, kernel_call(): pl.pallas_call(body, out_shape=out_shape, in_specs=[WHOLE] * len(operands...  8.93 us
    all_to_all x1, starting transfers between devices, dense_steps(): lax.all_to_all(messages, ('rack', 'expert'), split_axis=0, concat_axis=0,...  7.3 us
    all_to_all x1, waiting for transfers between devices, dense_steps(): lax.all_to_all(outgoing.reshape(token_count, half_width // 128, 128), ('r...  6.47 us
    all_to_all x1, starting transfers between devices, dense_steps(): lax.all_to_all(outgoing.reshape(token_count, half_width // 128, 128), ('r...  5.59 us
  transfers between devices with their start and end apart: 25, of which 22 were waited for; matrix products, arithmetic and copies ran while one was open for 8% of the time, Pallas kernels for 0%

profile of v2, /device:TPU:0, one launch (start us, length us, event | category | flops | bytes accessed | tf_op | source)
XLA Modules:
  0.0 120.7 jit_solution(2449697291912109926)
XLA Ops:
  0.0 0.7 convert_reduce_fusion.1
  0.8 0.7 convert_reduce_fusion
  1.6 0.8 reduce.2
  2.5 0.7 broadcast_in_dim.70
  3.2 7.3 %all-to-all-start = ((bf16[32,16,128]{2,1,0:T(8,128)(2,1)}), bf16[32,16,128]{2,1,0:T(8,128)(2,1)S(1)}, u32[]{:S(2)}, u32[]{:S(2)}) async-start(bf16[32,16,128]{2,1,0:T(8,128)(2,1)} %bitcast), calls=%async_computation | async-start | bytes 262144 | tf_op jit(solution)/shard_map/all_to_all | solution.py:128
  10.5 0.7 broadcast_in_dim.71
  11.2 9.1 %copy.14 = bf16[224,8,2,1024]{3,1,2,0:T(8,128)(2,1)} copy(bf16[224,8,2,1024]{3,2,1,0:T(2,128)(2,1)} %bitcast.39) | data formatting | bytes 14680064
  20.4 0.2 fusion.5
  21.0 3.1 %copy-done = bf16[224,8,2,1024]{3,1,2,0:T(8,128)(2,1)S(1)} copy-done((bf16[224,8,2,1024]{3,1,2,0:T(8,128)(2,1)S(1)}, bf16[224,8,2,1024]{3,1,2,0:T(8,128)(2,1)}, u32[]{:S(2)}) %copy-start) | copy-done | bytes 7340056
  24.1 1.4 %shard_map.64 = (f32[32,2048]{1,0:T(8,128)S(1)}, bf16[32,2176]{1,0:T(8,128)(2,1)S(1)}) custom-call(f32[32,1792]{1,0:T(8,128)S(1)} %slice.36.refs_0_, f32[1,1792]{1,0:T(1,128)S(1)} %broadcast_select_fusion.1.refs_1_.refs_3_, bf16[1792,2048]{1,0:T(8,128)(2,1)S(1)} %bitcast.31), custom_call_target="tpu_custom_call" | custom-call | flops 234881024 | bytes 7576576 | tf_op jit(solution)/shard_map/pallas_call | solution.py:41
  25.4 1.8 %collective-permute-start = (bf16[32,2176]{1,0:T(8,128)(2,1)S(1)}, bf16[32,2176]{1,0:T(8,128)(2,1)S(1)}, u32[]{:S(2)}, u32[]{:S(2)}) collective-permute-start(bf16[32,2176]{1,0:T(8,128)(2,1)S(1)} %get-tuple-element.23.message_ref), channel_id=1, source_target_pairs={{0,1},{1,0},{2,3},{3,2},{4,5},{5,4},{6,7},{7,6},{8,9},{9,8},{10,11... | collective-permute-start | bytes 417800 | tf_op jit(solution)/shard_map/ppermute | solution.py:19
  27.3 4.0 %collective-permute-done.swapped_ref = bf16[32,2176]{1,0:T(8,128)(2,1)S(1)} collective-permute-done((bf16[32,2176]{1,0:T(8,128)(2,1)S(1)}, bf16[32,2176]{1,0:T(8,128)(2,1)S(1)}, u32[]{:S(2)}, u32[]{:S(2)}) %collective-permute-start) | collective-permute-done | bytes 139296 | tf_op jit(solution)/shard_map/ppermute | solution.py:19
  31.3 2.0 %copy-done.2 = bf16[1,1,1024,1792]{3,2,1,0:T(8,128)(2,1)S(1)} copy-done((bf16[1,1,1024,1792]{3,2,1,0:T(8,128)(2,1)S(1)}, bf16[1,1,1024,1792]{3,2,1,0:T(8,128)(2,1)}, u32[]{:S(2)}) %copy-start.2) | copy-done | bytes 3670040
  33.3 0.9 shard_map.65
  34.3 1.2 %collective-permute-done.1 = bf16[16,1792]{1,0:T(8,128)(2,1)S(1)} collective-permute-done((bf16[16,1792]{1,0:T(8,128)(2,1)S(1)}, bf16[16,1792]{1,0:T(8,128)(2,1)S(1)}, u32[]{:S(2)}, u32[]{:S(2)}) %collective-permute-start.1) | collective-permute-done | bytes 57376 | tf_op jit(solution)/shard_map/ppermute | solution.py:19
  35.5 2.6 %collective-permute-start.4 = (bf16[16,1792]{1,0:T(8,128)(2,1)S(1)}, bf16[16,1792]{1,0:T(8,128)(2,1)S(1)}, u32[]{:S(2)}, u32[]{:S(2)}) collective-permute-start(bf16[16,1792]{1,0:T(8,128)(2,1)S(1)} %add_convert_fusion.8), channel_id=1, source_target_pairs={{0,24},{4,28},{8,16},{12,20},{16,8},{20,12},{24,0},{28,4},{1,25},{... | collective-permute-start | bytes 172040 | tf_op jit(solution)/shard_map/ppermute | solution.py:19
  38.2 0.6 collective-permute-start.3
  38.7 0.4 collective-permute-start.2
  39.1 1.6 %collective-permute-done.4 = bf16[16,1792]{1,0:T(8,128)(2,1)S(1)} collective-permute-done((bf16[16,1792]{1,0:T(8,128)(2,1)S(1)}, bf16[16,1792]{1,0:T(8,128)(2,1)S(1)}, u32[]{:S(2)}, u32[]{:S(2)}) %collective-permute-start.4) | collective-permute-done | bytes 57376 | tf_op jit(solution)/shard_map/ppermute | solution.py:19
  40.7 1.7 %collective-permute-done.3 = bf16[16,1792]{1,0:T(8,128)(2,1)S(1)} collective-permute-done((bf16[16,1792]{1,0:T(8,128)(2,1)S(1)}, bf16[16,1792]{1,0:T(8,128)(2,1)S(1)}, u32[]{:S(2)}, u32[]{:S(2)}) %collective-permute-start.3) | collective-permute-done | bytes 57376 | tf_op jit(solution)/shard_map/ppermute | solution.py:19
  42.3 0.6 collective-permute-done.2
  42.9 2.4 %collective-permute-start.5 = (bf16[16,1792]{1,0:T(8,128)(2,1)S(1)}, bf16[16,1792]{1,0:T(8,128)(2,1)S(1)}, u32[]{:S(2)}, u32[]{:S(2)}) collective-permute-start(bf16[16,1792]{1,0:T(8,128)(2,1)S(1)} %add_convert_fusion.7), channel_id=1, source_target_pairs={{0,2},{1,3},{2,0},{3,1},{4,6},{5,7},{6,4},{7,5},{8,10},{9,11},{10,... | collective-permute-start | bytes 172040 | tf_op jit(solution)/shard_map/ppermute | solution.py:19
  45.4 2.7 %collective-permute-done.5 = bf16[16,1792]{1,0:T(8,128)(2,1)S(1)} collective-permute-done((bf16[16,1792]{1,0:T(8,128)(2,1)S(1)}, bf16[16,1792]{1,0:T(8,128)(2,1)S(1)}, u32[]{:S(2)}, u32[]{:S(2)}) %collective-permute-start.5) | collective-permute-done | bytes 57376 | tf_op jit(solution)/shard_map/ppermute | solution.py:19
  48.2 1.2 %collective-permute-done.6.refs_2_ = bf16[16,1792]{1,0:T(8,128)(2,1)S(1)} collective-permute-done((bf16[16,1792]{1,0:T(8,128)(2,1)S(1)}, bf16[16,1792]{1,0:T(8,128)(2,1)S(1)}, u32[]{:S(2)}, u32[]{:S(2)}) %collective-permute-start.6) | collective-permute-done | bytes 57376 | tf_op jit(solution)/shard_map/ppermute | solution.py:19
  49.4 1.4 %shard_map.66 = (f32[32,1792]{1,0:T(8,128)S(1)}, f32[32,2048]{1,0:T(8,128)S(1)}, bf16[32,2176]{1,0:T(8,128)(2,1)S(1)}) custom-call(f32[32,1792]{1,0:T(8,128)S(1)} %slice.36.refs_0_, bf16[16,1792]{1,0:T(8,128)(2,1)S(1)} %add_convert_fusion.6.refs_1_, bf16[16,1792]{1,0:T(8,128)(2,1)S(1)} %collective-permute-done.6.refs_2_, ...), custom_call_target="tpu_custom_call" | custom-call | flops 234881024 | bytes 7691264 | tf_op jit(solution)/shard_map/pallas_call | solution.py:41
  50.8 1.5 %collective-permute-start.7 = (bf16[32,2176]{1,0:T(8,128)(2,1)S(1)}, bf16[32,2176]{1,0:T(8,128)(2,1)S(1)}, u32[]{:S(2)}, u32[]{:S(2)}) collective-permute-start(bf16[32,2176]{1,0:T(8,128)(2,1)S(1)} %get-tuple-element.28.message_ref), channel_id=1, source_target_pairs={{0,1},{1,0},{2,3},{3,2},{4,5},{5,4},{6,7},{7,6},{8,9},{9,8},{10,11... | collective-permute-start | bytes 417800 | tf_op jit(solution)/shard_map/ppermute | solution.py:19
  52.3 4.3 %collective-permute-done.7.swapped_ref = bf16[32,2176]{1,0:T(8,128)(2,1)S(1)} collective-permute-done((bf16[32,2176]{1,0:T(8,128)(2,1)S(1)}, bf16[32,2176]{1,0:T(8,128)(2,1)S(1)}, u32[]{:S(2)}, u32[]{:S(2)}) %collective-permute-start.7) | collective-permute-done | bytes 139296 | tf_op jit(solution)/shard_map/ppermute | solution.py:19
  56.6 0.9 shard_map.67
  57.5 1.2 %collective-permute-done.8 = bf16[16,1792]{1,0:T(8,128)(2,1)S(1)} collective-permute-done((bf16[16,1792]{1,0:T(8,128)(2,1)S(1)}, bf16[16,1792]{1,0:T(8,128)(2,1)S(1)}, u32[]{:S(2)}, u32[]{:S(2)}) %collective-permute-start.8) | collective-permute-done | bytes 57376 | tf_op jit(solution)/shard_map/ppermute | solution.py:19
  58.8 1.5 %collective-permute-start.11 = (bf16[16,1792]{1,0:T(8,128)(2,1)S(1)}, bf16[16,1792]{1,0:T(8,128)(2,1)S(1)}, u32[]{:S(2)}, u32[]{:S(2)}) collective-permute-start(bf16[16,1792]{1,0:T(8,128)(2,1)S(1)} %add_convert_fusion.5), channel_id=1, source_target_pairs={{0,24},{4,28},{8,16},{12,20},{16,8},{20,12},{24,0},{28,4},{1,25},{... | collective-permute-start | bytes 172040 | tf_op jit(solution)/shard_map/ppermute | solution.py:19
  60.3 0.9 collective-permute-start.10
  61.2 1.1 collective-permute-start.9
  62.3 1.6 %collective-permute-done.11 = bf16[16,1792]{1,0:T(8,128)(2,1)S(1)} collective-permute-done((bf16[16,1792]{1,0:T(8,128)(2,1)S(1)}, bf16[16,1792]{1,0:T(8,128)(2,1)S(1)}, u32[]{:S(2)}, u32[]{:S(2)}) %collective-permute-start.11) | collective-permute-done | bytes 57376 | tf_op jit(solution)/shard_map/ppermute | solution.py:19
  64.0 1.0 collective-permute-done.10
  64.9 0.4 collective-permute-done.9
  65.4 2.5 %collective-permute-start.12 = (bf16[16,1792]{1,0:T(8,128)(2,1)S(1)}, bf16[16,1792]{1,0:T(8,128)(2,1)S(1)}, u32[]{:S(2)}, u32[]{:S(2)}) collective-permute-start(bf16[16,1792]{1,0:T(8,128)(2,1)S(1)} %add_convert_fusion.4), channel_id=1, source_target_pairs={{0,2},{1,3},{2,0},{3,1},{4,6},{5,7},{6,4},{7,5},{8,10},{9,11},{10,... | collective-permute-start | bytes 172040 | tf_op jit(solution)/shard_map/ppermute | solution.py:19
  67.9 3.6 %collective-permute-done.12 = bf16[16,1792]{1,0:T(8,128)(2,1)S(1)} collective-permute-done((bf16[16,1792]{1,0:T(8,128)(2,1)S(1)}, bf16[16,1792]{1,0:T(8,128)(2,1)S(1)}, u32[]{:S(2)}, u32[]{:S(2)}) %collective-permute-start.12) | collective-permute-done | bytes 57376 | tf_op jit(solution)/shard_map/ppermute | solution.py:19
  71.6 1.2 %collective-permute-done.13.refs_2_ = bf16[16,1792]{1,0:T(8,128)(2,1)S(1)} collective-permute-done((bf16[16,1792]{1,0:T(8,128)(2,1)S(1)}, bf16[16,1792]{1,0:T(8,128)(2,1)S(1)}, u32[]{:S(2)}, u32[]{:S(2)}) %collective-permute-start.13) | collective-permute-done | bytes 57376 | tf_op jit(solution)/shard_map/ppermute | solution.py:19
  72.8 1.4 %shard_map.68 = (f32[32,1792]{1,0:T(8,128)S(1)}, f32[32,2048]{1,0:T(8,128)S(1)}, bf16[32,2176]{1,0:T(8,128)(2,1)S(1)}) custom-call(f32[32,1792]{1,0:T(8,128)S(1)} %get-tuple-element.26.refs_0_, bf16[16,1792]{1,0:T(8,128)(2,1)S(1)} %add_convert_fusion.3.refs_1_, bf16[16,1792]{1,0:T(8,128)(2,1)S(1)} %collective-permute-done.13.refs_2_, ...), custom_call_target="tpu_custom_call" | custom-call | flops 234881024 | bytes 7691264 | tf_op jit(solution)/shard_map/pallas_call | solution.py:41
  74.2 0.3 collective-permute-start.14
  74.5 5.5 %collective-permute-done.14.swapped_ref = bf16[32,2176]{1,0:T(8,128)(2,1)S(1)} collective-permute-done((bf16[32,2176]{1,0:T(8,128)(2,1)S(1)}, bf16[32,2176]{1,0:T(8,128)(2,1)S(1)}, u32[]{:S(2)}, u32[]{:S(2)}) %collective-permute-start.14) | collective-permute-done | bytes 139296 | tf_op jit(solution)/shard_map/ppermute | solution.py:19
  80.0 0.9 shard_map.69
  80.9 1.2 %collective-permute-done.15 = bf16[16,1792]{1,0:T(8,128)(2,1)S(1)} collective-permute-done((bf16[16,1792]{1,0:T(8,128)(2,1)S(1)}, bf16[16,1792]{1,0:T(8,128)(2,1)S(1)}, u32[]{:S(2)}, u32[]{:S(2)}) %collective-permute-start.15) | collective-permute-done | bytes 57376 | tf_op jit(solution)/shard_map/ppermute | solution.py:19
  82.2 1.1 collective-permute-start.18
  83.3 0.6 collective-permute-start.17
  83.9 1.8 %collective-permute-start.16 = (bf16[16,1792]{1,0:T(8,128)(2,1)S(1)}, bf16[16,1792]{1,0:T(8,128)(2,1)S(1)}, u32[]{:S(2)}, u32[]{:S(2)}) collective-permute-start(bf16[16,1792]{1,0:T(8,128)(2,1)S(1)} %add_convert_fusion.2), channel_id=1, source_target_pairs={{0,8},{4,12},{8,0},{12,4},{16,24},{20,28},{24,16},{28,20},{1,9},{5... | collective-permute-start | bytes 172040 | tf_op jit(solution)/shard_map/ppermute | solution.py:19
  85.7 1.9 %collective-permute-done.18 = bf16[16,1792]{1,0:T(8,128)(2,1)S(1)} collective-permute-done((bf16[16,1792]{1,0:T(8,128)(2,1)S(1)}, bf16[16,1792]{1,0:T(8,128)(2,1)S(1)}, u32[]{:S(2)}, u32[]{:S(2)}) %collective-permute-start.18) | collective-permute-done | bytes 57376 | tf_op jit(solution)/shard_map/ppermute | solution.py:19
  87.6 0.6 collective-permute-done.17
  88.3 2.9 %collective-permute-start.19 = (bf16[16,1792]{1,0:T(8,128)(2,1)S(1)}, bf16[16,1792]{1,0:T(8,128)(2,1)S(1)}, u32[]{:S(2)}, u32[]{:S(2)}) collective-permute-start(bf16[16,1792]{1,0:T(8,128)(2,1)S(1)} %add_convert_fusion.1), channel_id=1, source_target_pairs={{0,2},{1,3},{2,0},{3,1},{4,6},{5,7},{6,4},{7,5},{8,10},{9,11},{10,... | collective-permute-start | bytes 172040 | tf_op jit(solution)/shard_map/ppermute | solution.py:19
  91.2 2.3 %collective-permute-done.19 = bf16[16,1792]{1,0:T(8,128)(2,1)S(1)} collective-permute-done((bf16[16,1792]{1,0:T(8,128)(2,1)S(1)}, bf16[16,1792]{1,0:T(8,128)(2,1)S(1)}, u32[]{:S(2)}, u32[]{:S(2)}) %collective-permute-start.19) | collective-permute-done | bytes 57376 | tf_op jit(solution)/shard_map/ppermute | solution.py:19
  93.6 1.2 %collective-permute-done.20.refs_2_ = bf16[16,1792]{1,0:T(8,128)(2,1)S(1)} collective-permute-done((bf16[16,1792]{1,0:T(8,128)(2,1)S(1)}, bf16[16,1792]{1,0:T(8,128)(2,1)S(1)}, u32[]{:S(2)}, u32[]{:S(2)}) %collective-permute-start.20) | collective-permute-done | bytes 57376 | tf_op jit(solution)/shard_map/ppermute | solution.py:19
  94.8 1.4 %shard_map.70 = (f32[32,1792]{1,0:T(8,128)S(1)}, f32[32,2048]{1,0:T(8,128)S(1)}, bf16[32,2176]{1,0:T(8,128)(2,1)S(1)}) custom-call(f32[32,1792]{1,0:T(8,128)S(1)} %get-tuple-element.31.refs_0_, bf16[16,1792]{1,0:T(8,128)(2,1)S(1)} %add_convert_fusion.refs_1_, bf16[16,1792]{1,0:T(8,128)(2,1)S(1)} %collective-permute-done.20.refs_2_, ...), custom_call_target="tpu_custom_call" | custom-call | flops 234881024 | bytes 7691264 | tf_op jit(solution)/shard_map/pallas_call | solution.py:41
  96.2 1.6 %collective-permute-start.22 = (bf16[32,2176]{1,0:T(8,128)(2,1)S(1)}, bf16[32,2176]{1,0:T(8,128)(2,1)S(1)}, u32[]{:S(2)}, u32[]{:S(2)}) collective-permute-start(bf16[32,2176]{1,0:T(8,128)(2,1)S(1)} %get-tuple-element.38.message_ref), channel_id=1, source_target_pairs={{0,1},{1,0},{2,3},{3,2},{4,5},{5,4},{6,7},{7,6},{8,9},{9,8},{10,11... | collective-permute-start | bytes 417800 | tf_op jit(solution)/shard_map/ppermute | solution.py:19
  97.8 4.1 %collective-permute-done.22.swapped_ref = bf16[32,2176]{1,0:T(8,128)(2,1)S(1)} collective-permute-done((bf16[32,2176]{1,0:T(8,128)(2,1)S(1)}, bf16[32,2176]{1,0:T(8,128)(2,1)S(1)}, u32[]{:S(2)}, u32[]{:S(2)}) %collective-permute-start.22) | collective-permute-done | bytes 139296 | tf_op jit(solution)/shard_map/ppermute | solution.py:19
  102.0 2.0 %copy-done.4 = bf16[1,1,1024,1792]{3,2,1,0:T(8,128)(2,1)S(1)} copy-done((bf16[1,1,1024,1792]{3,2,1,0:T(8,128)(2,1)S(1)}, bf16[1,1,1024,1792]{3,2,1,0:T(8,128)(2,1)}, u32[]{:S(2)}) %copy-start.4) | copy-done | bytes 3670040
  104.0 0.9 shard_map.71
  104.9 0.2 convolution_convert_fusion
  105.1 0.8 reshape.308
  105.9 5.6 %all-to-all-start.1 = ((bf16[32,14,128]{2,1,0:T(8,128)(2,1)}), bf16[32,14,128]{2,1,0:T(8,128)(2,1)S(1)}, u32[]{:S(2)}, u32[]{:S(2)}) async-start(bf16[32,14,128]{2,1,0:T(8,128)(2,1)} %reshape.308), calls=%async_computation.1 | async-start | bytes 262144 | tf_op jit(solution)/shard_map/all_to_all | solution.py:203
  111.5 0.1 select_reduce_fusion.1
  111.6 1.8 %collective-permute-start.21 = (f32[1,1792]{1,0:T(1,128)S(1)}, f32[1,1792]{1,0:T(1,128)S(1)}, u32[]{:S(2)}, u32[]{:S(2)}) collective-permute-start(f32[1,1792]{1,0:T(1,128)S(1)} %broadcast_in_dim.75), channel_id=1, source_target_pairs={{0,1},{1,0},{2,3},{3,2},{4,5},{5,4},{6,7},{7,6},{8,9},{9,8},{10,11... | collective-permute-start | bytes 21512 | tf_op jit(solution)/shard_map/ppermute | solution.py:19
  113.5 6.5 %all-to-all-done.1 = bf16[32,14,128]{2,1,0:T(8,128)(2,1)S(1)} async-done(((bf16[32,14,128]{2,1,0:T(8,128)(2,1)}), bf16[32,14,128]{2,1,0:T(8,128)(2,1)S(1)}, u32[]{:S(2)}, u32[]{:S(2)}) %all-to-all-start.1) | async-done | bytes 114720 | tf_op jit(solution)/shard_map/all_to_all | solution.py:203
  119.9 0.1 fusion.3
  120.1 0.6 fusion.9
  (47 shorter events, 1.5 us)
Async XLA Ops:
  3.2 17.2 %all-to-all-start = ((bf16[32,16,128]{2,1,0:T(8,128)(2,1)}), bf16[32,16,128]{2,1,0:T(8,128)(2,1)S(1)}, u32[]{:S(2)}, u32[]{:S(2)}) async-start(bf16[32,16,128]{2,1,0:T(8,128)(2,1)} %bitcast), calls=%async_computation | async-start | bytes 262144 | tf_op jit(solution)/shard_map/all_to_all | solution.py:128
  21.0 3.1 %copy-start = (bf16[224,8,2,1024]{3,1,2,0:T(8,128)(2,1)S(1)}, bf16[224,8,2,1024]{3,1,2,0:T(8,128)(2,1)}, u32[]{:S(2)}) copy-start(bf16[224,8,2,1024]{3,1,2,0:T(8,128)(2,1)} %copy.14) | copy-start | bytes 22020100
  24.1 25.4 %copy-start.1 = (bf16[224,8,2,1024]{3,1,2,0:T(8,128)(2,1)S(1)}, bf16[224,8,2,1024]{3,1,2,0:T(8,128)(2,1)}, u32[]{:S(2)}) copy-start(bf16[224,8,2,1024]{3,1,2,0:T(8,128)(2,1)} %copy.14) | copy-start | bytes 22020100
  25.4 5.9 %collective-permute-start = (bf16[32,2176]{1,0:T(8,128)(2,1)S(1)}, bf16[32,2176]{1,0:T(8,128)(2,1)S(1)}, u32[]{:S(2)}, u32[]{:S(2)}) collective-permute-start(bf16[32,2176]{1,0:T(8,128)(2,1)S(1)} %get-tuple-element.23.message_ref), channel_id=1, source_target_pairs={{0,1},{1,0},{2,3},{3,2},{4,5},{5,4},{6,7},{7,6},{8,9},{9,8},{10,11... | collective-permute-start | bytes 417800 | tf_op jit(solution)/shard_map/ppermute | solution.py:19
  31.3 2.0 %copy-start.2 = (bf16[1,1,1024,1792]{3,2,1,0:T(8,128)(2,1)S(1)}, bf16[1,1,1024,1792]{3,2,1,0:T(8,128)(2,1)}, u32[]{:S(2)}) copy-start(bf16[1,1,1024,1792]{3,2,1,0:T(8,128)(2,1)} %param.11) | copy-start | bytes 11010052
  33.3 23.2 %copy-start.3 = (bf16[1,1,1024,1792]{3,2,1,0:T(8,128)(2,1)S(1)}, bf16[1,1,1024,1792]{3,2,1,0:T(8,128)(2,1)}, u32[]{:S(2)}) copy-start(bf16[1,1,1024,1792]{3,2,1,0:T(8,128)(2,1)} %param.11) | copy-start | bytes 11010052
  34.2 1.3 %collective-permute-start.1 = (bf16[16,1792]{1,0:T(8,128)(2,1)S(1)}, bf16[16,1792]{1,0:T(8,128)(2,1)S(1)}, u32[]{:S(2)}, u32[]{:S(2)}) collective-permute-start(bf16[16,1792]{1,0:T(8,128)(2,1)S(1)} %get-tuple-element.25), channel_id=1, source_target_pairs={{0,4},{4,0},{8,12},{12,8},{16,20},{20,16},{24,28},{28,24},{1,5},{5... | collective-permute-start | bytes 172040 | tf_op jit(solution)/shard_map/ppermute | solution.py:19
  35.5 5.1 %collective-permute-start.4 = (bf16[16,1792]{1,0:T(8,128)(2,1)S(1)}, bf16[16,1792]{1,0:T(8,128)(2,1)S(1)}, u32[]{:S(2)}, u32[]{:S(2)}) collective-permute-start(bf16[16,1792]{1,0:T(8,128)(2,1)S(1)} %add_convert_fusion.8), channel_id=1, source_target_pairs={{0,24},{4,28},{8,16},{12,20},{16,8},{20,12},{24,0},{28,4},{1,25},{... | collective-permute-start | bytes 172040 | tf_op jit(solution)/shard_map/ppermute | solution.py:19
  38.2 4.2 %collective-permute-start.3 = (bf16[16,1792]{1,0:T(8,128)(2,1)S(1)}, bf16[16,1792]{1,0:T(8,128)(2,1)S(1)}, u32[]{:S(2)}, u32[]{:S(2)}) collective-permute-start(bf16[16,1792]{1,0:T(8,128)(2,1)S(1)} %add_convert_fusion.8), channel_id=1, source_target_pairs={{0,16},{4,20},{8,24},{12,28},{16,0},{20,4},{24,8},{28,12},{1,17},{... | collective-permute-start | bytes 172040 | tf_op jit(solution)/shard_map/ppermute | solution.py:19
  38.7 4.2 %collective-permute-start.2 = (bf16[16,1792]{1,0:T(8,128)(2,1)S(1)}, bf16[16,1792]{1,0:T(8,128)(2,1)S(1)}, u32[]{:S(2)}, u32[]{:S(2)}) collective-permute-start(bf16[16,1792]{1,0:T(8,128)(2,1)S(1)} %add_convert_fusion.8), channel_id=1, source_target_pairs={{0,8},{4,12},{8,0},{12,4},{16,24},{20,28},{24,16},{28,20},{1,9},{5... | collective-permute-start | bytes 172040 | tf_op jit(solution)/shard_map/ppermute | solution.py:19
  42.9 5.1 %collective-permute-start.5 = (bf16[16,1792]{1,0:T(8,128)(2,1)S(1)}, bf16[16,1792]{1,0:T(8,128)(2,1)S(1)}, u32[]{:S(2)}, u32[]{:S(2)}) collective-permute-start(bf16[16,1792]{1,0:T(8,128)(2,1)S(1)} %add_convert_fusion.7), channel_id=1, source_target_pairs={{0,2},{1,3},{2,0},{3,1},{4,6},{5,7},{6,4},{7,5},{8,10},{9,11},{10,... | collective-permute-start | bytes 172040 | tf_op jit(solution)/shard_map/ppermute | solution.py:19
  48.1 1.3 %collective-permute-start.6 = (bf16[16,1792]{1,0:T(8,128)(2,1)S(1)}, bf16[16,1792]{1,0:T(8,128)(2,1)S(1)}, u32[]{:S(2)}, u32[]{:S(2)}) collective-permute-start(bf16[16,1792]{1,0:T(8,128)(2,1)S(1)} %add_convert_fusion.6.refs_1_), channel_id=1, source_target_pairs={{0,4},{4,0},{8,12},{12,8},{16,20},{20,16},{24,28},{28,24},{1,5},{5... | collective-permute-start | bytes 172040 | tf_op jit(solution)/shard_map/ppermute | solution.py:19
  50.8 5.8 %collective-permute-start.7 = (bf16[32,2176]{1,0:T(8,128)(2,1)S(1)}, bf16[32,2176]{1,0:T(8,128)(2,1)S(1)}, u32[]{:S(2)}, u32[]{:S(2)}) collective-permute-start(bf16[32,2176]{1,0:T(8,128)(2,1)S(1)} %get-tuple-element.28.message_ref), channel_id=1, source_target_pairs={{0,1},{1,0},{2,3},{3,2},{4,5},{5,4},{6,7},{7,6},{8,9},{9,8},{10,11... | collective-permute-start | bytes 417800 | tf_op jit(solution)/shard_map/ppermute | solution.py:19
  57.4 1.3 %collective-permute-start.8 = (bf16[16,1792]{1,0:T(8,128)(2,1)S(1)}, bf16[16,1792]{1,0:T(8,128)(2,1)S(1)}, u32[]{:S(2)}, u32[]{:S(2)}) collective-permute-start(bf16[16,1792]{1,0:T(8,128)(2,1)S(1)} %get-tuple-element.30), channel_id=1, source_target_pairs={{0,4},{4,0},{8,12},{12,8},{16,20},{20,16},{24,28},{28,24},{1,5},{5... | collective-permute-start | bytes 172040 | tf_op jit(solution)/shard_map/ppermute | solution.py:19
  58.8 5.2 %collective-permute-start.11 = (bf16[16,1792]{1,0:T(8,128)(2,1)S(1)}, bf16[16,1792]{1,0:T(8,128)(2,1)S(1)}, u32[]{:S(2)}, u32[]{:S(2)}) collective-permute-start(bf16[16,1792]{1,0:T(8,128)(2,1)S(1)} %add_convert_fusion.5), channel_id=1, source_target_pairs={{0,24},{4,28},{8,16},{12,20},{16,8},{20,12},{24,0},{28,4},{1,25},{... | collective-permute-start | bytes 172040 | tf_op jit(solution)/shard_map/ppermute | solution.py:19
  60.3 4.6 %collective-permute-start.10 = (bf16[16,1792]{1,0:T(8,128)(2,1)S(1)}, bf16[16,1792]{1,0:T(8,128)(2,1)S(1)}, u32[]{:S(2)}, u32[]{:S(2)}) collective-permute-start(bf16[16,1792]{1,0:T(8,128)(2,1)S(1)} %add_convert_fusion.5), channel_id=1, source_target_pairs={{0,16},{4,20},{8,24},{12,28},{16,0},{20,4},{24,8},{28,12},{1,17},{... | collective-permute-start | bytes 172040 | tf_op jit(solution)/shard_map/ppermute | solution.py:19
  61.2 4.2 %collective-permute-start.9 = (bf16[16,1792]{1,0:T(8,128)(2,1)S(1)}, bf16[16,1792]{1,0:T(8,128)(2,1)S(1)}, u32[]{:S(2)}, u32[]{:S(2)}) collective-permute-start(bf16[16,1792]{1,0:T(8,128)(2,1)S(1)} %add_convert_fusion.5), channel_id=1, source_target_pairs={{0,8},{4,12},{8,0},{12,4},{16,24},{20,28},{24,16},{28,20},{1,9},{5... | collective-permute-start | bytes 172040 | tf_op jit(solution)/shard_map/ppermute | solution.py:19
  65.4 6.1 %collective-permute-start.12 = (bf16[16,1792]{1,0:T(8,128)(2,1)S(1)}, bf16[16,1792]{1,0:T(8,128)(2,1)S(1)}, u32[]{:S(2)}, u32[]{:S(2)}) collective-permute-start(bf16[16,1792]{1,0:T(8,128)(2,1)S(1)} %add_convert_fusion.4), channel_id=1, source_target_pairs={{0,2},{1,3},{2,0},{3,1},{4,6},{5,7},{6,4},{7,5},{8,10},{9,11},{10,... | collective-permute-start | bytes 172040 | tf_op jit(solution)/shard_map/ppermute | solution.py:19
  71.5 1.3 %collective-permute-start.13 = (bf16[16,1792]{1,0:T(8,128)(2,1)S(1)}, bf16[16,1792]{1,0:T(8,128)(2,1)S(1)}, u32[]{:S(2)}, u32[]{:S(2)}) collective-permute-start(bf16[16,1792]{1,0:T(8,128)(2,1)S(1)} %add_convert_fusion.3.refs_1_), channel_id=1, source_target_pairs={{0,4},{4,0},{8,12},{12,8},{16,20},{20,16},{24,28},{28,24},{1,5},{5... | collective-permute-start | bytes 172040 | tf_op jit(solution)/shard_map/ppermute | solution.py:19
  74.2 5.8 %collective-permute-start.14 = (bf16[32,2176]{1,0:T(8,128)(2,1)S(1)}, bf16[32,2176]{1,0:T(8,128)(2,1)S(1)}, u32[]{:S(2)}, u32[]{:S(2)}) collective-permute-start(bf16[32,2176]{1,0:T(8,128)(2,1)S(1)} %get-tuple-element.33.message_ref), channel_id=1, source_target_pairs={{0,1},{1,0},{2,3},{3,2},{4,5},{5,4},{6,7},{7,6},{8,9},{9,8},{10,11... | collective-permute-start | bytes 417800 | tf_op jit(solution)/shard_map/ppermute | solution.py:19
  80.8 1.3 %collective-permute-start.15 = (bf16[16,1792]{1,0:T(8,128)(2,1)S(1)}, bf16[16,1792]{1,0:T(8,128)(2,1)S(1)}, u32[]{:S(2)}, u32[]{:S(2)}) collective-permute-start(bf16[16,1792]{1,0:T(8,128)(2,1)S(1)} %get-tuple-element.35), channel_id=1, source_target_pairs={{0,4},{4,0},{8,12},{12,8},{16,20},{20,16},{24,28},{28,24},{1,5},{5... | collective-permute-start | bytes 172040 | tf_op jit(solution)/shard_map/ppermute | solution.py:19
  82.2 5.5 %collective-permute-start.18 = (bf16[16,1792]{1,0:T(8,128)(2,1)S(1)}, bf16[16,1792]{1,0:T(8,128)(2,1)S(1)}, u32[]{:S(2)}, u32[]{:S(2)}) collective-permute-start(bf16[16,1792]{1,0:T(8,128)(2,1)S(1)} %add_convert_fusion.2), channel_id=1, source_target_pairs={{0,24},{4,28},{8,16},{12,20},{16,8},{20,12},{24,0},{28,4},{1,25},{... | collective-permute-start | bytes 172040 | tf_op jit(solution)/shard_map/ppermute | solution.py:19
  83.3 4.9 %collective-permute-start.17 = (bf16[16,1792]{1,0:T(8,128)(2,1)S(1)}, bf16[16,1792]{1,0:T(8,128)(2,1)S(1)}, u32[]{:S(2)}, u32[]{:S(2)}) collective-permute-start(bf16[16,1792]{1,0:T(8,128)(2,1)S(1)} %add_convert_fusion.2), channel_id=1, source_target_pairs={{0,16},{4,20},{8,24},{12,28},{16,0},{20,4},{24,8},{28,12},{1,17},{... | collective-permute-start | bytes 172040 | tf_op jit(solution)/shard_map/ppermute | solution.py:19
  83.9 4.4 %collective-permute-start.16 = (bf16[16,1792]{1,0:T(8,128)(2,1)S(1)}, bf16[16,1792]{1,0:T(8,128)(2,1)S(1)}, u32[]{:S(2)}, u32[]{:S(2)}) collective-permute-start(bf16[16,1792]{1,0:T(8,128)(2,1)S(1)} %add_convert_fusion.2), channel_id=1, source_target_pairs={{0,8},{4,12},{8,0},{12,4},{16,24},{20,28},{24,16},{28,20},{1,9},{5... | collective-permute-start | bytes 172040 | tf_op jit(solution)/shard_map/ppermute | solution.py:19
  88.3 5.2 %collective-permute-start.19 = (bf16[16,1792]{1,0:T(8,128)(2,1)S(1)}, bf16[16,1792]{1,0:T(8,128)(2,1)S(1)}, u32[]{:S(2)}, u32[]{:S(2)}) collective-permute-start(bf16[16,1792]{1,0:T(8,128)(2,1)S(1)} %add_convert_fusion.1), channel_id=1, source_target_pairs={{0,2},{1,3},{2,0},{3,1},{4,6},{5,7},{6,4},{7,5},{8,10},{9,11},{10,... | collective-permute-start | bytes 172040 | tf_op jit(solution)/shard_map/ppermute | solution.py:19
  93.5 1.3 %collective-permute-start.20 = (bf16[16,1792]{1,0:T(8,128)(2,1)S(1)}, bf16[16,1792]{1,0:T(8,128)(2,1)S(1)}, u32[]{:S(2)}, u32[]{:S(2)}) collective-permute-start(bf16[16,1792]{1,0:T(8,128)(2,1)S(1)} %add_convert_fusion.refs_1_), channel_id=1, source_target_pairs={{0,4},{4,0},{8,12},{12,8},{16,20},{20,16},{24,28},{28,24},{1,5},{5... | collective-permute-start | bytes 172040 | tf_op jit(solution)/shard_map/ppermute | solution.py:19
  96.2 5.8 %collective-permute-start.22 = (bf16[32,2176]{1,0:T(8,128)(2,1)S(1)}, bf16[32,2176]{1,0:T(8,128)(2,1)S(1)}, u32[]{:S(2)}, u32[]{:S(2)}) collective-permute-start(bf16[32,2176]{1,0:T(8,128)(2,1)S(1)} %get-tuple-element.38.message_ref), channel_id=1, source_target_pairs={{0,1},{1,0},{2,3},{3,2},{4,5},{5,4},{6,7},{7,6},{8,9},{9,8},{10,11... | collective-permute-start | bytes 417800 | tf_op jit(solution)/shard_map/ppermute | solution.py:19
  102.0 2.0 %copy-start.4 = (bf16[1,1,1024,1792]{3,2,1,0:T(8,128)(2,1)S(1)}, bf16[1,1,1024,1792]{3,2,1,0:T(8,128)(2,1)}, u32[]{:S(2)}) copy-start(bf16[1,1,1024,1792]{3,2,1,0:T(8,128)(2,1)} %param.11) | copy-start | bytes 11010052
  105.9 14.1 %all-to-all-start.1 = ((bf16[32,14,128]{2,1,0:T(8,128)(2,1)}), bf16[32,14,128]{2,1,0:T(8,128)(2,1)S(1)}, u32[]{:S(2)}, u32[]{:S(2)}) async-start(bf16[32,14,128]{2,1,0:T(8,128)(2,1)} %reshape.308), calls=%async_computation.1 | async-start | bytes 262144 | tf_op jit(solution)/shard_map/all_to_all | solution.py:203
  111.6 8.5 %collective-permute-start.21 = (f32[1,1792]{1,0:T(1,128)S(1)}, f32[1,1792]{1,0:T(1,128)S(1)}, u32[]{:S(2)}, u32[]{:S(2)}) collective-permute-start(f32[1,1792]{1,0:T(1,128)S(1)} %broadcast_in_dim.75), channel_id=1, source_target_pairs={{0,1},{1,0},{2,3},{3,2},{4,5},{5,4},{6,7},{7,6},{8,9},{9,8},{10,11... | collective-permute-start | bytes 21512 | tf_op jit(solution)/shard_map/ppermute | solution.py:19

commit v3 on v0

--- a/solution.py
+++ b/solution.py
@@ -1,6 +1,10 @@
+import functools
+
 import jax
 import jax.numpy as jnp
 from jax import lax
+from jax.experimental import pallas as pl
+from jax.experimental.pallas import tpu as pltpu
 from jax.sharding import PartitionSpec as P
 
 TOP = 8
@@ -9,6 +13,326 @@
 
 def swapped(shard, axis, bit):
     return lax.ppermute(shard, axis, [(i, i ^ 1 << bit) for i in range(lax.axis_size(axis))])
+
+
+def exchanged(shard, axis, mask):
+    return lax.ppermute(shard, axis, [(i, i ^ mask) for i in range(lax.axis_size(axis))])
+
+
+def widened(values):
+    return values.astype(jnp.float32)
+
+
+def rounded(values):
+    return values.astype(jnp.bfloat16)
+
+
+WHOLE = pl.BlockSpec(memory_space=pltpu.VMEM)
+IN_HBM = pl.BlockSpec(memory_space=pltpu.HBM)
+LANES = 128
+
+
+def in_vmem(shape, dtype):
+    return pltpu.VMEM(shape, dtype)
+
+
+def kernel_call(body, out_shape, operands, flops=0, in_hbm=(), scratch=(), limit=4):
+    operands = [pltpu.with_memory_space_constraint(o, pltpu.VMEM) for o in operands]
+    in_hbm = [pltpu.with_memory_space_constraint(o, pltpu.HBM) for o in in_hbm]
+    read = sum(o.size * o.dtype.itemsize for o in [*operands, *in_hbm])
+    return pl.pallas_call(
+        body,
+        out_shape=out_shape,
+        in_specs=[WHOLE] * len(operands) + [IN_HBM] * len(in_hbm),
+        out_specs=[WHOLE] * len(out_shape),
+        scratch_shapes=scratch,
+        compiler_params=pltpu.CompilerParams(vmem_limit_bytes=limit * 2**20),
+        cost_estimate=pl.CostEstimate(flops=flops, bytes_accessed=read, transcendentals=0),
+    )(*operands, *in_hbm)
+
+
+def column_blocks(width):
+    block = next(b for b in (512, 256, 128, width) if width % b == 0)
+    return [slice(start, start + block) for start in range(0, width, block)]
+
+
+def row_blocks(values, start, stop):
+    return [values[:, at : at + LANES] for at in range(start, stop, LANES)]
+
+
+def message_body(hidden_in, ids_in, levels_in, gain_in, own_ref, other_ref, gain_ref, hidden, ids, levels, gain, semaphores):
+    copies = [
+        pltpu.make_async_copy(source, target, semaphores.at[k])
+        for k, (source, target) in enumerate(
+            [(hidden_in, hidden), (ids_in, ids), (levels_in, levels), (gain_in, gain)]
+        )
+    ]
+    for copy in copies:
+        copy.start()
+    for copy in copies:
+        copy.wait()
+    half_width = hidden.shape[1] // 2
+    half_rows = half_width // LANES
+    is_first = lax.axis_index("expert") % 2 == 0
+    row = lax.broadcasted_iota(jnp.int32, own_ref.shape, 0)
+
+    def route_row(ref):
+        values = [widened(ref[step]) for step in range(ref.shape[0])]
+        used = len(values) * values[0].shape[1]
+        return jnp.concatenate(values + [jnp.zeros((1, LANES - used), jnp.float32)], axis=1)
+
+    routing = [route_row(ids), route_row(levels)]
+    features = widened(hidden[...])
+    first = row_blocks(features, 0, half_width)
+    second = row_blocks(features, half_width, 2 * half_width)
+    for target, pairs in ((own_ref, zip(first, second)), (other_ref, zip(second, first))):
+        message = jnp.zeros(own_ref.shape, jnp.float32)
+        for place, values in enumerate([jnp.where(is_first, a, b) for a, b in pairs] + routing):
+            message = jnp.where(row == place, values, message)
+        target[...] = rounded(message)
+    for place in range(half_rows):
+        gain_ref[:, place * LANES : (place + 1) * LANES] = jnp.where(
+            is_first, gain[place : place + 1], gain[half_rows + place : half_rows + place + 1]
+        )
+
+
+def weights_body(gate_up_ref, weight_ref, arrived_ref, semaphores):
+    part = arrived_ref.shape[2]
+    count = semaphores.shape[0]
+    block = arrived_ref.shape[0] // count
+    blocks = [pl.ds(k * block, block) for k in range(count)]
+    copies = [
+        pltpu.make_async_copy(gate_up_ref.at[rows], arrived_ref.at[rows], semaphores.at[k])
+        for k, rows in enumerate(blocks)
+    ]
+    for copy in copies:
+        copy.start()
+    for copy, rows in zip(copies, blocks):
+        copy.wait()
+        weight_ref[rows] = arrived_ref[rows].reshape(block, 2 * part)
+
+
+def joined_body(ready_ref, *refs):
+    *pieces, out_ref = refs
+    size = out_ref.shape[0] // len(pieces)
+    for k, piece in enumerate(pieces):
+        out_ref[k * size : (k + 1) * size] = piece[...].reshape(size, *out_ref.shape[1:])
+
+
+def own_place_of(group_count):
+    return lax.axis_index("rack") // 2 * group_count + lax.axis_index("expert")
+
+
+def placed(gathered_refs, half_width, group_count):
+    wide = jnp.concatenate([ref[...].reshape(ref.shape[0], -1) for ref in gathered_refs], axis=0)
+    count = wide.shape[0]
+    place = lax.broadcasted_iota(jnp.int32, (count, count), 0)
+    source = lax.broadcasted_iota(jnp.int32, (count, count), 1)
+    to_place = rounded(jnp.where(place == (source ^ own_place_of(group_count)), 1.0, 0.0))
+    wide = jnp.dot(to_place, wide, preferred_element_type=jnp.float32)
+    residual = wide[:, :half_width]
+    ids = wide[:, half_width : half_width + LANES]
+    levels = wide[:, half_width + LANES : half_width + 2 * LANES]
+    lane = lax.broadcasted_iota(jnp.int32, ids.shape, 1)
+    chosen = ids == lax.axis_index("rack").astype(jnp.float32)
+    mixing = jnp.zeros(ids.shape, jnp.float32)
+    for step in range(STEPS):
+        of_step = lane // TOP == step
+        total = jnp.sum(jnp.where(of_step, levels, 0.0), axis=1, keepdims=True)
+        share = jnp.sum(jnp.where(of_step & chosen, levels / total, 0.0), axis=1, keepdims=True)
+        mixing = jnp.where(lane == step, widened(rounded(share)), mixing)
+    return residual, mixing
+
+
+def gate_up_body(step, group_count, *refs):
+    first, last = step == 0, step == STEPS - 1
+    if first:
+        *gathered_refs, gain_ref, weight_ref, residual_ref, mixing_ref, product_ref, message_ref = refs
+        residual, mixing_ref[...] = placed(gathered_refs, gain_ref.shape[1], group_count)
+        residual_ref[...] = residual
+    else:
+        before_ref, own_ref, other_ref, gain_ref, weight_ref, *residual_refs, product_ref, message_ref = refs
+        update = jnp.concatenate([own_ref[...], other_ref[...]], axis=0)
+        residual = before_ref[...] + widened(update)
+        if last:
+            place = lax.broadcasted_iota(jnp.int32, (residual.shape[0], 1), 0)
+            own_place = own_place_of(group_count)
+            for ref, wanted in zip(residual_refs, (own_place, own_place ^ 1)):
+                ref[...] = jnp.sum(jnp.where(place == wanted, residual, 0.0), axis=0, keepdims=True)
+        else:
+            residual_refs[0][...] = residual
+    scaled = rounded(residual * gain_ref[...])
+    width = weight_ref.shape[1]
+    for columns in column_blocks(width):
+        product = jnp.dot(scaled, weight_ref[:, columns], preferred_element_type=jnp.float32)
+        product_ref[:, columns] = product
+        message_ref[:, columns] = rounded(product)
+    square_sum = jnp.sum(residual * residual, axis=1, keepdims=True)
+    square_high = widened(rounded(square_sum))
+    lane = lax.broadcasted_iota(jnp.int32, (residual.shape[0], LANES), 1)
+    tail = jnp.where(lane == 0, square_high, square_sum - square_high)
+    message_ref[:, width:] = rounded(tail)
+
+
+def token_matrix(count, group_count):
+    token = lax.broadcasted_iota(jnp.int32, (count, count), 0)
+    place = lax.broadcasted_iota(jnp.int32, (count, count), 1)
+    rack = token // group_count
+    core = (rack + lax.axis_index("rack")) % 2
+    matches = core * (count // 2) + rack // 2 * group_count + token % group_count == place
+    return rounded(jnp.where(matches, 1.0, 0.0))
+
+
+def down_body(step, model_width, group_count, product_ref, message_ref, swapped_ref, mixing_ref, weight_ref, *out_refs):
+    width = product_ref.shape[1]
+    part = width // 2
+    tails = widened(message_ref[:, width:]) + widened(swapped_ref[:, width:])
+    square_sum = tails[:, 0:1] + tails[:, 1:2]
+    scale = lax.rsqrt(square_sum / model_width + 1e-06)
+    whole = product_ref[...] + widened(swapped_ref[:, :width])
+    gate = whole[:, :part] * scale
+    up = whole[:, part:] * scale
+    activated = rounded(gate / (1.0 + jnp.exp(-gate)) * up)
+    mixing = mixing_ref[...]
+    count = mixing.shape[0]
+    last = step == STEPS - 1
+    if last:
+        to_tokens = token_matrix(count, group_count)
+        activated = rounded(jnp.dot(to_tokens, activated, preferred_element_type=jnp.float32))
+        mixing = jnp.dot(to_tokens, rounded(mixing), preferred_element_type=jnp.float32)
+    mixing = mixing[:, step : step + 1]
+    for columns in column_blocks(weight_ref.shape[1]):
+        term = jnp.dot(activated, weight_ref[:, columns], preferred_element_type=jnp.float32)
+        update = widened(rounded(term)) * mixing
+        if last:
+            blocks = slice(columns.start // LANES, columns.stop // LANES)
+            out_refs[0][:, blocks] = rounded(update).reshape(count, -1, LANES)
+        else:
+            out_refs[0][:, columns] = update[: count // 2]
+            out_refs[1][:, columns] = rounded(update[count // 2 :])
+
+
+def result_body(arrived_ref, own_ref, other_ref, out_ref):
+    count, half_width = arrived_ref.shape[0], own_ref.shape[1]
+    terms = widened(arrived_ref[...].reshape(count, half_width))
+    of_first = lax.broadcasted_iota(jnp.int32, (count, 1), 0) % 2 == 0
+    is_first = lax.axis_index("expert") % 2 == 0
+    own, other = own_ref[...], other_ref[...]
+    out_ref[:, :half_width] = jnp.where(is_first, own, other) + jnp.sum(
+        jnp.where(of_first, terms, 0.0), axis=0, keepdims=True
+    )
+    out_ref[:, half_width:] = jnp.where(is_first, other, own) + jnp.sum(
+        jnp.where(of_first, 0.0, terms), axis=0, keepdims=True
+    )
+
+
+def dense_steps(hidden_in, norm_gain, expert_ids, gate_levels, w_gate_up, w_down):
+    rack_count = lax.axis_size("rack")
+    group_count = lax.axis_size("expert")
+    core_rows = rack_count // 2 * group_count
+    token_count = 2 * core_rows
+    model_width = hidden_in.shape[1]
+    half_width = model_width // 2
+    part_width = w_down.shape[2]
+    product_width = 2 * part_width
+    product_flops = 2 * token_count * half_width * product_width
+
+    block_shape = (half_width // LANES + 2, LANES)
+    sources = [hidden_in, expert_ids, gate_levels, norm_gain.reshape(-1, LANES)]
+    own, other, gain_half = kernel_call(
+        message_body,
+        [
+            in_vmem(block_shape, jnp.bfloat16),
+            in_vmem(block_shape, jnp.bfloat16),
+            in_vmem((1, half_width), jnp.float32),
+        ],
+        [],
+        in_hbm=sources,
+        scratch=[*(in_vmem(a.shape, a.dtype) for a in sources), pltpu.SemaphoreType.DMA((len(sources),))],
+    )
+    block = next(b for b in (128, 16, half_width) if half_width % b == 0)
+    (gate_up_weight,) = kernel_call(
+        weights_body,
+        [in_vmem((half_width, product_width), jnp.bfloat16)],
+        [],
+        in_hbm=[w_gate_up[0, 0]],
+        scratch=[
+            in_vmem((half_width, 2, part_width), jnp.bfloat16),
+            pltpu.SemaphoreType.DMA((half_width // block,)),
+        ],
+        limit=12,
+    )
+
+    def joined(ready, pieces, count):
+        out_shape = [in_vmem((count,) + block_shape, jnp.bfloat16)]
+        return kernel_call(joined_body, out_shape, [ready, *pieces])[0]
+
+    rows = [own] + [exchanged(other if mask % 2 else own, "expert", mask) for mask in range(1, group_count)]
+    rows = joined(gate_up_weight, rows, group_count)
+    rows = [rows] + [exchanged(rows, "rack", mask) for mask in range(2, rack_count, 2)]
+    rows = joined(gate_up_weight, rows, core_rows)
+    gathered = [rows, exchanged(rows, "rack", 1)]
+
+    for step_index in range(STEPS):
+        last = step_index == STEPS - 1
+        products = [
+            in_vmem((token_count, product_width), jnp.float32),
+            in_vmem((token_count, product_width + LANES), jnp.bfloat16),
+        ]
+        kept = [in_vmem((token_count, half_width), jnp.float32)]
+        if step_index == 0:
+            operands = gathered
+            kept += [in_vmem((token_count, LANES), jnp.float32)]
+        else:
+            operands = [residual, sent, received]
+        if last:
+            kept = [in_vmem((1, half_width), jnp.float32)] * 2
+        *kept, product, message = kernel_call(
+            functools.partial(gate_up_body, step_index, group_count),
+            kept + products,
+            operands + [gain_half, gate_up_weight],
+            product_flops,
+        )
+        if step_index == 0:
+            residual, mixing = kept
+        else:
+            residual = kept[0]
+        swapped_rows = exchanged(message, "expert", 1)
+        if last:
+            own_row, other_row = kept
+            other_row = exchanged(other_row, "expert", 1)
+            swapped_rows, other_row = lax.optimization_barrier((swapped_rows, other_row))
+            updates = [in_vmem((token_count, half_width // LANES, LANES), jnp.bfloat16)]
+        else:
+            updates = [
+                in_vmem((core_rows, half_width), jnp.float32),
+                in_vmem((core_rows, half_width), jnp.bfloat16),
+            ]
+        updates = kernel_call(
+            functools.partial(down_body, step_index, model_width, group_count),
+            updates,
+            [product, message, swapped_rows, mixing, w_down[0, 0]],
+            product_flops // 2,
+        )
+        if last:
+            break
+        update = updates[0] + widened(exchanged(updates[1], "rack", 1))
+        sent = rounded(update)
+        update = widened(sent)
+        for mask in range(2, rack_count, 2):
+            update = update + widened(exchanged(sent, "rack", mask))
+        sent = rounded(update)
+        update = widened(sent)
+        for mask in range(2, group_count, 2):
+            update = update + widened(exchanged(sent, "expert", mask))
+        sent = rounded(update)
+        received = exchanged(sent, "rack", 1)
+
+    arrived = lax.all_to_all(updates[0], ("rack", "expert"), split_axis=0, concat_axis=0, tiled=True)
+    (result,) = kernel_call(
+        result_body, [jax.ShapeDtypeStruct((1, model_width), jnp.float32)], [arrived, own_row, other_row]
+    )
+    return result
 
 
 def per_device(hidden_in, norm_gain, expert_ids, gate_levels, w_gate_up, w_down):
@@ -95,6 +419,7 @@
         P("rack", "expert", None, None),
     )
     out_specs = P(("rack", "expert"), None)
+    dense = mesh.shape["rack"] <= TOP
     return jax.shard_map(
-        per_device, mesh=mesh, in_specs=in_specs, out_specs=out_specs, check_vma=False
-    )
+        dense_steps if dense else per_device, mesh=mesh, in_specs=in_specs, out_specs=out_specs, check_vma=False
+    )

time: 283 us -> 108 us (0.38)
  blocking collectives: 145 us -> 12.7 us
  matrix products: 23.2 us -> 0 us
  local copies, waits for them, and re-layouts: 17.1 us -> 0.01 us
  Pallas kernels: 0 us -> 14 us
  other arithmetic: 8.63 us -> 0.19 us
  waiting for transfers between devices: 55.5 us -> 47.2 us
  starting transfers between devices: 28.8 us -> 33.4 us
  between operations: 3.16 us -> 0.18 us
    all_gather x6 -> x0, blocking collectives: 78.1 us -> none  [the longest x4 52.4 us: per_device(): rack_normed = lax.all_gather(normed, 'expert', axis=0, tiled=True)]
    unnamed x4 -> x0, blocking collectives: 66.6 us -> none
    all_to_all x8 -> x0, waiting for transfers between devices: 36.1 us -> none  [the longest x4 20.8 us: per_device(): lax.all_to_all(partial_value, 'rack', split_axis=0, concat_axis=0, tiled=...]
    ppermute x4 -> x30, starting transfers between devices: 0.52 us -> 33.4 us  [exchanged(): lax.ppermute(shard, axis, [(i, i ^ mask) for i in range(lax.axis_size(axi...]
    all_to_all x8 -> x0, starting transfers between devices: 28.3 us -> none  [the longest x4 14.3 us: per_device(): lax.all_to_all(partial_value, 'rack', split_axis=0, concat_axis=0, tiled=...]
    ppermute x4 -> x30, waiting for transfers between devices: 19.4 us -> 47.2 us  [exchanged(): lax.ppermute(shard, axis, [(i, i ^ mask) for i in range(lax.axis_size(axi...]
    dot_general x16 -> x0, matrix products: 23.2 us -> none  [the longest x4 18.4 us: per_device(): jnp.dot(flat_rows, gate_up_weight, preferred_element_type=jnp.float32)]
    pallas_call x0 -> x13, Pallas kernels: none -> 14 us  [kernel_call(): pl.pallas_call(body, out_shape=out_shape, in_specs=[WHOLE] * len(operands...]
  transfers between devices with their start and end apart: 12 -> 30, of which waited for: 11 -> 27; matrix products, arithmetic and copies ran while one was open for 4% -> 0% of each run, Pallas kernels for 0% -> 3%
where the time goes in v3:
time: 108 us
  waiting for transfers between devices  47.2 us (44%)
  starting transfers between devices  33.4 us (31%)
  Pallas kernels  14 us (13%)
  blocking collectives  12.7 us (12%)
    ppermute x30, waiting for transfers between devices, exchanged(): lax.ppermute(shard, axis, [(i, i ^ mask) for i in range(lax.axis_size(axi...  47.2 us
    ppermute x30, starting transfers between devices, exchanged(): lax.ppermute(shard, axis, [(i, i ^ mask) for i in range(lax.axis_size(axi...  33.4 us
    pallas_call x13, Pallas kernels, kernel_call(): pl.pallas_call(body, out_shape=out_shape, in_specs=[WHOLE] * len(operands...  14 us
    all_to_all x1, blocking collectives, dense_steps(): lax.all_to_all(updates[0], ('rack', 'expert'), split_axis=0, concat_axis=...  12.7 us
  transfers between devices with their start and end apart: 30, of which 27 were waited for; matrix products, arithmetic and copies ran while one was open for 0% of the time, Pallas kernels for 3%

profile of v3, /device:TPU:0, one launch (start us, length us, event | category | flops | bytes accessed | tf_op | source)
XLA Modules:
  0.0 107.7 jit_solution(13254177363063937051)
XLA Ops:
  0.0 0.9 shard_map.65
  0.9 4.1 %collective-permute-start.1 = (bf16[16,128]{1,0:T(8,128)(2,1)S(1)}, bf16[16,128]{1,0:T(8,128)(2,1)S(1)}, u32[]{:S(2)}, u32[]{:S(2)}) collective-permute-start(bf16[16,128]{1,0:T(8,128)(2,1)S(1)} %get-tuple-element.30.refs_0_), channel_id=1, source_target_pairs={{0,2},{1,3},{2,0},{3,1},{4,6},{5,7},{6,4},{7,5},{8,10},{9,11},{10,... | collective-permute-start | bytes 12296 | tf_op jit(solution)/shard_map/ppermute | solution.py:19
  5.0 1.3 %collective-permute-start.2 = (bf16[16,128]{1,0:T(8,128)(2,1)S(1)}, bf16[16,128]{1,0:T(8,128)(2,1)S(1)}, u32[]{:S(2)}, u32[]{:S(2)}) collective-permute-start(bf16[16,128]{1,0:T(8,128)(2,1)S(1)} %get-tuple-element.31), channel_id=1, source_target_pairs={{0,3},{1,2},{2,1},{3,0},{4,7},{5,6},{6,5},{7,4},{8,11},{9,10},{10,... | collective-permute-start | bytes 12296 | tf_op jit(solution)/shard_map/ppermute | solution.py:19
  6.3 0.2 collective-permute-start
  6.6 3.3 %shard_map.64.ready_ref.refs_3_.refs_4_ = bf16[1792,2048]{1,0:T(8,128)(2,1)S(1)} custom-call(bf16[1792,2,1024]{2,1,0:T(2,128)(2,1)} %bitcast.7), custom_call_target="tpu_custom_call" | custom-call | bytes 7340032 | tf_op jit(solution)/shard_map/pallas_call | solution.py:43
  9.9 0.5 collective-permute-done.2.refs_3_
  10.4 2.5 %collective-permute-start.5 = (bf16[4,16,128]{2,1,0:T(8,128)(2,1)S(1)}, bf16[4,16,128]{2,1,0:T(8,128)(2,1)S(1)}, u32[]{:S(2)}, u32[]{:S(2)}) collective-permute-start(bf16[4,16,128]{2,1,0:T(8,128)(2,1)S(1)} %shard_map.66.refs_0_), channel_id=1, source_target_pairs={{0,24},{4,28},{8,16},{12,20},{16,8},{20,12},{24,0},{28,4},{1,25},{... | collective-permute-start | bytes 49160 | tf_op jit(solution)/shard_map/ppermute | solution.py:19
  12.9 0.5 collective-permute-start.4
  13.4 0.5 collective-permute-start.3
  14.0 1.1 %collective-permute-done.5.refs_3_ = bf16[4,16,128]{2,1,0:T(8,128)(2,1)S(1)} collective-permute-done((bf16[4,16,128]{2,1,0:T(8,128)(2,1)S(1)}, bf16[4,16,128]{2,1,0:T(8,128)(2,1)S(1)}, u32[]{:S(2)}, u32[]{:S(2)}) %collective-permute-start.5) | collective-permute-done | bytes 16416 | tf_op jit(solution)/shard_map/ppermute | solution.py:19
  15.1 1.5 %collective-permute-done.4.refs_2_ = bf16[4,16,128]{2,1,0:T(8,128)(2,1)S(1)} collective-permute-done((bf16[4,16,128]{2,1,0:T(8,128)(2,1)S(1)}, bf16[4,16,128]{2,1,0:T(8,128)(2,1)S(1)}, u32[]{:S(2)}, u32[]{:S(2)}) %collective-permute-start.4) | collective-permute-done | bytes 16416 | tf_op jit(solution)/shard_map/ppermute | solution.py:19
  16.7 0.5 collective-permute-done.3.refs_1_
  17.2 1.2 %collective-permute-done.6.refs_1_ = bf16[16,16,128]{2,1,0:T(8,128)(2,1)S(1)} collective-permute-done((bf16[16,16,128]{2,1,0:T(8,128)(2,1)S(1)}, bf16[16,16,128]{2,1,0:T(8,128)(2,1)S(1)}, u32[]{:S(2)}, u32[]{:S(2)}) %collective-permute-start.6) | collective-permute-done | bytes 65568 | tf_op jit(solution)/shard_map/ppermute | solution.py:19
  18.4 1.5 %shard_map.68 = (f32[32,1792]{1,0:T(8,128)S(1)}, f32[32,128]{1,0:T(8,128)S(1)}, f32[32,2048]{1,0:T(8,128)S(1)}, bf16[32,2176]{1,0:T(8,128)(2,1)S(1)}) custom-call(bf16[16,16,128]{2,1,0:T(8,128)(2,1)S(1)} %shard_map.67.refs_0_, bf16[16,16,128]{2,1,0:T(8,128)(2,1)S(1)} %collective-permute-done.6.refs_1_, f32[1,1792]{1,0:T(1,128)S(1)} %get-tuple-element.32.refs_2_.refs_3_, ...), custom_call_target="tpu_custom_call" | custom-call | flops 234881024 | bytes 7478272 | tf_op jit(solution)/shard_map/pallas_call | solution.py:43
  19.9 1.4 %collective-permute-start.7 = (bf16[32,2176]{1,0:T(8,128)(2,1)S(1)}, bf16[32,2176]{1,0:T(8,128)(2,1)S(1)}, u32[]{:S(2)}, u32[]{:S(2)}) collective-permute-start(bf16[32,2176]{1,0:T(8,128)(2,1)S(1)} %get-tuple-element.35.message_ref), channel_id=1, source_target_pairs={{0,1},{1,0},{2,3},{3,2},{4,5},{5,4},{6,7},{7,6},{8,9},{9,8},{10,11... | collective-permute-start | bytes 417800 | tf_op jit(solution)/shard_map/ppermute | solution.py:19
  21.3 4.4 %collective-permute-done.7.swapped_ref = bf16[32,2176]{1,0:T(8,128)(2,1)S(1)} collective-permute-done((bf16[32,2176]{1,0:T(8,128)(2,1)S(1)}, bf16[32,2176]{1,0:T(8,128)(2,1)S(1)}, u32[]{:S(2)}, u32[]{:S(2)}) %collective-permute-start.7) | collective-permute-done | bytes 139296 | tf_op jit(solution)/shard_map/ppermute | solution.py:19
  25.7 0.9 shard_map.69
  26.5 0.1 collective-permute-start.8
  26.6 1.2 %collective-permute-done.8 = bf16[16,1792]{1,0:T(8,128)(2,1)S(1)} collective-permute-done((bf16[16,1792]{1,0:T(8,128)(2,1)S(1)}, bf16[16,1792]{1,0:T(8,128)(2,1)S(1)}, u32[]{:S(2)}, u32[]{:S(2)}) %collective-permute-start.8) | collective-permute-done | bytes 57376 | tf_op jit(solution)/shard_map/ppermute | solution.py:19
  27.9 1.6 %collective-permute-start.11 = (bf16[16,1792]{1,0:T(8,128)(2,1)S(1)}, bf16[16,1792]{1,0:T(8,128)(2,1)S(1)}, u32[]{:S(2)}, u32[]{:S(2)}) collective-permute-start(bf16[16,1792]{1,0:T(8,128)(2,1)S(1)} %add_convert_fusion.8), channel_id=1, source_target_pairs={{0,24},{4,28},{8,16},{12,20},{16,8},{20,12},{24,0},{28,4},{1,25},{... | collective-permute-start | bytes 172040 | tf_op jit(solution)/shard_map/ppermute | solution.py:19
  29.4 0.5 collective-permute-start.10
  29.9 1.5 %collective-permute-start.9 = (bf16[16,1792]{1,0:T(8,128)(2,1)S(1)}, bf16[16,1792]{1,0:T(8,128)(2,1)S(1)}, u32[]{:S(2)}, u32[]{:S(2)}) collective-permute-start(bf16[16,1792]{1,0:T(8,128)(2,1)S(1)} %add_convert_fusion.8), channel_id=1, source_target_pairs={{0,8},{4,12},{8,0},{12,4},{16,24},{20,28},{24,16},{28,20},{1,9},{5... | collective-permute-start | bytes 172040 | tf_op jit(solution)/shard_map/ppermute | solution.py:19
  31.4 1.6 %collective-permute-done.11 = bf16[16,1792]{1,0:T(8,128)(2,1)S(1)} collective-permute-done((bf16[16,1792]{1,0:T(8,128)(2,1)S(1)}, bf16[16,1792]{1,0:T(8,128)(2,1)S(1)}, u32[]{:S(2)}, u32[]{:S(2)}) %collective-permute-start.11) | collective-permute-done | bytes 57376 | tf_op jit(solution)/shard_map/ppermute | solution.py:19
  33.1 1.0 collective-permute-done.10
  34.1 2.4 %collective-permute-start.12 = (bf16[16,1792]{1,0:T(8,128)(2,1)S(1)}, bf16[16,1792]{1,0:T(8,128)(2,1)S(1)}, u32[]{:S(2)}, u32[]{:S(2)}) collective-permute-start(bf16[16,1792]{1,0:T(8,128)(2,1)S(1)} %add_convert_fusion.7), channel_id=1, source_target_pairs={{0,2},{1,3},{2,0},{3,1},{4,6},{5,7},{6,4},{7,5},{8,10},{9,11},{10,... | collective-permute-start | bytes 172040 | tf_op jit(solution)/shard_map/ppermute | solution.py:19
  36.6 3.0 %collective-permute-done.12 = bf16[16,1792]{1,0:T(8,128)(2,1)S(1)} collective-permute-done((bf16[16,1792]{1,0:T(8,128)(2,1)S(1)}, bf16[16,1792]{1,0:T(8,128)(2,1)S(1)}, u32[]{:S(2)}, u32[]{:S(2)}) %collective-permute-start.12) | collective-permute-done | bytes 57376 | tf_op jit(solution)/shard_map/ppermute | solution.py:19
  39.5 0.1 collective-permute-start.13
  39.6 1.2 %collective-permute-done.13.refs_2_ = bf16[16,1792]{1,0:T(8,128)(2,1)S(1)} collective-permute-done((bf16[16,1792]{1,0:T(8,128)(2,1)S(1)}, bf16[16,1792]{1,0:T(8,128)(2,1)S(1)}, u32[]{:S(2)}, u32[]{:S(2)}) %collective-permute-start.13) | collective-permute-done | bytes 57376 | tf_op jit(solution)/shard_map/ppermute | solution.py:19
  40.8 1.4 %shard_map.70 = (f32[32,1792]{1,0:T(8,128)S(1)}, f32[32,2048]{1,0:T(8,128)S(1)}, bf16[32,2176]{1,0:T(8,128)(2,1)S(1)}) custom-call(f32[32,1792]{1,0:T(8,128)S(1)} %get-tuple-element.33.refs_0_, bf16[16,1792]{1,0:T(8,128)(2,1)S(1)} %add_convert_fusion.6.refs_1_, bf16[16,1792]{1,0:T(8,128)(2,1)S(1)} %collective-permute-done.13.refs_2_, ...), custom_call_target="tpu_custom_call" | custom-call | flops 234881024 | bytes 7691264 | tf_op jit(solution)/shard_map/pallas_call | solution.py:43
  42.2 1.2 %collective-permute-start.14 = (bf16[32,2176]{1,0:T(8,128)(2,1)S(1)}, bf16[32,2176]{1,0:T(8,128)(2,1)S(1)}, u32[]{:S(2)}, u32[]{:S(2)}) collective-permute-start(bf16[32,2176]{1,0:T(8,128)(2,1)S(1)} %get-tuple-element.41.message_ref), channel_id=1, source_target_pairs={{0,1},{1,0},{2,3},{3,2},{4,5},{5,4},{6,7},{7,6},{8,9},{9,8},{10,11... | collective-permute-start | bytes 417800 | tf_op jit(solution)/shard_map/ppermute | solution.py:19
  43.4 4.6 %collective-permute-done.14.swapped_ref = bf16[32,2176]{1,0:T(8,128)(2,1)S(1)} collective-permute-done((bf16[32,2176]{1,0:T(8,128)(2,1)S(1)}, bf16[32,2176]{1,0:T(8,128)(2,1)S(1)}, u32[]{:S(2)}, u32[]{:S(2)}) %collective-permute-start.14) | collective-permute-done | bytes 139296 | tf_op jit(solution)/shard_map/ppermute | solution.py:19
  48.0 0.9 shard_map.71
  48.9 0.1 collective-permute-start.15
  49.0 1.2 %collective-permute-done.15 = bf16[16,1792]{1,0:T(8,128)(2,1)S(1)} collective-permute-done((bf16[16,1792]{1,0:T(8,128)(2,1)S(1)}, bf16[16,1792]{1,0:T(8,128)(2,1)S(1)}, u32[]{:S(2)}, u32[]{:S(2)}) %collective-permute-start.15) | collective-permute-done | bytes 57376 | tf_op jit(solution)/shard_map/ppermute | solution.py:19
  50.2 2.3 %collective-permute-start.18 = (bf16[16,1792]{1,0:T(8,128)(2,1)S(1)}, bf16[16,1792]{1,0:T(8,128)(2,1)S(1)}, u32[]{:S(2)}, u32[]{:S(2)}) collective-permute-start(bf16[16,1792]{1,0:T(8,128)(2,1)S(1)} %add_convert_fusion.5), channel_id=1, source_target_pairs={{0,24},{4,28},{8,16},{12,20},{16,8},{20,12},{24,0},{28,4},{1,25},{... | collective-permute-start | bytes 172040 | tf_op jit(solution)/shard_map/ppermute | solution.py:19
  52.5 0.5 collective-permute-start.17
  53.0 0.8 collective-permute-start.16
  53.8 1.6 %collective-permute-done.18 = bf16[16,1792]{1,0:T(8,128)(2,1)S(1)} collective-permute-done((bf16[16,1792]{1,0:T(8,128)(2,1)S(1)}, bf16[16,1792]{1,0:T(8,128)(2,1)S(1)}, u32[]{:S(2)}, u32[]{:S(2)}) %collective-permute-start.18) | collective-permute-done | bytes 57376 | tf_op jit(solution)/shard_map/ppermute | solution.py:19
  55.4 1.3 %collective-permute-done.17 = bf16[16,1792]{1,0:T(8,128)(2,1)S(1)} collective-permute-done((bf16[16,1792]{1,0:T(8,128)(2,1)S(1)}, bf16[16,1792]{1,0:T(8,128)(2,1)S(1)}, u32[]{:S(2)}, u32[]{:S(2)}) %collective-permute-start.17) | collective-permute-done | bytes 57376 | tf_op jit(solution)/shard_map/ppermute | solution.py:19
  56.7 0.5 collective-permute-done.16
  57.2 2.4 %collective-permute-start.19 = (bf16[16,1792]{1,0:T(8,128)(2,1)S(1)}, bf16[16,1792]{1,0:T(8,128)(2,1)S(1)}, u32[]{:S(2)}, u32[]{:S(2)}) collective-permute-start(bf16[16,1792]{1,0:T(8,128)(2,1)S(1)} %add_convert_fusion.4), channel_id=1, source_target_pairs={{0,2},{1,3},{2,0},{3,1},{4,6},{5,7},{6,4},{7,5},{8,10},{9,11},{10,... | collective-permute-start | bytes 172040 | tf_op jit(solution)/shard_map/ppermute | solution.py:19
  59.6 2.7 %collective-permute-done.19 = bf16[16,1792]{1,0:T(8,128)(2,1)S(1)} collective-permute-done((bf16[16,1792]{1,0:T(8,128)(2,1)S(1)}, bf16[16,1792]{1,0:T(8,128)(2,1)S(1)}, u32[]{:S(2)}, u32[]{:S(2)}) %collective-permute-start.19) | collective-permute-done | bytes 57376 | tf_op jit(solution)/shard_map/ppermute | solution.py:19
  62.4 1.2 %collective-permute-done.20.refs_2_ = bf16[16,1792]{1,0:T(8,128)(2,1)S(1)} collective-permute-done((bf16[16,1792]{1,0:T(8,128)(2,1)S(1)}, bf16[16,1792]{1,0:T(8,128)(2,1)S(1)}, u32[]{:S(2)}, u32[]{:S(2)}) %collective-permute-start.20) | collective-permute-done | bytes 57376 | tf_op jit(solution)/shard_map/ppermute | solution.py:19
  63.7 1.4 %shard_map.72 = (f32[32,1792]{1,0:T(8,128)S(1)}, f32[32,2048]{1,0:T(8,128)S(1)}, bf16[32,2176]{1,0:T(8,128)(2,1)S(1)}) custom-call(f32[32,1792]{1,0:T(8,128)S(1)} %get-tuple-element.39.refs_0_, bf16[16,1792]{1,0:T(8,128)(2,1)S(1)} %add_convert_fusion.3.refs_1_, bf16[16,1792]{1,0:T(8,128)(2,1)S(1)} %collective-permute-done.20.refs_2_, ...), custom_call_target="tpu_custom_call" | custom-call | flops 234881024 | bytes 7691264 | tf_op jit(solution)/shard_map/pallas_call | solution.py:43
  65.1 1.4 %collective-permute-start.21 = (bf16[32,2176]{1,0:T(8,128)(2,1)S(1)}, bf16[32,2176]{1,0:T(8,128)(2,1)S(1)}, u32[]{:S(2)}, u32[]{:S(2)}) collective-permute-start(bf16[32,2176]{1,0:T(8,128)(2,1)S(1)} %get-tuple-element.46.message_ref), channel_id=1, source_target_pairs={{0,1},{1,0},{2,3},{3,2},{4,5},{5,4},{6,7},{7,6},{8,9},{9,8},{10,11... | collective-permute-start | bytes 417800 | tf_op jit(solution)/shard_map/ppermute | solution.py:19
  66.4 4.4 %collective-permute-done.21.swapped_ref = bf16[32,2176]{1,0:T(8,128)(2,1)S(1)} collective-permute-done((bf16[32,2176]{1,0:T(8,128)(2,1)S(1)}, bf16[32,2176]{1,0:T(8,128)(2,1)S(1)}, u32[]{:S(2)}, u32[]{:S(2)}) %collective-permute-start.21) | collective-permute-done | bytes 139296 | tf_op jit(solution)/shard_map/ppermute | solution.py:19
  70.8 0.9 shard_map.73
  71.8 1.2 %collective-permute-done.22 = bf16[16,1792]{1,0:T(8,128)(2,1)S(1)} collective-permute-done((bf16[16,1792]{1,0:T(8,128)(2,1)S(1)}, bf16[16,1792]{1,0:T(8,128)(2,1)S(1)}, u32[]{:S(2)}, u32[]{:S(2)}) %collective-permute-start.22) | collective-permute-done | bytes 57376 | tf_op jit(solution)/shard_map/ppermute | solution.py:19
  73.0 1.6 %collective-permute-start.25 = (bf16[16,1792]{1,0:T(8,128)(2,1)S(1)}, bf16[16,1792]{1,0:T(8,128)(2,1)S(1)}, u32[]{:S(2)}, u32[]{:S(2)}) collective-permute-start(bf16[16,1792]{1,0:T(8,128)(2,1)S(1)} %add_convert_fusion.2), channel_id=1, source_target_pairs={{0,24},{4,28},{8,16},{12,20},{16,8},{20,12},{24,0},{28,4},{1,25},{... | collective-permute-start | bytes 172040 | tf_op jit(solution)/shard_map/ppermute | solution.py:19
  74.6 0.8 collective-permute-start.24
  75.3 1.2 %collective-permute-start.23 = (bf16[16,1792]{1,0:T(8,128)(2,1)S(1)}, bf16[16,1792]{1,0:T(8,128)(2,1)S(1)}, u32[]{:S(2)}, u32[]{:S(2)}) collective-permute-start(bf16[16,1792]{1,0:T(8,128)(2,1)S(1)} %add_convert_fusion.2), channel_id=1, source_target_pairs={{0,8},{4,12},{8,0},{12,4},{16,24},{20,28},{24,16},{28,20},{1,9},{5... | collective-permute-start | bytes 172040 | tf_op jit(solution)/shard_map/ppermute | solution.py:19
  76.6 1.6 %collective-permute-done.25 = bf16[16,1792]{1,0:T(8,128)(2,1)S(1)} collective-permute-done((bf16[16,1792]{1,0:T(8,128)(2,1)S(1)}, bf16[16,1792]{1,0:T(8,128)(2,1)S(1)}, u32[]{:S(2)}, u32[]{:S(2)}) %collective-permute-start.25) | collective-permute-done | bytes 57376 | tf_op jit(solution)/shard_map/ppermute | solution.py:19
  78.2 1.0 collective-permute-done.24
  79.2 0.3 collective-permute-done.23
  79.6 2.2 %collective-permute-start.26 = (bf16[16,1792]{1,0:T(8,128)(2,1)S(1)}, bf16[16,1792]{1,0:T(8,128)(2,1)S(1)}, u32[]{:S(2)}, u32[]{:S(2)}) collective-permute-start(bf16[16,1792]{1,0:T(8,128)(2,1)S(1)} %add_convert_fusion.1), channel_id=1, source_target_pairs={{0,2},{1,3},{2,0},{3,1},{4,6},{5,7},{6,4},{7,5},{8,10},{9,11},{10,... | collective-permute-start | bytes 172040 | tf_op jit(solution)/shard_map/ppermute | solution.py:19
  81.8 2.9 %collective-permute-done.26 = bf16[16,1792]{1,0:T(8,128)(2,1)S(1)} collective-permute-done((bf16[16,1792]{1,0:T(8,128)(2,1)S(1)}, bf16[16,1792]{1,0:T(8,128)(2,1)S(1)}, u32[]{:S(2)}, u32[]{:S(2)}) %collective-permute-start.26) | collective-permute-done | bytes 57376 | tf_op jit(solution)/shard_map/ppermute | solution.py:19
  84.8 1.2 %collective-permute-done.27.refs_2_ = bf16[16,1792]{1,0:T(8,128)(2,1)S(1)} collective-permute-done((bf16[16,1792]{1,0:T(8,128)(2,1)S(1)}, bf16[16,1792]{1,0:T(8,128)(2,1)S(1)}, u32[]{:S(2)}, u32[]{:S(2)}) %collective-permute-start.27) | collective-permute-done | bytes 57376 | tf_op jit(solution)/shard_map/ppermute | solution.py:19
  86.0 1.4 %shard_map.74 = (f32[1,1792]{1,0:T(1,128)S(1)}, f32[1,1792]{1,0:T(1,128)S(1)}, f32[32,2048]{1,0:T(8,128)S(1)}, bf16[32,2176]{1,0:T(8,128)(2,1)S(1)}) custom-call(f32[32,1792]{1,0:T(8,128)S(1)} %get-tuple-element.44.refs_0_, bf16[16,1792]{1,0:T(8,128)(2,1)S(1)} %add_convert_fusion.refs_1_, bf16[16,1792]{1,0:T(8,128)(2,1)S(1)} %collective-permute-done.27.refs_2_, ...), custom_call_target="tpu_custom_call" | custom-call | flops 234881024 | bytes 7691264 | tf_op jit(solution)/shard_map/pallas_call | solution.py:43
  87.4 1.2 %collective-permute-start.28 = (bf16[32,2176]{1,0:T(8,128)(2,1)S(1)}, bf16[32,2176]{1,0:T(8,128)(2,1)S(1)}, u32[]{:S(2)}, u32[]{:S(2)}) collective-permute-start(bf16[32,2176]{1,0:T(8,128)(2,1)S(1)} %get-tuple-element.50.message_ref), channel_id=1, source_target_pairs={{0,1},{1,0},{2,3},{3,2},{4,5},{5,4},{6,7},{7,6},{8,9},{9,8},{10,11... | collective-permute-start | bytes 417800 | tf_op jit(solution)/shard_map/ppermute | solution.py:19
  88.6 0.9 collective-permute-start.29
  89.5 3.9 %collective-permute-done.29.other_ref = f32[1,1792]{1,0:T(1,128)S(1)} collective-permute-done((f32[1,1792]{1,0:T(1,128)S(1)}, f32[1,1792]{1,0:T(1,128)S(1)}, u32[]{:S(2)}, u32[]{:S(2)}) %collective-permute-start.29) | collective-permute-done | bytes 7200 | tf_op jit(solution)/shard_map/ppermute | solution.py:19
  93.4 0.9 shard_map.75
  94.3 12.7 %all_to_all.5.arrived_ref = bf16[32,14,128]{2,1,0:T(8,128)(2,1)S(1)} all-to-all(bf16[32,14,128]{2,1,0:T(8,128)(2,1)S(1)} %shard_map.75), channel_id=1, replica_groups=mesh['rack'=8,'expert'=4] {'rack','expert'}, dimensions={0} | all-to-all | bytes 229376 | tf_op jit(solution)/shard_map/all_to_all | solution.py:331
  106.9 0.7 shard_map.76
  (21 shorter events, 0.5 us)
Async XLA Ops:
  0.9 9.0 %collective-permute-start.1 = (bf16[16,128]{1,0:T(8,128)(2,1)S(1)}, bf16[16,128]{1,0:T(8,128)(2,1)S(1)}, u32[]{:S(2)}, u32[]{:S(2)}) collective-permute-start(bf16[16,128]{1,0:T(8,128)(2,1)S(1)} %get-tuple-element.30.refs_0_), channel_id=1, source_target_pairs={{0,2},{1,3},{2,0},{3,1},{4,6},{5,7},{6,4},{7,5},{8,10},{9,11},{10,... | collective-permute-start | bytes 12296 | tf_op jit(solution)/shard_map/ppermute | solution.py:19
  5.0 5.4 %collective-permute-start.2 = (bf16[16,128]{1,0:T(8,128)(2,1)S(1)}, bf16[16,128]{1,0:T(8,128)(2,1)S(1)}, u32[]{:S(2)}, u32[]{:S(2)}) collective-permute-start(bf16[16,128]{1,0:T(8,128)(2,1)S(1)} %get-tuple-element.31), channel_id=1, source_target_pairs={{0,3},{1,2},{2,1},{3,0},{4,7},{5,6},{6,5},{7,4},{8,11},{9,10},{10,... | collective-permute-start | bytes 12296 | tf_op jit(solution)/shard_map/ppermute | solution.py:19
  6.3 4.1 %collective-permute-start = (bf16[16,128]{1,0:T(8,128)(2,1)S(1)}, bf16[16,128]{1,0:T(8,128)(2,1)S(1)}, u32[]{:S(2)}, u32[]{:S(2)}) collective-permute-start(bf16[16,128]{1,0:T(8,128)(2,1)S(1)} %get-tuple-element.31), channel_id=1, source_target_pairs={{0,1},{1,0},{2,3},{3,2},{4,5},{5,4},{6,7},{7,6},{8,9},{9,8},{10,11... | collective-permute-start | bytes 12296 | tf_op jit(solution)/shard_map/ppermute | solution.py:19
  10.4 15.3 %copy-start = (bf16[1,1,1024,1792]{3,2,1,0:T(8,128)(2,1)S(1)}, bf16[1,1,1024,1792]{3,2,1,0:T(8,128)(2,1)}, u32[]{:S(2)}) copy-start(bf16[1,1,1024,1792]{3,2,1,0:T(8,128)(2,1)} %param.11) | copy-start | bytes 11010052
  10.4 4.7 %collective-permute-start.5 = (bf16[4,16,128]{2,1,0:T(8,128)(2,1)S(1)}, bf16[4,16,128]{2,1,0:T(8,128)(2,1)S(1)}, u32[]{:S(2)}, u32[]{:S(2)}) collective-permute-start(bf16[4,16,128]{2,1,0:T(8,128)(2,1)S(1)} %shard_map.66.refs_0_), channel_id=1, source_target_pairs={{0,24},{4,28},{8,16},{12,20},{16,8},{20,12},{24,0},{28,4},{1,25},{... | collective-permute-start | bytes 49160 | tf_op jit(solution)/shard_map/ppermute | solution.py:19
  12.9 3.7 %collective-permute-start.4 = (bf16[4,16,128]{2,1,0:T(8,128)(2,1)S(1)}, bf16[4,16,128]{2,1,0:T(8,128)(2,1)S(1)}, u32[]{:S(2)}, u32[]{:S(2)}) collective-permute-start(bf16[4,16,128]{2,1,0:T(8,128)(2,1)S(1)} %shard_map.66.refs_0_), channel_id=1, source_target_pairs={{0,16},{4,20},{8,24},{12,28},{16,0},{20,4},{24,8},{28,12},{1,17},{... | collective-permute-start | bytes 49160 | tf_op jit(solution)/shard_map/ppermute | solution.py:19
  13.4 3.7 %collective-permute-start.3 = (bf16[4,16,128]{2,1,0:T(8,128)(2,1)S(1)}, bf16[4,16,128]{2,1,0:T(8,128)(2,1)S(1)}, u32[]{:S(2)}, u32[]{:S(2)}) collective-permute-start(bf16[4,16,128]{2,1,0:T(8,128)(2,1)S(1)} %shard_map.66.refs_0_), channel_id=1, source_target_pairs={{0,8},{4,12},{8,0},{12,4},{16,24},{20,28},{24,16},{28,20},{1,9},{5... | collective-permute-start | bytes 49160 | tf_op jit(solution)/shard_map/ppermute | solution.py:19
  17.2 1.3 %collective-permute-start.6 = (bf16[16,16,128]{2,1,0:T(8,128)(2,1)S(1)}, bf16[16,16,128]{2,1,0:T(8,128)(2,1)S(1)}, u32[]{:S(2)}, u32[]{:S(2)}) collective-permute-start(bf16[16,16,128]{2,1,0:T(8,128)(2,1)S(1)} %shard_map.67.refs_0_), channel_id=1, source_target_pairs={{0,4},{4,0},{8,12},{12,8},{16,20},{20,16},{24,28},{28,24},{1,5},{5... | collective-permute-start | bytes 196616 | tf_op jit(solution)/shard_map/ppermute | solution.py:19
  19.9 5.8 %collective-permute-start.7 = (bf16[32,2176]{1,0:T(8,128)(2,1)S(1)}, bf16[32,2176]{1,0:T(8,128)(2,1)S(1)}, u32[]{:S(2)}, u32[]{:S(2)}) collective-permute-start(bf16[32,2176]{1,0:T(8,128)(2,1)S(1)} %get-tuple-element.35.message_ref), channel_id=1, source_target_pairs={{0,1},{1,0},{2,3},{3,2},{4,5},{5,4},{6,7},{7,6},{8,9},{9,8},{10,11... | collective-permute-start | bytes 417800 | tf_op jit(solution)/shard_map/ppermute | solution.py:19
  26.5 1.3 %collective-permute-start.8 = (bf16[16,1792]{1,0:T(8,128)(2,1)S(1)}, bf16[16,1792]{1,0:T(8,128)(2,1)S(1)}, u32[]{:S(2)}, u32[]{:S(2)}) collective-permute-start(bf16[16,1792]{1,0:T(8,128)(2,1)S(1)} %get-tuple-element.38), channel_id=1, source_target_pairs={{0,4},{4,0},{8,12},{12,8},{16,20},{20,16},{24,28},{28,24},{1,5},{5... | collective-permute-start | bytes 172040 | tf_op jit(solution)/shard_map/ppermute | solution.py:19
  27.9 5.2 %collective-permute-start.11 = (bf16[16,1792]{1,0:T(8,128)(2,1)S(1)}, bf16[16,1792]{1,0:T(8,128)(2,1)S(1)}, u32[]{:S(2)}, u32[]{:S(2)}) collective-permute-start(bf16[16,1792]{1,0:T(8,128)(2,1)S(1)} %add_convert_fusion.8), channel_id=1, source_target_pairs={{0,24},{4,28},{8,16},{12,20},{16,8},{20,12},{24,0},{28,4},{1,25},{... | collective-permute-start | bytes 172040 | tf_op jit(solution)/shard_map/ppermute | solution.py:19
  29.4 4.6 %collective-permute-start.10 = (bf16[16,1792]{1,0:T(8,128)(2,1)S(1)}, bf16[16,1792]{1,0:T(8,128)(2,1)S(1)}, u32[]{:S(2)}, u32[]{:S(2)}) collective-permute-start(bf16[16,1792]{1,0:T(8,128)(2,1)S(1)} %add_convert_fusion.8), channel_id=1, source_target_pairs={{0,16},{4,20},{8,24},{12,28},{16,0},{20,4},{24,8},{28,12},{1,17},{... | collective-permute-start | bytes 172040 | tf_op jit(solution)/shard_map/ppermute | solution.py:19
  29.9 4.2 %collective-permute-start.9 = (bf16[16,1792]{1,0:T(8,128)(2,1)S(1)}, bf16[16,1792]{1,0:T(8,128)(2,1)S(1)}, u32[]{:S(2)}, u32[]{:S(2)}) collective-permute-start(bf16[16,1792]{1,0:T(8,128)(2,1)S(1)} %add_convert_fusion.8), channel_id=1, source_target_pairs={{0,8},{4,12},{8,0},{12,4},{16,24},{20,28},{24,16},{28,20},{1,9},{5... | collective-permute-start | bytes 172040 | tf_op jit(solution)/shard_map/ppermute | solution.py:19
  34.1 5.4 %collective-permute-start.12 = (bf16[16,1792]{1,0:T(8,128)(2,1)S(1)}, bf16[16,1792]{1,0:T(8,128)(2,1)S(1)}, u32[]{:S(2)}, u32[]{:S(2)}) collective-permute-start(bf16[16,1792]{1,0:T(8,128)(2,1)S(1)} %add_convert_fusion.7), channel_id=1, source_target_pairs={{0,2},{1,3},{2,0},{3,1},{4,6},{5,7},{6,4},{7,5},{8,10},{9,11},{10,... | collective-permute-start | bytes 172040 | tf_op jit(solution)/shard_map/ppermute | solution.py:19
  39.5 1.3 %collective-permute-start.13 = (bf16[16,1792]{1,0:T(8,128)(2,1)S(1)}, bf16[16,1792]{1,0:T(8,128)(2,1)S(1)}, u32[]{:S(2)}, u32[]{:S(2)}) collective-permute-start(bf16[16,1792]{1,0:T(8,128)(2,1)S(1)} %add_convert_fusion.6.refs_1_), channel_id=1, source_target_pairs={{0,4},{4,0},{8,12},{12,8},{16,20},{20,16},{24,28},{28,24},{1,5},{5... | collective-permute-start | bytes 172040 | tf_op jit(solution)/shard_map/ppermute | solution.py:19
  42.2 5.8 %collective-permute-start.14 = (bf16[32,2176]{1,0:T(8,128)(2,1)S(1)}, bf16[32,2176]{1,0:T(8,128)(2,1)S(1)}, u32[]{:S(2)}, u32[]{:S(2)}) collective-permute-start(bf16[32,2176]{1,0:T(8,128)(2,1)S(1)} %get-tuple-element.41.message_ref), channel_id=1, source_target_pairs={{0,1},{1,0},{2,3},{3,2},{4,5},{5,4},{6,7},{7,6},{8,9},{9,8},{10,11... | collective-permute-start | bytes 417800 | tf_op jit(solution)/shard_map/ppermute | solution.py:19
  48.9 1.3 %collective-permute-start.15 = (bf16[16,1792]{1,0:T(8,128)(2,1)S(1)}, bf16[16,1792]{1,0:T(8,128)(2,1)S(1)}, u32[]{:S(2)}, u32[]{:S(2)}) collective-permute-start(bf16[16,1792]{1,0:T(8,128)(2,1)S(1)} %get-tuple-element.43), channel_id=1, source_target_pairs={{0,4},{4,0},{8,12},{12,8},{16,20},{20,16},{24,28},{28,24},{1,5},{5... | collective-permute-start | bytes 172040 | tf_op jit(solution)/shard_map/ppermute | solution.py:19
  50.2 5.2 %collective-permute-start.18 = (bf16[16,1792]{1,0:T(8,128)(2,1)S(1)}, bf16[16,1792]{1,0:T(8,128)(2,1)S(1)}, u32[]{:S(2)}, u32[]{:S(2)}) collective-permute-start(bf16[16,1792]{1,0:T(8,128)(2,1)S(1)} %add_convert_fusion.5), channel_id=1, source_target_pairs={{0,24},{4,28},{8,16},{12,20},{16,8},{20,12},{24,0},{28,4},{1,25},{... | collective-permute-start | bytes 172040 | tf_op jit(solution)/shard_map/ppermute | solution.py:19
  52.5 4.2 %collective-permute-start.17 = (bf16[16,1792]{1,0:T(8,128)(2,1)S(1)}, bf16[16,1792]{1,0:T(8,128)(2,1)S(1)}, u32[]{:S(2)}, u32[]{:S(2)}) collective-permute-start(bf16[16,1792]{1,0:T(8,128)(2,1)S(1)} %add_convert_fusion.5), channel_id=1, source_target_pairs={{0,16},{4,20},{8,24},{12,28},{16,0},{20,4},{24,8},{28,12},{1,17},{... | collective-permute-start | bytes 172040 | tf_op jit(solution)/shard_map/ppermute | solution.py:19
  53.0 4.2 %collective-permute-start.16 = (bf16[16,1792]{1,0:T(8,128)(2,1)S(1)}, bf16[16,1792]{1,0:T(8,128)(2,1)S(1)}, u32[]{:S(2)}, u32[]{:S(2)}) collective-permute-start(bf16[16,1792]{1,0:T(8,128)(2,1)S(1)} %add_convert_fusion.5), channel_id=1, source_target_pairs={{0,8},{4,12},{8,0},{12,4},{16,24},{20,28},{24,16},{28,20},{1,9},{5... | collective-permute-start | bytes 172040 | tf_op jit(solution)/shard_map/ppermute | solution.py:19
  57.2 5.1 %collective-permute-start.19 = (bf16[16,1792]{1,0:T(8,128)(2,1)S(1)}, bf16[16,1792]{1,0:T(8,128)(2,1)S(1)}, u32[]{:S(2)}, u32[]{:S(2)}) collective-permute-start(bf16[16,1792]{1,0:T(8,128)(2,1)S(1)} %add_convert_fusion.4), channel_id=1, source_target_pairs={{0,2},{1,3},{2,0},{3,1},{4,6},{5,7},{6,4},{7,5},{8,10},{9,11},{10,... | collective-permute-start | bytes 172040 | tf_op jit(solution)/shard_map/ppermute | solution.py:19
  62.4 1.3 %collective-permute-start.20 = (bf16[16,1792]{1,0:T(8,128)(2,1)S(1)}, bf16[16,1792]{1,0:T(8,128)(2,1)S(1)}, u32[]{:S(2)}, u32[]{:S(2)}) collective-permute-start(bf16[16,1792]{1,0:T(8,128)(2,1)S(1)} %add_convert_fusion.3.refs_1_), channel_id=1, source_target_pairs={{0,4},{4,0},{8,12},{12,8},{16,20},{20,16},{24,28},{28,24},{1,5},{5... | collective-permute-start | bytes 172040 | tf_op jit(solution)/shard_map/ppermute | solution.py:19
  65.1 5.8 %collective-permute-start.21 = (bf16[32,2176]{1,0:T(8,128)(2,1)S(1)}, bf16[32,2176]{1,0:T(8,128)(2,1)S(1)}, u32[]{:S(2)}, u32[]{:S(2)}) collective-permute-start(bf16[32,2176]{1,0:T(8,128)(2,1)S(1)} %get-tuple-element.46.message_ref), channel_id=1, source_target_pairs={{0,1},{1,0},{2,3},{3,2},{4,5},{5,4},{6,7},{7,6},{8,9},{9,8},{10,11... | collective-permute-start | bytes 417800 | tf_op jit(solution)/shard_map/ppermute | solution.py:19
  71.7 1.3 %collective-permute-start.22 = (bf16[16,1792]{1,0:T(8,128)(2,1)S(1)}, bf16[16,1792]{1,0:T(8,128)(2,1)S(1)}, u32[]{:S(2)}, u32[]{:S(2)}) collective-permute-start(bf16[16,1792]{1,0:T(8,128)(2,1)S(1)} %get-tuple-element.48), channel_id=1, source_target_pairs={{0,4},{4,0},{8,12},{12,8},{16,20},{20,16},{24,28},{28,24},{1,5},{5... | collective-permute-start | bytes 172040 | tf_op jit(solution)/shard_map/ppermute | solution.py:19
  73.0 5.2 %collective-permute-start.25 = (bf16[16,1792]{1,0:T(8,128)(2,1)S(1)}, bf16[16,1792]{1,0:T(8,128)(2,1)S(1)}, u32[]{:S(2)}, u32[]{:S(2)}) collective-permute-start(bf16[16,1792]{1,0:T(8,128)(2,1)S(1)} %add_convert_fusion.2), channel_id=1, source_target_pairs={{0,24},{4,28},{8,16},{12,20},{16,8},{20,12},{24,0},{28,4},{1,25},{... | collective-permute-start | bytes 172040 | tf_op jit(solution)/shard_map/ppermute | solution.py:19
  74.6 4.6 %collective-permute-start.24 = (bf16[16,1792]{1,0:T(8,128)(2,1)S(1)}, bf16[16,1792]{1,0:T(8,128)(2,1)S(1)}, u32[]{:S(2)}, u32[]{:S(2)}) collective-permute-start(bf16[16,1792]{1,0:T(8,128)(2,1)S(1)} %add_convert_fusion.2), channel_id=1, source_target_pairs={{0,16},{4,20},{8,24},{12,28},{16,0},{20,4},{24,8},{28,12},{1,17},{... | collective-permute-start | bytes 172040 | tf_op jit(solution)/shard_map/ppermute | solution.py:19
  75.3 4.2 %collective-permute-start.23 = (bf16[16,1792]{1,0:T(8,128)(2,1)S(1)}, bf16[16,1792]{1,0:T(8,128)(2,1)S(1)}, u32[]{:S(2)}, u32[]{:S(2)}) collective-permute-start(bf16[16,1792]{1,0:T(8,128)(2,1)S(1)} %add_convert_fusion.2), channel_id=1, source_target_pairs={{0,8},{4,12},{8,0},{12,4},{16,24},{20,28},{24,16},{28,20},{1,9},{5... | collective-permute-start | bytes 172040 | tf_op jit(solution)/shard_map/ppermute | solution.py:19
  79.6 5.2 %collective-permute-start.26 = (bf16[16,1792]{1,0:T(8,128)(2,1)S(1)}, bf16[16,1792]{1,0:T(8,128)(2,1)S(1)}, u32[]{:S(2)}, u32[]{:S(2)}) collective-permute-start(bf16[16,1792]{1,0:T(8,128)(2,1)S(1)} %add_convert_fusion.1), channel_id=1, source_target_pairs={{0,2},{1,3},{2,0},{3,1},{4,6},{5,7},{6,4},{7,5},{8,10},{9,11},{10,... | collective-permute-start | bytes 172040 | tf_op jit(solution)/shard_map/ppermute | solution.py:19
  84.7 1.3 %collective-permute-start.27 = (bf16[16,1792]{1,0:T(8,128)(2,1)S(1)}, bf16[16,1792]{1,0:T(8,128)(2,1)S(1)}, u32[]{:S(2)}, u32[]{:S(2)}) collective-permute-start(bf16[16,1792]{1,0:T(8,128)(2,1)S(1)} %add_convert_fusion.refs_1_), channel_id=1, source_target_pairs={{0,4},{4,0},{8,12},{12,8},{16,20},{20,16},{24,28},{28,24},{1,5},{5... | collective-permute-start | bytes 172040 | tf_op jit(solution)/shard_map/ppermute | solution.py:19
  87.4 5.9 %collective-permute-start.28 = (bf16[32,2176]{1,0:T(8,128)(2,1)S(1)}, bf16[32,2176]{1,0:T(8,128)(2,1)S(1)}, u32[]{:S(2)}, u32[]{:S(2)}) collective-permute-start(bf16[32,2176]{1,0:T(8,128)(2,1)S(1)} %get-tuple-element.50.message_ref), channel_id=1, source_target_pairs={{0,1},{1,0},{2,3},{3,2},{4,5},{5,4},{6,7},{7,6},{8,9},{9,8},{10,11... | collective-permute-start | bytes 417800 | tf_op jit(solution)/shard_map/ppermute | solution.py:19
  88.6 4.7 %collective-permute-start.29 = (f32[1,1792]{1,0:T(1,128)S(1)}, f32[1,1792]{1,0:T(1,128)S(1)}, u32[]{:S(2)}, u32[]{:S(2)}) collective-permute-start(f32[1,1792]{1,0:T(1,128)S(1)} %get-tuple-element.51), channel_id=1, source_target_pairs={{0,1},{1,0},{2,3},{3,2},{4,5},{5,4},{6,7},{7,6},{8,9},{9,8},{10,11... | collective-permute-start | bytes 21512 | tf_op jit(solution)/shard_map/ppermute | solution.py:19

commit v4 on v3

--- a/solution.py
+++ b/solution.py
@@ -27,9 +27,26 @@
     return values.astype(jnp.bfloat16)
 
 
+def exchanged_both(shard, rack_mask, expert_mask):
+    groups = lax.axis_size("expert")
+    pairs = [
+        (rack * groups + group, (rack ^ rack_mask) * groups + (group ^ expert_mask))
+        for rack in range(lax.axis_size("rack"))
+        for group in range(groups)
+    ]
+    return lax.ppermute(shard, ("rack", "expert"), pairs)
+
+
+def gather_masks(rack_count, group_count):
+    near = [(rack, group) for group in (0, 1) for rack in (0, 2)]
+    far = [(rack, group) for group in range(0, group_count, 2) for rack in range(0, rack_count, 4)]
+    return near, far
+
+
 WHOLE = pl.BlockSpec(memory_space=pltpu.VMEM)
 IN_HBM = pl.BlockSpec(memory_space=pltpu.HBM)
 LANES = 128
+PIECES = 2
 
 
 def in_vmem(shape, dtype):
@@ -123,12 +140,17 @@
     return lax.axis_index("rack") // 2 * group_count + lax.axis_index("expert")
 
 
-def placed(gathered_refs, half_width, group_count):
+def placed(gathered_refs, half_width, rack_count, group_count):
     wide = jnp.concatenate([ref[...].reshape(ref.shape[0], -1) for ref in gathered_refs], axis=0)
     count = wide.shape[0]
     place = lax.broadcasted_iota(jnp.int32, (count, count), 0)
     source = lax.broadcasted_iota(jnp.int32, (count, count), 1)
-    to_place = rounded(jnp.where(place == (source ^ own_place_of(group_count)), 1.0, 0.0))
+    near, far = gather_masks(rack_count, group_count)
+    distance = source // (count // 2) * (count // 2)
+    for masks, index in ((near, source % len(near)), (far, source // len(near) % len(far))):
+        for k, (rack, group) in enumerate(masks):
+            distance = distance + jnp.where(index == k, rack // 2 * group_count + group, 0)
+    to_place = rounded(jnp.where(place == (distance ^ own_place_of(group_count)), 1.0, 0.0))
     wide = jnp.dot(to_place, wide, preferred_element_type=jnp.float32)
     residual = wide[:, :half_width]
     ids = wide[:, half_width : half_width + LANES]
@@ -144,14 +166,27 @@
     return residual, mixing
 
 
-def gate_up_body(step, group_count, *refs):
+def piece_columns(piece, part):
+    size = part // PIECES
+    return [slice(start, start + size) for start in (piece * size, part + piece * size)]
+
+
+def multiplied(scaled, weight_ref, piece, product_ref, message_ref):
+    size = weight_ref.shape[1] // 2 // PIECES
+    for k, columns in enumerate(piece_columns(piece, weight_ref.shape[1] // 2)):
+        product = jnp.dot(scaled, weight_ref[:, columns], preferred_element_type=jnp.float32)
+        product_ref[:, k * size : (k + 1) * size] = product
+        message_ref[:, k * size : (k + 1) * size] = rounded(product)
+
+
+def first_piece_body(step, rack_count, group_count, *refs):
     first, last = step == 0, step == STEPS - 1
     if first:
-        *gathered_refs, gain_ref, weight_ref, residual_ref, mixing_ref, product_ref, message_ref = refs
-        residual, mixing_ref[...] = placed(gathered_refs, gain_ref.shape[1], group_count)
+        *gathered_refs, gain_ref, weight_ref, residual_ref, mixing_ref, scaled_ref, product_ref, message_ref = refs
+        residual, mixing_ref[...] = placed(gathered_refs, gain_ref.shape[1], rack_count, group_count)
         residual_ref[...] = residual
     else:
-        before_ref, own_ref, other_ref, gain_ref, weight_ref, *residual_refs, product_ref, message_ref = refs
+        before_ref, own_ref, other_ref, gain_ref, weight_ref, *residual_refs, scaled_ref, product_ref, message_ref = refs
         update = jnp.concatenate([own_ref[...], other_ref[...]], axis=0)
         residual = before_ref[...] + widened(update)
         if last:
@@ -162,16 +197,17 @@
         else:
             residual_refs[0][...] = residual
     scaled = rounded(residual * gain_ref[...])
-    width = weight_ref.shape[1]
-    for columns in column_blocks(width):
-        product = jnp.dot(scaled, weight_ref[:, columns], preferred_element_type=jnp.float32)
-        product_ref[:, columns] = product
-        message_ref[:, columns] = rounded(product)
+    scaled_ref[...] = scaled
+    multiplied(scaled, weight_ref, 0, product_ref, message_ref)
     square_sum = jnp.sum(residual * residual, axis=1, keepdims=True)
     square_high = widened(rounded(square_sum))
     lane = lax.broadcasted_iota(jnp.int32, (residual.shape[0], LANES), 1)
     tail = jnp.where(lane == 0, square_high, square_sum - square_high)
-    message_ref[:, width:] = rounded(tail)
+    message_ref[:, product_ref.shape[1] :] = rounded(tail)
+
+
+def other_piece_body(piece, scaled_ref, weight_ref, product_ref, message_ref):
+    multiplied(scaled_ref[...], weight_ref, piece, product_ref, message_ref)
 
 
 def token_matrix(count, group_count):
@@ -183,15 +219,15 @@
     return rounded(jnp.where(matches, 1.0, 0.0))
 
 
-def down_body(step, model_width, group_count, product_ref, message_ref, swapped_ref, mixing_ref, weight_ref, *out_refs):
+def down_body(step, piece, model_width, group_count, tail_ref, other_tail_ref, product_ref, swapped_ref, mixing_ref, weight_ref, *refs):
     width = product_ref.shape[1]
-    part = width // 2
-    tails = widened(message_ref[:, width:]) + widened(swapped_ref[:, width:])
+    size = width // 2
+    tails = widened(tail_ref[:, width:]) + widened(other_tail_ref[:, width:])
     square_sum = tails[:, 0:1] + tails[:, 1:2]
     scale = lax.rsqrt(square_sum / model_width + 1e-06)
     whole = product_ref[...] + widened(swapped_ref[:, :width])
-    gate = whole[:, :part] * scale
-    up = whole[:, part:] * scale
+    gate = whole[:, :size] * scale
+    up = whole[:, size:] * scale
     activated = rounded(gate / (1.0 + jnp.exp(-gate)) * up)
     mixing = mixing_ref[...]
     count = mixing.shape[0]
@@ -201,8 +237,15 @@
         activated = rounded(jnp.dot(to_tokens, activated, preferred_element_type=jnp.float32))
         mixing = jnp.dot(to_tokens, rounded(mixing), preferred_element_type=jnp.float32)
     mixing = mixing[:, step : step + 1]
+    rows = slice(piece * size, (piece + 1) * size)
+    before_refs, out_refs = (refs[:1], refs[1:]) if piece else ((), refs)
     for columns in column_blocks(weight_ref.shape[1]):
-        term = jnp.dot(activated, weight_ref[:, columns], preferred_element_type=jnp.float32)
+        term = jnp.dot(activated, weight_ref[rows, columns], preferred_element_type=jnp.float32)
+        for ref in before_refs:
+            term = term + ref[:, columns]
+        if piece < PIECES - 1:
+            out_refs[0][:, columns] = term
+            continue
         update = widened(rounded(term)) * mixing
         if last:
             blocks = slice(columns.start // LANES, columns.stop // LANES)
@@ -267,18 +310,17 @@
         out_shape = [in_vmem((count,) + block_shape, jnp.bfloat16)]
         return kernel_call(joined_body, out_shape, [ready, *pieces])[0]
 
-    rows = [own] + [exchanged(other if mask % 2 else own, "expert", mask) for mask in range(1, group_count)]
-    rows = joined(gate_up_weight, rows, group_count)
-    rows = [rows] + [exchanged(rows, "rack", mask) for mask in range(2, rack_count, 2)]
+    near, far = gather_masks(rack_count, group_count)
+    rows = [own] + [exchanged_both(other if group else own, rack, group) for rack, group in near[1:]]
+    rows = joined(gate_up_weight, rows, len(near))
+    rows = [rows] + [exchanged_both(rows, rack, group) for rack, group in far[1:]]
     rows = joined(gate_up_weight, rows, core_rows)
     gathered = [rows, exchanged(rows, "rack", 1)]
 
+    piece_width = product_width // PIECES
     for step_index in range(STEPS):
         last = step_index == STEPS - 1
-        products = [
-            in_vmem((token_count, product_width), jnp.float32),
-            in_vmem((token_count, product_width + LANES), jnp.bfloat16),
-        ]
+        product_shape = in_vmem((token_count, piece_width), jnp.float32)
         kept = [in_vmem((token_count, half_width), jnp.float32)]
         if step_index == 0:
             operands = gathered
@@ -287,34 +329,53 @@
             operands = [residual, sent, received]
         if last:
             kept = [in_vmem((1, half_width), jnp.float32)] * 2
-        *kept, product, message = kernel_call(
-            functools.partial(gate_up_body, step_index, group_count),
-            kept + products,
+        *kept, scaled, product, message = kernel_call(
+            functools.partial(first_piece_body, step_index, rack_count, group_count),
+            [
+                *kept,
+                in_vmem((token_count, half_width), jnp.bfloat16),
+                product_shape,
+                in_vmem((token_count, piece_width + LANES), jnp.bfloat16),
+            ],
             operands + [gain_half, gate_up_weight],
-            product_flops,
+            product_flops // PIECES,
         )
         if step_index == 0:
             residual, mixing = kept
         else:
             residual = kept[0]
-        swapped_rows = exchanged(message, "expert", 1)
+        products, swapped = [product], [exchanged(message, "expert", 1)]
+        for piece in range(1, PIECES):
+            product, piece_message = kernel_call(
+                functools.partial(other_piece_body, piece),
+                [product_shape, in_vmem((token_count, piece_width), jnp.bfloat16)],
+                [scaled, gate_up_weight],
+                product_flops // PIECES,
+            )
+            products.append(product)
+            swapped.append(exchanged(piece_message, "expert", 1))
         if last:
             own_row, other_row = kept
             other_row = exchanged(other_row, "expert", 1)
-            swapped_rows, other_row = lax.optimization_barrier((swapped_rows, other_row))
-            updates = [in_vmem((token_count, half_width // LANES, LANES), jnp.bfloat16)]
-        else:
-            updates = [
-                in_vmem((core_rows, half_width), jnp.float32),
-                in_vmem((core_rows, half_width), jnp.bfloat16),
-            ]
-        updates = kernel_call(
-            functools.partial(down_body, step_index, model_width, group_count),
-            updates,
-            [product, message, swapped_rows, mixing, w_down[0, 0]],
-            product_flops // 2,
-        )
+        updates = []
+        for piece in range(PIECES):
+            if piece < PIECES - 1:
+                shapes = [in_vmem((token_count, half_width), jnp.float32)]
+            elif last:
+                shapes = [in_vmem((token_count, half_width // LANES, LANES), jnp.bfloat16)]
+            else:
+                shapes = [
+                    in_vmem((core_rows, half_width), jnp.float32),
+                    in_vmem((core_rows, half_width), jnp.bfloat16),
+                ]
+            updates = kernel_call(
+                functools.partial(down_body, step_index, piece, model_width, group_count),
+                shapes,
+                [message, swapped[0], products[piece], swapped[piece], mixing, w_down[0, 0], *updates],
+                product_flops // 2 // PIECES,
+            )
         if last:
+            updates = lax.optimization_barrier((updates[0], other_row))
             break
         update = updates[0] + widened(exchanged(updates[1], "rack", 1))
         sent = rounded(update)
@@ -330,7 +391,7 @@
 
     arrived = lax.all_to_all(updates[0], ("rack", "expert"), split_axis=0, concat_axis=0, tiled=True)
     (result,) = kernel_call(
-        result_body, [jax.ShapeDtypeStruct((1, model_width), jnp.float32)], [arrived, own_row, other_row]
+        result_body, [jax.ShapeDtypeStruct((1, model_width), jnp.float32)], [arrived, own_row, updates[1]]
     )
     return result
 

time: 108 us -> 106 us (0.981)
  waiting for transfers between devices: 47.2 us -> 44.8 us
  blocking collectives: 12.7 us -> 10.6 us
  Pallas kernels: 14 us -> 15.6 us
    ppermute x0 -> x6, starting transfers between devices: none -> 9.04 us  [exchanged_both(): return lax.ppermute(shard, ('rack', 'expert'), pairs)]
    ppermute x30 -> x28, starting transfers between devices: 33.4 us -> 25.2 us  [exchanged(): lax.ppermute(shard, axis, [(i, i ^ mask) for i in range(lax.axis_size(axi...]
    ppermute x30 -> x28, waiting for transfers between devices: 47.2 us -> 40.6 us  [exchanged(): lax.ppermute(shard, axis, [(i, i ^ mask) for i in range(lax.axis_size(axi...]
    ppermute x0 -> x6, waiting for transfers between devices: none -> 4.23 us  [exchanged_both(): return lax.ppermute(shard, ('rack', 'expert'), pairs)]
    all_to_all x1, blocking collectives: 12.7 us -> 10.6 us  [dense_steps(): lax.all_to_all(updates[0], ('rack', 'expert'), split_axis=0, concat_axis=...]
    pallas_call x13 -> x21, Pallas kernels: 14 us -> 15.6 us  [kernel_call(): pl.pallas_call(body, out_shape=out_shape, in_specs=[WHOLE] * len(operands...]
  transfers between devices with their start and end apart: 30 -> 34, of which waited for: 27 -> 29; matrix products, arithmetic and copies ran while one was open for 0% -> 0% of each run, Pallas kernels for 3% -> 9%
where the time goes in v4:
time: 106 us
  waiting for transfers between devices  44.8 us (42%)
  starting transfers between devices  34.3 us (32%)
  Pallas kernels  15.6 us (15%)
  blocking collectives  10.6 us (10%)
    ppermute x28, waiting for transfers between devices, exchanged(): lax.ppermute(shard, axis, [(i, i ^ mask) for i in range(lax.axis_size(axi...  40.6 us
    ppermute x28, starting transfers between devices, exchanged(): lax.ppermute(shard, axis, [(i, i ^ mask) for i in range(lax.axis_size(axi...  25.2 us
    pallas_call x21, Pallas kernels, kernel_call(): pl.pallas_call(body, out_shape=out_shape, in_specs=[WHOLE] * len(operands...  15.6 us
    all_to_all x1, blocking collectives, dense_steps(): lax.all_to_all(updates[0], ('rack', 'expert'), split_axis=0, concat_axis=...  10.6 us
    ppermute x6, starting transfers between devices, exchanged_both(): return lax.ppermute(shard, ('rack', 'expert'), pairs)  9.04 us
    ppermute x6, waiting for transfers between devices, exchanged_both(): return lax.ppermute(shard, ('rack', 'expert'), pairs)  4.23 us
  transfers between devices with their start and end apart: 34, of which 29 were waited for; matrix products, arithmetic and copies ran while one was open for 0% of the time, Pallas kernels for 9%

profile of v4, /device:TPU:0, one launch (start us, length us, event | category | flops | bytes accessed | tf_op | source)
XLA Modules:
  0.0 105.6 jit_solution(13055078862720844863)
XLA Ops:
  0.0 0.9 shard_map.65
  0.9 3.0 %collective-permute-start = (bf16[16,128]{1,0:T(8,128)(2,1)S(1)}, bf16[16,128]{1,0:T(8,128)(2,1)S(1)}, u32[]{:S(2)}, u32[]{:S(2)}) collective-permute-start(bf16[16,128]{1,0:T(8,128)(2,1)S(1)} %get-tuple-element.42.refs_0_), channel_id=1, source_target_pairs={{0,8},{1,9},{2,10},{3,11},{4,12},{5,13},{6,14},{7,15},{8,0},{9,1},... | collective-permute-start | bytes 12296 | tf_op jit(solution)/shard_map/ppermute | solution.py:37
  3.9 1.5 %collective-permute-start.2 = (bf16[16,128]{1,0:T(8,128)(2,1)S(1)}, bf16[16,128]{1,0:T(8,128)(2,1)S(1)}, u32[]{:S(2)}, u32[]{:S(2)}) collective-permute-start(bf16[16,128]{1,0:T(8,128)(2,1)S(1)} %get-tuple-element.43), channel_id=1, source_target_pairs={{0,9},{1,8},{2,11},{3,10},{4,13},{5,12},{6,15},{7,14},{8,1},{9,0},... | collective-permute-start | bytes 12296 | tf_op jit(solution)/shard_map/ppermute | solution.py:37
  5.5 3.3 %shard_map.64.ready_ref.refs_3_.weight_ref.refs_4_ = bf16[1792,2048]{1,0:T(8,128)(2,1)S(1)} custom-call(bf16[1792,2,1024]{2,1,0:T(2,128)(2,1)} %bitcast.11), custom_call_target="tpu_custom_call" | custom-call | bytes 7340032 | tf_op jit(solution)/shard_map/pallas_call | solution.py:60
  9.0 3.8 %collective-permute-start.5 = (bf16[4,16,128]{2,1,0:T(8,128)(2,1)S(1)}, bf16[4,16,128]{2,1,0:T(8,128)(2,1)S(1)}, u32[]{:S(2)}, u32[]{:S(2)}) collective-permute-start(bf16[4,16,128]{2,1,0:T(8,128)(2,1)S(1)} %shard_map.66.refs_0_), channel_id=1, source_target_pairs={{0,18},{1,19},{2,16},{3,17},{4,22},{5,23},{6,20},{7,21},{8,26},{9,... | collective-permute-start | bytes 49160 | tf_op jit(solution)/shard_map/ppermute | solution.py:37
  13.5 1.1 %collective-permute-done.5.refs_3_ = bf16[4,16,128]{2,1,0:T(8,128)(2,1)S(1)} collective-permute-done((bf16[4,16,128]{2,1,0:T(8,128)(2,1)S(1)}, bf16[4,16,128]{2,1,0:T(8,128)(2,1)S(1)}, u32[]{:S(2)}, u32[]{:S(2)}) %collective-permute-start.5) | collective-permute-done | bytes 16416 | tf_op jit(solution)/shard_map/ppermute | solution.py:37
  14.6 2.9 %collective-permute-done.4.refs_2_ = bf16[4,16,128]{2,1,0:T(8,128)(2,1)S(1)} collective-permute-done((bf16[4,16,128]{2,1,0:T(8,128)(2,1)S(1)}, bf16[4,16,128]{2,1,0:T(8,128)(2,1)S(1)}, u32[]{:S(2)}, u32[]{:S(2)}) %collective-permute-start.4) | collective-permute-done | bytes 16416 | tf_op jit(solution)/shard_map/ppermute | solution.py:37
  17.6 1.2 %collective-permute-done.6.refs_1_ = bf16[16,16,128]{2,1,0:T(8,128)(2,1)S(1)} collective-permute-done((bf16[16,16,128]{2,1,0:T(8,128)(2,1)S(1)}, bf16[16,16,128]{2,1,0:T(8,128)(2,1)S(1)}, u32[]{:S(2)}, u32[]{:S(2)}) %collective-permute-start.6) | collective-permute-done | bytes 65568 | tf_op jit(solution)/shard_map/ppermute | solution.py:19
  18.8 0.8 shard_map.68
  19.7 1.6 %collective-permute-start.7 = (bf16[32,1152]{1,0:T(8,128)(2,1)S(1)}, bf16[32,1152]{1,0:T(8,128)(2,1)S(1)}, u32[]{:S(2)}, u32[]{:S(2)}) collective-permute-start(bf16[32,1152]{1,0:T(8,128)(2,1)S(1)} %get-tuple-element.46.tail_ref), channel_id=1, source_target_pairs={{0,1},{1,0},{2,3},{3,2},{4,5},{5,4},{6,7},{7,6},{8,9},{9,8},{10,11... | collective-permute-start | bytes 221192 | tf_op jit(solution)/shard_map/ppermute | solution.py:19
  21.3 0.7 shard_map.69
  22.5 1.6 %collective-permute-done.7.other_tail_ref.swapped_ref = bf16[32,1152]{1,0:T(8,128)(2,1)S(1)} collective-permute-done((bf16[32,1152]{1,0:T(8,128)(2,1)S(1)}, bf16[32,1152]{1,0:T(8,128)(2,1)S(1)}, u32[]{:S(2)}, u32[]{:S(2)}) %collective-permute-start.7) | collective-permute-done | bytes 73760 | tf_op jit(solution)/shard_map/ppermute | solution.py:19
  24.1 0.5 shard_map.70.refs_0_
  24.6 1.7 %collective-permute-done.8.swapped_ref = bf16[32,1024]{1,0:T(8,128)(2,1)S(1)} collective-permute-done((bf16[32,1024]{1,0:T(8,128)(2,1)S(1)}, bf16[32,1024]{1,0:T(8,128)(2,1)S(1)}, u32[]{:S(2)}, u32[]{:S(2)}) %collective-permute-start.8) | collective-permute-done | bytes 65568 | tf_op jit(solution)/shard_map/ppermute | solution.py:19
  26.3 0.6 shard_map.71
  26.9 1.2 %collective-permute-done.9 = bf16[16,1792]{1,0:T(8,128)(2,1)S(1)} collective-permute-done((bf16[16,1792]{1,0:T(8,128)(2,1)S(1)}, bf16[16,1792]{1,0:T(8,128)(2,1)S(1)}, u32[]{:S(2)}, u32[]{:S(2)}) %collective-permute-start.9) | collective-permute-done | bytes 57376 | tf_op jit(solution)/shard_map/ppermute | solution.py:19
  28.2 1.5 %collective-permute-start.12 = (bf16[16,1792]{1,0:T(8,128)(2,1)S(1)}, bf16[16,1792]{1,0:T(8,128)(2,1)S(1)}, u32[]{:S(2)}, u32[]{:S(2)}) collective-permute-start(bf16[16,1792]{1,0:T(8,128)(2,1)S(1)} %add_convert_fusion.8), channel_id=1, source_target_pairs={{0,24},{4,28},{8,16},{12,20},{16,8},{20,12},{24,0},{28,4},{1,25},{... | collective-permute-start | bytes 172040 | tf_op jit(solution)/shard_map/ppermute | solution.py:19
  29.7 1.5 %collective-permute-start.11 = (bf16[16,1792]{1,0:T(8,128)(2,1)S(1)}, bf16[16,1792]{1,0:T(8,128)(2,1)S(1)}, u32[]{:S(2)}, u32[]{:S(2)}) collective-permute-start(bf16[16,1792]{1,0:T(8,128)(2,1)S(1)} %add_convert_fusion.8), channel_id=1, source_target_pairs={{0,16},{4,20},{8,24},{12,28},{16,0},{20,4},{24,8},{28,12},{1,17},{... | collective-permute-start | bytes 172040 | tf_op jit(solution)/shard_map/ppermute | solution.py:19
  31.7 1.6 %collective-permute-done.12 = bf16[16,1792]{1,0:T(8,128)(2,1)S(1)} collective-permute-done((bf16[16,1792]{1,0:T(8,128)(2,1)S(1)}, bf16[16,1792]{1,0:T(8,128)(2,1)S(1)}, u32[]{:S(2)}, u32[]{:S(2)}) %collective-permute-start.12) | collective-permute-done | bytes 57376 | tf_op jit(solution)/shard_map/ppermute | solution.py:19
  33.4 1.0 collective-permute-done.11
  34.4 1.0 collective-permute-done.10
  35.4 2.0 %collective-permute-start.13 = (bf16[16,1792]{1,0:T(8,128)(2,1)S(1)}, bf16[16,1792]{1,0:T(8,128)(2,1)S(1)}, u32[]{:S(2)}, u32[]{:S(2)}) collective-permute-start(bf16[16,1792]{1,0:T(8,128)(2,1)S(1)} %add_convert_fusion.7), channel_id=1, source_target_pairs={{0,2},{1,3},{2,0},{3,1},{4,6},{5,7},{6,4},{7,5},{8,10},{9,11},{10,... | collective-permute-start | bytes 172040 | tf_op jit(solution)/shard_map/ppermute | solution.py:19
  37.5 3.7 %collective-permute-done.13 = bf16[16,1792]{1,0:T(8,128)(2,1)S(1)} collective-permute-done((bf16[16,1792]{1,0:T(8,128)(2,1)S(1)}, bf16[16,1792]{1,0:T(8,128)(2,1)S(1)}, u32[]{:S(2)}, u32[]{:S(2)}) %collective-permute-start.13) | collective-permute-done | bytes 57376 | tf_op jit(solution)/shard_map/ppermute | solution.py:19
  41.3 1.2 %collective-permute-done.14.refs_2_ = bf16[16,1792]{1,0:T(8,128)(2,1)S(1)} collective-permute-done((bf16[16,1792]{1,0:T(8,128)(2,1)S(1)}, bf16[16,1792]{1,0:T(8,128)(2,1)S(1)}, u32[]{:S(2)}, u32[]{:S(2)}) %collective-permute-start.14) | collective-permute-done | bytes 57376 | tf_op jit(solution)/shard_map/ppermute | solution.py:19
  42.5 0.7 shard_map.72
  43.6 0.7 shard_map.73
  44.3 1.8 %collective-permute-start.16 = (bf16[32,1024]{1,0:T(8,128)(2,1)S(1)}, bf16[32,1024]{1,0:T(8,128)(2,1)S(1)}, u32[]{:S(2)}, u32[]{:S(2)}) collective-permute-start(bf16[32,1024]{1,0:T(8,128)(2,1)S(1)} %get-tuple-element.58), channel_id=1, source_target_pairs={{0,1},{1,0},{2,3},{3,2},{4,5},{5,4},{6,7},{7,6},{8,9},{9,8},{10,11... | collective-permute-start | bytes 196616 | tf_op jit(solution)/shard_map/ppermute | solution.py:19
  46.1 2.3 %collective-permute-done.15.other_tail_ref.swapped_ref = bf16[32,1152]{1,0:T(8,128)(2,1)S(1)} collective-permute-done((bf16[32,1152]{1,0:T(8,128)(2,1)S(1)}, bf16[32,1152]{1,0:T(8,128)(2,1)S(1)}, u32[]{:S(2)}, u32[]{:S(2)}) %collective-permute-start.15) | collective-permute-done | bytes 73760 | tf_op jit(solution)/shard_map/ppermute | solution.py:19
  48.3 0.5 shard_map.74.refs_0_
  49.1 0.6 shard_map.75
  49.7 1.2 %collective-permute-done.17 = bf16[16,1792]{1,0:T(8,128)(2,1)S(1)} collective-permute-done((bf16[16,1792]{1,0:T(8,128)(2,1)S(1)}, bf16[16,1792]{1,0:T(8,128)(2,1)S(1)}, u32[]{:S(2)}, u32[]{:S(2)}) %collective-permute-start.17) | collective-permute-done | bytes 57376 | tf_op jit(solution)/shard_map/ppermute | solution.py:19
  50.9 0.6 collective-permute-start.20
  51.6 1.5 %collective-permute-start.19 = (bf16[16,1792]{1,0:T(8,128)(2,1)S(1)}, bf16[16,1792]{1,0:T(8,128)(2,1)S(1)}, u32[]{:S(2)}, u32[]{:S(2)}) collective-permute-start(bf16[16,1792]{1,0:T(8,128)(2,1)S(1)} %add_convert_fusion.5), channel_id=1, source_target_pairs={{0,16},{4,20},{8,24},{12,28},{16,0},{20,4},{24,8},{28,12},{1,17},{... | collective-permute-start | bytes 172040 | tf_op jit(solution)/shard_map/ppermute | solution.py:19
  53.0 1.5 %collective-permute-start.18 = (bf16[16,1792]{1,0:T(8,128)(2,1)S(1)}, bf16[16,1792]{1,0:T(8,128)(2,1)S(1)}, u32[]{:S(2)}, u32[]{:S(2)}) collective-permute-start(bf16[16,1792]{1,0:T(8,128)(2,1)S(1)} %add_convert_fusion.5), channel_id=1, source_target_pairs={{0,8},{4,12},{8,0},{12,4},{16,24},{20,28},{24,16},{28,20},{1,9},{5... | collective-permute-start | bytes 172040 | tf_op jit(solution)/shard_map/ppermute | solution.py:19
  54.5 2.0 %collective-permute-done.20 = bf16[16,1792]{1,0:T(8,128)(2,1)S(1)} collective-permute-done((bf16[16,1792]{1,0:T(8,128)(2,1)S(1)}, bf16[16,1792]{1,0:T(8,128)(2,1)S(1)}, u32[]{:S(2)}, u32[]{:S(2)}) %collective-permute-start.20) | collective-permute-done | bytes 57376 | tf_op jit(solution)/shard_map/ppermute | solution.py:19
  56.5 0.7 collective-permute-done.18
  57.2 1.4 %collective-permute-start.21 = (bf16[16,1792]{1,0:T(8,128)(2,1)S(1)}, bf16[16,1792]{1,0:T(8,128)(2,1)S(1)}, u32[]{:S(2)}, u32[]{:S(2)}) collective-permute-start(bf16[16,1792]{1,0:T(8,128)(2,1)S(1)} %add_convert_fusion.4), channel_id=1, source_target_pairs={{0,2},{1,3},{2,0},{3,1},{4,6},{5,7},{6,4},{7,5},{8,10},{9,11},{10,... | collective-permute-start | bytes 172040 | tf_op jit(solution)/shard_map/ppermute | solution.py:19
  58.7 3.7 %collective-permute-done.21 = bf16[16,1792]{1,0:T(8,128)(2,1)S(1)} collective-permute-done((bf16[16,1792]{1,0:T(8,128)(2,1)S(1)}, bf16[16,1792]{1,0:T(8,128)(2,1)S(1)}, u32[]{:S(2)}, u32[]{:S(2)}) %collective-permute-start.21) | collective-permute-done | bytes 57376 | tf_op jit(solution)/shard_map/ppermute | solution.py:19
  62.5 1.2 %collective-permute-done.22.refs_2_ = bf16[16,1792]{1,0:T(8,128)(2,1)S(1)} collective-permute-done((bf16[16,1792]{1,0:T(8,128)(2,1)S(1)}, bf16[16,1792]{1,0:T(8,128)(2,1)S(1)}, u32[]{:S(2)}, u32[]{:S(2)}) %collective-permute-start.22) | collective-permute-done | bytes 57376 | tf_op jit(solution)/shard_map/ppermute | solution.py:19
  63.7 0.7 shard_map.76
  64.4 1.4 %collective-permute-start.23 = (bf16[32,1152]{1,0:T(8,128)(2,1)S(1)}, bf16[32,1152]{1,0:T(8,128)(2,1)S(1)}, u32[]{:S(2)}, u32[]{:S(2)}) collective-permute-start(bf16[32,1152]{1,0:T(8,128)(2,1)S(1)} %get-tuple-element.63.tail_ref), channel_id=1, source_target_pairs={{0,1},{1,0},{2,3},{3,2},{4,5},{5,4},{6,7},{7,6},{8,9},{9,8},{10,11... | collective-permute-start | bytes 221192 | tf_op jit(solution)/shard_map/ppermute | solution.py:19
  65.8 0.7 shard_map.77
  66.5 0.7 collective-permute-start.24
  67.3 1.6 %collective-permute-done.23.other_tail_ref.swapped_ref = bf16[32,1152]{1,0:T(8,128)(2,1)S(1)} collective-permute-done((bf16[32,1152]{1,0:T(8,128)(2,1)S(1)}, bf16[32,1152]{1,0:T(8,128)(2,1)S(1)}, u32[]{:S(2)}, u32[]{:S(2)}) %collective-permute-start.23) | collective-permute-done | bytes 73760 | tf_op jit(solution)/shard_map/ppermute | solution.py:19
  68.8 0.5 shard_map.78.refs_0_
  69.4 1.4 %collective-permute-done.24.swapped_ref = bf16[32,1024]{1,0:T(8,128)(2,1)S(1)} collective-permute-done((bf16[32,1024]{1,0:T(8,128)(2,1)S(1)}, bf16[32,1024]{1,0:T(8,128)(2,1)S(1)}, u32[]{:S(2)}, u32[]{:S(2)}) %collective-permute-start.24) | collective-permute-done | bytes 65568 | tf_op jit(solution)/shard_map/ppermute | solution.py:19
  70.8 0.6 shard_map.79
  71.4 1.2 %collective-permute-done.25 = bf16[16,1792]{1,0:T(8,128)(2,1)S(1)} collective-permute-done((bf16[16,1792]{1,0:T(8,128)(2,1)S(1)}, bf16[16,1792]{1,0:T(8,128)(2,1)S(1)}, u32[]{:S(2)}, u32[]{:S(2)}) %collective-permute-start.25) | collective-permute-done | bytes 57376 | tf_op jit(solution)/shard_map/ppermute | solution.py:19
  72.7 1.5 %collective-permute-start.28 = (bf16[16,1792]{1,0:T(8,128)(2,1)S(1)}, bf16[16,1792]{1,0:T(8,128)(2,1)S(1)}, u32[]{:S(2)}, u32[]{:S(2)}) collective-permute-start(bf16[16,1792]{1,0:T(8,128)(2,1)S(1)} %add_convert_fusion.2), channel_id=1, source_target_pairs={{0,24},{4,28},{8,16},{12,20},{16,8},{20,12},{24,0},{28,4},{1,25},{... | collective-permute-start | bytes 172040 | tf_op jit(solution)/shard_map/ppermute | solution.py:19
  74.2 1.5 %collective-permute-start.27 = (bf16[16,1792]{1,0:T(8,128)(2,1)S(1)}, bf16[16,1792]{1,0:T(8,128)(2,1)S(1)}, u32[]{:S(2)}, u32[]{:S(2)}) collective-permute-start(bf16[16,1792]{1,0:T(8,128)(2,1)S(1)} %add_convert_fusion.2), channel_id=1, source_target_pairs={{0,16},{4,20},{8,24},{12,28},{16,0},{20,4},{24,8},{28,12},{1,17},{... | collective-permute-start | bytes 172040 | tf_op jit(solution)/shard_map/ppermute | solution.py:19
  76.2 1.6 %collective-permute-done.28 = bf16[16,1792]{1,0:T(8,128)(2,1)S(1)} collective-permute-done((bf16[16,1792]{1,0:T(8,128)(2,1)S(1)}, bf16[16,1792]{1,0:T(8,128)(2,1)S(1)}, u32[]{:S(2)}, u32[]{:S(2)}) %collective-permute-start.28) | collective-permute-done | bytes 57376 | tf_op jit(solution)/shard_map/ppermute | solution.py:19
  77.9 1.0 collective-permute-done.27
  78.9 1.0 collective-permute-done.26
  79.9 2.0 %collective-permute-start.29 = (bf16[16,1792]{1,0:T(8,128)(2,1)S(1)}, bf16[16,1792]{1,0:T(8,128)(2,1)S(1)}, u32[]{:S(2)}, u32[]{:S(2)}) collective-permute-start(bf16[16,1792]{1,0:T(8,128)(2,1)S(1)} %add_convert_fusion.1), channel_id=1, source_target_pairs={{0,2},{1,3},{2,0},{3,1},{4,6},{5,7},{6,4},{7,5},{8,10},{9,11},{10,... | collective-permute-start | bytes 172040 | tf_op jit(solution)/shard_map/ppermute | solution.py:19
  81.9 3.7 %collective-permute-done.29 = bf16[16,1792]{1,0:T(8,128)(2,1)S(1)} collective-permute-done((bf16[16,1792]{1,0:T(8,128)(2,1)S(1)}, bf16[16,1792]{1,0:T(8,128)(2,1)S(1)}, u32[]{:S(2)}, u32[]{:S(2)}) %collective-permute-start.29) | collective-permute-done | bytes 57376 | tf_op jit(solution)/shard_map/ppermute | solution.py:19
  85.8 1.2 %collective-permute-done.30.refs_2_ = bf16[16,1792]{1,0:T(8,128)(2,1)S(1)} collective-permute-done((bf16[16,1792]{1,0:T(8,128)(2,1)S(1)}, bf16[16,1792]{1,0:T(8,128)(2,1)S(1)}, u32[]{:S(2)}, u32[]{:S(2)}) %collective-permute-start.30) | collective-permute-done | bytes 57376 | tf_op jit(solution)/shard_map/ppermute | solution.py:19
  87.0 0.8 shard_map.80
  88.1 0.7 shard_map.81
  88.8 1.8 %collective-permute-start.32 = (bf16[32,1024]{1,0:T(8,128)(2,1)S(1)}, bf16[32,1024]{1,0:T(8,128)(2,1)S(1)}, u32[]{:S(2)}, u32[]{:S(2)}) collective-permute-start(bf16[32,1024]{1,0:T(8,128)(2,1)S(1)} %get-tuple-element.73), channel_id=1, source_target_pairs={{0,1},{1,0},{2,3},{3,2},{4,5},{5,4},{6,7},{7,6},{8,9},{9,8},{10,11... | collective-permute-start | bytes 196616 | tf_op jit(solution)/shard_map/ppermute | solution.py:19
  90.8 2.0 %collective-permute-done.31.other_tail_ref.swapped_ref = bf16[32,1152]{1,0:T(8,128)(2,1)S(1)} collective-permute-done((bf16[32,1152]{1,0:T(8,128)(2,1)S(1)}, bf16[32,1152]{1,0:T(8,128)(2,1)S(1)}, u32[]{:S(2)}, u32[]{:S(2)}) %collective-permute-start.31) | collective-permute-done | bytes 73760 | tf_op jit(solution)/shard_map/ppermute | solution.py:19
  92.9 0.7 shard_map.82.refs_0_
  93.6 0.7 shard_map.83
  94.3 10.6 %all_to_all.5.arrived_ref = bf16[32,14,128]{2,1,0:T(8,128)(2,1)S(1)} all-to-all(bf16[32,14,128]{2,1,0:T(8,128)(2,1)S(1)} %shard_map.83), channel_id=1, replica_groups=mesh['rack'=8,'expert'=4] {'rack','expert'}, dimensions={0} | all-to-all | bytes 229376 | tf_op jit(solution)/shard_map/all_to_all | solution.py:392
  104.9 0.7 shard_map.84
  (37 shorter events, 4.2 us)
Async XLA Ops:
  0.9 7.9 %collective-permute-start = (bf16[16,128]{1,0:T(8,128)(2,1)S(1)}, bf16[16,128]{1,0:T(8,128)(2,1)S(1)}, u32[]{:S(2)}, u32[]{:S(2)}) collective-permute-start(bf16[16,128]{1,0:T(8,128)(2,1)S(1)} %get-tuple-element.42.refs_0_), channel_id=1, source_target_pairs={{0,8},{1,9},{2,10},{3,11},{4,12},{5,13},{6,14},{7,15},{8,0},{9,1},... | collective-permute-start | bytes 12296 | tf_op jit(solution)/shard_map/ppermute | solution.py:37
  3.9 4.9 %collective-permute-start.2 = (bf16[16,128]{1,0:T(8,128)(2,1)S(1)}, bf16[16,128]{1,0:T(8,128)(2,1)S(1)}, u32[]{:S(2)}, u32[]{:S(2)}) collective-permute-start(bf16[16,128]{1,0:T(8,128)(2,1)S(1)} %get-tuple-element.43), channel_id=1, source_target_pairs={{0,9},{1,8},{2,11},{3,10},{4,13},{5,12},{6,15},{7,14},{8,1},{9,0},... | collective-permute-start | bytes 12296 | tf_op jit(solution)/shard_map/ppermute | solution.py:37
  5.4 3.6 %collective-permute-start.1 = (bf16[16,128]{1,0:T(8,128)(2,1)S(1)}, bf16[16,128]{1,0:T(8,128)(2,1)S(1)}, u32[]{:S(2)}, u32[]{:S(2)}) collective-permute-start(bf16[16,128]{1,0:T(8,128)(2,1)S(1)} %get-tuple-element.43), channel_id=1, source_target_pairs={{0,1},{1,0},{2,3},{3,2},{4,5},{5,4},{6,7},{7,6},{8,9},{9,8},{10,11... | collective-permute-start | bytes 12296 | tf_op jit(solution)/shard_map/ppermute | solution.py:37
  9.0 5.5 %collective-permute-start.5 = (bf16[4,16,128]{2,1,0:T(8,128)(2,1)S(1)}, bf16[4,16,128]{2,1,0:T(8,128)(2,1)S(1)}, u32[]{:S(2)}, u32[]{:S(2)}) collective-permute-start(bf16[4,16,128]{2,1,0:T(8,128)(2,1)S(1)} %shard_map.66.refs_0_), channel_id=1, source_target_pairs={{0,18},{1,19},{2,16},{3,17},{4,22},{5,23},{6,20},{7,21},{8,26},{9,... | collective-permute-start | bytes 49160 | tf_op jit(solution)/shard_map/ppermute | solution.py:37
  12.9 4.6 %collective-permute-start.4 = (bf16[4,16,128]{2,1,0:T(8,128)(2,1)S(1)}, bf16[4,16,128]{2,1,0:T(8,128)(2,1)S(1)}, u32[]{:S(2)}, u32[]{:S(2)}) collective-permute-start(bf16[4,16,128]{2,1,0:T(8,128)(2,1)S(1)} %shard_map.66.refs_0_), channel_id=1, source_target_pairs={{0,2},{1,3},{2,0},{3,1},{4,6},{5,7},{6,4},{7,5},{8,10},{9,11},{10,... | collective-permute-start | bytes 49160 | tf_op jit(solution)/shard_map/ppermute | solution.py:37
  13.2 4.3 %collective-permute-start.3 = (bf16[4,16,128]{2,1,0:T(8,128)(2,1)S(1)}, bf16[4,16,128]{2,1,0:T(8,128)(2,1)S(1)}, u32[]{:S(2)}, u32[]{:S(2)}) collective-permute-start(bf16[4,16,128]{2,1,0:T(8,128)(2,1)S(1)} %shard_map.66.refs_0_), channel_id=1, source_target_pairs={{0,16},{1,17},{2,18},{3,19},{4,20},{5,21},{6,22},{7,23},{8,24},{9,... | collective-permute-start | bytes 49160 | tf_op jit(solution)/shard_map/ppermute | solution.py:37
  17.5 1.3 %collective-permute-start.6 = (bf16[16,16,128]{2,1,0:T(8,128)(2,1)S(1)}, bf16[16,16,128]{2,1,0:T(8,128)(2,1)S(1)}, u32[]{:S(2)}, u32[]{:S(2)}) collective-permute-start(bf16[16,16,128]{2,1,0:T(8,128)(2,1)S(1)} %shard_map.67.refs_0_), channel_id=1, source_target_pairs={{0,4},{4,0},{8,12},{12,8},{16,20},{20,16},{24,28},{28,24},{1,5},{5... | collective-permute-start | bytes 196616 | tf_op jit(solution)/shard_map/ppermute | solution.py:19
  18.8 5.2 %copy-start = (bf16[1,1,1024,1792]{3,2,1,0:T(8,128)(2,1)S(1)}, bf16[1,1,1024,1792]{3,2,1,0:T(8,128)(2,1)}, u32[]{:S(2)}) copy-start(bf16[1,1,1024,1792]{3,2,1,0:T(8,128)(2,1)} %param.11) | copy-start | bytes 11010052
  19.7 4.4 %collective-permute-start.7 = (bf16[32,1152]{1,0:T(8,128)(2,1)S(1)}, bf16[32,1152]{1,0:T(8,128)(2,1)S(1)}, u32[]{:S(2)}, u32[]{:S(2)}) collective-permute-start(bf16[32,1152]{1,0:T(8,128)(2,1)S(1)} %get-tuple-element.46.tail_ref), channel_id=1, source_target_pairs={{0,1},{1,0},{2,3},{3,2},{4,5},{5,4},{6,7},{7,6},{8,9},{9,8},{10,11... | collective-permute-start | bytes 221192 | tf_op jit(solution)/shard_map/ppermute | solution.py:19
  22.0 4.3 %collective-permute-start.8 = (bf16[32,1024]{1,0:T(8,128)(2,1)S(1)}, bf16[32,1024]{1,0:T(8,128)(2,1)S(1)}, u32[]{:S(2)}, u32[]{:S(2)}) collective-permute-start(bf16[32,1024]{1,0:T(8,128)(2,1)S(1)} %get-tuple-element.49), channel_id=1, source_target_pairs={{0,1},{1,0},{2,3},{3,2},{4,5},{5,4},{6,7},{7,6},{8,9},{9,8},{10,11... | collective-permute-start | bytes 196616 | tf_op jit(solution)/shard_map/ppermute | solution.py:19
  26.9 1.3 %collective-permute-start.9 = (bf16[16,1792]{1,0:T(8,128)(2,1)S(1)}, bf16[16,1792]{1,0:T(8,128)(2,1)S(1)}, u32[]{:S(2)}, u32[]{:S(2)}) collective-permute-start(bf16[16,1792]{1,0:T(8,128)(2,1)S(1)} %get-tuple-element.53), channel_id=1, source_target_pairs={{0,4},{4,0},{8,12},{12,8},{16,20},{20,16},{24,28},{28,24},{1,5},{5... | collective-permute-start | bytes 172040 | tf_op jit(solution)/shard_map/ppermute | solution.py:19
  28.2 5.2 %collective-permute-start.12 = (bf16[16,1792]{1,0:T(8,128)(2,1)S(1)}, bf16[16,1792]{1,0:T(8,128)(2,1)S(1)}, u32[]{:S(2)}, u32[]{:S(2)}) collective-permute-start(bf16[16,1792]{1,0:T(8,128)(2,1)S(1)} %add_convert_fusion.8), channel_id=1, source_target_pairs={{0,24},{4,28},{8,16},{12,20},{16,8},{20,12},{24,0},{28,4},{1,25},{... | collective-permute-start | bytes 172040 | tf_op jit(solution)/shard_map/ppermute | solution.py:19
  29.7 4.7 %collective-permute-start.11 = (bf16[16,1792]{1,0:T(8,128)(2,1)S(1)}, bf16[16,1792]{1,0:T(8,128)(2,1)S(1)}, u32[]{:S(2)}, u32[]{:S(2)}) collective-permute-start(bf16[16,1792]{1,0:T(8,128)(2,1)S(1)} %add_convert_fusion.8), channel_id=1, source_target_pairs={{0,16},{4,20},{8,24},{12,28},{16,0},{20,4},{24,8},{28,12},{1,17},{... | collective-permute-start | bytes 172040 | tf_op jit(solution)/shard_map/ppermute | solution.py:19
  31.2 4.2 %collective-permute-start.10 = (bf16[16,1792]{1,0:T(8,128)(2,1)S(1)}, bf16[16,1792]{1,0:T(8,128)(2,1)S(1)}, u32[]{:S(2)}, u32[]{:S(2)}) collective-permute-start(bf16[16,1792]{1,0:T(8,128)(2,1)S(1)} %add_convert_fusion.8), channel_id=1, source_target_pairs={{0,8},{4,12},{8,0},{12,4},{16,24},{20,28},{24,16},{28,20},{1,9},{5... | collective-permute-start | bytes 172040 | tf_op jit(solution)/shard_map/ppermute | solution.py:19
  35.4 5.8 %collective-permute-start.13 = (bf16[16,1792]{1,0:T(8,128)(2,1)S(1)}, bf16[16,1792]{1,0:T(8,128)(2,1)S(1)}, u32[]{:S(2)}, u32[]{:S(2)}) collective-permute-start(bf16[16,1792]{1,0:T(8,128)(2,1)S(1)} %add_convert_fusion.7), channel_id=1, source_target_pairs={{0,2},{1,3},{2,0},{3,1},{4,6},{5,7},{6,4},{7,5},{8,10},{9,11},{10,... | collective-permute-start | bytes 172040 | tf_op jit(solution)/shard_map/ppermute | solution.py:19
  41.2 1.3 %collective-permute-start.14 = (bf16[16,1792]{1,0:T(8,128)(2,1)S(1)}, bf16[16,1792]{1,0:T(8,128)(2,1)S(1)}, u32[]{:S(2)}, u32[]{:S(2)}) collective-permute-start(bf16[16,1792]{1,0:T(8,128)(2,1)S(1)} %add_convert_fusion.6.refs_1_), channel_id=1, source_target_pairs={{0,4},{4,0},{8,12},{12,8},{16,20},{20,16},{24,28},{28,24},{1,5},{5... | collective-permute-start | bytes 172040 | tf_op jit(solution)/shard_map/ppermute | solution.py:19
  43.3 5.1 %collective-permute-start.15 = (bf16[32,1152]{1,0:T(8,128)(2,1)S(1)}, bf16[32,1152]{1,0:T(8,128)(2,1)S(1)}, u32[]{:S(2)}, u32[]{:S(2)}) collective-permute-start(bf16[32,1152]{1,0:T(8,128)(2,1)S(1)} %get-tuple-element.55.tail_ref), channel_id=1, source_target_pairs={{0,1},{1,0},{2,3},{3,2},{4,5},{5,4},{6,7},{7,6},{8,9},{9,8},{10,11... | collective-permute-start | bytes 221192 | tf_op jit(solution)/shard_map/ppermute | solution.py:19
  44.3 4.8 %collective-permute-start.16 = (bf16[32,1024]{1,0:T(8,128)(2,1)S(1)}, bf16[32,1024]{1,0:T(8,128)(2,1)S(1)}, u32[]{:S(2)}, u32[]{:S(2)}) collective-permute-start(bf16[32,1024]{1,0:T(8,128)(2,1)S(1)} %get-tuple-element.58), channel_id=1, source_target_pairs={{0,1},{1,0},{2,3},{3,2},{4,5},{5,4},{6,7},{7,6},{8,9},{9,8},{10,11... | collective-permute-start | bytes 196616 | tf_op jit(solution)/shard_map/ppermute | solution.py:19
  49.6 1.3 %collective-permute-start.17 = (bf16[16,1792]{1,0:T(8,128)(2,1)S(1)}, bf16[16,1792]{1,0:T(8,128)(2,1)S(1)}, u32[]{:S(2)}, u32[]{:S(2)}) collective-permute-start(bf16[16,1792]{1,0:T(8,128)(2,1)S(1)} %get-tuple-element.61), channel_id=1, source_target_pairs={{0,4},{4,0},{8,12},{12,8},{16,20},{20,16},{24,28},{28,24},{1,5},{5... | collective-permute-start | bytes 172040 | tf_op jit(solution)/shard_map/ppermute | solution.py:19
  50.9 5.6 %collective-permute-start.20 = (bf16[16,1792]{1,0:T(8,128)(2,1)S(1)}, bf16[16,1792]{1,0:T(8,128)(2,1)S(1)}, u32[]{:S(2)}, u32[]{:S(2)}) collective-permute-start(bf16[16,1792]{1,0:T(8,128)(2,1)S(1)} %add_convert_fusion.5), channel_id=1, source_target_pairs={{0,24},{4,28},{8,16},{12,20},{16,8},{20,12},{24,0},{28,4},{1,25},{... | collective-permute-start | bytes 172040 | tf_op jit(solution)/shard_map/ppermute | solution.py:19
  51.6 5.0 %collective-permute-start.19 = (bf16[16,1792]{1,0:T(8,128)(2,1)S(1)}, bf16[16,1792]{1,0:T(8,128)(2,1)S(1)}, u32[]{:S(2)}, u32[]{:S(2)}) collective-permute-start(bf16[16,1792]{1,0:T(8,128)(2,1)S(1)} %add_convert_fusion.5), channel_id=1, source_target_pairs={{0,16},{4,20},{8,24},{12,28},{16,0},{20,4},{24,8},{28,12},{1,17},{... | collective-permute-start | bytes 172040 | tf_op jit(solution)/shard_map/ppermute | solution.py:19
  53.0 4.2 %collective-permute-start.18 = (bf16[16,1792]{1,0:T(8,128)(2,1)S(1)}, bf16[16,1792]{1,0:T(8,128)(2,1)S(1)}, u32[]{:S(2)}, u32[]{:S(2)}) collective-permute-start(bf16[16,1792]{1,0:T(8,128)(2,1)S(1)} %add_convert_fusion.5), channel_id=1, source_target_pairs={{0,8},{4,12},{8,0},{12,4},{16,24},{20,28},{24,16},{28,20},{1,9},{5... | collective-permute-start | bytes 172040 | tf_op jit(solution)/shard_map/ppermute | solution.py:19
  57.2 5.1 %collective-permute-start.21 = (bf16[16,1792]{1,0:T(8,128)(2,1)S(1)}, bf16[16,1792]{1,0:T(8,128)(2,1)S(1)}, u32[]{:S(2)}, u32[]{:S(2)}) collective-permute-start(bf16[16,1792]{1,0:T(8,128)(2,1)S(1)} %add_convert_fusion.4), channel_id=1, source_target_pairs={{0,2},{1,3},{2,0},{3,1},{4,6},{5,7},{6,4},{7,5},{8,10},{9,11},{10,... | collective-permute-start | bytes 172040 | tf_op jit(solution)/shard_map/ppermute | solution.py:19
  62.4 1.3 %collective-permute-start.22 = (bf16[16,1792]{1,0:T(8,128)(2,1)S(1)}, bf16[16,1792]{1,0:T(8,128)(2,1)S(1)}, u32[]{:S(2)}, u32[]{:S(2)}) collective-permute-start(bf16[16,1792]{1,0:T(8,128)(2,1)S(1)} %add_convert_fusion.3.refs_1_), channel_id=1, source_target_pairs={{0,4},{4,0},{8,12},{12,8},{16,20},{20,16},{24,28},{28,24},{1,5},{5... | collective-permute-start | bytes 172040 | tf_op jit(solution)/shard_map/ppermute | solution.py:19
  64.4 4.4 %collective-permute-start.23 = (bf16[32,1152]{1,0:T(8,128)(2,1)S(1)}, bf16[32,1152]{1,0:T(8,128)(2,1)S(1)}, u32[]{:S(2)}, u32[]{:S(2)}) collective-permute-start(bf16[32,1152]{1,0:T(8,128)(2,1)S(1)} %get-tuple-element.63.tail_ref), channel_id=1, source_target_pairs={{0,1},{1,0},{2,3},{3,2},{4,5},{5,4},{6,7},{7,6},{8,9},{9,8},{10,11... | collective-permute-start | bytes 221192 | tf_op jit(solution)/shard_map/ppermute | solution.py:19
  66.5 4.3 %collective-permute-start.24 = (bf16[32,1024]{1,0:T(8,128)(2,1)S(1)}, bf16[32,1024]{1,0:T(8,128)(2,1)S(1)}, u32[]{:S(2)}, u32[]{:S(2)}) collective-permute-start(bf16[32,1024]{1,0:T(8,128)(2,1)S(1)} %get-tuple-element.66), channel_id=1, source_target_pairs={{0,1},{1,0},{2,3},{3,2},{4,5},{5,4},{6,7},{7,6},{8,9},{9,8},{10,11... | collective-permute-start | bytes 196616 | tf_op jit(solution)/shard_map/ppermute | solution.py:19
  71.4 1.3 %collective-permute-start.25 = (bf16[16,1792]{1,0:T(8,128)(2,1)S(1)}, bf16[16,1792]{1,0:T(8,128)(2,1)S(1)}, u32[]{:S(2)}, u32[]{:S(2)}) collective-permute-start(bf16[16,1792]{1,0:T(8,128)(2,1)S(1)} %get-tuple-element.69), channel_id=1, source_target_pairs={{0,4},{4,0},{8,12},{12,8},{16,20},{20,16},{24,28},{28,24},{1,5},{5... | collective-permute-start | bytes 172040 | tf_op jit(solution)/shard_map/ppermute | solution.py:19
  72.7 5.2 %collective-permute-start.28 = (bf16[16,1792]{1,0:T(8,128)(2,1)S(1)}, bf16[16,1792]{1,0:T(8,128)(2,1)S(1)}, u32[]{:S(2)}, u32[]{:S(2)}) collective-permute-start(bf16[16,1792]{1,0:T(8,128)(2,1)S(1)} %add_convert_fusion.2), channel_id=1, source_target_pairs={{0,24},{4,28},{8,16},{12,20},{16,8},{20,12},{24,0},{28,4},{1,25},{... | collective-permute-start | bytes 172040 | tf_op jit(solution)/shard_map/ppermute | solution.py:19
  74.2 4.7 %collective-permute-start.27 = (bf16[16,1792]{1,0:T(8,128)(2,1)S(1)}, bf16[16,1792]{1,0:T(8,128)(2,1)S(1)}, u32[]{:S(2)}, u32[]{:S(2)}) collective-permute-start(bf16[16,1792]{1,0:T(8,128)(2,1)S(1)} %add_convert_fusion.2), channel_id=1, source_target_pairs={{0,16},{4,20},{8,24},{12,28},{16,0},{20,4},{24,8},{28,12},{1,17},{... | collective-permute-start | bytes 172040 | tf_op jit(solution)/shard_map/ppermute | solution.py:19
  75.7 4.2 %collective-permute-start.26 = (bf16[16,1792]{1,0:T(8,128)(2,1)S(1)}, bf16[16,1792]{1,0:T(8,128)(2,1)S(1)}, u32[]{:S(2)}, u32[]{:S(2)}) collective-permute-start(bf16[16,1792]{1,0:T(8,128)(2,1)S(1)} %add_convert_fusion.2), channel_id=1, source_target_pairs={{0,8},{4,12},{8,0},{12,4},{16,24},{20,28},{24,16},{28,20},{1,9},{5... | collective-permute-start | bytes 172040 | tf_op jit(solution)/shard_map/ppermute | solution.py:19
  79.9 5.8 %collective-permute-start.29 = (bf16[16,1792]{1,0:T(8,128)(2,1)S(1)}, bf16[16,1792]{1,0:T(8,128)(2,1)S(1)}, u32[]{:S(2)}, u32[]{:S(2)}) collective-permute-start(bf16[16,1792]{1,0:T(8,128)(2,1)S(1)} %add_convert_fusion.1), channel_id=1, source_target_pairs={{0,2},{1,3},{2,0},{3,1},{4,6},{5,7},{6,4},{7,5},{8,10},{9,11},{10,... | collective-permute-start | bytes 172040 | tf_op jit(solution)/shard_map/ppermute | solution.py:19
  85.7 1.3 %collective-permute-start.30 = (bf16[16,1792]{1,0:T(8,128)(2,1)S(1)}, bf16[16,1792]{1,0:T(8,128)(2,1)S(1)}, u32[]{:S(2)}, u32[]{:S(2)}) collective-permute-start(bf16[16,1792]{1,0:T(8,128)(2,1)S(1)} %add_convert_fusion.refs_1_), channel_id=1, source_target_pairs={{0,4},{4,0},{8,12},{12,8},{16,20},{20,16},{24,28},{28,24},{1,5},{5... | collective-permute-start | bytes 172040 | tf_op jit(solution)/shard_map/ppermute | solution.py:19
  87.8 5.1 %collective-permute-start.31 = (bf16[32,1152]{1,0:T(8,128)(2,1)S(1)}, bf16[32,1152]{1,0:T(8,128)(2,1)S(1)}, u32[]{:S(2)}, u32[]{:S(2)}) collective-permute-start(bf16[32,1152]{1,0:T(8,128)(2,1)S(1)} %get-tuple-element.70.tail_ref), channel_id=1, source_target_pairs={{0,1},{1,0},{2,3},{3,2},{4,5},{5,4},{6,7},{7,6},{8,9},{9,8},{10,11... | collective-permute-start | bytes 221192 | tf_op jit(solution)/shard_map/ppermute | solution.py:19
  88.8 4.8 %collective-permute-start.32 = (bf16[32,1024]{1,0:T(8,128)(2,1)S(1)}, bf16[32,1024]{1,0:T(8,128)(2,1)S(1)}, u32[]{:S(2)}, u32[]{:S(2)}) collective-permute-start(bf16[32,1024]{1,0:T(8,128)(2,1)S(1)} %get-tuple-element.73), channel_id=1, source_target_pairs={{0,1},{1,0},{2,3},{3,2},{4,5},{5,4},{6,7},{7,6},{8,9},{9,8},{10,11... | collective-permute-start | bytes 196616 | tf_op jit(solution)/shard_map/ppermute | solution.py:19
  90.6 3.7 %collective-permute-start.33 = (f32[1,1792]{1,0:T(1,128)S(1)}, f32[1,1792]{1,0:T(1,128)S(1)}, u32[]{:S(2)}, u32[]{:S(2)}) collective-permute-start(f32[1,1792]{1,0:T(1,128)S(1)} %get-tuple-element.75), channel_id=1, source_target_pairs={{0,1},{1,0},{2,3},{3,2},{4,5},{5,4},{6,7},{7,6},{8,9},{9,8},{10,11... | collective-permute-start | bytes 21512 | tf_op jit(solution)/shard_map/ppermute | solution.py:19

commit v5 on v4

--- a/solution.py
+++ b/solution.py
@@ -37,9 +37,14 @@
     return lax.ppermute(shard, ("rack", "expert"), pairs)
 
 
+def crossed(rack_mask, expert_mask):
+    changed = bin(rack_mask >> 1).count("1") + bin(expert_mask >> 1).count("1")
+    return rack_mask ^ changed % 2, expert_mask
+
+
 def gather_masks(rack_count, group_count):
-    near = [(rack, group) for group in (0, 1) for rack in (0, 2)]
-    far = [(rack, group) for group in range(0, group_count, 2) for rack in range(0, rack_count, 4)]
+    near = [(0, 0), (2, 0), (1, 1), (3, 1)]
+    far = [crossed(rack, group) for group in range(0, group_count, 2) for rack in range(0, rack_count, 4)]
     return near, far
 
 
@@ -113,13 +118,16 @@
         )
 
 
-def weights_body(gate_up_ref, weight_ref, arrived_ref, semaphores):
+def weights_body(*refs, first, before):
+    gate_up_ref, weight_ref, arrived_ref, semaphores = refs[before:]
     part = arrived_ref.shape[2]
     count = semaphores.shape[0]
     block = arrived_ref.shape[0] // count
     blocks = [pl.ds(k * block, block) for k in range(count)]
     copies = [
-        pltpu.make_async_copy(gate_up_ref.at[rows], arrived_ref.at[rows], semaphores.at[k])
+        pltpu.make_async_copy(
+            gate_up_ref.at[pl.ds(first + k * block, block)], arrived_ref.at[rows], semaphores.at[k]
+        )
         for k, rows in enumerate(blocks)
     ]
     for copy in copies:
@@ -129,15 +137,23 @@
         weight_ref[rows] = arrived_ref[rows].reshape(block, 2 * part)
 
 
-def joined_body(ready_ref, *refs):
-    *pieces, out_ref = refs
+def joined_body(piece_count, *refs):
+    pieces, out_ref = refs[:piece_count], refs[-1]
     size = out_ref.shape[0] // len(pieces)
     for k, piece in enumerate(pieces):
         out_ref[k * size : (k + 1) * size] = piece[...].reshape(size, *out_ref.shape[1:])
 
 
-def own_place_of(group_count):
-    return lax.axis_index("rack") // 2 * group_count + lax.axis_index("expert")
+def own_core_of():
+    rack, group = lax.axis_index("rack"), lax.axis_index("expert") // 2
+    bits = [rack // 2**k for k in range(lax.axis_size("rack").bit_length() - 1)]
+    bits += [group // 2**k for k in range(lax.axis_size("expert").bit_length() - 2)]
+    return sum(bits) % 2
+
+
+def own_place_of(core_rows, group_count):
+    rack = lax.axis_index("rack")
+    return (rack + own_core_of()) % 2 * core_rows + rack // 2 * group_count + lax.axis_index("expert")
 
 
 def placed(gathered_refs, half_width, rack_count, group_count):
@@ -149,8 +165,10 @@
     distance = source // (count // 2) * (count // 2)
     for masks, index in ((near, source % len(near)), (far, source // len(near) % len(far))):
         for k, (rack, group) in enumerate(masks):
-            distance = distance + jnp.where(index == k, rack // 2 * group_count + group, 0)
-    to_place = rounded(jnp.where(place == (distance ^ own_place_of(group_count)), 1.0, 0.0))
+            step = rack % 2 * (count // 2) + rack // 2 * group_count + group
+            distance = distance ^ jnp.where(index == k, step, 0)
+    own_place = own_place_of(count // 2, group_count)
+    to_place = rounded(jnp.where(place == (distance ^ own_place), 1.0, 0.0))
     wide = jnp.dot(to_place, wide, preferred_element_type=jnp.float32)
     residual = wide[:, :half_width]
     ids = wide[:, half_width : half_width + LANES]
@@ -171,10 +189,12 @@
     return [slice(start, start + size) for start in (piece * size, part + piece * size)]
 
 
-def multiplied(scaled, weight_ref, piece, product_ref, message_ref):
-    size = weight_ref.shape[1] // 2 // PIECES
-    for k, columns in enumerate(piece_columns(piece, weight_ref.shape[1] // 2)):
-        product = jnp.dot(scaled, weight_ref[:, columns], preferred_element_type=jnp.float32)
+def multiplied(scaled, upper_ref, lower_ref, piece, product_ref, message_ref):
+    depth, width = upper_ref.shape
+    size = width // 2 // PIECES
+    for k, columns in enumerate(piece_columns(piece, width // 2)):
+        product = jnp.dot(scaled[:, :depth], upper_ref[:, columns], preferred_element_type=jnp.float32)
+        product += jnp.dot(scaled[:, depth:], lower_ref[:, columns], preferred_element_type=jnp.float32)
         product_ref[:, k * size : (k + 1) * size] = product
         message_ref[:, k * size : (k + 1) * size] = rounded(product)
 
@@ -182,23 +202,23 @@
 def first_piece_body(step, rack_count, group_count, *refs):
     first, last = step == 0, step == STEPS - 1
     if first:
-        *gathered_refs, gain_ref, weight_ref, residual_ref, mixing_ref, scaled_ref, product_ref, message_ref = refs
+        *gathered_refs, gain_ref, upper_ref, lower_ref, residual_ref, mixing_ref, scaled_ref, product_ref, message_ref = refs
         residual, mixing_ref[...] = placed(gathered_refs, gain_ref.shape[1], rack_count, group_count)
         residual_ref[...] = residual
     else:
-        before_ref, own_ref, other_ref, gain_ref, weight_ref, *residual_refs, scaled_ref, product_ref, message_ref = refs
+        before_ref, own_ref, other_ref, gain_ref, upper_ref, lower_ref, *residual_refs, scaled_ref, product_ref, message_ref = refs
         update = jnp.concatenate([own_ref[...], other_ref[...]], axis=0)
         residual = before_ref[...] + widened(update)
         if last:
             place = lax.broadcasted_iota(jnp.int32, (residual.shape[0], 1), 0)
-            own_place = own_place_of(group_count)
+            own_place = own_place_of(residual.shape[0] // 2, group_count)
             for ref, wanted in zip(residual_refs, (own_place, own_place ^ 1)):
                 ref[...] = jnp.sum(jnp.where(place == wanted, residual, 0.0), axis=0, keepdims=True)
         else:
             residual_refs[0][...] = residual
     scaled = rounded(residual * gain_ref[...])
     scaled_ref[...] = scaled
-    multiplied(scaled, weight_ref, 0, product_ref, message_ref)
+    multiplied(scaled, upper_ref, lower_ref, 0, product_ref, message_ref)
     square_sum = jnp.sum(residual * residual, axis=1, keepdims=True)
     square_high = widened(rounded(square_sum))
     lane = lax.broadcasted_iota(jnp.int32, (residual.shape[0], LANES), 1)
@@ -206,15 +226,15 @@
     message_ref[:, product_ref.shape[1] :] = rounded(tail)
 
 
-def other_piece_body(piece, scaled_ref, weight_ref, product_ref, message_ref):
-    multiplied(scaled_ref[...], weight_ref, piece, product_ref, message_ref)
+def other_piece_body(piece, scaled_ref, upper_ref, lower_ref, product_ref, message_ref):
+    multiplied(scaled_ref[...], upper_ref, lower_ref, piece, product_ref, message_ref)
 
 
 def token_matrix(count, group_count):
     token = lax.broadcasted_iota(jnp.int32, (count, count), 0)
     place = lax.broadcasted_iota(jnp.int32, (count, count), 1)
     rack = token // group_count
-    core = (rack + lax.axis_index("rack")) % 2
+    core = (rack + own_core_of()) % 2
     matches = core * (count // 2) + rack // 2 * group_count + token % group_count == place
     return rounded(jnp.where(matches, 1.0, 0.0))
 
@@ -294,27 +314,33 @@
         scratch=[*(in_vmem(a.shape, a.dtype) for a in sources), pltpu.SemaphoreType.DMA((len(sources),))],
     )
     block = next(b for b in (128, 16, half_width) if half_width % b == 0)
-    (gate_up_weight,) = kernel_call(
-        weights_body,
-        [in_vmem((half_width, product_width), jnp.bfloat16)],
-        [],
-        in_hbm=[w_gate_up[0, 0]],
-        scratch=[
-            in_vmem((half_width, 2, part_width), jnp.bfloat16),
-            pltpu.SemaphoreType.DMA((half_width // block,)),
-        ],
-        limit=12,
-    )
-
-    def joined(ready, pieces, count):
+
+    def turned(start, stop, *before):
+        return kernel_call(
+            functools.partial(weights_body, first=start, before=len(before)),
+            [in_vmem((stop - start, product_width), jnp.bfloat16)],
+            before,
+            in_hbm=[w_gate_up[0, 0]],
+            scratch=[
+                in_vmem((stop - start, 2, part_width), jnp.bfloat16),
+                pltpu.SemaphoreType.DMA(((stop - start) // block,)),
+            ],
+            limit=12,
+        )[0]
+
+    def joined(pieces, count, *before):
         out_shape = [in_vmem((count,) + block_shape, jnp.bfloat16)]
-        return kernel_call(joined_body, out_shape, [ready, *pieces])[0]
+        return kernel_call(functools.partial(joined_body, len(pieces)), out_shape, [*pieces, *before])[0]
 
     near, far = gather_masks(rack_count, group_count)
+    middle = -(-half_width // 2 // 256) * 256
+    upper = turned(0, middle)
     rows = [own] + [exchanged_both(other if group else own, rack, group) for rack, group in near[1:]]
-    rows = joined(gate_up_weight, rows, len(near))
+    rows = joined(rows, len(near), upper)
+    lower = turned(middle, half_width, rows)
+    gate_up_weights = [upper, lower]
     rows = [rows] + [exchanged_both(rows, rack, group) for rack, group in far[1:]]
-    rows = joined(gate_up_weight, rows, core_rows)
+    rows = joined(rows, core_rows, lower)
     gathered = [rows, exchanged(rows, "rack", 1)]
 
     piece_width = product_width // PIECES
@@ -337,7 +363,7 @@
                 product_shape,
                 in_vmem((token_count, piece_width + LANES), jnp.bfloat16),
             ],
-            operands + [gain_half, gate_up_weight],
+            operands + [gain_half, *gate_up_weights],
             product_flops // PIECES,
         )
         if step_index == 0:
@@ -349,7 +375,7 @@
             product, piece_message = kernel_call(
                 functools.partial(other_piece_body, piece),
                 [product_shape, in_vmem((token_count, piece_width), jnp.bfloat16)],
-                [scaled, gate_up_weight],
+                [scaled, *gate_up_weights],
                 product_flops // PIECES,
             )
             products.append(product)
@@ -381,11 +407,11 @@
         sent = rounded(update)
         update = widened(sent)
         for mask in range(2, rack_count, 2):
-            update = update + widened(exchanged(sent, "rack", mask))
+            update = update + widened(exchanged_both(sent, *crossed(mask, 0)))
         sent = rounded(update)
         update = widened(sent)
         for mask in range(2, group_count, 2):
-            update = update + widened(exchanged(sent, "expert", mask))
+            update = update + widened(exchanged_both(sent, *crossed(0, mask)))
         sent = rounded(update)
         received = exchanged(sent, "rack", 1)
 

time: 106 us -> 105 us (level)
  waiting for transfers between devices: 44.8 us -> 42.3 us
  blocking collectives: 10.6 us -> 11.7 us
    ppermute x28 -> x16, waiting for transfers between devices: 40.6 us -> 18.4 us  [exchanged(): lax.ppermute(shard, axis, [(i, i ^ mask) for i in range(lax.axis_size(axi...]
    ppermute x6 -> x18, waiting for transfers between devices: 4.23 us -> 23.9 us  [exchanged_both(): return lax.ppermute(shard, ('rack', 'expert'), pairs)]
    ppermute x28 -> x16, starting transfers between devices: 25.2 us -> 9.63 us  [exchanged(): lax.ppermute(shard, axis, [(i, i ^ mask) for i in range(lax.axis_size(axi...]
    ppermute x6 -> x18, starting transfers between devices: 9.04 us -> 23.7 us  [exchanged_both(): return lax.ppermute(shard, ('rack', 'expert'), pairs)]
    all_to_all x1, blocking collectives: 10.6 us -> 11.7 us  [dense_steps(): lax.all_to_all(updates[0], ('rack', 'expert'), split_axis=0, concat_axis=...]
    pallas_call x21 -> x22, Pallas kernels: 15.6 us -> 16.6 us  [kernel_call(): pl.pallas_call(body, out_shape=out_shape, in_specs=[WHOLE] * len(operands...]
  transfers between devices with their start and end apart: 34 -> 34, of which waited for: 29 -> 26; matrix products, arithmetic and copies ran while one was open for 0% -> 0% of each run, Pallas kernels for 9% -> 10%
where the time goes in v5:
time: 105 us; the launch traced here: 104 us
  waiting for transfers between devices  42.3 us (40%)
  starting transfers between devices  33.3 us (32%)
  Pallas kernels  16.6 us (16%)
  blocking collectives  11.7 us (11%)
    ppermute x18, waiting for transfers between devices, exchanged_both(): return lax.ppermute(shard, ('rack', 'expert'), pairs)  23.9 us
    ppermute x18, starting transfers between devices, exchanged_both(): return lax.ppermute(shard, ('rack', 'expert'), pairs)  23.7 us
    ppermute x16, waiting for transfers between devices, exchanged(): lax.ppermute(shard, axis, [(i, i ^ mask) for i in range(lax.axis_size(axi...  18.4 us
    pallas_call x22, Pallas kernels, kernel_call(): pl.pallas_call(body, out_shape=out_shape, in_specs=[WHOLE] * len(operands...  16.6 us
    all_to_all x1, blocking collectives, dense_steps(): lax.all_to_all(updates[0], ('rack', 'expert'), split_axis=0, concat_axis=...  11.7 us
    ppermute x16, starting transfers between devices, exchanged(): lax.ppermute(shard, axis, [(i, i ^ mask) for i in range(lax.axis_size(axi...  9.63 us
  transfers between devices with their start and end apart: 34, of which 26 were waited for; matrix products, arithmetic and copies ran while one was open for 0% of the time, Pallas kernels for 10%

profile of v5, /device:TPU:0, one launch (start us, length us, event | category | flops | bytes accessed | tf_op | source)
XLA Modules:
  0.0 104.3 jit_solution(6172607477467659622)
XLA Ops:
  0.0 0.9 shard_map.64
  0.9 3.0 %collective-permute-start = (bf16[16,128]{1,0:T(8,128)(2,1)S(1)}, bf16[16,128]{1,0:T(8,128)(2,1)S(1)}, u32[]{:S(2)}, u32[]{:S(2)}) collective-permute-start(bf16[16,128]{1,0:T(8,128)(2,1)S(1)} %get-tuple-element.42.refs_0_), channel_id=1, source_target_pairs={{0,8},{1,9},{2,10},{3,11},{4,12},{5,13},{6,14},{7,15},{8,0},{9,1},... | collective-permute-start | bytes 12296 | tf_op jit(solution)/shard_map/ppermute | solution.py:37
  3.9 0.7 collective-permute-start.2
  4.6 0.6 collective-permute-start.1
  5.1 2.3 %shard_map.65.refs_4_.refs_3_.upper_ref = bf16[1024,2048]{1,0:T(8,128)(2,1)S(1)} custom-call(bf16[1792,2,1024]{2,1,0:T(2,128)(2,1)} %bitcast.11), custom_call_target="tpu_custom_call" | custom-call | bytes 7340032 | tf_op jit(solution)/shard_map/pallas_call | solution.py:65
  7.8 3.8 %collective-permute-start.5 = (bf16[4,16,128]{2,1,0:T(8,128)(2,1)S(1)}, bf16[4,16,128]{2,1,0:T(8,128)(2,1)S(1)}, u32[]{:S(2)}, u32[]{:S(2)}) collective-permute-start(bf16[4,16,128]{2,1,0:T(8,128)(2,1)S(1)} %shard_map.66.refs_0_), channel_id=1, source_target_pairs={{0,18},{1,19},{2,16},{3,17},{4,22},{5,23},{6,20},{7,21},{8,26},{9,... | collective-permute-start | bytes 49160 | tf_op jit(solution)/shard_map/ppermute | solution.py:37
  12.0 2.0 %shard_map.67.refs_4_.lower_ref.refs_5_ = bf16[768,2048]{1,0:T(8,128)(2,1)S(1)} custom-call(bf16[4,16,128]{2,1,0:T(8,128)(2,1)S(1)} %shard_map.66.refs_0_, bf16[1792,2,1024]{2,1,0:T(2,128)(2,1)} %bitcast.12), custom_call_target="tpu_custom_call" | custom-call | bytes 7356416 | tf_op jit(solution)/shard_map/pallas_call | solution.py:65
  14.0 1.7 %collective-permute-done.4.refs_2_ = bf16[4,16,128]{2,1,0:T(8,128)(2,1)S(1)} collective-permute-done((bf16[4,16,128]{2,1,0:T(8,128)(2,1)S(1)}, bf16[4,16,128]{2,1,0:T(8,128)(2,1)S(1)}, u32[]{:S(2)}, u32[]{:S(2)}) %collective-permute-start.4) | collective-permute-done | bytes 16416 | tf_op jit(solution)/shard_map/ppermute | solution.py:37
  16.0 1.0 collective-permute-done.6.refs_1_
  17.0 0.9 shard_map.69
  17.9 1.6 %collective-permute-start.7 = (bf16[32,1152]{1,0:T(8,128)(2,1)S(1)}, bf16[32,1152]{1,0:T(8,128)(2,1)S(1)}, u32[]{:S(2)}, u32[]{:S(2)}) collective-permute-start(bf16[32,1152]{1,0:T(8,128)(2,1)S(1)} %get-tuple-element.46.tail_ref), channel_id=1, source_target_pairs={{0,1},{1,0},{2,3},{3,2},{4,5},{5,4},{6,7},{7,6},{8,9},{9,8},{10,11... | collective-permute-start | bytes 221192 | tf_op jit(solution)/shard_map/ppermute | solution.py:19
  19.5 0.7 shard_map.70
  20.3 0.5 collective-permute-start.8
  20.7 1.7 %collective-permute-done.7.other_tail_ref.swapped_ref = bf16[32,1152]{1,0:T(8,128)(2,1)S(1)} collective-permute-done((bf16[32,1152]{1,0:T(8,128)(2,1)S(1)}, bf16[32,1152]{1,0:T(8,128)(2,1)S(1)}, u32[]{:S(2)}, u32[]{:S(2)}) %collective-permute-start.7) | collective-permute-done | bytes 73760 | tf_op jit(solution)/shard_map/ppermute | solution.py:19
  22.4 0.5 shard_map.71.refs_0_
  22.9 1.6 %collective-permute-done.8.swapped_ref = bf16[32,1024]{1,0:T(8,128)(2,1)S(1)} collective-permute-done((bf16[32,1024]{1,0:T(8,128)(2,1)S(1)}, bf16[32,1024]{1,0:T(8,128)(2,1)S(1)}, u32[]{:S(2)}, u32[]{:S(2)}) %collective-permute-start.8) | collective-permute-done | bytes 65568 | tf_op jit(solution)/shard_map/ppermute | solution.py:19
  24.5 0.6 shard_map.72
  25.2 1.2 %collective-permute-done.9 = bf16[16,1792]{1,0:T(8,128)(2,1)S(1)} collective-permute-done((bf16[16,1792]{1,0:T(8,128)(2,1)S(1)}, bf16[16,1792]{1,0:T(8,128)(2,1)S(1)}, u32[]{:S(2)}, u32[]{:S(2)}) %collective-permute-start.9) | collective-permute-done | bytes 57376 | tf_op jit(solution)/shard_map/ppermute | solution.py:19
  26.4 1.5 %collective-permute-start.12 = (bf16[16,1792]{1,0:T(8,128)(2,1)S(1)}, bf16[16,1792]{1,0:T(8,128)(2,1)S(1)}, u32[]{:S(2)}, u32[]{:S(2)}) collective-permute-start(bf16[16,1792]{1,0:T(8,128)(2,1)S(1)} %add_convert_fusion.8), channel_id=1, source_target_pairs={{0,24},{1,25},{2,26},{3,27},{4,28},{5,29},{6,30},{7,31},{8,16},{9,... | collective-permute-start | bytes 172040 | tf_op jit(solution)/shard_map/ppermute | solution.py:37
  27.9 1.0 collective-permute-start.11
  28.9 0.8 collective-permute-start.10
  29.7 2.0 %collective-permute-done.12 = bf16[16,1792]{1,0:T(8,128)(2,1)S(1)} collective-permute-done((bf16[16,1792]{1,0:T(8,128)(2,1)S(1)}, bf16[16,1792]{1,0:T(8,128)(2,1)S(1)}, u32[]{:S(2)}, u32[]{:S(2)}) %collective-permute-start.12) | collective-permute-done | bytes 57376 | tf_op jit(solution)/shard_map/ppermute | solution.py:37
  31.7 1.0 collective-permute-done.11
  32.8 1.8 %collective-permute-start.13 = (bf16[16,1792]{1,0:T(8,128)(2,1)S(1)}, bf16[16,1792]{1,0:T(8,128)(2,1)S(1)}, u32[]{:S(2)}, u32[]{:S(2)}) collective-permute-start(bf16[16,1792]{1,0:T(8,128)(2,1)S(1)} %add_convert_fusion.7), channel_id=1, source_target_pairs={{0,6},{1,7},{2,4},{3,5},{4,2},{5,3},{6,0},{7,1},{8,14},{9,15},{10,... | collective-permute-start | bytes 172040 | tf_op jit(solution)/shard_map/ppermute | solution.py:37
  34.6 4.3 %collective-permute-done.13 = bf16[16,1792]{1,0:T(8,128)(2,1)S(1)} collective-permute-done((bf16[16,1792]{1,0:T(8,128)(2,1)S(1)}, bf16[16,1792]{1,0:T(8,128)(2,1)S(1)}, u32[]{:S(2)}, u32[]{:S(2)}) %collective-permute-start.13) | collective-permute-done | bytes 57376 | tf_op jit(solution)/shard_map/ppermute | solution.py:37
  39.1 1.1 %collective-permute-done.14.refs_2_ = bf16[16,1792]{1,0:T(8,128)(2,1)S(1)} collective-permute-done((bf16[16,1792]{1,0:T(8,128)(2,1)S(1)}, bf16[16,1792]{1,0:T(8,128)(2,1)S(1)}, u32[]{:S(2)}, u32[]{:S(2)}) %collective-permute-start.14) | collective-permute-done | bytes 57376 | tf_op jit(solution)/shard_map/ppermute | solution.py:19
  40.2 0.7 shard_map.73
  41.0 0.7 shard_map.74
  41.7 2.0 %collective-permute-start.16 = (bf16[32,1024]{1,0:T(8,128)(2,1)S(1)}, bf16[32,1024]{1,0:T(8,128)(2,1)S(1)}, u32[]{:S(2)}, u32[]{:S(2)}) collective-permute-start(bf16[32,1024]{1,0:T(8,128)(2,1)S(1)} %get-tuple-element.58), channel_id=1, source_target_pairs={{0,1},{1,0},{2,3},{3,2},{4,5},{5,4},{6,7},{7,6},{8,9},{9,8},{10,11... | collective-permute-start | bytes 196616 | tf_op jit(solution)/shard_map/ppermute | solution.py:19
  43.8 2.3 %collective-permute-done.15.other_tail_ref.swapped_ref = bf16[32,1152]{1,0:T(8,128)(2,1)S(1)} collective-permute-done((bf16[32,1152]{1,0:T(8,128)(2,1)S(1)}, bf16[32,1152]{1,0:T(8,128)(2,1)S(1)}, u32[]{:S(2)}, u32[]{:S(2)}) %collective-permute-start.15) | collective-permute-done | bytes 73760 | tf_op jit(solution)/shard_map/ppermute | solution.py:19
  46.0 0.5 shard_map.75.refs_0_
  46.7 0.6 shard_map.76
  47.4 1.2 %collective-permute-done.17 = bf16[16,1792]{1,0:T(8,128)(2,1)S(1)} collective-permute-done((bf16[16,1792]{1,0:T(8,128)(2,1)S(1)}, bf16[16,1792]{1,0:T(8,128)(2,1)S(1)}, u32[]{:S(2)}, u32[]{:S(2)}) %collective-permute-start.17) | collective-permute-done | bytes 57376 | tf_op jit(solution)/shard_map/ppermute | solution.py:19
  48.6 1.6 %collective-permute-start.20 = (bf16[16,1792]{1,0:T(8,128)(2,1)S(1)}, bf16[16,1792]{1,0:T(8,128)(2,1)S(1)}, u32[]{:S(2)}, u32[]{:S(2)}) collective-permute-start(bf16[16,1792]{1,0:T(8,128)(2,1)S(1)} %add_convert_fusion.5), channel_id=1, source_target_pairs={{0,24},{1,25},{2,26},{3,27},{4,28},{5,29},{6,30},{7,31},{8,16},{9,... | collective-permute-start | bytes 172040 | tf_op jit(solution)/shard_map/ppermute | solution.py:37
  50.2 0.6 collective-permute-start.19
  50.8 1.1 %collective-permute-start.18 = (bf16[16,1792]{1,0:T(8,128)(2,1)S(1)}, bf16[16,1792]{1,0:T(8,128)(2,1)S(1)}, u32[]{:S(2)}, u32[]{:S(2)}) collective-permute-start(bf16[16,1792]{1,0:T(8,128)(2,1)S(1)} %add_convert_fusion.5), channel_id=1, source_target_pairs={{0,12},{1,13},{2,14},{3,15},{4,8},{5,9},{6,10},{7,11},{8,4},{9,5},... | collective-permute-start | bytes 172040 | tf_op jit(solution)/shard_map/ppermute | solution.py:37
  51.9 1.9 %collective-permute-done.20 = bf16[16,1792]{1,0:T(8,128)(2,1)S(1)} collective-permute-done((bf16[16,1792]{1,0:T(8,128)(2,1)S(1)}, bf16[16,1792]{1,0:T(8,128)(2,1)S(1)}, u32[]{:S(2)}, u32[]{:S(2)}) %collective-permute-start.20) | collective-permute-done | bytes 57376 | tf_op jit(solution)/shard_map/ppermute | solution.py:37
  53.8 1.2 %collective-permute-done.19 = bf16[16,1792]{1,0:T(8,128)(2,1)S(1)} collective-permute-done((bf16[16,1792]{1,0:T(8,128)(2,1)S(1)}, bf16[16,1792]{1,0:T(8,128)(2,1)S(1)}, u32[]{:S(2)}, u32[]{:S(2)}) %collective-permute-start.19) | collective-permute-done | bytes 57376 | tf_op jit(solution)/shard_map/ppermute | solution.py:37
  55.0 1.8 %collective-permute-start.21 = (bf16[16,1792]{1,0:T(8,128)(2,1)S(1)}, bf16[16,1792]{1,0:T(8,128)(2,1)S(1)}, u32[]{:S(2)}, u32[]{:S(2)}) collective-permute-start(bf16[16,1792]{1,0:T(8,128)(2,1)S(1)} %add_convert_fusion.4), channel_id=1, source_target_pairs={{0,6},{1,7},{2,4},{3,5},{4,2},{5,3},{6,0},{7,1},{8,14},{9,15},{10,... | collective-permute-start | bytes 172040 | tf_op jit(solution)/shard_map/ppermute | solution.py:37
  56.9 4.3 %collective-permute-done.21 = bf16[16,1792]{1,0:T(8,128)(2,1)S(1)} collective-permute-done((bf16[16,1792]{1,0:T(8,128)(2,1)S(1)}, bf16[16,1792]{1,0:T(8,128)(2,1)S(1)}, u32[]{:S(2)}, u32[]{:S(2)}) %collective-permute-start.21) | collective-permute-done | bytes 57376 | tf_op jit(solution)/shard_map/ppermute | solution.py:37
  61.4 1.1 %collective-permute-done.22.refs_2_ = bf16[16,1792]{1,0:T(8,128)(2,1)S(1)} collective-permute-done((bf16[16,1792]{1,0:T(8,128)(2,1)S(1)}, bf16[16,1792]{1,0:T(8,128)(2,1)S(1)}, u32[]{:S(2)}, u32[]{:S(2)}) %collective-permute-start.22) | collective-permute-done | bytes 57376 | tf_op jit(solution)/shard_map/ppermute | solution.py:19
  62.5 0.7 shard_map.77
  63.4 0.7 shard_map.78
  64.2 1.9 %collective-permute-start.24 = (bf16[32,1024]{1,0:T(8,128)(2,1)S(1)}, bf16[32,1024]{1,0:T(8,128)(2,1)S(1)}, u32[]{:S(2)}, u32[]{:S(2)}) collective-permute-start(bf16[32,1024]{1,0:T(8,128)(2,1)S(1)} %get-tuple-element.66), channel_id=1, source_target_pairs={{0,1},{1,0},{2,3},{3,2},{4,5},{5,4},{6,7},{7,6},{8,9},{9,8},{10,11... | collective-permute-start | bytes 196616 | tf_op jit(solution)/shard_map/ppermute | solution.py:19
  66.0 2.3 %collective-permute-done.23.other_tail_ref.swapped_ref = bf16[32,1152]{1,0:T(8,128)(2,1)S(1)} collective-permute-done((bf16[32,1152]{1,0:T(8,128)(2,1)S(1)}, bf16[32,1152]{1,0:T(8,128)(2,1)S(1)}, u32[]{:S(2)}, u32[]{:S(2)}) %collective-permute-start.23) | collective-permute-done | bytes 73760 | tf_op jit(solution)/shard_map/ppermute | solution.py:19
  68.3 0.5 shard_map.79.refs_0_
  69.0 0.6 shard_map.80
  69.7 1.2 %collective-permute-done.25 = bf16[16,1792]{1,0:T(8,128)(2,1)S(1)} collective-permute-done((bf16[16,1792]{1,0:T(8,128)(2,1)S(1)}, bf16[16,1792]{1,0:T(8,128)(2,1)S(1)}, u32[]{:S(2)}, u32[]{:S(2)}) %collective-permute-start.25) | collective-permute-done | bytes 57376 | tf_op jit(solution)/shard_map/ppermute | solution.py:19
  70.9 1.5 %collective-permute-start.28 = (bf16[16,1792]{1,0:T(8,128)(2,1)S(1)}, bf16[16,1792]{1,0:T(8,128)(2,1)S(1)}, u32[]{:S(2)}, u32[]{:S(2)}) collective-permute-start(bf16[16,1792]{1,0:T(8,128)(2,1)S(1)} %add_convert_fusion.2), channel_id=1, source_target_pairs={{0,24},{1,25},{2,26},{3,27},{4,28},{5,29},{6,30},{7,31},{8,16},{9,... | collective-permute-start | bytes 172040 | tf_op jit(solution)/shard_map/ppermute | solution.py:37
  72.4 0.5 collective-permute-start.27
  72.9 1.3 %collective-permute-start.26 = (bf16[16,1792]{1,0:T(8,128)(2,1)S(1)}, bf16[16,1792]{1,0:T(8,128)(2,1)S(1)}, u32[]{:S(2)}, u32[]{:S(2)}) collective-permute-start(bf16[16,1792]{1,0:T(8,128)(2,1)S(1)} %add_convert_fusion.2), channel_id=1, source_target_pairs={{0,12},{1,13},{2,14},{3,15},{4,8},{5,9},{6,10},{7,11},{8,4},{9,5},... | collective-permute-start | bytes 172040 | tf_op jit(solution)/shard_map/ppermute | solution.py:37
  74.2 2.0 %collective-permute-done.28 = bf16[16,1792]{1,0:T(8,128)(2,1)S(1)} collective-permute-done((bf16[16,1792]{1,0:T(8,128)(2,1)S(1)}, bf16[16,1792]{1,0:T(8,128)(2,1)S(1)}, u32[]{:S(2)}, u32[]{:S(2)}) %collective-permute-start.28) | collective-permute-done | bytes 57376 | tf_op jit(solution)/shard_map/ppermute | solution.py:37
  76.1 1.0 collective-permute-done.27
  77.2 1.8 %collective-permute-start.29 = (bf16[16,1792]{1,0:T(8,128)(2,1)S(1)}, bf16[16,1792]{1,0:T(8,128)(2,1)S(1)}, u32[]{:S(2)}, u32[]{:S(2)}) collective-permute-start(bf16[16,1792]{1,0:T(8,128)(2,1)S(1)} %add_convert_fusion.1), channel_id=1, source_target_pairs={{0,6},{1,7},{2,4},{3,5},{4,2},{5,3},{6,0},{7,1},{8,14},{9,15},{10,... | collective-permute-start | bytes 172040 | tf_op jit(solution)/shard_map/ppermute | solution.py:37
  79.0 4.3 %collective-permute-done.29 = bf16[16,1792]{1,0:T(8,128)(2,1)S(1)} collective-permute-done((bf16[16,1792]{1,0:T(8,128)(2,1)S(1)}, bf16[16,1792]{1,0:T(8,128)(2,1)S(1)}, u32[]{:S(2)}, u32[]{:S(2)}) %collective-permute-start.29) | collective-permute-done | bytes 57376 | tf_op jit(solution)/shard_map/ppermute | solution.py:37
  83.5 1.1 %collective-permute-done.30.refs_2_ = bf16[16,1792]{1,0:T(8,128)(2,1)S(1)} collective-permute-done((bf16[16,1792]{1,0:T(8,128)(2,1)S(1)}, bf16[16,1792]{1,0:T(8,128)(2,1)S(1)}, u32[]{:S(2)}, u32[]{:S(2)}) %collective-permute-start.30) | collective-permute-done | bytes 57376 | tf_op jit(solution)/shard_map/ppermute | solution.py:19
  84.6 0.7 shard_map.81
  85.6 0.7 shard_map.82
  86.3 1.9 %collective-permute-start.32 = (bf16[32,1024]{1,0:T(8,128)(2,1)S(1)}, bf16[32,1024]{1,0:T(8,128)(2,1)S(1)}, u32[]{:S(2)}, u32[]{:S(2)}) collective-permute-start(bf16[32,1024]{1,0:T(8,128)(2,1)S(1)} %get-tuple-element.73), channel_id=1, source_target_pairs={{0,1},{1,0},{2,3},{3,2},{4,5},{5,4},{6,7},{7,6},{8,9},{9,8},{10,11... | collective-permute-start | bytes 196616 | tf_op jit(solution)/shard_map/ppermute | solution.py:19
  88.4 2.1 %collective-permute-done.31.other_tail_ref.swapped_ref = bf16[32,1152]{1,0:T(8,128)(2,1)S(1)} collective-permute-done((bf16[32,1152]{1,0:T(8,128)(2,1)S(1)}, bf16[32,1152]{1,0:T(8,128)(2,1)S(1)}, u32[]{:S(2)}, u32[]{:S(2)}) %collective-permute-start.31) | collective-permute-done | bytes 73760 | tf_op jit(solution)/shard_map/ppermute | solution.py:19
  90.5 0.7 shard_map.83.refs_0_
  91.2 0.7 shard_map.84
  91.9 11.7 %all_to_all.5.arrived_ref = bf16[32,14,128]{2,1,0:T(8,128)(2,1)S(1)} all-to-all(bf16[32,14,128]{2,1,0:T(8,128)(2,1)S(1)} %shard_map.84), channel_id=1, replica_groups=mesh['rack'=8,'expert'=4] {'rack','expert'}, dimensions={0} | all-to-all | bytes 229376 | tf_op jit(solution)/shard_map/all_to_all | solution.py:418
  103.6 0.7 shard_map.85
  (38 shorter events, 3.1 us)
Async XLA Ops:
  0.9 6.6 %collective-permute-start = (bf16[16,128]{1,0:T(8,128)(2,1)S(1)}, bf16[16,128]{1,0:T(8,128)(2,1)S(1)}, u32[]{:S(2)}, u32[]{:S(2)}) collective-permute-start(bf16[16,128]{1,0:T(8,128)(2,1)S(1)} %get-tuple-element.42.refs_0_), channel_id=1, source_target_pairs={{0,8},{1,9},{2,10},{3,11},{4,12},{5,13},{6,14},{7,15},{8,0},{9,1},... | collective-permute-start | bytes 12296 | tf_op jit(solution)/shard_map/ppermute | solution.py:37
  3.9 3.9 %collective-permute-start.2 = (bf16[16,128]{1,0:T(8,128)(2,1)S(1)}, bf16[16,128]{1,0:T(8,128)(2,1)S(1)}, u32[]{:S(2)}, u32[]{:S(2)}) collective-permute-start(bf16[16,128]{1,0:T(8,128)(2,1)S(1)} %get-tuple-element.43), channel_id=1, source_target_pairs={{0,13},{1,12},{2,15},{3,14},{4,9},{5,8},{6,11},{7,10},{8,5},{9,4},... | collective-permute-start | bytes 12296 | tf_op jit(solution)/shard_map/ppermute | solution.py:37
  4.6 3.2 %collective-permute-start.1 = (bf16[16,128]{1,0:T(8,128)(2,1)S(1)}, bf16[16,128]{1,0:T(8,128)(2,1)S(1)}, u32[]{:S(2)}, u32[]{:S(2)}) collective-permute-start(bf16[16,128]{1,0:T(8,128)(2,1)S(1)} %get-tuple-element.43), channel_id=1, source_target_pairs={{0,5},{1,4},{2,7},{3,6},{4,1},{5,0},{6,3},{7,2},{8,13},{9,12},{10,... | collective-permute-start | bytes 12296 | tf_op jit(solution)/shard_map/ppermute | solution.py:37
  7.8 6.2 %collective-permute-start.5 = (bf16[4,16,128]{2,1,0:T(8,128)(2,1)S(1)}, bf16[4,16,128]{2,1,0:T(8,128)(2,1)S(1)}, u32[]{:S(2)}, u32[]{:S(2)}) collective-permute-start(bf16[4,16,128]{2,1,0:T(8,128)(2,1)S(1)} %shard_map.66.refs_0_), channel_id=1, source_target_pairs={{0,18},{1,19},{2,16},{3,17},{4,22},{5,23},{6,20},{7,21},{8,26},{9,... | collective-permute-start | bytes 49160 | tf_op jit(solution)/shard_map/ppermute | solution.py:37
  11.6 4.1 %collective-permute-start.4 = (bf16[4,16,128]{2,1,0:T(8,128)(2,1)S(1)}, bf16[4,16,128]{2,1,0:T(8,128)(2,1)S(1)}, u32[]{:S(2)}, u32[]{:S(2)}) collective-permute-start(bf16[4,16,128]{2,1,0:T(8,128)(2,1)S(1)} %shard_map.66.refs_0_), channel_id=1, source_target_pairs={{0,6},{1,7},{2,4},{3,5},{4,2},{5,3},{6,0},{7,1},{8,14},{9,15},{10,... | collective-permute-start | bytes 49160 | tf_op jit(solution)/shard_map/ppermute | solution.py:37
  11.8 3.9 %collective-permute-start.3 = (bf16[4,16,128]{2,1,0:T(8,128)(2,1)S(1)}, bf16[4,16,128]{2,1,0:T(8,128)(2,1)S(1)}, u32[]{:S(2)}, u32[]{:S(2)}) collective-permute-start(bf16[4,16,128]{2,1,0:T(8,128)(2,1)S(1)} %shard_map.66.refs_0_), channel_id=1, source_target_pairs={{0,20},{1,21},{2,22},{3,23},{4,16},{5,17},{6,18},{7,19},{8,28},{9,... | collective-permute-start | bytes 49160 | tf_op jit(solution)/shard_map/ppermute | solution.py:37
  15.7 1.3 %collective-permute-start.6 = (bf16[16,16,128]{2,1,0:T(8,128)(2,1)S(1)}, bf16[16,16,128]{2,1,0:T(8,128)(2,1)S(1)}, u32[]{:S(2)}, u32[]{:S(2)}) collective-permute-start(bf16[16,16,128]{2,1,0:T(8,128)(2,1)S(1)} %shard_map.68.refs_0_), channel_id=1, source_target_pairs={{0,4},{4,0},{8,12},{12,8},{16,20},{20,16},{24,28},{28,24},{1,5},{5... | collective-permute-start | bytes 196616 | tf_op jit(solution)/shard_map/ppermute | solution.py:19
  17.9 4.5 %copy-start = (bf16[1,1,1024,1792]{3,2,1,0:T(8,128)(2,1)S(1)}, bf16[1,1,1024,1792]{3,2,1,0:T(8,128)(2,1)}, u32[]{:S(2)}) copy-start(bf16[1,1,1024,1792]{3,2,1,0:T(8,128)(2,1)} %param.11) | copy-start | bytes 11010052
  17.9 4.5 %collective-permute-start.7 = (bf16[32,1152]{1,0:T(8,128)(2,1)S(1)}, bf16[32,1152]{1,0:T(8,128)(2,1)S(1)}, u32[]{:S(2)}, u32[]{:S(2)}) collective-permute-start(bf16[32,1152]{1,0:T(8,128)(2,1)S(1)} %get-tuple-element.46.tail_ref), channel_id=1, source_target_pairs={{0,1},{1,0},{2,3},{3,2},{4,5},{5,4},{6,7},{7,6},{8,9},{9,8},{10,11... | collective-permute-start | bytes 221192 | tf_op jit(solution)/shard_map/ppermute | solution.py:19
  20.3 4.3 %collective-permute-start.8 = (bf16[32,1024]{1,0:T(8,128)(2,1)S(1)}, bf16[32,1024]{1,0:T(8,128)(2,1)S(1)}, u32[]{:S(2)}, u32[]{:S(2)}) collective-permute-start(bf16[32,1024]{1,0:T(8,128)(2,1)S(1)} %get-tuple-element.49), channel_id=1, source_target_pairs={{0,1},{1,0},{2,3},{3,2},{4,5},{5,4},{6,7},{7,6},{8,9},{9,8},{10,11... | collective-permute-start | bytes 196616 | tf_op jit(solution)/shard_map/ppermute | solution.py:19
  25.1 1.3 %collective-permute-start.9 = (bf16[16,1792]{1,0:T(8,128)(2,1)S(1)}, bf16[16,1792]{1,0:T(8,128)(2,1)S(1)}, u32[]{:S(2)}, u32[]{:S(2)}) collective-permute-start(bf16[16,1792]{1,0:T(8,128)(2,1)S(1)} %get-tuple-element.53), channel_id=1, source_target_pairs={{0,4},{4,0},{8,12},{12,8},{16,20},{20,16},{24,28},{28,24},{1,5},{5... | collective-permute-start | bytes 172040 | tf_op jit(solution)/shard_map/ppermute | solution.py:19
  26.4 5.2 %collective-permute-start.12 = (bf16[16,1792]{1,0:T(8,128)(2,1)S(1)}, bf16[16,1792]{1,0:T(8,128)(2,1)S(1)}, u32[]{:S(2)}, u32[]{:S(2)}) collective-permute-start(bf16[16,1792]{1,0:T(8,128)(2,1)S(1)} %add_convert_fusion.8), channel_id=1, source_target_pairs={{0,24},{1,25},{2,26},{3,27},{4,28},{5,29},{6,30},{7,31},{8,16},{9,... | collective-permute-start | bytes 172040 | tf_op jit(solution)/shard_map/ppermute | solution.py:37
  27.9 4.8 %collective-permute-start.11 = (bf16[16,1792]{1,0:T(8,128)(2,1)S(1)}, bf16[16,1792]{1,0:T(8,128)(2,1)S(1)}, u32[]{:S(2)}, u32[]{:S(2)}) collective-permute-start(bf16[16,1792]{1,0:T(8,128)(2,1)S(1)} %add_convert_fusion.8), channel_id=1, source_target_pairs={{0,20},{1,21},{2,22},{3,23},{4,16},{5,17},{6,18},{7,19},{8,28},{9,... | collective-permute-start | bytes 172040 | tf_op jit(solution)/shard_map/ppermute | solution.py:37
  28.9 3.8 %collective-permute-start.10 = (bf16[16,1792]{1,0:T(8,128)(2,1)S(1)}, bf16[16,1792]{1,0:T(8,128)(2,1)S(1)}, u32[]{:S(2)}, u32[]{:S(2)}) collective-permute-start(bf16[16,1792]{1,0:T(8,128)(2,1)S(1)} %add_convert_fusion.8), channel_id=1, source_target_pairs={{0,12},{1,13},{2,14},{3,15},{4,8},{5,9},{6,10},{7,11},{8,4},{9,5},... | collective-permute-start | bytes 172040 | tf_op jit(solution)/shard_map/ppermute | solution.py:37
  32.8 6.1 %collective-permute-start.13 = (bf16[16,1792]{1,0:T(8,128)(2,1)S(1)}, bf16[16,1792]{1,0:T(8,128)(2,1)S(1)}, u32[]{:S(2)}, u32[]{:S(2)}) collective-permute-start(bf16[16,1792]{1,0:T(8,128)(2,1)S(1)} %add_convert_fusion.7), channel_id=1, source_target_pairs={{0,6},{1,7},{2,4},{3,5},{4,2},{5,3},{6,0},{7,1},{8,14},{9,15},{10,... | collective-permute-start | bytes 172040 | tf_op jit(solution)/shard_map/ppermute | solution.py:37
  38.9 1.3 %collective-permute-start.14 = (bf16[16,1792]{1,0:T(8,128)(2,1)S(1)}, bf16[16,1792]{1,0:T(8,128)(2,1)S(1)}, u32[]{:S(2)}, u32[]{:S(2)}) collective-permute-start(bf16[16,1792]{1,0:T(8,128)(2,1)S(1)} %add_convert_fusion.6.refs_1_), channel_id=1, source_target_pairs={{0,4},{4,0},{8,12},{12,8},{16,20},{20,16},{24,28},{28,24},{1,5},{5... | collective-permute-start | bytes 172040 | tf_op jit(solution)/shard_map/ppermute | solution.py:19
  40.9 5.1 %collective-permute-start.15 = (bf16[32,1152]{1,0:T(8,128)(2,1)S(1)}, bf16[32,1152]{1,0:T(8,128)(2,1)S(1)}, u32[]{:S(2)}, u32[]{:S(2)}) collective-permute-start(bf16[32,1152]{1,0:T(8,128)(2,1)S(1)} %get-tuple-element.55.tail_ref), channel_id=1, source_target_pairs={{0,1},{1,0},{2,3},{3,2},{4,5},{5,4},{6,7},{7,6},{8,9},{9,8},{10,11... | collective-permute-start | bytes 221192 | tf_op jit(solution)/shard_map/ppermute | solution.py:19
  41.7 5.0 %collective-permute-start.16 = (bf16[32,1024]{1,0:T(8,128)(2,1)S(1)}, bf16[32,1024]{1,0:T(8,128)(2,1)S(1)}, u32[]{:S(2)}, u32[]{:S(2)}) collective-permute-start(bf16[32,1024]{1,0:T(8,128)(2,1)S(1)} %get-tuple-element.58), channel_id=1, source_target_pairs={{0,1},{1,0},{2,3},{3,2},{4,5},{5,4},{6,7},{7,6},{8,9},{9,8},{10,11... | collective-permute-start | bytes 196616 | tf_op jit(solution)/shard_map/ppermute | solution.py:19
  47.3 1.3 %collective-permute-start.17 = (bf16[16,1792]{1,0:T(8,128)(2,1)S(1)}, bf16[16,1792]{1,0:T(8,128)(2,1)S(1)}, u32[]{:S(2)}, u32[]{:S(2)}) collective-permute-start(bf16[16,1792]{1,0:T(8,128)(2,1)S(1)} %get-tuple-element.61), channel_id=1, source_target_pairs={{0,4},{4,0},{8,12},{12,8},{16,20},{20,16},{24,28},{28,24},{1,5},{5... | collective-permute-start | bytes 172040 | tf_op jit(solution)/shard_map/ppermute | solution.py:19
  48.6 5.2 %collective-permute-start.20 = (bf16[16,1792]{1,0:T(8,128)(2,1)S(1)}, bf16[16,1792]{1,0:T(8,128)(2,1)S(1)}, u32[]{:S(2)}, u32[]{:S(2)}) collective-permute-start(bf16[16,1792]{1,0:T(8,128)(2,1)S(1)} %add_convert_fusion.5), channel_id=1, source_target_pairs={{0,24},{1,25},{2,26},{3,27},{4,28},{5,29},{6,30},{7,31},{8,16},{9,... | collective-permute-start | bytes 172040 | tf_op jit(solution)/shard_map/ppermute | solution.py:37
  50.2 4.8 %collective-permute-start.19 = (bf16[16,1792]{1,0:T(8,128)(2,1)S(1)}, bf16[16,1792]{1,0:T(8,128)(2,1)S(1)}, u32[]{:S(2)}, u32[]{:S(2)}) collective-permute-start(bf16[16,1792]{1,0:T(8,128)(2,1)S(1)} %add_convert_fusion.5), channel_id=1, source_target_pairs={{0,20},{1,21},{2,22},{3,23},{4,16},{5,17},{6,18},{7,19},{8,28},{9,... | collective-permute-start | bytes 172040 | tf_op jit(solution)/shard_map/ppermute | solution.py:37
  50.8 4.2 %collective-permute-start.18 = (bf16[16,1792]{1,0:T(8,128)(2,1)S(1)}, bf16[16,1792]{1,0:T(8,128)(2,1)S(1)}, u32[]{:S(2)}, u32[]{:S(2)}) collective-permute-start(bf16[16,1792]{1,0:T(8,128)(2,1)S(1)} %add_convert_fusion.5), channel_id=1, source_target_pairs={{0,12},{1,13},{2,14},{3,15},{4,8},{5,9},{6,10},{7,11},{8,4},{9,5},... | collective-permute-start | bytes 172040 | tf_op jit(solution)/shard_map/ppermute | solution.py:37
  55.0 6.1 %collective-permute-start.21 = (bf16[16,1792]{1,0:T(8,128)(2,1)S(1)}, bf16[16,1792]{1,0:T(8,128)(2,1)S(1)}, u32[]{:S(2)}, u32[]{:S(2)}) collective-permute-start(bf16[16,1792]{1,0:T(8,128)(2,1)S(1)} %add_convert_fusion.4), channel_id=1, source_target_pairs={{0,6},{1,7},{2,4},{3,5},{4,2},{5,3},{6,0},{7,1},{8,14},{9,15},{10,... | collective-permute-start | bytes 172040 | tf_op jit(solution)/shard_map/ppermute | solution.py:37
  61.2 1.3 %collective-permute-start.22 = (bf16[16,1792]{1,0:T(8,128)(2,1)S(1)}, bf16[16,1792]{1,0:T(8,128)(2,1)S(1)}, u32[]{:S(2)}, u32[]{:S(2)}) collective-permute-start(bf16[16,1792]{1,0:T(8,128)(2,1)S(1)} %add_convert_fusion.3.refs_1_), channel_id=1, source_target_pairs={{0,4},{4,0},{8,12},{12,8},{16,20},{20,16},{24,28},{28,24},{1,5},{5... | collective-permute-start | bytes 172040 | tf_op jit(solution)/shard_map/ppermute | solution.py:19
  63.2 5.1 %collective-permute-start.23 = (bf16[32,1152]{1,0:T(8,128)(2,1)S(1)}, bf16[32,1152]{1,0:T(8,128)(2,1)S(1)}, u32[]{:S(2)}, u32[]{:S(2)}) collective-permute-start(bf16[32,1152]{1,0:T(8,128)(2,1)S(1)} %get-tuple-element.63.tail_ref), channel_id=1, source_target_pairs={{0,1},{1,0},{2,3},{3,2},{4,5},{5,4},{6,7},{7,6},{8,9},{9,8},{10,11... | collective-permute-start | bytes 221192 | tf_op jit(solution)/shard_map/ppermute | solution.py:19
  64.2 4.8 %collective-permute-start.24 = (bf16[32,1024]{1,0:T(8,128)(2,1)S(1)}, bf16[32,1024]{1,0:T(8,128)(2,1)S(1)}, u32[]{:S(2)}, u32[]{:S(2)}) collective-permute-start(bf16[32,1024]{1,0:T(8,128)(2,1)S(1)} %get-tuple-element.66), channel_id=1, source_target_pairs={{0,1},{1,0},{2,3},{3,2},{4,5},{5,4},{6,7},{7,6},{8,9},{9,8},{10,11... | collective-permute-start | bytes 196616 | tf_op jit(solution)/shard_map/ppermute | solution.py:19
  69.6 1.3 %collective-permute-start.25 = (bf16[16,1792]{1,0:T(8,128)(2,1)S(1)}, bf16[16,1792]{1,0:T(8,128)(2,1)S(1)}, u32[]{:S(2)}, u32[]{:S(2)}) collective-permute-start(bf16[16,1792]{1,0:T(8,128)(2,1)S(1)} %get-tuple-element.69), channel_id=1, source_target_pairs={{0,4},{4,0},{8,12},{12,8},{16,20},{20,16},{24,28},{28,24},{1,5},{5... | collective-permute-start | bytes 172040 | tf_op jit(solution)/shard_map/ppermute | solution.py:19
  70.9 5.2 %collective-permute-start.28 = (bf16[16,1792]{1,0:T(8,128)(2,1)S(1)}, bf16[16,1792]{1,0:T(8,128)(2,1)S(1)}, u32[]{:S(2)}, u32[]{:S(2)}) collective-permute-start(bf16[16,1792]{1,0:T(8,128)(2,1)S(1)} %add_convert_fusion.2), channel_id=1, source_target_pairs={{0,24},{1,25},{2,26},{3,27},{4,28},{5,29},{6,30},{7,31},{8,16},{9,... | collective-permute-start | bytes 172040 | tf_op jit(solution)/shard_map/ppermute | solution.py:37
  72.4 4.8 %collective-permute-start.27 = (bf16[16,1792]{1,0:T(8,128)(2,1)S(1)}, bf16[16,1792]{1,0:T(8,128)(2,1)S(1)}, u32[]{:S(2)}, u32[]{:S(2)}) collective-permute-start(bf16[16,1792]{1,0:T(8,128)(2,1)S(1)} %add_convert_fusion.2), channel_id=1, source_target_pairs={{0,20},{1,21},{2,22},{3,23},{4,16},{5,17},{6,18},{7,19},{8,28},{9,... | collective-permute-start | bytes 172040 | tf_op jit(solution)/shard_map/ppermute | solution.py:37
  72.9 4.3 %collective-permute-start.26 = (bf16[16,1792]{1,0:T(8,128)(2,1)S(1)}, bf16[16,1792]{1,0:T(8,128)(2,1)S(1)}, u32[]{:S(2)}, u32[]{:S(2)}) collective-permute-start(bf16[16,1792]{1,0:T(8,128)(2,1)S(1)} %add_convert_fusion.2), channel_id=1, source_target_pairs={{0,12},{1,13},{2,14},{3,15},{4,8},{5,9},{6,10},{7,11},{8,4},{9,5},... | collective-permute-start | bytes 172040 | tf_op jit(solution)/shard_map/ppermute | solution.py:37
  77.2 6.1 %collective-permute-start.29 = (bf16[16,1792]{1,0:T(8,128)(2,1)S(1)}, bf16[16,1792]{1,0:T(8,128)(2,1)S(1)}, u32[]{:S(2)}, u32[]{:S(2)}) collective-permute-start(bf16[16,1792]{1,0:T(8,128)(2,1)S(1)} %add_convert_fusion.1), channel_id=1, source_target_pairs={{0,6},{1,7},{2,4},{3,5},{4,2},{5,3},{6,0},{7,1},{8,14},{9,15},{10,... | collective-permute-start | bytes 172040 | tf_op jit(solution)/shard_map/ppermute | solution.py:37
  83.3 1.3 %collective-permute-start.30 = (bf16[16,1792]{1,0:T(8,128)(2,1)S(1)}, bf16[16,1792]{1,0:T(8,128)(2,1)S(1)}, u32[]{:S(2)}, u32[]{:S(2)}) collective-permute-start(bf16[16,1792]{1,0:T(8,128)(2,1)S(1)} %add_convert_fusion.refs_1_), channel_id=1, source_target_pairs={{0,4},{4,0},{8,12},{12,8},{16,20},{20,16},{24,28},{28,24},{1,5},{5... | collective-permute-start | bytes 172040 | tf_op jit(solution)/shard_map/ppermute | solution.py:19
  85.4 5.1 %collective-permute-start.31 = (bf16[32,1152]{1,0:T(8,128)(2,1)S(1)}, bf16[32,1152]{1,0:T(8,128)(2,1)S(1)}, u32[]{:S(2)}, u32[]{:S(2)}) collective-permute-start(bf16[32,1152]{1,0:T(8,128)(2,1)S(1)} %get-tuple-element.70.tail_ref), channel_id=1, source_target_pairs={{0,1},{1,0},{2,3},{3,2},{4,5},{5,4},{6,7},{7,6},{8,9},{9,8},{10,11... | collective-permute-start | bytes 221192 | tf_op jit(solution)/shard_map/ppermute | solution.py:19
  86.3 4.9 %collective-permute-start.32 = (bf16[32,1024]{1,0:T(8,128)(2,1)S(1)}, bf16[32,1024]{1,0:T(8,128)(2,1)S(1)}, u32[]{:S(2)}, u32[]{:S(2)}) collective-permute-start(bf16[32,1024]{1,0:T(8,128)(2,1)S(1)} %get-tuple-element.73), channel_id=1, source_target_pairs={{0,1},{1,0},{2,3},{3,2},{4,5},{5,4},{6,7},{7,6},{8,9},{9,8},{10,11... | collective-permute-start | bytes 196616 | tf_op jit(solution)/shard_map/ppermute | solution.py:19
  88.2 3.7 %collective-permute-start.33 = (f32[1,1792]{1,0:T(1,128)S(1)}, f32[1,1792]{1,0:T(1,128)S(1)}, u32[]{:S(2)}, u32[]{:S(2)}) collective-permute-start(f32[1,1792]{1,0:T(1,128)S(1)} %get-tuple-element.75), channel_id=1, source_target_pairs={{0,1},{1,0},{2,3},{3,2},{4,5},{5,4},{6,7},{7,6},{8,9},{9,8},{10,11... | collective-permute-start | bytes 21512 | tf_op jit(solution)/shard_map/ppermute | solution.py:19

commit v6 on v5

--- a/solution.py
+++ b/solution.py
@@ -230,15 +230,6 @@
     multiplied(scaled_ref[...], upper_ref, lower_ref, piece, product_ref, message_ref)
 
 
-def token_matrix(count, group_count):
-    token = lax.broadcasted_iota(jnp.int32, (count, count), 0)
-    place = lax.broadcasted_iota(jnp.int32, (count, count), 1)
-    rack = token // group_count
-    core = (rack + own_core_of()) % 2
-    matches = core * (count // 2) + rack // 2 * group_count + token % group_count == place
-    return rounded(jnp.where(matches, 1.0, 0.0))
-
-
 def down_body(step, piece, model_width, group_count, tail_ref, other_tail_ref, product_ref, swapped_ref, mixing_ref, weight_ref, *refs):
     width = product_ref.shape[1]
     size = width // 2
@@ -252,27 +243,26 @@
     mixing = mixing_ref[...]
     count = mixing.shape[0]
     last = step == STEPS - 1
-    if last:
-        to_tokens = token_matrix(count, group_count)
-        activated = rounded(jnp.dot(to_tokens, activated, preferred_element_type=jnp.float32))
-        mixing = jnp.dot(to_tokens, rounded(mixing), preferred_element_type=jnp.float32)
     mixing = mixing[:, step : step + 1]
     rows = slice(piece * size, (piece + 1) * size)
     before_refs, out_refs = (refs[:1], refs[1:]) if piece else ((), refs)
-    for columns in column_blocks(weight_ref.shape[1]):
+    final = piece == PIECES - 1
+    for columns in [slice(0, weight_ref.shape[1])] if last and final else column_blocks(weight_ref.shape[1]):
         term = jnp.dot(activated, weight_ref[rows, columns], preferred_element_type=jnp.float32)
         for ref in before_refs:
             term = term + ref[:, columns]
-        if piece < PIECES - 1:
+        if not final:
             out_refs[0][:, columns] = term
             continue
         update = widened(rounded(term)) * mixing
-        if last:
-            blocks = slice(columns.start // LANES, columns.stop // LANES)
-            out_refs[0][:, blocks] = rounded(update).reshape(count, -1, LANES)
-        else:
+        if not last:
             out_refs[0][:, columns] = update[: count // 2]
             out_refs[1][:, columns] = rounded(update[count // 2 :])
+            continue
+        blocks = rounded(update).reshape(count, -1, LANES)
+        for start in range(0, count, group_count):
+            chip, core = start % (count // 2) // group_count, (start // (count // 2) + own_core_of()) % 2
+            out_refs[0][pl.ds((2 * chip + core) * group_count, group_count)] = blocks[start : start + group_count]
 
 
 def result_body(arrived_ref, own_ref, other_ref, out_ref):

time: 105 us -> 105 us (level)
  no operation moved by 1% of the time
where the time goes in v6:
time: 105 us; the launch traced here: 104 us
  waiting for transfers between devices  42.4 us (40%)
  starting transfers between devices  33.3 us (32%)
  Pallas kernels  16.4 us (16%)
  blocking collectives  11.7 us (11%)
    ppermute x18, waiting for transfers between devices, exchanged_both(): return lax.ppermute(shard, ('rack', 'expert'), pairs)  23.9 us
    ppermute x18, starting transfers between devices, exchanged_both(): return lax.ppermute(shard, ('rack', 'expert'), pairs)  23.7 us
    ppermute x16, waiting for transfers between devices, exchanged(): lax.ppermute(shard, axis, [(i, i ^ mask) for i in range(lax.axis_size(axi...  18.5 us
    pallas_call x22, Pallas kernels, kernel_call(): pl.pallas_call(body, out_shape=out_shape, in_specs=[WHOLE] * len(operands...  16.4 us
    all_to_all x1, blocking collectives, dense_steps(): lax.all_to_all(updates[0], ('rack', 'expert'), split_axis=0, concat_axis=...  11.7 us
    ppermute x16, starting transfers between devices, exchanged(): lax.ppermute(shard, axis, [(i, i ^ mask) for i in range(lax.axis_size(axi...  9.63 us
  transfers between devices with their start and end apart: 34, of which 26 were waited for; matrix products, arithmetic and copies ran while one was open for 0% of the time, Pallas kernels for 10%

profile of v6, /device:TPU:0, one launch (start us, length us, event | category | flops | bytes accessed | tf_op | source)
XLA Modules:
  0.0 104.2 jit_solution(15385074223477619923)
XLA Ops:
  0.0 0.9 shard_map.64
  0.9 3.0 %collective-permute-start = (bf16[16,128]{1,0:T(8,128)(2,1)S(1)}, bf16[16,128]{1,0:T(8,128)(2,1)S(1)}, u32[]{:S(2)}, u32[]{:S(2)}) collective-permute-start(bf16[16,128]{1,0:T(8,128)(2,1)S(1)} %get-tuple-element.42.refs_0_), channel_id=1, source_target_pairs={{0,8},{1,9},{2,10},{3,11},{4,12},{5,13},{6,14},{7,15},{8,0},{9,1},... | collective-permute-start | bytes 12296 | tf_op jit(solution)/shard_map/ppermute | solution.py:37
  3.9 0.7 collective-permute-start.2
  4.6 0.6 collective-permute-start.1
  5.1 2.3 %shard_map.65.refs_4_.refs_3_.upper_ref = bf16[1024,2048]{1,0:T(8,128)(2,1)S(1)} custom-call(bf16[1792,2,1024]{2,1,0:T(2,128)(2,1)} %bitcast.11), custom_call_target="tpu_custom_call" | custom-call | bytes 7340032 | tf_op jit(solution)/shard_map/pallas_call | solution.py:65
  7.8 3.8 %collective-permute-start.5 = (bf16[4,16,128]{2,1,0:T(8,128)(2,1)S(1)}, bf16[4,16,128]{2,1,0:T(8,128)(2,1)S(1)}, u32[]{:S(2)}, u32[]{:S(2)}) collective-permute-start(bf16[4,16,128]{2,1,0:T(8,128)(2,1)S(1)} %shard_map.66.refs_0_), channel_id=1, source_target_pairs={{0,18},{1,19},{2,16},{3,17},{4,22},{5,23},{6,20},{7,21},{8,26},{9,... | collective-permute-start | bytes 49160 | tf_op jit(solution)/shard_map/ppermute | solution.py:37
  12.0 2.0 %shard_map.67.refs_4_.lower_ref.refs_5_ = bf16[768,2048]{1,0:T(8,128)(2,1)S(1)} custom-call(bf16[4,16,128]{2,1,0:T(8,128)(2,1)S(1)} %shard_map.66.refs_0_, bf16[1792,2,1024]{2,1,0:T(2,128)(2,1)} %bitcast.12), custom_call_target="tpu_custom_call" | custom-call | bytes 7356416 | tf_op jit(solution)/shard_map/pallas_call | solution.py:65
  14.0 1.7 %collective-permute-done.4.refs_2_ = bf16[4,16,128]{2,1,0:T(8,128)(2,1)S(1)} collective-permute-done((bf16[4,16,128]{2,1,0:T(8,128)(2,1)S(1)}, bf16[4,16,128]{2,1,0:T(8,128)(2,1)S(1)}, u32[]{:S(2)}, u32[]{:S(2)}) %collective-permute-start.4) | collective-permute-done | bytes 16416 | tf_op jit(solution)/shard_map/ppermute | solution.py:37
  16.0 1.0 collective-permute-done.6.refs_1_
  17.0 0.9 shard_map.69
  17.9 1.6 %collective-permute-start.7 = (bf16[32,1152]{1,0:T(8,128)(2,1)S(1)}, bf16[32,1152]{1,0:T(8,128)(2,1)S(1)}, u32[]{:S(2)}, u32[]{:S(2)}) collective-permute-start(bf16[32,1152]{1,0:T(8,128)(2,1)S(1)} %get-tuple-element.46.tail_ref), channel_id=1, source_target_pairs={{0,1},{1,0},{2,3},{3,2},{4,5},{5,4},{6,7},{7,6},{8,9},{9,8},{10,11... | collective-permute-start | bytes 221192 | tf_op jit(solution)/shard_map/ppermute | solution.py:19
  19.5 0.7 shard_map.70
  20.3 0.5 collective-permute-start.8
  20.7 1.7 %collective-permute-done.7.other_tail_ref.swapped_ref = bf16[32,1152]{1,0:T(8,128)(2,1)S(1)} collective-permute-done((bf16[32,1152]{1,0:T(8,128)(2,1)S(1)}, bf16[32,1152]{1,0:T(8,128)(2,1)S(1)}, u32[]{:S(2)}, u32[]{:S(2)}) %collective-permute-start.7) | collective-permute-done | bytes 73760 | tf_op jit(solution)/shard_map/ppermute | solution.py:19
  22.4 0.5 shard_map.71.refs_0_
  22.9 1.6 %collective-permute-done.8.swapped_ref = bf16[32,1024]{1,0:T(8,128)(2,1)S(1)} collective-permute-done((bf16[32,1024]{1,0:T(8,128)(2,1)S(1)}, bf16[32,1024]{1,0:T(8,128)(2,1)S(1)}, u32[]{:S(2)}, u32[]{:S(2)}) %collective-permute-start.8) | collective-permute-done | bytes 65568 | tf_op jit(solution)/shard_map/ppermute | solution.py:19
  24.5 0.6 shard_map.72
  25.2 1.2 %collective-permute-done.9 = bf16[16,1792]{1,0:T(8,128)(2,1)S(1)} collective-permute-done((bf16[16,1792]{1,0:T(8,128)(2,1)S(1)}, bf16[16,1792]{1,0:T(8,128)(2,1)S(1)}, u32[]{:S(2)}, u32[]{:S(2)}) %collective-permute-start.9) | collective-permute-done | bytes 57376 | tf_op jit(solution)/shard_map/ppermute | solution.py:19
  26.4 1.5 %collective-permute-start.12 = (bf16[16,1792]{1,0:T(8,128)(2,1)S(1)}, bf16[16,1792]{1,0:T(8,128)(2,1)S(1)}, u32[]{:S(2)}, u32[]{:S(2)}) collective-permute-start(bf16[16,1792]{1,0:T(8,128)(2,1)S(1)} %add_convert_fusion.8), channel_id=1, source_target_pairs={{0,24},{1,25},{2,26},{3,27},{4,28},{5,29},{6,30},{7,31},{8,16},{9,... | collective-permute-start | bytes 172040 | tf_op jit(solution)/shard_map/ppermute | solution.py:37
  27.9 1.0 collective-permute-start.11
  28.9 0.8 collective-permute-start.10
  29.7 2.0 %collective-permute-done.12 = bf16[16,1792]{1,0:T(8,128)(2,1)S(1)} collective-permute-done((bf16[16,1792]{1,0:T(8,128)(2,1)S(1)}, bf16[16,1792]{1,0:T(8,128)(2,1)S(1)}, u32[]{:S(2)}, u32[]{:S(2)}) %collective-permute-start.12) | collective-permute-done | bytes 57376 | tf_op jit(solution)/shard_map/ppermute | solution.py:37
  31.7 1.0 collective-permute-done.11
  32.8 1.8 %collective-permute-start.13 = (bf16[16,1792]{1,0:T(8,128)(2,1)S(1)}, bf16[16,1792]{1,0:T(8,128)(2,1)S(1)}, u32[]{:S(2)}, u32[]{:S(2)}) collective-permute-start(bf16[16,1792]{1,0:T(8,128)(2,1)S(1)} %add_convert_fusion.7), channel_id=1, source_target_pairs={{0,6},{1,7},{2,4},{3,5},{4,2},{5,3},{6,0},{7,1},{8,14},{9,15},{10,... | collective-permute-start | bytes 172040 | tf_op jit(solution)/shard_map/ppermute | solution.py:37
  34.6 4.3 %collective-permute-done.13 = bf16[16,1792]{1,0:T(8,128)(2,1)S(1)} collective-permute-done((bf16[16,1792]{1,0:T(8,128)(2,1)S(1)}, bf16[16,1792]{1,0:T(8,128)(2,1)S(1)}, u32[]{:S(2)}, u32[]{:S(2)}) %collective-permute-start.13) | collective-permute-done | bytes 57376 | tf_op jit(solution)/shard_map/ppermute | solution.py:37
  39.1 1.1 %collective-permute-done.14.refs_2_ = bf16[16,1792]{1,0:T(8,128)(2,1)S(1)} collective-permute-done((bf16[16,1792]{1,0:T(8,128)(2,1)S(1)}, bf16[16,1792]{1,0:T(8,128)(2,1)S(1)}, u32[]{:S(2)}, u32[]{:S(2)}) %collective-permute-start.14) | collective-permute-done | bytes 57376 | tf_op jit(solution)/shard_map/ppermute | solution.py:19
  40.2 0.7 shard_map.73
  41.0 0.7 shard_map.74
  41.7 2.0 %collective-permute-start.16 = (bf16[32,1024]{1,0:T(8,128)(2,1)S(1)}, bf16[32,1024]{1,0:T(8,128)(2,1)S(1)}, u32[]{:S(2)}, u32[]{:S(2)}) collective-permute-start(bf16[32,1024]{1,0:T(8,128)(2,1)S(1)} %get-tuple-element.58), channel_id=1, source_target_pairs={{0,1},{1,0},{2,3},{3,2},{4,5},{5,4},{6,7},{7,6},{8,9},{9,8},{10,11... | collective-permute-start | bytes 196616 | tf_op jit(solution)/shard_map/ppermute | solution.py:19
  43.8 2.3 %collective-permute-done.15.other_tail_ref.swapped_ref = bf16[32,1152]{1,0:T(8,128)(2,1)S(1)} collective-permute-done((bf16[32,1152]{1,0:T(8,128)(2,1)S(1)}, bf16[32,1152]{1,0:T(8,128)(2,1)S(1)}, u32[]{:S(2)}, u32[]{:S(2)}) %collective-permute-start.15) | collective-permute-done | bytes 73760 | tf_op jit(solution)/shard_map/ppermute | solution.py:19
  46.0 0.5 shard_map.75.refs_0_
  46.7 0.6 shard_map.76
  47.4 1.2 %collective-permute-done.17 = bf16[16,1792]{1,0:T(8,128)(2,1)S(1)} collective-permute-done((bf16[16,1792]{1,0:T(8,128)(2,1)S(1)}, bf16[16,1792]{1,0:T(8,128)(2,1)S(1)}, u32[]{:S(2)}, u32[]{:S(2)}) %collective-permute-start.17) | collective-permute-done | bytes 57376 | tf_op jit(solution)/shard_map/ppermute | solution.py:19
  48.6 1.6 %collective-permute-start.20 = (bf16[16,1792]{1,0:T(8,128)(2,1)S(1)}, bf16[16,1792]{1,0:T(8,128)(2,1)S(1)}, u32[]{:S(2)}, u32[]{:S(2)}) collective-permute-start(bf16[16,1792]{1,0:T(8,128)(2,1)S(1)} %add_convert_fusion.5), channel_id=1, source_target_pairs={{0,24},{1,25},{2,26},{3,27},{4,28},{5,29},{6,30},{7,31},{8,16},{9,... | collective-permute-start | bytes 172040 | tf_op jit(solution)/shard_map/ppermute | solution.py:37
  50.2 0.6 collective-permute-start.19
  50.8 1.1 %collective-permute-start.18 = (bf16[16,1792]{1,0:T(8,128)(2,1)S(1)}, bf16[16,1792]{1,0:T(8,128)(2,1)S(1)}, u32[]{:S(2)}, u32[]{:S(2)}) collective-permute-start(bf16[16,1792]{1,0:T(8,128)(2,1)S(1)} %add_convert_fusion.5), channel_id=1, source_target_pairs={{0,12},{1,13},{2,14},{3,15},{4,8},{5,9},{6,10},{7,11},{8,4},{9,5},... | collective-permute-start | bytes 172040 | tf_op jit(solution)/shard_map/ppermute | solution.py:37
  51.9 1.9 %collective-permute-done.20 = bf16[16,1792]{1,0:T(8,128)(2,1)S(1)} collective-permute-done((bf16[16,1792]{1,0:T(8,128)(2,1)S(1)}, bf16[16,1792]{1,0:T(8,128)(2,1)S(1)}, u32[]{:S(2)}, u32[]{:S(2)}) %collective-permute-start.20) | collective-permute-done | bytes 57376 | tf_op jit(solution)/shard_map/ppermute | solution.py:37
  53.8 1.2 %collective-permute-done.19 = bf16[16,1792]{1,0:T(8,128)(2,1)S(1)} collective-permute-done((bf16[16,1792]{1,0:T(8,128)(2,1)S(1)}, bf16[16,1792]{1,0:T(8,128)(2,1)S(1)}, u32[]{:S(2)}, u32[]{:S(2)}) %collective-permute-start.19) | collective-permute-done | bytes 57376 | tf_op jit(solution)/shard_map/ppermute | solution.py:37
  55.0 1.8 %collective-permute-start.21 = (bf16[16,1792]{1,0:T(8,128)(2,1)S(1)}, bf16[16,1792]{1,0:T(8,128)(2,1)S(1)}, u32[]{:S(2)}, u32[]{:S(2)}) collective-permute-start(bf16[16,1792]{1,0:T(8,128)(2,1)S(1)} %add_convert_fusion.4), channel_id=1, source_target_pairs={{0,6},{1,7},{2,4},{3,5},{4,2},{5,3},{6,0},{7,1},{8,14},{9,15},{10,... | collective-permute-start | bytes 172040 | tf_op jit(solution)/shard_map/ppermute | solution.py:37
  56.9 4.3 %collective-permute-done.21 = bf16[16,1792]{1,0:T(8,128)(2,1)S(1)} collective-permute-done((bf16[16,1792]{1,0:T(8,128)(2,1)S(1)}, bf16[16,1792]{1,0:T(8,128)(2,1)S(1)}, u32[]{:S(2)}, u32[]{:S(2)}) %collective-permute-start.21) | collective-permute-done | bytes 57376 | tf_op jit(solution)/shard_map/ppermute | solution.py:37
  61.4 1.1 %collective-permute-done.22.refs_2_ = bf16[16,1792]{1,0:T(8,128)(2,1)S(1)} collective-permute-done((bf16[16,1792]{1,0:T(8,128)(2,1)S(1)}, bf16[16,1792]{1,0:T(8,128)(2,1)S(1)}, u32[]{:S(2)}, u32[]{:S(2)}) %collective-permute-start.22) | collective-permute-done | bytes 57376 | tf_op jit(solution)/shard_map/ppermute | solution.py:19
  62.5 0.7 shard_map.77
  63.4 0.7 shard_map.78
  64.2 1.9 %collective-permute-start.24 = (bf16[32,1024]{1,0:T(8,128)(2,1)S(1)}, bf16[32,1024]{1,0:T(8,128)(2,1)S(1)}, u32[]{:S(2)}, u32[]{:S(2)}) collective-permute-start(bf16[32,1024]{1,0:T(8,128)(2,1)S(1)} %get-tuple-element.66), channel_id=1, source_target_pairs={{0,1},{1,0},{2,3},{3,2},{4,5},{5,4},{6,7},{7,6},{8,9},{9,8},{10,11... | collective-permute-start | bytes 196616 | tf_op jit(solution)/shard_map/ppermute | solution.py:19
  66.0 2.3 %collective-permute-done.23.other_tail_ref.swapped_ref = bf16[32,1152]{1,0:T(8,128)(2,1)S(1)} collective-permute-done((bf16[32,1152]{1,0:T(8,128)(2,1)S(1)}, bf16[32,1152]{1,0:T(8,128)(2,1)S(1)}, u32[]{:S(2)}, u32[]{:S(2)}) %collective-permute-start.23) | collective-permute-done | bytes 73760 | tf_op jit(solution)/shard_map/ppermute | solution.py:19
  68.3 0.5 shard_map.79.refs_0_
  69.0 0.6 shard_map.80
  69.7 1.2 %collective-permute-done.25 = bf16[16,1792]{1,0:T(8,128)(2,1)S(1)} collective-permute-done((bf16[16,1792]{1,0:T(8,128)(2,1)S(1)}, bf16[16,1792]{1,0:T(8,128)(2,1)S(1)}, u32[]{:S(2)}, u32[]{:S(2)}) %collective-permute-start.25) | collective-permute-done | bytes 57376 | tf_op jit(solution)/shard_map/ppermute | solution.py:19
  70.9 1.5 %collective-permute-start.28 = (bf16[16,1792]{1,0:T(8,128)(2,1)S(1)}, bf16[16,1792]{1,0:T(8,128)(2,1)S(1)}, u32[]{:S(2)}, u32[]{:S(2)}) collective-permute-start(bf16[16,1792]{1,0:T(8,128)(2,1)S(1)} %add_convert_fusion.2), channel_id=1, source_target_pairs={{0,24},{1,25},{2,26},{3,27},{4,28},{5,29},{6,30},{7,31},{8,16},{9,... | collective-permute-start | bytes 172040 | tf_op jit(solution)/shard_map/ppermute | solution.py:37
  72.4 0.5 collective-permute-start.27
  72.9 1.3 %collective-permute-start.26 = (bf16[16,1792]{1,0:T(8,128)(2,1)S(1)}, bf16[16,1792]{1,0:T(8,128)(2,1)S(1)}, u32[]{:S(2)}, u32[]{:S(2)}) collective-permute-start(bf16[16,1792]{1,0:T(8,128)(2,1)S(1)} %add_convert_fusion.2), channel_id=1, source_target_pairs={{0,12},{1,13},{2,14},{3,15},{4,8},{5,9},{6,10},{7,11},{8,4},{9,5},... | collective-permute-start | bytes 172040 | tf_op jit(solution)/shard_map/ppermute | solution.py:37
  74.2 2.0 %collective-permute-done.28 = bf16[16,1792]{1,0:T(8,128)(2,1)S(1)} collective-permute-done((bf16[16,1792]{1,0:T(8,128)(2,1)S(1)}, bf16[16,1792]{1,0:T(8,128)(2,1)S(1)}, u32[]{:S(2)}, u32[]{:S(2)}) %collective-permute-start.28) | collective-permute-done | bytes 57376 | tf_op jit(solution)/shard_map/ppermute | solution.py:37
  76.1 1.0 collective-permute-done.27
  77.2 1.8 %collective-permute-start.29 = (bf16[16,1792]{1,0:T(8,128)(2,1)S(1)}, bf16[16,1792]{1,0:T(8,128)(2,1)S(1)}, u32[]{:S(2)}, u32[]{:S(2)}) collective-permute-start(bf16[16,1792]{1,0:T(8,128)(2,1)S(1)} %add_convert_fusion.1), channel_id=1, source_target_pairs={{0,6},{1,7},{2,4},{3,5},{4,2},{5,3},{6,0},{7,1},{8,14},{9,15},{10,... | collective-permute-start | bytes 172040 | tf_op jit(solution)/shard_map/ppermute | solution.py:37
  79.0 4.3 %collective-permute-done.29 = bf16[16,1792]{1,0:T(8,128)(2,1)S(1)} collective-permute-done((bf16[16,1792]{1,0:T(8,128)(2,1)S(1)}, bf16[16,1792]{1,0:T(8,128)(2,1)S(1)}, u32[]{:S(2)}, u32[]{:S(2)}) %collective-permute-start.29) | collective-permute-done | bytes 57376 | tf_op jit(solution)/shard_map/ppermute | solution.py:37
  83.5 1.1 %collective-permute-done.30.refs_2_ = bf16[16,1792]{1,0:T(8,128)(2,1)S(1)} collective-permute-done((bf16[16,1792]{1,0:T(8,128)(2,1)S(1)}, bf16[16,1792]{1,0:T(8,128)(2,1)S(1)}, u32[]{:S(2)}, u32[]{:S(2)}) %collective-permute-start.30) | collective-permute-done | bytes 57376 | tf_op jit(solution)/shard_map/ppermute | solution.py:19
  84.6 0.7 shard_map.81
  85.6 0.7 shard_map.82
  86.3 1.9 %collective-permute-start.32 = (bf16[32,1024]{1,0:T(8,128)(2,1)S(1)}, bf16[32,1024]{1,0:T(8,128)(2,1)S(1)}, u32[]{:S(2)}, u32[]{:S(2)}) collective-permute-start(bf16[32,1024]{1,0:T(8,128)(2,1)S(1)} %get-tuple-element.73), channel_id=1, source_target_pairs={{0,1},{1,0},{2,3},{3,2},{4,5},{5,4},{6,7},{7,6},{8,9},{9,8},{10,11... | collective-permute-start | bytes 196616 | tf_op jit(solution)/shard_map/ppermute | solution.py:19
  88.4 2.1 %collective-permute-done.31.other_tail_ref.swapped_ref = bf16[32,1152]{1,0:T(8,128)(2,1)S(1)} collective-permute-done((bf16[32,1152]{1,0:T(8,128)(2,1)S(1)}, bf16[32,1152]{1,0:T(8,128)(2,1)S(1)}, u32[]{:S(2)}, u32[]{:S(2)}) %collective-permute-start.31) | collective-permute-done | bytes 73760 | tf_op jit(solution)/shard_map/ppermute | solution.py:19
  90.5 0.5 shard_map.83.refs_0_
  91.2 0.6 shard_map.84
  91.8 11.7 %all_to_all.5.arrived_ref = bf16[32,14,128]{2,1,0:T(8,128)(2,1)S(1)} all-to-all(bf16[32,14,128]{2,1,0:T(8,128)(2,1)S(1)} %shard_map.84), channel_id=1, replica_groups=mesh['rack'=8,'expert'=4] {'rack','expert'}, dimensions={0} | all-to-all | bytes 229376 | tf_op jit(solution)/shard_map/all_to_all | solution.py:408
  103.5 0.7 shard_map.85
  (38 shorter events, 3.2 us)
Async XLA Ops:
  0.9 6.6 %collective-permute-start = (bf16[16,128]{1,0:T(8,128)(2,1)S(1)}, bf16[16,128]{1,0:T(8,128)(2,1)S(1)}, u32[]{:S(2)}, u32[]{:S(2)}) collective-permute-start(bf16[16,128]{1,0:T(8,128)(2,1)S(1)} %get-tuple-element.42.refs_0_), channel_id=1, source_target_pairs={{0,8},{1,9},{2,10},{3,11},{4,12},{5,13},{6,14},{7,15},{8,0},{9,1},... | collective-permute-start | bytes 12296 | tf_op jit(solution)/shard_map/ppermute | solution.py:37
  3.9 3.9 %collective-permute-start.2 = (bf16[16,128]{1,0:T(8,128)(2,1)S(1)}, bf16[16,128]{1,0:T(8,128)(2,1)S(1)}, u32[]{:S(2)}, u32[]{:S(2)}) collective-permute-start(bf16[16,128]{1,0:T(8,128)(2,1)S(1)} %get-tuple-element.43), channel_id=1, source_target_pairs={{0,13},{1,12},{2,15},{3,14},{4,9},{5,8},{6,11},{7,10},{8,5},{9,4},... | collective-permute-start | bytes 12296 | tf_op jit(solution)/shard_map/ppermute | solution.py:37
  4.6 3.2 %collective-permute-start.1 = (bf16[16,128]{1,0:T(8,128)(2,1)S(1)}, bf16[16,128]{1,0:T(8,128)(2,1)S(1)}, u32[]{:S(2)}, u32[]{:S(2)}) collective-permute-start(bf16[16,128]{1,0:T(8,128)(2,1)S(1)} %get-tuple-element.43), channel_id=1, source_target_pairs={{0,5},{1,4},{2,7},{3,6},{4,1},{5,0},{6,3},{7,2},{8,13},{9,12},{10,... | collective-permute-start | bytes 12296 | tf_op jit(solution)/shard_map/ppermute | solution.py:37
  7.8 6.2 %collective-permute-start.5 = (bf16[4,16,128]{2,1,0:T(8,128)(2,1)S(1)}, bf16[4,16,128]{2,1,0:T(8,128)(2,1)S(1)}, u32[]{:S(2)}, u32[]{:S(2)}) collective-permute-start(bf16[4,16,128]{2,1,0:T(8,128)(2,1)S(1)} %shard_map.66.refs_0_), channel_id=1, source_target_pairs={{0,18},{1,19},{2,16},{3,17},{4,22},{5,23},{6,20},{7,21},{8,26},{9,... | collective-permute-start | bytes 49160 | tf_op jit(solution)/shard_map/ppermute | solution.py:37
  11.6 4.1 %collective-permute-start.4 = (bf16[4,16,128]{2,1,0:T(8,128)(2,1)S(1)}, bf16[4,16,128]{2,1,0:T(8,128)(2,1)S(1)}, u32[]{:S(2)}, u32[]{:S(2)}) collective-permute-start(bf16[4,16,128]{2,1,0:T(8,128)(2,1)S(1)} %shard_map.66.refs_0_), channel_id=1, source_target_pairs={{0,6},{1,7},{2,4},{3,5},{4,2},{5,3},{6,0},{7,1},{8,14},{9,15},{10,... | collective-permute-start | bytes 49160 | tf_op jit(solution)/shard_map/ppermute | solution.py:37
  11.8 3.9 %collective-permute-start.3 = (bf16[4,16,128]{2,1,0:T(8,128)(2,1)S(1)}, bf16[4,16,128]{2,1,0:T(8,128)(2,1)S(1)}, u32[]{:S(2)}, u32[]{:S(2)}) collective-permute-start(bf16[4,16,128]{2,1,0:T(8,128)(2,1)S(1)} %shard_map.66.refs_0_), channel_id=1, source_target_pairs={{0,20},{1,21},{2,22},{3,23},{4,16},{5,17},{6,18},{7,19},{8,28},{9,... | collective-permute-start | bytes 49160 | tf_op jit(solution)/shard_map/ppermute | solution.py:37
  15.7 1.3 %collective-permute-start.6 = (bf16[16,16,128]{2,1,0:T(8,128)(2,1)S(1)}, bf16[16,16,128]{2,1,0:T(8,128)(2,1)S(1)}, u32[]{:S(2)}, u32[]{:S(2)}) collective-permute-start(bf16[16,16,128]{2,1,0:T(8,128)(2,1)S(1)} %shard_map.68.refs_0_), channel_id=1, source_target_pairs={{0,4},{4,0},{8,12},{12,8},{16,20},{20,16},{24,28},{28,24},{1,5},{5... | collective-permute-start | bytes 196616 | tf_op jit(solution)/shard_map/ppermute | solution.py:19
  17.9 4.5 %copy-start = (bf16[1,1,1024,1792]{3,2,1,0:T(8,128)(2,1)S(1)}, bf16[1,1,1024,1792]{3,2,1,0:T(8,128)(2,1)}, u32[]{:S(2)}) copy-start(bf16[1,1,1024,1792]{3,2,1,0:T(8,128)(2,1)} %param.11) | copy-start | bytes 11010052
  17.9 4.5 %collective-permute-start.7 = (bf16[32,1152]{1,0:T(8,128)(2,1)S(1)}, bf16[32,1152]{1,0:T(8,128)(2,1)S(1)}, u32[]{:S(2)}, u32[]{:S(2)}) collective-permute-start(bf16[32,1152]{1,0:T(8,128)(2,1)S(1)} %get-tuple-element.46.tail_ref), channel_id=1, source_target_pairs={{0,1},{1,0},{2,3},{3,2},{4,5},{5,4},{6,7},{7,6},{8,9},{9,8},{10,11... | collective-permute-start | bytes 221192 | tf_op jit(solution)/shard_map/ppermute | solution.py:19
  20.3 4.3 %collective-permute-start.8 = (bf16[32,1024]{1,0:T(8,128)(2,1)S(1)}, bf16[32,1024]{1,0:T(8,128)(2,1)S(1)}, u32[]{:S(2)}, u32[]{:S(2)}) collective-permute-start(bf16[32,1024]{1,0:T(8,128)(2,1)S(1)} %get-tuple-element.49), channel_id=1, source_target_pairs={{0,1},{1,0},{2,3},{3,2},{4,5},{5,4},{6,7},{7,6},{8,9},{9,8},{10,11... | collective-permute-start | bytes 196616 | tf_op jit(solution)/shard_map/ppermute | solution.py:19
  25.1 1.3 %collective-permute-start.9 = (bf16[16,1792]{1,0:T(8,128)(2,1)S(1)}, bf16[16,1792]{1,0:T(8,128)(2,1)S(1)}, u32[]{:S(2)}, u32[]{:S(2)}) collective-permute-start(bf16[16,1792]{1,0:T(8,128)(2,1)S(1)} %get-tuple-element.53), channel_id=1, source_target_pairs={{0,4},{4,0},{8,12},{12,8},{16,20},{20,16},{24,28},{28,24},{1,5},{5... | collective-permute-start | bytes 172040 | tf_op jit(solution)/shard_map/ppermute | solution.py:19
  26.4 5.2 %collective-permute-start.12 = (bf16[16,1792]{1,0:T(8,128)(2,1)S(1)}, bf16[16,1792]{1,0:T(8,128)(2,1)S(1)}, u32[]{:S(2)}, u32[]{:S(2)}) collective-permute-start(bf16[16,1792]{1,0:T(8,128)(2,1)S(1)} %add_convert_fusion.8), channel_id=1, source_target_pairs={{0,24},{1,25},{2,26},{3,27},{4,28},{5,29},{6,30},{7,31},{8,16},{9,... | collective-permute-start | bytes 172040 | tf_op jit(solution)/shard_map/ppermute | solution.py:37
  27.9 4.8 %collective-permute-start.11 = (bf16[16,1792]{1,0:T(8,128)(2,1)S(1)}, bf16[16,1792]{1,0:T(8,128)(2,1)S(1)}, u32[]{:S(2)}, u32[]{:S(2)}) collective-permute-start(bf16[16,1792]{1,0:T(8,128)(2,1)S(1)} %add_convert_fusion.8), channel_id=1, source_target_pairs={{0,20},{1,21},{2,22},{3,23},{4,16},{5,17},{6,18},{7,19},{8,28},{9,... | collective-permute-start | bytes 172040 | tf_op jit(solution)/shard_map/ppermute | solution.py:37
  28.9 3.8 %collective-permute-start.10 = (bf16[16,1792]{1,0:T(8,128)(2,1)S(1)}, bf16[16,1792]{1,0:T(8,128)(2,1)S(1)}, u32[]{:S(2)}, u32[]{:S(2)}) collective-permute-start(bf16[16,1792]{1,0:T(8,128)(2,1)S(1)} %add_convert_fusion.8), channel_id=1, source_target_pairs={{0,12},{1,13},{2,14},{3,15},{4,8},{5,9},{6,10},{7,11},{8,4},{9,5},... | collective-permute-start | bytes 172040 | tf_op jit(solution)/shard_map/ppermute | solution.py:37
  32.8 6.1 %collective-permute-start.13 = (bf16[16,1792]{1,0:T(8,128)(2,1)S(1)}, bf16[16,1792]{1,0:T(8,128)(2,1)S(1)}, u32[]{:S(2)}, u32[]{:S(2)}) collective-permute-start(bf16[16,1792]{1,0:T(8,128)(2,1)S(1)} %add_convert_fusion.7), channel_id=1, source_target_pairs={{0,6},{1,7},{2,4},{3,5},{4,2},{5,3},{6,0},{7,1},{8,14},{9,15},{10,... | collective-permute-start | bytes 172040 | tf_op jit(solution)/shard_map/ppermute | solution.py:37
  38.9 1.3 %collective-permute-start.14 = (bf16[16,1792]{1,0:T(8,128)(2,1)S(1)}, bf16[16,1792]{1,0:T(8,128)(2,1)S(1)}, u32[]{:S(2)}, u32[]{:S(2)}) collective-permute-start(bf16[16,1792]{1,0:T(8,128)(2,1)S(1)} %add_convert_fusion.6.refs_1_), channel_id=1, source_target_pairs={{0,4},{4,0},{8,12},{12,8},{16,20},{20,16},{24,28},{28,24},{1,5},{5... | collective-permute-start | bytes 172040 | tf_op jit(solution)/shard_map/ppermute | solution.py:19
  40.9 5.1 %collective-permute-start.15 = (bf16[32,1152]{1,0:T(8,128)(2,1)S(1)}, bf16[32,1152]{1,0:T(8,128)(2,1)S(1)}, u32[]{:S(2)}, u32[]{:S(2)}) collective-permute-start(bf16[32,1152]{1,0:T(8,128)(2,1)S(1)} %get-tuple-element.55.tail_ref), channel_id=1, source_target_pairs={{0,1},{1,0},{2,3},{3,2},{4,5},{5,4},{6,7},{7,6},{8,9},{9,8},{10,11... | collective-permute-start | bytes 221192 | tf_op jit(solution)/shard_map/ppermute | solution.py:19
  41.7 5.0 %collective-permute-start.16 = (bf16[32,1024]{1,0:T(8,128)(2,1)S(1)}, bf16[32,1024]{1,0:T(8,128)(2,1)S(1)}, u32[]{:S(2)}, u32[]{:S(2)}) collective-permute-start(bf16[32,1024]{1,0:T(8,128)(2,1)S(1)} %get-tuple-element.58), channel_id=1, source_target_pairs={{0,1},{1,0},{2,3},{3,2},{4,5},{5,4},{6,7},{7,6},{8,9},{9,8},{10,11... | collective-permute-start | bytes 196616 | tf_op jit(solution)/shard_map/ppermute | solution.py:19
  47.3 1.3 %collective-permute-start.17 = (bf16[16,1792]{1,0:T(8,128)(2,1)S(1)}, bf16[16,1792]{1,0:T(8,128)(2,1)S(1)}, u32[]{:S(2)}, u32[]{:S(2)}) collective-permute-start(bf16[16,1792]{1,0:T(8,128)(2,1)S(1)} %get-tuple-element.61), channel_id=1, source_target_pairs={{0,4},{4,0},{8,12},{12,8},{16,20},{20,16},{24,28},{28,24},{1,5},{5... | collective-permute-start | bytes 172040 | tf_op jit(solution)/shard_map/ppermute | solution.py:19
  48.6 5.2 %collective-permute-start.20 = (bf16[16,1792]{1,0:T(8,128)(2,1)S(1)}, bf16[16,1792]{1,0:T(8,128)(2,1)S(1)}, u32[]{:S(2)}, u32[]{:S(2)}) collective-permute-start(bf16[16,1792]{1,0:T(8,128)(2,1)S(1)} %add_convert_fusion.5), channel_id=1, source_target_pairs={{0,24},{1,25},{2,26},{3,27},{4,28},{5,29},{6,30},{7,31},{8,16},{9,... | collective-permute-start | bytes 172040 | tf_op jit(solution)/shard_map/ppermute | solution.py:37
  50.2 4.8 %collective-permute-start.19 = (bf16[16,1792]{1,0:T(8,128)(2,1)S(1)}, bf16[16,1792]{1,0:T(8,128)(2,1)S(1)}, u32[]{:S(2)}, u32[]{:S(2)}) collective-permute-start(bf16[16,1792]{1,0:T(8,128)(2,1)S(1)} %add_convert_fusion.5), channel_id=1, source_target_pairs={{0,20},{1,21},{2,22},{3,23},{4,16},{5,17},{6,18},{7,19},{8,28},{9,... | collective-permute-start | bytes 172040 | tf_op jit(solution)/shard_map/ppermute | solution.py:37
  50.8 4.2 %collective-permute-start.18 = (bf16[16,1792]{1,0:T(8,128)(2,1)S(1)}, bf16[16,1792]{1,0:T(8,128)(2,1)S(1)}, u32[]{:S(2)}, u32[]{:S(2)}) collective-permute-start(bf16[16,1792]{1,0:T(8,128)(2,1)S(1)} %add_convert_fusion.5), channel_id=1, source_target_pairs={{0,12},{1,13},{2,14},{3,15},{4,8},{5,9},{6,10},{7,11},{8,4},{9,5},... | collective-permute-start | bytes 172040 | tf_op jit(solution)/shard_map/ppermute | solution.py:37
  55.0 6.1 %collective-permute-start.21 = (bf16[16,1792]{1,0:T(8,128)(2,1)S(1)}, bf16[16,1792]{1,0:T(8,128)(2,1)S(1)}, u32[]{:S(2)}, u32[]{:S(2)}) collective-permute-start(bf16[16,1792]{1,0:T(8,128)(2,1)S(1)} %add_convert_fusion.4), channel_id=1, source_target_pairs={{0,6},{1,7},{2,4},{3,5},{4,2},{5,3},{6,0},{7,1},{8,14},{9,15},{10,... | collective-permute-start | bytes 172040 | tf_op jit(solution)/shard_map/ppermute | solution.py:37
  61.2 1.3 %collective-permute-start.22 = (bf16[16,1792]{1,0:T(8,128)(2,1)S(1)}, bf16[16,1792]{1,0:T(8,128)(2,1)S(1)}, u32[]{:S(2)}, u32[]{:S(2)}) collective-permute-start(bf16[16,1792]{1,0:T(8,128)(2,1)S(1)} %add_convert_fusion.3.refs_1_), channel_id=1, source_target_pairs={{0,4},{4,0},{8,12},{12,8},{16,20},{20,16},{24,28},{28,24},{1,5},{5... | collective-permute-start | bytes 172040 | tf_op jit(solution)/shard_map/ppermute | solution.py:19
  63.2 5.1 %collective-permute-start.23 = (bf16[32,1152]{1,0:T(8,128)(2,1)S(1)}, bf16[32,1152]{1,0:T(8,128)(2,1)S(1)}, u32[]{:S(2)}, u32[]{:S(2)}) collective-permute-start(bf16[32,1152]{1,0:T(8,128)(2,1)S(1)} %get-tuple-element.63.tail_ref), channel_id=1, source_target_pairs={{0,1},{1,0},{2,3},{3,2},{4,5},{5,4},{6,7},{7,6},{8,9},{9,8},{10,11... | collective-permute-start | bytes 221192 | tf_op jit(solution)/shard_map/ppermute | solution.py:19
  64.2 4.8 %collective-permute-start.24 = (bf16[32,1024]{1,0:T(8,128)(2,1)S(1)}, bf16[32,1024]{1,0:T(8,128)(2,1)S(1)}, u32[]{:S(2)}, u32[]{:S(2)}) collective-permute-start(bf16[32,1024]{1,0:T(8,128)(2,1)S(1)} %get-tuple-element.66), channel_id=1, source_target_pairs={{0,1},{1,0},{2,3},{3,2},{4,5},{5,4},{6,7},{7,6},{8,9},{9,8},{10,11... | collective-permute-start | bytes 196616 | tf_op jit(solution)/shard_map/ppermute | solution.py:19
  69.6 1.3 %collective-permute-start.25 = (bf16[16,1792]{1,0:T(8,128)(2,1)S(1)}, bf16[16,1792]{1,0:T(8,128)(2,1)S(1)}, u32[]{:S(2)}, u32[]{:S(2)}) collective-permute-start(bf16[16,1792]{1,0:T(8,128)(2,1)S(1)} %get-tuple-element.69), channel_id=1, source_target_pairs={{0,4},{4,0},{8,12},{12,8},{16,20},{20,16},{24,28},{28,24},{1,5},{5... | collective-permute-start | bytes 172040 | tf_op jit(solution)/shard_map/ppermute | solution.py:19
  70.9 5.2 %collective-permute-start.28 = (bf16[16,1792]{1,0:T(8,128)(2,1)S(1)}, bf16[16,1792]{1,0:T(8,128)(2,1)S(1)}, u32[]{:S(2)}, u32[]{:S(2)}) collective-permute-start(bf16[16,1792]{1,0:T(8,128)(2,1)S(1)} %add_convert_fusion.2), channel_id=1, source_target_pairs={{0,24},{1,25},{2,26},{3,27},{4,28},{5,29},{6,30},{7,31},{8,16},{9,... | collective-permute-start | bytes 172040 | tf_op jit(solution)/shard_map/ppermute | solution.py:37
  72.4 4.8 %collective-permute-start.27 = (bf16[16,1792]{1,0:T(8,128)(2,1)S(1)}, bf16[16,1792]{1,0:T(8,128)(2,1)S(1)}, u32[]{:S(2)}, u32[]{:S(2)}) collective-permute-start(bf16[16,1792]{1,0:T(8,128)(2,1)S(1)} %add_convert_fusion.2), channel_id=1, source_target_pairs={{0,20},{1,21},{2,22},{3,23},{4,16},{5,17},{6,18},{7,19},{8,28},{9,... | collective-permute-start | bytes 172040 | tf_op jit(solution)/shard_map/ppermute | solution.py:37
  72.9 4.3 %collective-permute-start.26 = (bf16[16,1792]{1,0:T(8,128)(2,1)S(1)}, bf16[16,1792]{1,0:T(8,128)(2,1)S(1)}, u32[]{:S(2)}, u32[]{:S(2)}) collective-permute-start(bf16[16,1792]{1,0:T(8,128)(2,1)S(1)} %add_convert_fusion.2), channel_id=1, source_target_pairs={{0,12},{1,13},{2,14},{3,15},{4,8},{5,9},{6,10},{7,11},{8,4},{9,5},... | collective-permute-start | bytes 172040 | tf_op jit(solution)/shard_map/ppermute | solution.py:37
  77.2 6.1 %collective-permute-start.29 = (bf16[16,1792]{1,0:T(8,128)(2,1)S(1)}, bf16[16,1792]{1,0:T(8,128)(2,1)S(1)}, u32[]{:S(2)}, u32[]{:S(2)}) collective-permute-start(bf16[16,1792]{1,0:T(8,128)(2,1)S(1)} %add_convert_fusion.1), channel_id=1, source_target_pairs={{0,6},{1,7},{2,4},{3,5},{4,2},{5,3},{6,0},{7,1},{8,14},{9,15},{10,... | collective-permute-start | bytes 172040 | tf_op jit(solution)/shard_map/ppermute | solution.py:37
  83.3 1.3 %collective-permute-start.30 = (bf16[16,1792]{1,0:T(8,128)(2,1)S(1)}, bf16[16,1792]{1,0:T(8,128)(2,1)S(1)}, u32[]{:S(2)}, u32[]{:S(2)}) collective-permute-start(bf16[16,1792]{1,0:T(8,128)(2,1)S(1)} %add_convert_fusion.refs_1_), channel_id=1, source_target_pairs={{0,4},{4,0},{8,12},{12,8},{16,20},{20,16},{24,28},{28,24},{1,5},{5... | collective-permute-start | bytes 172040 | tf_op jit(solution)/shard_map/ppermute | solution.py:19
  85.4 5.1 %collective-permute-start.31 = (bf16[32,1152]{1,0:T(8,128)(2,1)S(1)}, bf16[32,1152]{1,0:T(8,128)(2,1)S(1)}, u32[]{:S(2)}, u32[]{:S(2)}) collective-permute-start(bf16[32,1152]{1,0:T(8,128)(2,1)S(1)} %get-tuple-element.70.tail_ref), channel_id=1, source_target_pairs={{0,1},{1,0},{2,3},{3,2},{4,5},{5,4},{6,7},{7,6},{8,9},{9,8},{10,11... | collective-permute-start | bytes 221192 | tf_op jit(solution)/shard_map/ppermute | solution.py:19
  86.3 4.9 %collective-permute-start.32 = (bf16[32,1024]{1,0:T(8,128)(2,1)S(1)}, bf16[32,1024]{1,0:T(8,128)(2,1)S(1)}, u32[]{:S(2)}, u32[]{:S(2)}) collective-permute-start(bf16[32,1024]{1,0:T(8,128)(2,1)S(1)} %get-tuple-element.73), channel_id=1, source_target_pairs={{0,1},{1,0},{2,3},{3,2},{4,5},{5,4},{6,7},{7,6},{8,9},{9,8},{10,11... | collective-permute-start | bytes 196616 | tf_op jit(solution)/shard_map/ppermute | solution.py:19
  88.2 3.6 %collective-permute-start.33 = (f32[1,1792]{1,0:T(1,128)S(1)}, f32[1,1792]{1,0:T(1,128)S(1)}, u32[]{:S(2)}, u32[]{:S(2)}) collective-permute-start(f32[1,1792]{1,0:T(1,128)S(1)} %get-tuple-element.75), channel_id=1, source_target_pairs={{0,1},{1,0},{2,3},{3,2},{4,5},{5,4},{6,7},{7,6},{8,9},{9,8},{10,11... | collective-permute-start | bytes 21512 | tf_op jit(solution)/shard_map/ppermute | solution.py:19

commit v7 on v6

--- a/solution.py
+++ b/solution.py
@@ -207,8 +207,7 @@
         residual_ref[...] = residual
     else:
         before_ref, own_ref, other_ref, gain_ref, upper_ref, lower_ref, *residual_refs, scaled_ref, product_ref, message_ref = refs
-        update = jnp.concatenate([own_ref[...], other_ref[...]], axis=0)
-        residual = before_ref[...] + widened(update)
+        residual = before_ref[...] + jnp.concatenate([own_ref[...], widened(other_ref[...])], axis=0)
         if last:
             place = lax.broadcasted_iota(jnp.int32, (residual.shape[0], 1), 0)
             own_place = own_place_of(residual.shape[0] // 2, group_count)
@@ -342,7 +341,7 @@
             operands = gathered
             kept += [in_vmem((token_count, LANES), jnp.float32)]
         else:
-            operands = [residual, sent, received]
+            operands = [residual, update, received]
         if last:
             kept = [in_vmem((1, half_width), jnp.float32)] * 2
         *kept, scaled, product, message = kernel_call(
@@ -395,15 +394,12 @@
             break
         update = updates[0] + widened(exchanged(updates[1], "rack", 1))
         sent = rounded(update)
-        update = widened(sent)
         for mask in range(2, rack_count, 2):
             update = update + widened(exchanged_both(sent, *crossed(mask, 0)))
         sent = rounded(update)
-        update = widened(sent)
         for mask in range(2, group_count, 2):
             update = update + widened(exchanged_both(sent, *crossed(0, mask)))
-        sent = rounded(update)
-        received = exchanged(sent, "rack", 1)
+        received = exchanged(rounded(update), "rack", 1)
 
     arrived = lax.all_to_all(updates[0], ("rack", "expert"), split_axis=0, concat_axis=0, tiled=True)
     (result,) = kernel_call(

time: 105 us -> 105 us (level)
  no operation moved by 1% of the time
where the time goes in v7:
time: 105 us; the launch traced here: 104 us
  waiting for transfers between devices  42.5 us (40%)
  starting transfers between devices  33.3 us (32%)
  Pallas kernels  16.3 us (16%)
  blocking collectives  11.7 us (11%)
    ppermute x18, waiting for transfers between devices, exchanged_both(): return lax.ppermute(shard, ('rack', 'expert'), pairs)  23.9 us
    ppermute x18, starting transfers between devices, exchanged_both(): return lax.ppermute(shard, ('rack', 'expert'), pairs)  23.7 us
    ppermute x16, waiting for transfers between devices, exchanged(): lax.ppermute(shard, axis, [(i, i ^ mask) for i in range(lax.axis_size(axi...  18.5 us
    pallas_call x22, Pallas kernels, kernel_call(): pl.pallas_call(body, out_shape=out_shape, in_specs=[WHOLE] * len(operands...  16.3 us
    all_to_all x1, blocking collectives, dense_steps(): lax.all_to_all(updates[0], ('rack', 'expert'), split_axis=0, concat_axis=...  11.7 us
    ppermute x16, starting transfers between devices, exchanged(): lax.ppermute(shard, axis, [(i, i ^ mask) for i in range(lax.axis_size(axi...  9.61 us
  transfers between devices with their start and end apart: 34, of which 26 were waited for; matrix products, arithmetic and copies ran while one was open for 0% of the time, Pallas kernels for 10%

profile of v7, /device:TPU:0, one launch (start us, length us, event | category | flops | bytes accessed | tf_op | source)
XLA Modules:
  0.0 104.3 jit_solution(2928082771378295358)
XLA Ops:
  0.0 0.9 shard_map.64
  0.9 3.0 %collective-permute-start = (bf16[16,128]{1,0:T(8,128)(2,1)S(1)}, bf16[16,128]{1,0:T(8,128)(2,1)S(1)}, u32[]{:S(2)}, u32[]{:S(2)}) collective-permute-start(bf16[16,128]{1,0:T(8,128)(2,1)S(1)} %get-tuple-element.42.refs_0_), channel_id=1, source_target_pairs={{0,8},{1,9},{2,10},{3,11},{4,12},{5,13},{6,14},{7,15},{8,0},{9,1},... | collective-permute-start | bytes 12296 | tf_op jit(solution)/shard_map/ppermute | solution.py:37
  3.9 0.7 collective-permute-start.2
  4.6 0.6 collective-permute-start.1
  5.1 2.3 %shard_map.65.refs_4_.refs_3_.upper_ref = bf16[1024,2048]{1,0:T(8,128)(2,1)S(1)} custom-call(bf16[1792,2,1024]{2,1,0:T(2,128)(2,1)} %bitcast.11), custom_call_target="tpu_custom_call" | custom-call | bytes 7340032 | tf_op jit(solution)/shard_map/pallas_call | solution.py:65
  7.8 3.8 %collective-permute-start.5 = (bf16[4,16,128]{2,1,0:T(8,128)(2,1)S(1)}, bf16[4,16,128]{2,1,0:T(8,128)(2,1)S(1)}, u32[]{:S(2)}, u32[]{:S(2)}) collective-permute-start(bf16[4,16,128]{2,1,0:T(8,128)(2,1)S(1)} %shard_map.66.refs_0_), channel_id=1, source_target_pairs={{0,18},{1,19},{2,16},{3,17},{4,22},{5,23},{6,20},{7,21},{8,26},{9,... | collective-permute-start | bytes 49160 | tf_op jit(solution)/shard_map/ppermute | solution.py:37
  12.0 2.0 %shard_map.67.refs_4_.lower_ref.refs_5_ = bf16[768,2048]{1,0:T(8,128)(2,1)S(1)} custom-call(bf16[4,16,128]{2,1,0:T(8,128)(2,1)S(1)} %shard_map.66.refs_0_, bf16[1792,2,1024]{2,1,0:T(2,128)(2,1)} %bitcast.12), custom_call_target="tpu_custom_call" | custom-call | bytes 7356416 | tf_op jit(solution)/shard_map/pallas_call | solution.py:65
  14.0 1.7 %collective-permute-done.4.refs_2_ = bf16[4,16,128]{2,1,0:T(8,128)(2,1)S(1)} collective-permute-done((bf16[4,16,128]{2,1,0:T(8,128)(2,1)S(1)}, bf16[4,16,128]{2,1,0:T(8,128)(2,1)S(1)}, u32[]{:S(2)}, u32[]{:S(2)}) %collective-permute-start.4) | collective-permute-done | bytes 16416 | tf_op jit(solution)/shard_map/ppermute | solution.py:37
  16.0 1.0 collective-permute-done.6.refs_1_
  17.0 0.9 shard_map.69
  17.9 1.6 %collective-permute-start.7 = (bf16[32,1152]{1,0:T(8,128)(2,1)S(1)}, bf16[32,1152]{1,0:T(8,128)(2,1)S(1)}, u32[]{:S(2)}, u32[]{:S(2)}) collective-permute-start(bf16[32,1152]{1,0:T(8,128)(2,1)S(1)} %get-tuple-element.46.tail_ref), channel_id=1, source_target_pairs={{0,1},{1,0},{2,3},{3,2},{4,5},{5,4},{6,7},{7,6},{8,9},{9,8},{10,11... | collective-permute-start | bytes 221192 | tf_op jit(solution)/shard_map/ppermute | solution.py:19
  19.5 0.7 shard_map.70
  20.3 0.5 collective-permute-start.8
  20.7 1.7 %collective-permute-done.7.other_tail_ref.swapped_ref = bf16[32,1152]{1,0:T(8,128)(2,1)S(1)} collective-permute-done((bf16[32,1152]{1,0:T(8,128)(2,1)S(1)}, bf16[32,1152]{1,0:T(8,128)(2,1)S(1)}, u32[]{:S(2)}, u32[]{:S(2)}) %collective-permute-start.7) | collective-permute-done | bytes 73760 | tf_op jit(solution)/shard_map/ppermute | solution.py:19
  22.4 0.5 shard_map.71.refs_0_
  22.9 1.6 %collective-permute-done.8.swapped_ref = bf16[32,1024]{1,0:T(8,128)(2,1)S(1)} collective-permute-done((bf16[32,1024]{1,0:T(8,128)(2,1)S(1)}, bf16[32,1024]{1,0:T(8,128)(2,1)S(1)}, u32[]{:S(2)}, u32[]{:S(2)}) %collective-permute-start.8) | collective-permute-done | bytes 65568 | tf_op jit(solution)/shard_map/ppermute | solution.py:19
  24.5 0.6 shard_map.72
  25.2 1.2 %collective-permute-done.9 = bf16[16,1792]{1,0:T(8,128)(2,1)S(1)} collective-permute-done((bf16[16,1792]{1,0:T(8,128)(2,1)S(1)}, bf16[16,1792]{1,0:T(8,128)(2,1)S(1)}, u32[]{:S(2)}, u32[]{:S(2)}) %collective-permute-start.9) | collective-permute-done | bytes 57376 | tf_op jit(solution)/shard_map/ppermute | solution.py:19
  26.4 1.5 %collective-permute-start.12 = (bf16[16,1792]{1,0:T(8,128)(2,1)S(1)}, bf16[16,1792]{1,0:T(8,128)(2,1)S(1)}, u32[]{:S(2)}, u32[]{:S(2)}) collective-permute-start(bf16[16,1792]{1,0:T(8,128)(2,1)S(1)} %fusion), channel_id=1, source_target_pairs={{0,24},{1,25},{2,26},{3,27},{4,28},{5,29},{6,30},{7,31},{8,16},{9,... | collective-permute-start | bytes 172040 | tf_op jit(solution)/shard_map/ppermute | solution.py:37
  27.9 1.0 collective-permute-start.11
  28.9 0.8 collective-permute-start.10
  29.7 2.0 %collective-permute-done.12 = bf16[16,1792]{1,0:T(8,128)(2,1)S(1)} collective-permute-done((bf16[16,1792]{1,0:T(8,128)(2,1)S(1)}, bf16[16,1792]{1,0:T(8,128)(2,1)S(1)}, u32[]{:S(2)}, u32[]{:S(2)}) %collective-permute-start.12) | collective-permute-done | bytes 57376 | tf_op jit(solution)/shard_map/ppermute | solution.py:37
  31.7 1.0 collective-permute-done.11
  32.7 1.8 %collective-permute-start.13 = (bf16[16,1792]{1,0:T(8,128)(2,1)S(1)}, bf16[16,1792]{1,0:T(8,128)(2,1)S(1)}, u32[]{:S(2)}, u32[]{:S(2)}) collective-permute-start(bf16[16,1792]{1,0:T(8,128)(2,1)S(1)} %fusion.3), channel_id=1, source_target_pairs={{0,6},{1,7},{2,4},{3,5},{4,2},{5,3},{6,0},{7,1},{8,14},{9,15},{10,... | collective-permute-start | bytes 172040 | tf_op jit(solution)/shard_map/ppermute | solution.py:37
  34.6 4.3 %collective-permute-done.13 = bf16[16,1792]{1,0:T(8,128)(2,1)S(1)} collective-permute-done((bf16[16,1792]{1,0:T(8,128)(2,1)S(1)}, bf16[16,1792]{1,0:T(8,128)(2,1)S(1)}, u32[]{:S(2)}, u32[]{:S(2)}) %collective-permute-start.13) | collective-permute-done | bytes 57376 | tf_op jit(solution)/shard_map/ppermute | solution.py:37
  39.1 1.1 %collective-permute-done.14.refs_2_ = bf16[16,1792]{1,0:T(8,128)(2,1)S(1)} collective-permute-done((bf16[16,1792]{1,0:T(8,128)(2,1)S(1)}, bf16[16,1792]{1,0:T(8,128)(2,1)S(1)}, u32[]{:S(2)}, u32[]{:S(2)}) %collective-permute-start.14) | collective-permute-done | bytes 57376 | tf_op jit(solution)/shard_map/ppermute | solution.py:19
  40.2 0.7 shard_map.73
  41.0 0.7 shard_map.74
  41.7 2.0 %collective-permute-start.16 = (bf16[32,1024]{1,0:T(8,128)(2,1)S(1)}, bf16[32,1024]{1,0:T(8,128)(2,1)S(1)}, u32[]{:S(2)}, u32[]{:S(2)}) collective-permute-start(bf16[32,1024]{1,0:T(8,128)(2,1)S(1)} %get-tuple-element.58), channel_id=1, source_target_pairs={{0,1},{1,0},{2,3},{3,2},{4,5},{5,4},{6,7},{7,6},{8,9},{9,8},{10,11... | collective-permute-start | bytes 196616 | tf_op jit(solution)/shard_map/ppermute | solution.py:19
  43.8 2.3 %collective-permute-done.15.other_tail_ref.swapped_ref = bf16[32,1152]{1,0:T(8,128)(2,1)S(1)} collective-permute-done((bf16[32,1152]{1,0:T(8,128)(2,1)S(1)}, bf16[32,1152]{1,0:T(8,128)(2,1)S(1)}, u32[]{:S(2)}, u32[]{:S(2)}) %collective-permute-start.15) | collective-permute-done | bytes 73760 | tf_op jit(solution)/shard_map/ppermute | solution.py:19
  46.0 0.5 shard_map.75.refs_0_
  46.8 0.6 shard_map.76
  47.4 1.2 %collective-permute-done.17 = bf16[16,1792]{1,0:T(8,128)(2,1)S(1)} collective-permute-done((bf16[16,1792]{1,0:T(8,128)(2,1)S(1)}, bf16[16,1792]{1,0:T(8,128)(2,1)S(1)}, u32[]{:S(2)}, u32[]{:S(2)}) %collective-permute-start.17) | collective-permute-done | bytes 57376 | tf_op jit(solution)/shard_map/ppermute | solution.py:19
  48.6 1.6 %collective-permute-start.20 = (bf16[16,1792]{1,0:T(8,128)(2,1)S(1)}, bf16[16,1792]{1,0:T(8,128)(2,1)S(1)}, u32[]{:S(2)}, u32[]{:S(2)}) collective-permute-start(bf16[16,1792]{1,0:T(8,128)(2,1)S(1)} %fusion.1), channel_id=1, source_target_pairs={{0,24},{1,25},{2,26},{3,27},{4,28},{5,29},{6,30},{7,31},{8,16},{9,... | collective-permute-start | bytes 172040 | tf_op jit(solution)/shard_map/ppermute | solution.py:37
  50.2 0.6 collective-permute-start.19
  50.8 1.1 %collective-permute-start.18 = (bf16[16,1792]{1,0:T(8,128)(2,1)S(1)}, bf16[16,1792]{1,0:T(8,128)(2,1)S(1)}, u32[]{:S(2)}, u32[]{:S(2)}) collective-permute-start(bf16[16,1792]{1,0:T(8,128)(2,1)S(1)} %fusion.1), channel_id=1, source_target_pairs={{0,12},{1,13},{2,14},{3,15},{4,8},{5,9},{6,10},{7,11},{8,4},{9,5},... | collective-permute-start | bytes 172040 | tf_op jit(solution)/shard_map/ppermute | solution.py:37
  51.9 1.9 %collective-permute-done.20 = bf16[16,1792]{1,0:T(8,128)(2,1)S(1)} collective-permute-done((bf16[16,1792]{1,0:T(8,128)(2,1)S(1)}, bf16[16,1792]{1,0:T(8,128)(2,1)S(1)}, u32[]{:S(2)}, u32[]{:S(2)}) %collective-permute-start.20) | collective-permute-done | bytes 57376 | tf_op jit(solution)/shard_map/ppermute | solution.py:37
  53.8 1.2 %collective-permute-done.19 = bf16[16,1792]{1,0:T(8,128)(2,1)S(1)} collective-permute-done((bf16[16,1792]{1,0:T(8,128)(2,1)S(1)}, bf16[16,1792]{1,0:T(8,128)(2,1)S(1)}, u32[]{:S(2)}, u32[]{:S(2)}) %collective-permute-start.19) | collective-permute-done | bytes 57376 | tf_op jit(solution)/shard_map/ppermute | solution.py:37
  55.1 1.8 %collective-permute-start.21 = (bf16[16,1792]{1,0:T(8,128)(2,1)S(1)}, bf16[16,1792]{1,0:T(8,128)(2,1)S(1)}, u32[]{:S(2)}, u32[]{:S(2)}) collective-permute-start(bf16[16,1792]{1,0:T(8,128)(2,1)S(1)} %fusion.4), channel_id=1, source_target_pairs={{0,6},{1,7},{2,4},{3,5},{4,2},{5,3},{6,0},{7,1},{8,14},{9,15},{10,... | collective-permute-start | bytes 172040 | tf_op jit(solution)/shard_map/ppermute | solution.py:37
  56.9 4.3 %collective-permute-done.21 = bf16[16,1792]{1,0:T(8,128)(2,1)S(1)} collective-permute-done((bf16[16,1792]{1,0:T(8,128)(2,1)S(1)}, bf16[16,1792]{1,0:T(8,128)(2,1)S(1)}, u32[]{:S(2)}, u32[]{:S(2)}) %collective-permute-start.21) | collective-permute-done | bytes 57376 | tf_op jit(solution)/shard_map/ppermute | solution.py:37
  61.4 1.1 %collective-permute-done.22.refs_2_ = bf16[16,1792]{1,0:T(8,128)(2,1)S(1)} collective-permute-done((bf16[16,1792]{1,0:T(8,128)(2,1)S(1)}, bf16[16,1792]{1,0:T(8,128)(2,1)S(1)}, u32[]{:S(2)}, u32[]{:S(2)}) %collective-permute-start.22) | collective-permute-done | bytes 57376 | tf_op jit(solution)/shard_map/ppermute | solution.py:19
  62.5 0.7 shard_map.77
  63.5 0.7 shard_map.78
  64.2 1.9 %collective-permute-start.24 = (bf16[32,1024]{1,0:T(8,128)(2,1)S(1)}, bf16[32,1024]{1,0:T(8,128)(2,1)S(1)}, u32[]{:S(2)}, u32[]{:S(2)}) collective-permute-start(bf16[32,1024]{1,0:T(8,128)(2,1)S(1)} %get-tuple-element.66), channel_id=1, source_target_pairs={{0,1},{1,0},{2,3},{3,2},{4,5},{5,4},{6,7},{7,6},{8,9},{9,8},{10,11... | collective-permute-start | bytes 196616 | tf_op jit(solution)/shard_map/ppermute | solution.py:19
  66.1 2.3 %collective-permute-done.23.other_tail_ref.swapped_ref = bf16[32,1152]{1,0:T(8,128)(2,1)S(1)} collective-permute-done((bf16[32,1152]{1,0:T(8,128)(2,1)S(1)}, bf16[32,1152]{1,0:T(8,128)(2,1)S(1)}, u32[]{:S(2)}, u32[]{:S(2)}) %collective-permute-start.23) | collective-permute-done | bytes 73760 | tf_op jit(solution)/shard_map/ppermute | solution.py:19
  68.4 0.5 shard_map.79.refs_0_
  69.1 0.6 shard_map.80
  69.7 1.2 %collective-permute-done.25 = bf16[16,1792]{1,0:T(8,128)(2,1)S(1)} collective-permute-done((bf16[16,1792]{1,0:T(8,128)(2,1)S(1)}, bf16[16,1792]{1,0:T(8,128)(2,1)S(1)}, u32[]{:S(2)}, u32[]{:S(2)}) %collective-permute-start.25) | collective-permute-done | bytes 57376 | tf_op jit(solution)/shard_map/ppermute | solution.py:19
  70.9 1.5 %collective-permute-start.28 = (bf16[16,1792]{1,0:T(8,128)(2,1)S(1)}, bf16[16,1792]{1,0:T(8,128)(2,1)S(1)}, u32[]{:S(2)}, u32[]{:S(2)}) collective-permute-start(bf16[16,1792]{1,0:T(8,128)(2,1)S(1)} %fusion.2), channel_id=1, source_target_pairs={{0,24},{1,25},{2,26},{3,27},{4,28},{5,29},{6,30},{7,31},{8,16},{9,... | collective-permute-start | bytes 172040 | tf_op jit(solution)/shard_map/ppermute | solution.py:37
  72.4 0.5 collective-permute-start.27
  72.9 1.3 %collective-permute-start.26 = (bf16[16,1792]{1,0:T(8,128)(2,1)S(1)}, bf16[16,1792]{1,0:T(8,128)(2,1)S(1)}, u32[]{:S(2)}, u32[]{:S(2)}) collective-permute-start(bf16[16,1792]{1,0:T(8,128)(2,1)S(1)} %fusion.2), channel_id=1, source_target_pairs={{0,12},{1,13},{2,14},{3,15},{4,8},{5,9},{6,10},{7,11},{8,4},{9,5},... | collective-permute-start | bytes 172040 | tf_op jit(solution)/shard_map/ppermute | solution.py:37
  74.2 2.0 %collective-permute-done.28 = bf16[16,1792]{1,0:T(8,128)(2,1)S(1)} collective-permute-done((bf16[16,1792]{1,0:T(8,128)(2,1)S(1)}, bf16[16,1792]{1,0:T(8,128)(2,1)S(1)}, u32[]{:S(2)}, u32[]{:S(2)}) %collective-permute-start.28) | collective-permute-done | bytes 57376 | tf_op jit(solution)/shard_map/ppermute | solution.py:37
  76.2 1.0 collective-permute-done.27
  77.2 1.8 %collective-permute-start.29 = (bf16[16,1792]{1,0:T(8,128)(2,1)S(1)}, bf16[16,1792]{1,0:T(8,128)(2,1)S(1)}, u32[]{:S(2)}, u32[]{:S(2)}) collective-permute-start(bf16[16,1792]{1,0:T(8,128)(2,1)S(1)} %fusion.5), channel_id=1, source_target_pairs={{0,6},{1,7},{2,4},{3,5},{4,2},{5,3},{6,0},{7,1},{8,14},{9,15},{10,... | collective-permute-start | bytes 172040 | tf_op jit(solution)/shard_map/ppermute | solution.py:37
  79.0 4.3 %collective-permute-done.29 = bf16[16,1792]{1,0:T(8,128)(2,1)S(1)} collective-permute-done((bf16[16,1792]{1,0:T(8,128)(2,1)S(1)}, bf16[16,1792]{1,0:T(8,128)(2,1)S(1)}, u32[]{:S(2)}, u32[]{:S(2)}) %collective-permute-start.29) | collective-permute-done | bytes 57376 | tf_op jit(solution)/shard_map/ppermute | solution.py:37
  83.6 1.1 %collective-permute-done.30.refs_2_ = bf16[16,1792]{1,0:T(8,128)(2,1)S(1)} collective-permute-done((bf16[16,1792]{1,0:T(8,128)(2,1)S(1)}, bf16[16,1792]{1,0:T(8,128)(2,1)S(1)}, u32[]{:S(2)}, u32[]{:S(2)}) %collective-permute-start.30) | collective-permute-done | bytes 57376 | tf_op jit(solution)/shard_map/ppermute | solution.py:19
  84.7 0.7 shard_map.81
  85.7 0.7 shard_map.82
  86.4 1.9 %collective-permute-start.32 = (bf16[32,1024]{1,0:T(8,128)(2,1)S(1)}, bf16[32,1024]{1,0:T(8,128)(2,1)S(1)}, u32[]{:S(2)}, u32[]{:S(2)}) collective-permute-start(bf16[32,1024]{1,0:T(8,128)(2,1)S(1)} %get-tuple-element.73), channel_id=1, source_target_pairs={{0,1},{1,0},{2,3},{3,2},{4,5},{5,4},{6,7},{7,6},{8,9},{9,8},{10,11... | collective-permute-start | bytes 196616 | tf_op jit(solution)/shard_map/ppermute | solution.py:19
  88.4 2.1 %collective-permute-done.31.other_tail_ref.swapped_ref = bf16[32,1152]{1,0:T(8,128)(2,1)S(1)} collective-permute-done((bf16[32,1152]{1,0:T(8,128)(2,1)S(1)}, bf16[32,1152]{1,0:T(8,128)(2,1)S(1)}, u32[]{:S(2)}, u32[]{:S(2)}) %collective-permute-start.31) | collective-permute-done | bytes 73760 | tf_op jit(solution)/shard_map/ppermute | solution.py:19
  90.6 0.5 shard_map.83.refs_0_
  91.3 0.6 shard_map.84
  91.9 11.7 %all_to_all.5.arrived_ref = bf16[32,14,128]{2,1,0:T(8,128)(2,1)S(1)} all-to-all(bf16[32,14,128]{2,1,0:T(8,128)(2,1)S(1)} %shard_map.84), channel_id=1, replica_groups=mesh['rack'=8,'expert'=4] {'rack','expert'}, dimensions={0} | all-to-all | bytes 229376 | tf_op jit(solution)/shard_map/all_to_all | solution.py:404
  103.6 0.7 shard_map.85
  (38 shorter events, 3.3 us)
Async XLA Ops:
  0.9 6.6 %collective-permute-start = (bf16[16,128]{1,0:T(8,128)(2,1)S(1)}, bf16[16,128]{1,0:T(8,128)(2,1)S(1)}, u32[]{:S(2)}, u32[]{:S(2)}) collective-permute-start(bf16[16,128]{1,0:T(8,128)(2,1)S(1)} %get-tuple-element.42.refs_0_), channel_id=1, source_target_pairs={{0,8},{1,9},{2,10},{3,11},{4,12},{5,13},{6,14},{7,15},{8,0},{9,1},... | collective-permute-start | bytes 12296 | tf_op jit(solution)/shard_map/ppermute | solution.py:37
  3.9 3.9 %collective-permute-start.2 = (bf16[16,128]{1,0:T(8,128)(2,1)S(1)}, bf16[16,128]{1,0:T(8,128)(2,1)S(1)}, u32[]{:S(2)}, u32[]{:S(2)}) collective-permute-start(bf16[16,128]{1,0:T(8,128)(2,1)S(1)} %get-tuple-element.43), channel_id=1, source_target_pairs={{0,13},{1,12},{2,15},{3,14},{4,9},{5,8},{6,11},{7,10},{8,5},{9,4},... | collective-permute-start | bytes 12296 | tf_op jit(solution)/shard_map/ppermute | solution.py:37
  4.6 3.2 %collective-permute-start.1 = (bf16[16,128]{1,0:T(8,128)(2,1)S(1)}, bf16[16,128]{1,0:T(8,128)(2,1)S(1)}, u32[]{:S(2)}, u32[]{:S(2)}) collective-permute-start(bf16[16,128]{1,0:T(8,128)(2,1)S(1)} %get-tuple-element.43), channel_id=1, source_target_pairs={{0,5},{1,4},{2,7},{3,6},{4,1},{5,0},{6,3},{7,2},{8,13},{9,12},{10,... | collective-permute-start | bytes 12296 | tf_op jit(solution)/shard_map/ppermute | solution.py:37
  7.8 6.2 %collective-permute-start.5 = (bf16[4,16,128]{2,1,0:T(8,128)(2,1)S(1)}, bf16[4,16,128]{2,1,0:T(8,128)(2,1)S(1)}, u32[]{:S(2)}, u32[]{:S(2)}) collective-permute-start(bf16[4,16,128]{2,1,0:T(8,128)(2,1)S(1)} %shard_map.66.refs_0_), channel_id=1, source_target_pairs={{0,18},{1,19},{2,16},{3,17},{4,22},{5,23},{6,20},{7,21},{8,26},{9,... | collective-permute-start | bytes 49160 | tf_op jit(solution)/shard_map/ppermute | solution.py:37
  11.6 4.1 %collective-permute-start.4 = (bf16[4,16,128]{2,1,0:T(8,128)(2,1)S(1)}, bf16[4,16,128]{2,1,0:T(8,128)(2,1)S(1)}, u32[]{:S(2)}, u32[]{:S(2)}) collective-permute-start(bf16[4,16,128]{2,1,0:T(8,128)(2,1)S(1)} %shard_map.66.refs_0_), channel_id=1, source_target_pairs={{0,6},{1,7},{2,4},{3,5},{4,2},{5,3},{6,0},{7,1},{8,14},{9,15},{10,... | collective-permute-start | bytes 49160 | tf_op jit(solution)/shard_map/ppermute | solution.py:37
  11.8 3.9 %collective-permute-start.3 = (bf16[4,16,128]{2,1,0:T(8,128)(2,1)S(1)}, bf16[4,16,128]{2,1,0:T(8,128)(2,1)S(1)}, u32[]{:S(2)}, u32[]{:S(2)}) collective-permute-start(bf16[4,16,128]{2,1,0:T(8,128)(2,1)S(1)} %shard_map.66.refs_0_), channel_id=1, source_target_pairs={{0,20},{1,21},{2,22},{3,23},{4,16},{5,17},{6,18},{7,19},{8,28},{9,... | collective-permute-start | bytes 49160 | tf_op jit(solution)/shard_map/ppermute | solution.py:37
  15.7 1.3 %collective-permute-start.6 = (bf16[16,16,128]{2,1,0:T(8,128)(2,1)S(1)}, bf16[16,16,128]{2,1,0:T(8,128)(2,1)S(1)}, u32[]{:S(2)}, u32[]{:S(2)}) collective-permute-start(bf16[16,16,128]{2,1,0:T(8,128)(2,1)S(1)} %shard_map.68.refs_0_), channel_id=1, source_target_pairs={{0,4},{4,0},{8,12},{12,8},{16,20},{20,16},{24,28},{28,24},{1,5},{5... | collective-permute-start | bytes 196616 | tf_op jit(solution)/shard_map/ppermute | solution.py:19
  17.9 4.5 %copy-start = (bf16[1,1,1024,1792]{3,2,1,0:T(8,128)(2,1)S(1)}, bf16[1,1,1024,1792]{3,2,1,0:T(8,128)(2,1)}, u32[]{:S(2)}) copy-start(bf16[1,1,1024,1792]{3,2,1,0:T(8,128)(2,1)} %param.11) | copy-start | bytes 11010052
  17.9 4.5 %collective-permute-start.7 = (bf16[32,1152]{1,0:T(8,128)(2,1)S(1)}, bf16[32,1152]{1,0:T(8,128)(2,1)S(1)}, u32[]{:S(2)}, u32[]{:S(2)}) collective-permute-start(bf16[32,1152]{1,0:T(8,128)(2,1)S(1)} %get-tuple-element.46.tail_ref), channel_id=1, source_target_pairs={{0,1},{1,0},{2,3},{3,2},{4,5},{5,4},{6,7},{7,6},{8,9},{9,8},{10,11... | collective-permute-start | bytes 221192 | tf_op jit(solution)/shard_map/ppermute | solution.py:19
  20.3 4.3 %collective-permute-start.8 = (bf16[32,1024]{1,0:T(8,128)(2,1)S(1)}, bf16[32,1024]{1,0:T(8,128)(2,1)S(1)}, u32[]{:S(2)}, u32[]{:S(2)}) collective-permute-start(bf16[32,1024]{1,0:T(8,128)(2,1)S(1)} %get-tuple-element.49), channel_id=1, source_target_pairs={{0,1},{1,0},{2,3},{3,2},{4,5},{5,4},{6,7},{7,6},{8,9},{9,8},{10,11... | collective-permute-start | bytes 196616 | tf_op jit(solution)/shard_map/ppermute | solution.py:19
  25.1 1.3 %collective-permute-start.9 = (bf16[16,1792]{1,0:T(8,128)(2,1)S(1)}, bf16[16,1792]{1,0:T(8,128)(2,1)S(1)}, u32[]{:S(2)}, u32[]{:S(2)}) collective-permute-start(bf16[16,1792]{1,0:T(8,128)(2,1)S(1)} %get-tuple-element.53), channel_id=1, source_target_pairs={{0,4},{4,0},{8,12},{12,8},{16,20},{20,16},{24,28},{28,24},{1,5},{5... | collective-permute-start | bytes 172040 | tf_op jit(solution)/shard_map/ppermute | solution.py:19
  26.4 5.2 %collective-permute-start.12 = (bf16[16,1792]{1,0:T(8,128)(2,1)S(1)}, bf16[16,1792]{1,0:T(8,128)(2,1)S(1)}, u32[]{:S(2)}, u32[]{:S(2)}) collective-permute-start(bf16[16,1792]{1,0:T(8,128)(2,1)S(1)} %fusion), channel_id=1, source_target_pairs={{0,24},{1,25},{2,26},{3,27},{4,28},{5,29},{6,30},{7,31},{8,16},{9,... | collective-permute-start | bytes 172040 | tf_op jit(solution)/shard_map/ppermute | solution.py:37
  27.9 4.8 %collective-permute-start.11 = (bf16[16,1792]{1,0:T(8,128)(2,1)S(1)}, bf16[16,1792]{1,0:T(8,128)(2,1)S(1)}, u32[]{:S(2)}, u32[]{:S(2)}) collective-permute-start(bf16[16,1792]{1,0:T(8,128)(2,1)S(1)} %fusion), channel_id=1, source_target_pairs={{0,20},{1,21},{2,22},{3,23},{4,16},{5,17},{6,18},{7,19},{8,28},{9,... | collective-permute-start | bytes 172040 | tf_op jit(solution)/shard_map/ppermute | solution.py:37
  28.9 3.8 %collective-permute-start.10 = (bf16[16,1792]{1,0:T(8,128)(2,1)S(1)}, bf16[16,1792]{1,0:T(8,128)(2,1)S(1)}, u32[]{:S(2)}, u32[]{:S(2)}) collective-permute-start(bf16[16,1792]{1,0:T(8,128)(2,1)S(1)} %fusion), channel_id=1, source_target_pairs={{0,12},{1,13},{2,14},{3,15},{4,8},{5,9},{6,10},{7,11},{8,4},{9,5},... | collective-permute-start | bytes 172040 | tf_op jit(solution)/shard_map/ppermute | solution.py:37
  32.7 6.1 %collective-permute-start.13 = (bf16[16,1792]{1,0:T(8,128)(2,1)S(1)}, bf16[16,1792]{1,0:T(8,128)(2,1)S(1)}, u32[]{:S(2)}, u32[]{:S(2)}) collective-permute-start(bf16[16,1792]{1,0:T(8,128)(2,1)S(1)} %fusion.3), channel_id=1, source_target_pairs={{0,6},{1,7},{2,4},{3,5},{4,2},{5,3},{6,0},{7,1},{8,14},{9,15},{10,... | collective-permute-start | bytes 172040 | tf_op jit(solution)/shard_map/ppermute | solution.py:37
  38.9 1.3 %collective-permute-start.14 = (bf16[16,1792]{1,0:T(8,128)(2,1)S(1)}, bf16[16,1792]{1,0:T(8,128)(2,1)S(1)}, u32[]{:S(2)}, u32[]{:S(2)}) collective-permute-start(bf16[16,1792]{1,0:T(8,128)(2,1)S(1)} %get-tuple-element.83), channel_id=1, source_target_pairs={{0,4},{4,0},{8,12},{12,8},{16,20},{20,16},{24,28},{28,24},{1,5},{5... | collective-permute-start | bytes 172040 | tf_op jit(solution)/shard_map/ppermute | solution.py:19
  41.0 5.1 %collective-permute-start.15 = (bf16[32,1152]{1,0:T(8,128)(2,1)S(1)}, bf16[32,1152]{1,0:T(8,128)(2,1)S(1)}, u32[]{:S(2)}, u32[]{:S(2)}) collective-permute-start(bf16[32,1152]{1,0:T(8,128)(2,1)S(1)} %get-tuple-element.55.tail_ref), channel_id=1, source_target_pairs={{0,1},{1,0},{2,3},{3,2},{4,5},{5,4},{6,7},{7,6},{8,9},{9,8},{10,11... | collective-permute-start | bytes 221192 | tf_op jit(solution)/shard_map/ppermute | solution.py:19
  41.7 5.0 %collective-permute-start.16 = (bf16[32,1024]{1,0:T(8,128)(2,1)S(1)}, bf16[32,1024]{1,0:T(8,128)(2,1)S(1)}, u32[]{:S(2)}, u32[]{:S(2)}) collective-permute-start(bf16[32,1024]{1,0:T(8,128)(2,1)S(1)} %get-tuple-element.58), channel_id=1, source_target_pairs={{0,1},{1,0},{2,3},{3,2},{4,5},{5,4},{6,7},{7,6},{8,9},{9,8},{10,11... | collective-permute-start | bytes 196616 | tf_op jit(solution)/shard_map/ppermute | solution.py:19
  47.3 1.3 %collective-permute-start.17 = (bf16[16,1792]{1,0:T(8,128)(2,1)S(1)}, bf16[16,1792]{1,0:T(8,128)(2,1)S(1)}, u32[]{:S(2)}, u32[]{:S(2)}) collective-permute-start(bf16[16,1792]{1,0:T(8,128)(2,1)S(1)} %get-tuple-element.61), channel_id=1, source_target_pairs={{0,4},{4,0},{8,12},{12,8},{16,20},{20,16},{24,28},{28,24},{1,5},{5... | collective-permute-start | bytes 172040 | tf_op jit(solution)/shard_map/ppermute | solution.py:19
  48.6 5.2 %collective-permute-start.20 = (bf16[16,1792]{1,0:T(8,128)(2,1)S(1)}, bf16[16,1792]{1,0:T(8,128)(2,1)S(1)}, u32[]{:S(2)}, u32[]{:S(2)}) collective-permute-start(bf16[16,1792]{1,0:T(8,128)(2,1)S(1)} %fusion.1), channel_id=1, source_target_pairs={{0,24},{1,25},{2,26},{3,27},{4,28},{5,29},{6,30},{7,31},{8,16},{9,... | collective-permute-start | bytes 172040 | tf_op jit(solution)/shard_map/ppermute | solution.py:37
  50.2 4.8 %collective-permute-start.19 = (bf16[16,1792]{1,0:T(8,128)(2,1)S(1)}, bf16[16,1792]{1,0:T(8,128)(2,1)S(1)}, u32[]{:S(2)}, u32[]{:S(2)}) collective-permute-start(bf16[16,1792]{1,0:T(8,128)(2,1)S(1)} %fusion.1), channel_id=1, source_target_pairs={{0,20},{1,21},{2,22},{3,23},{4,16},{5,17},{6,18},{7,19},{8,28},{9,... | collective-permute-start | bytes 172040 | tf_op jit(solution)/shard_map/ppermute | solution.py:37
  50.8 4.2 %collective-permute-start.18 = (bf16[16,1792]{1,0:T(8,128)(2,1)S(1)}, bf16[16,1792]{1,0:T(8,128)(2,1)S(1)}, u32[]{:S(2)}, u32[]{:S(2)}) collective-permute-start(bf16[16,1792]{1,0:T(8,128)(2,1)S(1)} %fusion.1), channel_id=1, source_target_pairs={{0,12},{1,13},{2,14},{3,15},{4,8},{5,9},{6,10},{7,11},{8,4},{9,5},... | collective-permute-start | bytes 172040 | tf_op jit(solution)/shard_map/ppermute | solution.py:37
  55.1 6.1 %collective-permute-start.21 = (bf16[16,1792]{1,0:T(8,128)(2,1)S(1)}, bf16[16,1792]{1,0:T(8,128)(2,1)S(1)}, u32[]{:S(2)}, u32[]{:S(2)}) collective-permute-start(bf16[16,1792]{1,0:T(8,128)(2,1)S(1)} %fusion.4), channel_id=1, source_target_pairs={{0,6},{1,7},{2,4},{3,5},{4,2},{5,3},{6,0},{7,1},{8,14},{9,15},{10,... | collective-permute-start | bytes 172040 | tf_op jit(solution)/shard_map/ppermute | solution.py:37
  61.2 1.3 %collective-permute-start.22 = (bf16[16,1792]{1,0:T(8,128)(2,1)S(1)}, bf16[16,1792]{1,0:T(8,128)(2,1)S(1)}, u32[]{:S(2)}, u32[]{:S(2)}) collective-permute-start(bf16[16,1792]{1,0:T(8,128)(2,1)S(1)} %get-tuple-element.81), channel_id=1, source_target_pairs={{0,4},{4,0},{8,12},{12,8},{16,20},{20,16},{24,28},{28,24},{1,5},{5... | collective-permute-start | bytes 172040 | tf_op jit(solution)/shard_map/ppermute | solution.py:19
  63.3 5.1 %collective-permute-start.23 = (bf16[32,1152]{1,0:T(8,128)(2,1)S(1)}, bf16[32,1152]{1,0:T(8,128)(2,1)S(1)}, u32[]{:S(2)}, u32[]{:S(2)}) collective-permute-start(bf16[32,1152]{1,0:T(8,128)(2,1)S(1)} %get-tuple-element.63.tail_ref), channel_id=1, source_target_pairs={{0,1},{1,0},{2,3},{3,2},{4,5},{5,4},{6,7},{7,6},{8,9},{9,8},{10,11... | collective-permute-start | bytes 221192 | tf_op jit(solution)/shard_map/ppermute | solution.py:19
  64.2 4.8 %collective-permute-start.24 = (bf16[32,1024]{1,0:T(8,128)(2,1)S(1)}, bf16[32,1024]{1,0:T(8,128)(2,1)S(1)}, u32[]{:S(2)}, u32[]{:S(2)}) collective-permute-start(bf16[32,1024]{1,0:T(8,128)(2,1)S(1)} %get-tuple-element.66), channel_id=1, source_target_pairs={{0,1},{1,0},{2,3},{3,2},{4,5},{5,4},{6,7},{7,6},{8,9},{9,8},{10,11... | collective-permute-start | bytes 196616 | tf_op jit(solution)/shard_map/ppermute | solution.py:19
  69.6 1.3 %collective-permute-start.25 = (bf16[16,1792]{1,0:T(8,128)(2,1)S(1)}, bf16[16,1792]{1,0:T(8,128)(2,1)S(1)}, u32[]{:S(2)}, u32[]{:S(2)}) collective-permute-start(bf16[16,1792]{1,0:T(8,128)(2,1)S(1)} %get-tuple-element.69), channel_id=1, source_target_pairs={{0,4},{4,0},{8,12},{12,8},{16,20},{20,16},{24,28},{28,24},{1,5},{5... | collective-permute-start | bytes 172040 | tf_op jit(solution)/shard_map/ppermute | solution.py:19
  70.9 5.2 %collective-permute-start.28 = (bf16[16,1792]{1,0:T(8,128)(2,1)S(1)}, bf16[16,1792]{1,0:T(8,128)(2,1)S(1)}, u32[]{:S(2)}, u32[]{:S(2)}) collective-permute-start(bf16[16,1792]{1,0:T(8,128)(2,1)S(1)} %fusion.2), channel_id=1, source_target_pairs={{0,24},{1,25},{2,26},{3,27},{4,28},{5,29},{6,30},{7,31},{8,16},{9,... | collective-permute-start | bytes 172040 | tf_op jit(solution)/shard_map/ppermute | solution.py:37
  72.4 4.8 %collective-permute-start.27 = (bf16[16,1792]{1,0:T(8,128)(2,1)S(1)}, bf16[16,1792]{1,0:T(8,128)(2,1)S(1)}, u32[]{:S(2)}, u32[]{:S(2)}) collective-permute-start(bf16[16,1792]{1,0:T(8,128)(2,1)S(1)} %fusion.2), channel_id=1, source_target_pairs={{0,20},{1,21},{2,22},{3,23},{4,16},{5,17},{6,18},{7,19},{8,28},{9,... | collective-permute-start | bytes 172040 | tf_op jit(solution)/shard_map/ppermute | solution.py:37
  72.9 4.3 %collective-permute-start.26 = (bf16[16,1792]{1,0:T(8,128)(2,1)S(1)}, bf16[16,1792]{1,0:T(8,128)(2,1)S(1)}, u32[]{:S(2)}, u32[]{:S(2)}) collective-permute-start(bf16[16,1792]{1,0:T(8,128)(2,1)S(1)} %fusion.2), channel_id=1, source_target_pairs={{0,12},{1,13},{2,14},{3,15},{4,8},{5,9},{6,10},{7,11},{8,4},{9,5},... | collective-permute-start | bytes 172040 | tf_op jit(solution)/shard_map/ppermute | solution.py:37
  77.2 6.1 %collective-permute-start.29 = (bf16[16,1792]{1,0:T(8,128)(2,1)S(1)}, bf16[16,1792]{1,0:T(8,128)(2,1)S(1)}, u32[]{:S(2)}, u32[]{:S(2)}) collective-permute-start(bf16[16,1792]{1,0:T(8,128)(2,1)S(1)} %fusion.5), channel_id=1, source_target_pairs={{0,6},{1,7},{2,4},{3,5},{4,2},{5,3},{6,0},{7,1},{8,14},{9,15},{10,... | collective-permute-start | bytes 172040 | tf_op jit(solution)/shard_map/ppermute | solution.py:37
  83.4 1.3 %collective-permute-start.30 = (bf16[16,1792]{1,0:T(8,128)(2,1)S(1)}, bf16[16,1792]{1,0:T(8,128)(2,1)S(1)}, u32[]{:S(2)}, u32[]{:S(2)}) collective-permute-start(bf16[16,1792]{1,0:T(8,128)(2,1)S(1)} %get-tuple-element.79), channel_id=1, source_target_pairs={{0,4},{4,0},{8,12},{12,8},{16,20},{20,16},{24,28},{28,24},{1,5},{5... | collective-permute-start | bytes 172040 | tf_op jit(solution)/shard_map/ppermute | solution.py:19
  85.5 5.1 %collective-permute-start.31 = (bf16[32,1152]{1,0:T(8,128)(2,1)S(1)}, bf16[32,1152]{1,0:T(8,128)(2,1)S(1)}, u32[]{:S(2)}, u32[]{:S(2)}) collective-permute-start(bf16[32,1152]{1,0:T(8,128)(2,1)S(1)} %get-tuple-element.70.tail_ref), channel_id=1, source_target_pairs={{0,1},{1,0},{2,3},{3,2},{4,5},{5,4},{6,7},{7,6},{8,9},{9,8},{10,11... | collective-permute-start | bytes 221192 | tf_op jit(solution)/shard_map/ppermute | solution.py:19
  86.4 4.9 %collective-permute-start.32 = (bf16[32,1024]{1,0:T(8,128)(2,1)S(1)}, bf16[32,1024]{1,0:T(8,128)(2,1)S(1)}, u32[]{:S(2)}, u32[]{:S(2)}) collective-permute-start(bf16[32,1024]{1,0:T(8,128)(2,1)S(1)} %get-tuple-element.73), channel_id=1, source_target_pairs={{0,1},{1,0},{2,3},{3,2},{4,5},{5,4},{6,7},{7,6},{8,9},{9,8},{10,11... | collective-permute-start | bytes 196616 | tf_op jit(solution)/shard_map/ppermute | solution.py:19
  88.3 3.6 %collective-permute-start.33 = (f32[1,1792]{1,0:T(1,128)S(1)}, f32[1,1792]{1,0:T(1,128)S(1)}, u32[]{:S(2)}, u32[]{:S(2)}) collective-permute-start(f32[1,1792]{1,0:T(1,128)S(1)} %get-tuple-element.75), channel_id=1, source_target_pairs={{0,1},{1,0},{2,3},{3,2},{4,5},{5,4},{6,7},{7,6},{8,9},{9,8},{10,11... | collective-permute-start | bytes 21512 | tf_op jit(solution)/shard_map/ppermute | solution.py:19

commit v8 on v7

--- a/solution.py
+++ b/solution.py
@@ -43,7 +43,7 @@
 
 
 def gather_masks(rack_count, group_count):
-    near = [(0, 0), (2, 0), (1, 1), (3, 1)]
+    near = [(0, 0), (3, 0), (1, 1), (2, 1)]
     far = [crossed(rack, group) for group in range(0, group_count, 2) for rack in range(0, rack_count, 4)]
     return near, far
 

time: 105 us -> 104 us (level)
  transfers between devices with their start and end apart: 34 -> 34, of which waited for: 26 -> 27; matrix products, arithmetic and copies ran while one was open for 0% -> 0% of each run, Pallas kernels for 10% -> 10%
where the time goes in v8:
time: 104 us
  waiting for transfers between devices  42.8 us (41%)
  starting transfers between devices  32.8 us (32%)
  Pallas kernels  16.3 us (16%)
  blocking collectives  11.5 us (11%)
    ppermute x18, waiting for transfers between devices, exchanged_both(): return lax.ppermute(shard, ('rack', 'expert'), pairs)  24.2 us
    ppermute x18, starting transfers between devices, exchanged_both(): return lax.ppermute(shard, ('rack', 'expert'), pairs)  23.3 us
    ppermute x16, waiting for transfers between devices, exchanged(): lax.ppermute(shard, axis, [(i, i ^ mask) for i in range(lax.axis_size(axi...  18.7 us
    pallas_call x22, Pallas kernels, kernel_call(): pl.pallas_call(body, out_shape=out_shape, in_specs=[WHOLE] * len(operands...  16.3 us
    all_to_all x1, blocking collectives, dense_steps(): lax.all_to_all(updates[0], ('rack', 'expert'), split_axis=0, concat_axis=...  11.5 us
    ppermute x16, starting transfers between devices, exchanged(): lax.ppermute(shard, axis, [(i, i ^ mask) for i in range(lax.axis_size(axi...  9.49 us
  transfers between devices with their start and end apart: 34, of which 27 were waited for; matrix products, arithmetic and copies ran while one was open for 0% of the time, Pallas kernels for 10%

profile of v8, /device:TPU:0, one launch (start us, length us, event | category | flops | bytes accessed | tf_op | source)
XLA Modules:
  0.0 104.0 jit_solution(2300746913012264077)
XLA Ops:
  0.0 0.9 shard_map.64
  0.9 2.4 %collective-permute-start = (bf16[16,128]{1,0:T(8,128)(2,1)S(1)}, bf16[16,128]{1,0:T(8,128)(2,1)S(1)}, u32[]{:S(2)}, u32[]{:S(2)}) collective-permute-start(bf16[16,128]{1,0:T(8,128)(2,1)S(1)} %get-tuple-element.42.refs_0_), channel_id=1, source_target_pairs={{0,12},{1,13},{2,14},{3,15},{4,8},{5,9},{6,10},{7,11},{8,4},{9,5},... | collective-permute-start | bytes 12296 | tf_op jit(solution)/shard_map/ppermute | solution.py:37
  3.3 1.7 %collective-permute-start.2 = (bf16[16,128]{1,0:T(8,128)(2,1)S(1)}, bf16[16,128]{1,0:T(8,128)(2,1)S(1)}, u32[]{:S(2)}, u32[]{:S(2)}) collective-permute-start(bf16[16,128]{1,0:T(8,128)(2,1)S(1)} %get-tuple-element.43), channel_id=1, source_target_pairs={{0,9},{1,8},{2,11},{3,10},{4,13},{5,12},{6,15},{7,14},{8,1},{9,0},... | collective-permute-start | bytes 12296 | tf_op jit(solution)/shard_map/ppermute | solution.py:37
  5.2 2.3 %shard_map.65.refs_4_.refs_3_.upper_ref = bf16[1024,2048]{1,0:T(8,128)(2,1)S(1)} custom-call(bf16[1792,2,1024]{2,1,0:T(2,128)(2,1)} %bitcast.11), custom_call_target="tpu_custom_call" | custom-call | bytes 7340032 | tf_op jit(solution)/shard_map/pallas_call | solution.py:65
  8.0 3.5 %collective-permute-start.5 = (bf16[4,16,128]{2,1,0:T(8,128)(2,1)S(1)}, bf16[4,16,128]{2,1,0:T(8,128)(2,1)S(1)}, u32[]{:S(2)}, u32[]{:S(2)}) collective-permute-start(bf16[4,16,128]{2,1,0:T(8,128)(2,1)S(1)} %shard_map.66.refs_0_), channel_id=1, source_target_pairs={{0,18},{1,19},{2,16},{3,17},{4,22},{5,23},{6,20},{7,21},{8,26},{9,... | collective-permute-start | bytes 49160 | tf_op jit(solution)/shard_map/ppermute | solution.py:37
  11.6 0.6 collective-permute-start.3
  12.1 2.0 %shard_map.67.refs_4_.lower_ref.refs_5_ = bf16[768,2048]{1,0:T(8,128)(2,1)S(1)} custom-call(bf16[4,16,128]{2,1,0:T(8,128)(2,1)S(1)} %shard_map.66.refs_0_, bf16[1792,2,1024]{2,1,0:T(2,128)(2,1)} %bitcast.12), custom_call_target="tpu_custom_call" | custom-call | bytes 7356416 | tf_op jit(solution)/shard_map/pallas_call | solution.py:65
  14.1 1.5 %collective-permute-done.4.refs_2_ = bf16[4,16,128]{2,1,0:T(8,128)(2,1)S(1)} collective-permute-done((bf16[4,16,128]{2,1,0:T(8,128)(2,1)S(1)}, bf16[4,16,128]{2,1,0:T(8,128)(2,1)S(1)}, u32[]{:S(2)}, u32[]{:S(2)}) %collective-permute-start.4) | collective-permute-done | bytes 16416 | tf_op jit(solution)/shard_map/ppermute | solution.py:37
  15.8 1.1 %collective-permute-done.6.refs_1_ = bf16[16,16,128]{2,1,0:T(8,128)(2,1)S(1)} collective-permute-done((bf16[16,16,128]{2,1,0:T(8,128)(2,1)S(1)}, bf16[16,16,128]{2,1,0:T(8,128)(2,1)S(1)}, u32[]{:S(2)}, u32[]{:S(2)}) %collective-permute-start.6) | collective-permute-done | bytes 65568 | tf_op jit(solution)/shard_map/ppermute | solution.py:19
  17.0 0.9 shard_map.69
  17.9 1.6 %collective-permute-start.7 = (bf16[32,1152]{1,0:T(8,128)(2,1)S(1)}, bf16[32,1152]{1,0:T(8,128)(2,1)S(1)}, u32[]{:S(2)}, u32[]{:S(2)}) collective-permute-start(bf16[32,1152]{1,0:T(8,128)(2,1)S(1)} %get-tuple-element.46.tail_ref), channel_id=1, source_target_pairs={{0,1},{1,0},{2,3},{3,2},{4,5},{5,4},{6,7},{7,6},{8,9},{9,8},{10,11... | collective-permute-start | bytes 221192 | tf_op jit(solution)/shard_map/ppermute | solution.py:19
  19.5 0.7 shard_map.70
  20.2 0.5 collective-permute-start.8
  20.7 1.6 %collective-permute-done.7.other_tail_ref.swapped_ref = bf16[32,1152]{1,0:T(8,128)(2,1)S(1)} collective-permute-done((bf16[32,1152]{1,0:T(8,128)(2,1)S(1)}, bf16[32,1152]{1,0:T(8,128)(2,1)S(1)}, u32[]{:S(2)}, u32[]{:S(2)}) %collective-permute-start.7) | collective-permute-done | bytes 73760 | tf_op jit(solution)/shard_map/ppermute | solution.py:19
  22.3 0.5 shard_map.71.refs_0_
  22.8 1.7 %collective-permute-done.8.swapped_ref = bf16[32,1024]{1,0:T(8,128)(2,1)S(1)} collective-permute-done((bf16[32,1024]{1,0:T(8,128)(2,1)S(1)}, bf16[32,1024]{1,0:T(8,128)(2,1)S(1)}, u32[]{:S(2)}, u32[]{:S(2)}) %collective-permute-start.8) | collective-permute-done | bytes 65568 | tf_op jit(solution)/shard_map/ppermute | solution.py:19
  24.5 0.6 shard_map.72
  25.1 1.2 %collective-permute-done.9 = bf16[16,1792]{1,0:T(8,128)(2,1)S(1)} collective-permute-done((bf16[16,1792]{1,0:T(8,128)(2,1)S(1)}, bf16[16,1792]{1,0:T(8,128)(2,1)S(1)}, u32[]{:S(2)}, u32[]{:S(2)}) %collective-permute-start.9) | collective-permute-done | bytes 57376 | tf_op jit(solution)/shard_map/ppermute | solution.py:19
  26.4 1.5 %collective-permute-start.12 = (bf16[16,1792]{1,0:T(8,128)(2,1)S(1)}, bf16[16,1792]{1,0:T(8,128)(2,1)S(1)}, u32[]{:S(2)}, u32[]{:S(2)}) collective-permute-start(bf16[16,1792]{1,0:T(8,128)(2,1)S(1)} %fusion), channel_id=1, source_target_pairs={{0,24},{1,25},{2,26},{3,27},{4,28},{5,29},{6,30},{7,31},{8,16},{9,... | collective-permute-start | bytes 172040 | tf_op jit(solution)/shard_map/ppermute | solution.py:37
  27.8 1.0 collective-permute-start.11
  28.8 0.8 collective-permute-start.10
  29.7 2.0 %collective-permute-done.12 = bf16[16,1792]{1,0:T(8,128)(2,1)S(1)} collective-permute-done((bf16[16,1792]{1,0:T(8,128)(2,1)S(1)}, bf16[16,1792]{1,0:T(8,128)(2,1)S(1)}, u32[]{:S(2)}, u32[]{:S(2)}) %collective-permute-start.12) | collective-permute-done | bytes 57376 | tf_op jit(solution)/shard_map/ppermute | solution.py:37
  31.6 1.0 collective-permute-done.11
  32.6 1.7 %collective-permute-start.13 = (bf16[16,1792]{1,0:T(8,128)(2,1)S(1)}, bf16[16,1792]{1,0:T(8,128)(2,1)S(1)}, u32[]{:S(2)}, u32[]{:S(2)}) collective-permute-start(bf16[16,1792]{1,0:T(8,128)(2,1)S(1)} %fusion.3), channel_id=1, source_target_pairs={{0,6},{1,7},{2,4},{3,5},{4,2},{5,3},{6,0},{7,1},{8,14},{9,15},{10,... | collective-permute-start | bytes 172040 | tf_op jit(solution)/shard_map/ppermute | solution.py:37
  34.4 4.4 %collective-permute-done.13 = bf16[16,1792]{1,0:T(8,128)(2,1)S(1)} collective-permute-done((bf16[16,1792]{1,0:T(8,128)(2,1)S(1)}, bf16[16,1792]{1,0:T(8,128)(2,1)S(1)}, u32[]{:S(2)}, u32[]{:S(2)}) %collective-permute-start.13) | collective-permute-done | bytes 57376 | tf_op jit(solution)/shard_map/ppermute | solution.py:37
  39.0 1.1 %collective-permute-done.14.refs_2_ = bf16[16,1792]{1,0:T(8,128)(2,1)S(1)} collective-permute-done((bf16[16,1792]{1,0:T(8,128)(2,1)S(1)}, bf16[16,1792]{1,0:T(8,128)(2,1)S(1)}, u32[]{:S(2)}, u32[]{:S(2)}) %collective-permute-start.14) | collective-permute-done | bytes 57376 | tf_op jit(solution)/shard_map/ppermute | solution.py:19
  40.1 0.7 shard_map.73
  40.9 0.7 shard_map.74
  41.6 2.0 %collective-permute-start.16 = (bf16[32,1024]{1,0:T(8,128)(2,1)S(1)}, bf16[32,1024]{1,0:T(8,128)(2,1)S(1)}, u32[]{:S(2)}, u32[]{:S(2)}) collective-permute-start(bf16[32,1024]{1,0:T(8,128)(2,1)S(1)} %get-tuple-element.58), channel_id=1, source_target_pairs={{0,1},{1,0},{2,3},{3,2},{4,5},{5,4},{6,7},{7,6},{8,9},{9,8},{10,11... | collective-permute-start | bytes 196616 | tf_op jit(solution)/shard_map/ppermute | solution.py:19
  43.7 2.3 %collective-permute-done.15.other_tail_ref.swapped_ref = bf16[32,1152]{1,0:T(8,128)(2,1)S(1)} collective-permute-done((bf16[32,1152]{1,0:T(8,128)(2,1)S(1)}, bf16[32,1152]{1,0:T(8,128)(2,1)S(1)}, u32[]{:S(2)}, u32[]{:S(2)}) %collective-permute-start.15) | collective-permute-done | bytes 73760 | tf_op jit(solution)/shard_map/ppermute | solution.py:19
  45.9 0.5 shard_map.75.refs_0_
  46.6 0.6 shard_map.76
  47.3 1.2 %collective-permute-done.17 = bf16[16,1792]{1,0:T(8,128)(2,1)S(1)} collective-permute-done((bf16[16,1792]{1,0:T(8,128)(2,1)S(1)}, bf16[16,1792]{1,0:T(8,128)(2,1)S(1)}, u32[]{:S(2)}, u32[]{:S(2)}) %collective-permute-start.17) | collective-permute-done | bytes 57376 | tf_op jit(solution)/shard_map/ppermute | solution.py:19
  48.5 1.6 %collective-permute-start.20 = (bf16[16,1792]{1,0:T(8,128)(2,1)S(1)}, bf16[16,1792]{1,0:T(8,128)(2,1)S(1)}, u32[]{:S(2)}, u32[]{:S(2)}) collective-permute-start(bf16[16,1792]{1,0:T(8,128)(2,1)S(1)} %fusion.1), channel_id=1, source_target_pairs={{0,24},{1,25},{2,26},{3,27},{4,28},{5,29},{6,30},{7,31},{8,16},{9,... | collective-permute-start | bytes 172040 | tf_op jit(solution)/shard_map/ppermute | solution.py:37
  50.2 0.6 collective-permute-start.19
  50.8 1.0 %collective-permute-start.18 = (bf16[16,1792]{1,0:T(8,128)(2,1)S(1)}, bf16[16,1792]{1,0:T(8,128)(2,1)S(1)}, u32[]{:S(2)}, u32[]{:S(2)}) collective-permute-start(bf16[16,1792]{1,0:T(8,128)(2,1)S(1)} %fusion.1), channel_id=1, source_target_pairs={{0,12},{1,13},{2,14},{3,15},{4,8},{5,9},{6,10},{7,11},{8,4},{9,5},... | collective-permute-start | bytes 172040 | tf_op jit(solution)/shard_map/ppermute | solution.py:37
  51.8 1.9 %collective-permute-done.20 = bf16[16,1792]{1,0:T(8,128)(2,1)S(1)} collective-permute-done((bf16[16,1792]{1,0:T(8,128)(2,1)S(1)}, bf16[16,1792]{1,0:T(8,128)(2,1)S(1)}, u32[]{:S(2)}, u32[]{:S(2)}) %collective-permute-start.20) | collective-permute-done | bytes 57376 | tf_op jit(solution)/shard_map/ppermute | solution.py:37
  53.7 1.2 %collective-permute-done.19 = bf16[16,1792]{1,0:T(8,128)(2,1)S(1)} collective-permute-done((bf16[16,1792]{1,0:T(8,128)(2,1)S(1)}, bf16[16,1792]{1,0:T(8,128)(2,1)S(1)}, u32[]{:S(2)}, u32[]{:S(2)}) %collective-permute-start.19) | collective-permute-done | bytes 57376 | tf_op jit(solution)/shard_map/ppermute | solution.py:37
  54.9 1.7 %collective-permute-start.21 = (bf16[16,1792]{1,0:T(8,128)(2,1)S(1)}, bf16[16,1792]{1,0:T(8,128)(2,1)S(1)}, u32[]{:S(2)}, u32[]{:S(2)}) collective-permute-start(bf16[16,1792]{1,0:T(8,128)(2,1)S(1)} %fusion.4), channel_id=1, source_target_pairs={{0,6},{1,7},{2,4},{3,5},{4,2},{5,3},{6,0},{7,1},{8,14},{9,15},{10,... | collective-permute-start | bytes 172040 | tf_op jit(solution)/shard_map/ppermute | solution.py:37
  56.7 4.4 %collective-permute-done.21 = bf16[16,1792]{1,0:T(8,128)(2,1)S(1)} collective-permute-done((bf16[16,1792]{1,0:T(8,128)(2,1)S(1)}, bf16[16,1792]{1,0:T(8,128)(2,1)S(1)}, u32[]{:S(2)}, u32[]{:S(2)}) %collective-permute-start.21) | collective-permute-done | bytes 57376 | tf_op jit(solution)/shard_map/ppermute | solution.py:37
  61.3 1.1 %collective-permute-done.22.refs_2_ = bf16[16,1792]{1,0:T(8,128)(2,1)S(1)} collective-permute-done((bf16[16,1792]{1,0:T(8,128)(2,1)S(1)}, bf16[16,1792]{1,0:T(8,128)(2,1)S(1)}, u32[]{:S(2)}, u32[]{:S(2)}) %collective-permute-start.22) | collective-permute-done | bytes 57376 | tf_op jit(solution)/shard_map/ppermute | solution.py:19
  62.4 0.7 shard_map.77
  63.4 0.7 shard_map.78
  64.1 1.9 %collective-permute-start.24 = (bf16[32,1024]{1,0:T(8,128)(2,1)S(1)}, bf16[32,1024]{1,0:T(8,128)(2,1)S(1)}, u32[]{:S(2)}, u32[]{:S(2)}) collective-permute-start(bf16[32,1024]{1,0:T(8,128)(2,1)S(1)} %get-tuple-element.66), channel_id=1, source_target_pairs={{0,1},{1,0},{2,3},{3,2},{4,5},{5,4},{6,7},{7,6},{8,9},{9,8},{10,11... | collective-permute-start | bytes 196616 | tf_op jit(solution)/shard_map/ppermute | solution.py:19
  66.0 2.3 %collective-permute-done.23.other_tail_ref.swapped_ref = bf16[32,1152]{1,0:T(8,128)(2,1)S(1)} collective-permute-done((bf16[32,1152]{1,0:T(8,128)(2,1)S(1)}, bf16[32,1152]{1,0:T(8,128)(2,1)S(1)}, u32[]{:S(2)}, u32[]{:S(2)}) %collective-permute-start.23) | collective-permute-done | bytes 73760 | tf_op jit(solution)/shard_map/ppermute | solution.py:19
  68.2 0.5 shard_map.79.refs_0_
  68.9 0.6 shard_map.80
  69.6 1.2 %collective-permute-done.25 = bf16[16,1792]{1,0:T(8,128)(2,1)S(1)} collective-permute-done((bf16[16,1792]{1,0:T(8,128)(2,1)S(1)}, bf16[16,1792]{1,0:T(8,128)(2,1)S(1)}, u32[]{:S(2)}, u32[]{:S(2)}) %collective-permute-start.25) | collective-permute-done | bytes 57376 | tf_op jit(solution)/shard_map/ppermute | solution.py:19
  70.8 1.5 %collective-permute-start.28 = (bf16[16,1792]{1,0:T(8,128)(2,1)S(1)}, bf16[16,1792]{1,0:T(8,128)(2,1)S(1)}, u32[]{:S(2)}, u32[]{:S(2)}) collective-permute-start(bf16[16,1792]{1,0:T(8,128)(2,1)S(1)} %fusion.2), channel_id=1, source_target_pairs={{0,24},{1,25},{2,26},{3,27},{4,28},{5,29},{6,30},{7,31},{8,16},{9,... | collective-permute-start | bytes 172040 | tf_op jit(solution)/shard_map/ppermute | solution.py:37
  72.3 0.6 collective-permute-start.27
  72.9 1.2 %collective-permute-start.26 = (bf16[16,1792]{1,0:T(8,128)(2,1)S(1)}, bf16[16,1792]{1,0:T(8,128)(2,1)S(1)}, u32[]{:S(2)}, u32[]{:S(2)}) collective-permute-start(bf16[16,1792]{1,0:T(8,128)(2,1)S(1)} %fusion.2), channel_id=1, source_target_pairs={{0,12},{1,13},{2,14},{3,15},{4,8},{5,9},{6,10},{7,11},{8,4},{9,5},... | collective-permute-start | bytes 172040 | tf_op jit(solution)/shard_map/ppermute | solution.py:37
  74.1 2.0 %collective-permute-done.28 = bf16[16,1792]{1,0:T(8,128)(2,1)S(1)} collective-permute-done((bf16[16,1792]{1,0:T(8,128)(2,1)S(1)}, bf16[16,1792]{1,0:T(8,128)(2,1)S(1)}, u32[]{:S(2)}, u32[]{:S(2)}) %collective-permute-start.28) | collective-permute-done | bytes 57376 | tf_op jit(solution)/shard_map/ppermute | solution.py:37
  76.1 1.0 collective-permute-done.27
  77.1 1.7 %collective-permute-start.29 = (bf16[16,1792]{1,0:T(8,128)(2,1)S(1)}, bf16[16,1792]{1,0:T(8,128)(2,1)S(1)}, u32[]{:S(2)}, u32[]{:S(2)}) collective-permute-start(bf16[16,1792]{1,0:T(8,128)(2,1)S(1)} %fusion.5), channel_id=1, source_target_pairs={{0,6},{1,7},{2,4},{3,5},{4,2},{5,3},{6,0},{7,1},{8,14},{9,15},{10,... | collective-permute-start | bytes 172040 | tf_op jit(solution)/shard_map/ppermute | solution.py:37
  78.8 4.4 %collective-permute-done.29 = bf16[16,1792]{1,0:T(8,128)(2,1)S(1)} collective-permute-done((bf16[16,1792]{1,0:T(8,128)(2,1)S(1)}, bf16[16,1792]{1,0:T(8,128)(2,1)S(1)}, u32[]{:S(2)}, u32[]{:S(2)}) %collective-permute-start.29) | collective-permute-done | bytes 57376 | tf_op jit(solution)/shard_map/ppermute | solution.py:37
  83.5 1.1 %collective-permute-done.30.refs_2_ = bf16[16,1792]{1,0:T(8,128)(2,1)S(1)} collective-permute-done((bf16[16,1792]{1,0:T(8,128)(2,1)S(1)}, bf16[16,1792]{1,0:T(8,128)(2,1)S(1)}, u32[]{:S(2)}, u32[]{:S(2)}) %collective-permute-start.30) | collective-permute-done | bytes 57376 | tf_op jit(solution)/shard_map/ppermute | solution.py:19
  84.6 0.7 shard_map.81
  85.5 0.7 shard_map.82
  86.3 1.9 %collective-permute-start.32 = (bf16[32,1024]{1,0:T(8,128)(2,1)S(1)}, bf16[32,1024]{1,0:T(8,128)(2,1)S(1)}, u32[]{:S(2)}, u32[]{:S(2)}) collective-permute-start(bf16[32,1024]{1,0:T(8,128)(2,1)S(1)} %get-tuple-element.73), channel_id=1, source_target_pairs={{0,1},{1,0},{2,3},{3,2},{4,5},{5,4},{6,7},{7,6},{8,9},{9,8},{10,11... | collective-permute-start | bytes 196616 | tf_op jit(solution)/shard_map/ppermute | solution.py:19
  88.3 2.1 %collective-permute-done.31.other_tail_ref.swapped_ref = bf16[32,1152]{1,0:T(8,128)(2,1)S(1)} collective-permute-done((bf16[32,1152]{1,0:T(8,128)(2,1)S(1)}, bf16[32,1152]{1,0:T(8,128)(2,1)S(1)}, u32[]{:S(2)}, u32[]{:S(2)}) %collective-permute-start.31) | collective-permute-done | bytes 73760 | tf_op jit(solution)/shard_map/ppermute | solution.py:19
  90.4 0.5 shard_map.83.refs_0_
  91.2 0.6 shard_map.84
  91.8 11.5 %all_to_all.5.arrived_ref = bf16[32,14,128]{2,1,0:T(8,128)(2,1)S(1)} all-to-all(bf16[32,14,128]{2,1,0:T(8,128)(2,1)S(1)} %shard_map.84), channel_id=1, replica_groups=mesh['rack'=8,'expert'=4] {'rack','expert'}, dimensions={0} | all-to-all | bytes 229376 | tf_op jit(solution)/shard_map/all_to_all | solution.py:404
  103.3 0.7 shard_map.85
  (38 shorter events, 3.1 us)
Async XLA Ops:
  0.9 6.7 %collective-permute-start = (bf16[16,128]{1,0:T(8,128)(2,1)S(1)}, bf16[16,128]{1,0:T(8,128)(2,1)S(1)}, u32[]{:S(2)}, u32[]{:S(2)}) collective-permute-start(bf16[16,128]{1,0:T(8,128)(2,1)S(1)} %get-tuple-element.42.refs_0_), channel_id=1, source_target_pairs={{0,12},{1,13},{2,14},{3,15},{4,8},{5,9},{6,10},{7,11},{8,4},{9,5},... | collective-permute-start | bytes 12296 | tf_op jit(solution)/shard_map/ppermute | solution.py:37
  3.3 4.5 %collective-permute-start.2 = (bf16[16,128]{1,0:T(8,128)(2,1)S(1)}, bf16[16,128]{1,0:T(8,128)(2,1)S(1)}, u32[]{:S(2)}, u32[]{:S(2)}) collective-permute-start(bf16[16,128]{1,0:T(8,128)(2,1)S(1)} %get-tuple-element.43), channel_id=1, source_target_pairs={{0,9},{1,8},{2,11},{3,10},{4,13},{5,12},{6,15},{7,14},{8,1},{9,0},... | collective-permute-start | bytes 12296 | tf_op jit(solution)/shard_map/ppermute | solution.py:37
  5.0 3.0 %collective-permute-start.1 = (bf16[16,128]{1,0:T(8,128)(2,1)S(1)}, bf16[16,128]{1,0:T(8,128)(2,1)S(1)}, u32[]{:S(2)}, u32[]{:S(2)}) collective-permute-start(bf16[16,128]{1,0:T(8,128)(2,1)S(1)} %get-tuple-element.43), channel_id=1, source_target_pairs={{0,5},{1,4},{2,7},{3,6},{4,1},{5,0},{6,3},{7,2},{8,13},{9,12},{10,... | collective-permute-start | bytes 12296 | tf_op jit(solution)/shard_map/ppermute | solution.py:37
  8.0 6.1 %collective-permute-start.5 = (bf16[4,16,128]{2,1,0:T(8,128)(2,1)S(1)}, bf16[4,16,128]{2,1,0:T(8,128)(2,1)S(1)}, u32[]{:S(2)}, u32[]{:S(2)}) collective-permute-start(bf16[4,16,128]{2,1,0:T(8,128)(2,1)S(1)} %shard_map.66.refs_0_), channel_id=1, source_target_pairs={{0,18},{1,19},{2,16},{3,17},{4,22},{5,23},{6,20},{7,21},{8,26},{9,... | collective-permute-start | bytes 49160 | tf_op jit(solution)/shard_map/ppermute | solution.py:37
  11.6 4.1 %collective-permute-start.4 = (bf16[4,16,128]{2,1,0:T(8,128)(2,1)S(1)}, bf16[4,16,128]{2,1,0:T(8,128)(2,1)S(1)}, u32[]{:S(2)}, u32[]{:S(2)}) collective-permute-start(bf16[4,16,128]{2,1,0:T(8,128)(2,1)S(1)} %shard_map.66.refs_0_), channel_id=1, source_target_pairs={{0,6},{1,7},{2,4},{3,5},{4,2},{5,3},{6,0},{7,1},{8,14},{9,15},{10,... | collective-permute-start | bytes 49160 | tf_op jit(solution)/shard_map/ppermute | solution.py:37
  11.6 4.1 %collective-permute-start.3 = (bf16[4,16,128]{2,1,0:T(8,128)(2,1)S(1)}, bf16[4,16,128]{2,1,0:T(8,128)(2,1)S(1)}, u32[]{:S(2)}, u32[]{:S(2)}) collective-permute-start(bf16[4,16,128]{2,1,0:T(8,128)(2,1)S(1)} %shard_map.66.refs_0_), channel_id=1, source_target_pairs={{0,20},{1,21},{2,22},{3,23},{4,16},{5,17},{6,18},{7,19},{8,28},{9,... | collective-permute-start | bytes 49160 | tf_op jit(solution)/shard_map/ppermute | solution.py:37
  15.6 1.3 %collective-permute-start.6 = (bf16[16,16,128]{2,1,0:T(8,128)(2,1)S(1)}, bf16[16,16,128]{2,1,0:T(8,128)(2,1)S(1)}, u32[]{:S(2)}, u32[]{:S(2)}) collective-permute-start(bf16[16,16,128]{2,1,0:T(8,128)(2,1)S(1)} %shard_map.68.refs_0_), channel_id=1, source_target_pairs={{0,4},{4,0},{8,12},{12,8},{16,20},{20,16},{24,28},{28,24},{1,5},{5... | collective-permute-start | bytes 196616 | tf_op jit(solution)/shard_map/ppermute | solution.py:19
  17.8 4.4 %copy-start = (bf16[1,1,1024,1792]{3,2,1,0:T(8,128)(2,1)S(1)}, bf16[1,1,1024,1792]{3,2,1,0:T(8,128)(2,1)}, u32[]{:S(2)}) copy-start(bf16[1,1,1024,1792]{3,2,1,0:T(8,128)(2,1)} %param.11) | copy-start | bytes 11010052
  17.9 4.4 %collective-permute-start.7 = (bf16[32,1152]{1,0:T(8,128)(2,1)S(1)}, bf16[32,1152]{1,0:T(8,128)(2,1)S(1)}, u32[]{:S(2)}, u32[]{:S(2)}) collective-permute-start(bf16[32,1152]{1,0:T(8,128)(2,1)S(1)} %get-tuple-element.46.tail_ref), channel_id=1, source_target_pairs={{0,1},{1,0},{2,3},{3,2},{4,5},{5,4},{6,7},{7,6},{8,9},{9,8},{10,11... | collective-permute-start | bytes 221192 | tf_op jit(solution)/shard_map/ppermute | solution.py:19
  20.2 4.3 %collective-permute-start.8 = (bf16[32,1024]{1,0:T(8,128)(2,1)S(1)}, bf16[32,1024]{1,0:T(8,128)(2,1)S(1)}, u32[]{:S(2)}, u32[]{:S(2)}) collective-permute-start(bf16[32,1024]{1,0:T(8,128)(2,1)S(1)} %get-tuple-element.49), channel_id=1, source_target_pairs={{0,1},{1,0},{2,3},{3,2},{4,5},{5,4},{6,7},{7,6},{8,9},{9,8},{10,11... | collective-permute-start | bytes 196616 | tf_op jit(solution)/shard_map/ppermute | solution.py:19
  25.1 1.3 %collective-permute-start.9 = (bf16[16,1792]{1,0:T(8,128)(2,1)S(1)}, bf16[16,1792]{1,0:T(8,128)(2,1)S(1)}, u32[]{:S(2)}, u32[]{:S(2)}) collective-permute-start(bf16[16,1792]{1,0:T(8,128)(2,1)S(1)} %get-tuple-element.53), channel_id=1, source_target_pairs={{0,4},{4,0},{8,12},{12,8},{16,20},{20,16},{24,28},{28,24},{1,5},{5... | collective-permute-start | bytes 172040 | tf_op jit(solution)/shard_map/ppermute | solution.py:19
  26.4 5.2 %collective-permute-start.12 = (bf16[16,1792]{1,0:T(8,128)(2,1)S(1)}, bf16[16,1792]{1,0:T(8,128)(2,1)S(1)}, u32[]{:S(2)}, u32[]{:S(2)}) collective-permute-start(bf16[16,1792]{1,0:T(8,128)(2,1)S(1)} %fusion), channel_id=1, source_target_pairs={{0,24},{1,25},{2,26},{3,27},{4,28},{5,29},{6,30},{7,31},{8,16},{9,... | collective-permute-start | bytes 172040 | tf_op jit(solution)/shard_map/ppermute | solution.py:37
  27.8 4.8 %collective-permute-start.11 = (bf16[16,1792]{1,0:T(8,128)(2,1)S(1)}, bf16[16,1792]{1,0:T(8,128)(2,1)S(1)}, u32[]{:S(2)}, u32[]{:S(2)}) collective-permute-start(bf16[16,1792]{1,0:T(8,128)(2,1)S(1)} %fusion), channel_id=1, source_target_pairs={{0,20},{1,21},{2,22},{3,23},{4,16},{5,17},{6,18},{7,19},{8,28},{9,... | collective-permute-start | bytes 172040 | tf_op jit(solution)/shard_map/ppermute | solution.py:37
  28.8 3.8 %collective-permute-start.10 = (bf16[16,1792]{1,0:T(8,128)(2,1)S(1)}, bf16[16,1792]{1,0:T(8,128)(2,1)S(1)}, u32[]{:S(2)}, u32[]{:S(2)}) collective-permute-start(bf16[16,1792]{1,0:T(8,128)(2,1)S(1)} %fusion), channel_id=1, source_target_pairs={{0,12},{1,13},{2,14},{3,15},{4,8},{5,9},{6,10},{7,11},{8,4},{9,5},... | collective-permute-start | bytes 172040 | tf_op jit(solution)/shard_map/ppermute | solution.py:37
  32.6 6.1 %collective-permute-start.13 = (bf16[16,1792]{1,0:T(8,128)(2,1)S(1)}, bf16[16,1792]{1,0:T(8,128)(2,1)S(1)}, u32[]{:S(2)}, u32[]{:S(2)}) collective-permute-start(bf16[16,1792]{1,0:T(8,128)(2,1)S(1)} %fusion.3), channel_id=1, source_target_pairs={{0,6},{1,7},{2,4},{3,5},{4,2},{5,3},{6,0},{7,1},{8,14},{9,15},{10,... | collective-permute-start | bytes 172040 | tf_op jit(solution)/shard_map/ppermute | solution.py:37
  38.8 1.3 %collective-permute-start.14 = (bf16[16,1792]{1,0:T(8,128)(2,1)S(1)}, bf16[16,1792]{1,0:T(8,128)(2,1)S(1)}, u32[]{:S(2)}, u32[]{:S(2)}) collective-permute-start(bf16[16,1792]{1,0:T(8,128)(2,1)S(1)} %get-tuple-element.83), channel_id=1, source_target_pairs={{0,4},{4,0},{8,12},{12,8},{16,20},{20,16},{24,28},{28,24},{1,5},{5... | collective-permute-start | bytes 172040 | tf_op jit(solution)/shard_map/ppermute | solution.py:19
  40.8 5.1 %collective-permute-start.15 = (bf16[32,1152]{1,0:T(8,128)(2,1)S(1)}, bf16[32,1152]{1,0:T(8,128)(2,1)S(1)}, u32[]{:S(2)}, u32[]{:S(2)}) collective-permute-start(bf16[32,1152]{1,0:T(8,128)(2,1)S(1)} %get-tuple-element.55.tail_ref), channel_id=1, source_target_pairs={{0,1},{1,0},{2,3},{3,2},{4,5},{5,4},{6,7},{7,6},{8,9},{9,8},{10,11... | collective-permute-start | bytes 221192 | tf_op jit(solution)/shard_map/ppermute | solution.py:19
  41.6 5.0 %collective-permute-start.16 = (bf16[32,1024]{1,0:T(8,128)(2,1)S(1)}, bf16[32,1024]{1,0:T(8,128)(2,1)S(1)}, u32[]{:S(2)}, u32[]{:S(2)}) collective-permute-start(bf16[32,1024]{1,0:T(8,128)(2,1)S(1)} %get-tuple-element.58), channel_id=1, source_target_pairs={{0,1},{1,0},{2,3},{3,2},{4,5},{5,4},{6,7},{7,6},{8,9},{9,8},{10,11... | collective-permute-start | bytes 196616 | tf_op jit(solution)/shard_map/ppermute | solution.py:19
  47.2 1.3 %collective-permute-start.17 = (bf16[16,1792]{1,0:T(8,128)(2,1)S(1)}, bf16[16,1792]{1,0:T(8,128)(2,1)S(1)}, u32[]{:S(2)}, u32[]{:S(2)}) collective-permute-start(bf16[16,1792]{1,0:T(8,128)(2,1)S(1)} %get-tuple-element.61), channel_id=1, source_target_pairs={{0,4},{4,0},{8,12},{12,8},{16,20},{20,16},{24,28},{28,24},{1,5},{5... | collective-permute-start | bytes 172040 | tf_op jit(solution)/shard_map/ppermute | solution.py:19
  48.5 5.2 %collective-permute-start.20 = (bf16[16,1792]{1,0:T(8,128)(2,1)S(1)}, bf16[16,1792]{1,0:T(8,128)(2,1)S(1)}, u32[]{:S(2)}, u32[]{:S(2)}) collective-permute-start(bf16[16,1792]{1,0:T(8,128)(2,1)S(1)} %fusion.1), channel_id=1, source_target_pairs={{0,24},{1,25},{2,26},{3,27},{4,28},{5,29},{6,30},{7,31},{8,16},{9,... | collective-permute-start | bytes 172040 | tf_op jit(solution)/shard_map/ppermute | solution.py:37
  50.2 4.7 %collective-permute-start.19 = (bf16[16,1792]{1,0:T(8,128)(2,1)S(1)}, bf16[16,1792]{1,0:T(8,128)(2,1)S(1)}, u32[]{:S(2)}, u32[]{:S(2)}) collective-permute-start(bf16[16,1792]{1,0:T(8,128)(2,1)S(1)} %fusion.1), channel_id=1, source_target_pairs={{0,20},{1,21},{2,22},{3,23},{4,16},{5,17},{6,18},{7,19},{8,28},{9,... | collective-permute-start | bytes 172040 | tf_op jit(solution)/shard_map/ppermute | solution.py:37
  50.8 4.1 %collective-permute-start.18 = (bf16[16,1792]{1,0:T(8,128)(2,1)S(1)}, bf16[16,1792]{1,0:T(8,128)(2,1)S(1)}, u32[]{:S(2)}, u32[]{:S(2)}) collective-permute-start(bf16[16,1792]{1,0:T(8,128)(2,1)S(1)} %fusion.1), channel_id=1, source_target_pairs={{0,12},{1,13},{2,14},{3,15},{4,8},{5,9},{6,10},{7,11},{8,4},{9,5},... | collective-permute-start | bytes 172040 | tf_op jit(solution)/shard_map/ppermute | solution.py:37
  54.9 6.1 %collective-permute-start.21 = (bf16[16,1792]{1,0:T(8,128)(2,1)S(1)}, bf16[16,1792]{1,0:T(8,128)(2,1)S(1)}, u32[]{:S(2)}, u32[]{:S(2)}) collective-permute-start(bf16[16,1792]{1,0:T(8,128)(2,1)S(1)} %fusion.4), channel_id=1, source_target_pairs={{0,6},{1,7},{2,4},{3,5},{4,2},{5,3},{6,0},{7,1},{8,14},{9,15},{10,... | collective-permute-start | bytes 172040 | tf_op jit(solution)/shard_map/ppermute | solution.py:37
  61.1 1.3 %collective-permute-start.22 = (bf16[16,1792]{1,0:T(8,128)(2,1)S(1)}, bf16[16,1792]{1,0:T(8,128)(2,1)S(1)}, u32[]{:S(2)}, u32[]{:S(2)}) collective-permute-start(bf16[16,1792]{1,0:T(8,128)(2,1)S(1)} %get-tuple-element.81), channel_id=1, source_target_pairs={{0,4},{4,0},{8,12},{12,8},{16,20},{20,16},{24,28},{28,24},{1,5},{5... | collective-permute-start | bytes 172040 | tf_op jit(solution)/shard_map/ppermute | solution.py:19
  63.2 5.1 %collective-permute-start.23 = (bf16[32,1152]{1,0:T(8,128)(2,1)S(1)}, bf16[32,1152]{1,0:T(8,128)(2,1)S(1)}, u32[]{:S(2)}, u32[]{:S(2)}) collective-permute-start(bf16[32,1152]{1,0:T(8,128)(2,1)S(1)} %get-tuple-element.63.tail_ref), channel_id=1, source_target_pairs={{0,1},{1,0},{2,3},{3,2},{4,5},{5,4},{6,7},{7,6},{8,9},{9,8},{10,11... | collective-permute-start | bytes 221192 | tf_op jit(solution)/shard_map/ppermute | solution.py:19
  64.1 4.8 %collective-permute-start.24 = (bf16[32,1024]{1,0:T(8,128)(2,1)S(1)}, bf16[32,1024]{1,0:T(8,128)(2,1)S(1)}, u32[]{:S(2)}, u32[]{:S(2)}) collective-permute-start(bf16[32,1024]{1,0:T(8,128)(2,1)S(1)} %get-tuple-element.66), channel_id=1, source_target_pairs={{0,1},{1,0},{2,3},{3,2},{4,5},{5,4},{6,7},{7,6},{8,9},{9,8},{10,11... | collective-permute-start | bytes 196616 | tf_op jit(solution)/shard_map/ppermute | solution.py:19
  69.5 1.3 %collective-permute-start.25 = (bf16[16,1792]{1,0:T(8,128)(2,1)S(1)}, bf16[16,1792]{1,0:T(8,128)(2,1)S(1)}, u32[]{:S(2)}, u32[]{:S(2)}) collective-permute-start(bf16[16,1792]{1,0:T(8,128)(2,1)S(1)} %get-tuple-element.69), channel_id=1, source_target_pairs={{0,4},{4,0},{8,12},{12,8},{16,20},{20,16},{24,28},{28,24},{1,5},{5... | collective-permute-start | bytes 172040 | tf_op jit(solution)/shard_map/ppermute | solution.py:19
  70.8 5.2 %collective-permute-start.28 = (bf16[16,1792]{1,0:T(8,128)(2,1)S(1)}, bf16[16,1792]{1,0:T(8,128)(2,1)S(1)}, u32[]{:S(2)}, u32[]{:S(2)}) collective-permute-start(bf16[16,1792]{1,0:T(8,128)(2,1)S(1)} %fusion.2), channel_id=1, source_target_pairs={{0,24},{1,25},{2,26},{3,27},{4,28},{5,29},{6,30},{7,31},{8,16},{9,... | collective-permute-start | bytes 172040 | tf_op jit(solution)/shard_map/ppermute | solution.py:37
  72.3 4.8 %collective-permute-start.27 = (bf16[16,1792]{1,0:T(8,128)(2,1)S(1)}, bf16[16,1792]{1,0:T(8,128)(2,1)S(1)}, u32[]{:S(2)}, u32[]{:S(2)}) collective-permute-start(bf16[16,1792]{1,0:T(8,128)(2,1)S(1)} %fusion.2), channel_id=1, source_target_pairs={{0,20},{1,21},{2,22},{3,23},{4,16},{5,17},{6,18},{7,19},{8,28},{9,... | collective-permute-start | bytes 172040 | tf_op jit(solution)/shard_map/ppermute | solution.py:37
  72.9 4.2 %collective-permute-start.26 = (bf16[16,1792]{1,0:T(8,128)(2,1)S(1)}, bf16[16,1792]{1,0:T(8,128)(2,1)S(1)}, u32[]{:S(2)}, u32[]{:S(2)}) collective-permute-start(bf16[16,1792]{1,0:T(8,128)(2,1)S(1)} %fusion.2), channel_id=1, source_target_pairs={{0,12},{1,13},{2,14},{3,15},{4,8},{5,9},{6,10},{7,11},{8,4},{9,5},... | collective-permute-start | bytes 172040 | tf_op jit(solution)/shard_map/ppermute | solution.py:37
  77.1 6.1 %collective-permute-start.29 = (bf16[16,1792]{1,0:T(8,128)(2,1)S(1)}, bf16[16,1792]{1,0:T(8,128)(2,1)S(1)}, u32[]{:S(2)}, u32[]{:S(2)}) collective-permute-start(bf16[16,1792]{1,0:T(8,128)(2,1)S(1)} %fusion.5), channel_id=1, source_target_pairs={{0,6},{1,7},{2,4},{3,5},{4,2},{5,3},{6,0},{7,1},{8,14},{9,15},{10,... | collective-permute-start | bytes 172040 | tf_op jit(solution)/shard_map/ppermute | solution.py:37
  83.3 1.3 %collective-permute-start.30 = (bf16[16,1792]{1,0:T(8,128)(2,1)S(1)}, bf16[16,1792]{1,0:T(8,128)(2,1)S(1)}, u32[]{:S(2)}, u32[]{:S(2)}) collective-permute-start(bf16[16,1792]{1,0:T(8,128)(2,1)S(1)} %get-tuple-element.79), channel_id=1, source_target_pairs={{0,4},{4,0},{8,12},{12,8},{16,20},{20,16},{24,28},{28,24},{1,5},{5... | collective-permute-start | bytes 172040 | tf_op jit(solution)/shard_map/ppermute | solution.py:19
  85.3 5.1 %collective-permute-start.31 = (bf16[32,1152]{1,0:T(8,128)(2,1)S(1)}, bf16[32,1152]{1,0:T(8,128)(2,1)S(1)}, u32[]{:S(2)}, u32[]{:S(2)}) collective-permute-start(bf16[32,1152]{1,0:T(8,128)(2,1)S(1)} %get-tuple-element.70.tail_ref), channel_id=1, source_target_pairs={{0,1},{1,0},{2,3},{3,2},{4,5},{5,4},{6,7},{7,6},{8,9},{9,8},{10,11... | collective-permute-start | bytes 221192 | tf_op jit(solution)/shard_map/ppermute | solution.py:19
  86.3 4.9 %collective-permute-start.32 = (bf16[32,1024]{1,0:T(8,128)(2,1)S(1)}, bf16[32,1024]{1,0:T(8,128)(2,1)S(1)}, u32[]{:S(2)}, u32[]{:S(2)}) collective-permute-start(bf16[32,1024]{1,0:T(8,128)(2,1)S(1)} %get-tuple-element.73), channel_id=1, source_target_pairs={{0,1},{1,0},{2,3},{3,2},{4,5},{5,4},{6,7},{7,6},{8,9},{9,8},{10,11... | collective-permute-start | bytes 196616 | tf_op jit(solution)/shard_map/ppermute | solution.py:19
  88.1 3.6 %collective-permute-start.33 = (f32[1,1792]{1,0:T(1,128)S(1)}, f32[1,1792]{1,0:T(1,128)S(1)}, u32[]{:S(2)}, u32[]{:S(2)}) collective-permute-start(f32[1,1792]{1,0:T(1,128)S(1)} %get-tuple-element.75), channel_id=1, source_target_pairs={{0,1},{1,0},{2,3},{3,2},{4,5},{5,4},{6,7},{7,6},{8,9},{9,8},{10,11... | collective-permute-start | bytes 21512 | tf_op jit(solution)/shard_map/ppermute | solution.py:19

commit v9 on v8

--- a/solution.py
+++ b/solution.py
@@ -44,7 +44,11 @@
 
 def gather_masks(rack_count, group_count):
     near = [(0, 0), (3, 0), (1, 1), (2, 1)]
-    far = [crossed(rack, group) for group in range(0, group_count, 2) for rack in range(0, rack_count, 4)]
+    far = [
+        (rack ^ (group >> 1) % 2, group)
+        for group in range(0, group_count, 2)
+        for rack in range(0, rack_count, 4)
+    ]
     return near, far
 
 

time: 104 us -> 105 us (level)
  waiting for transfers between devices: 42.8 us -> 40 us
  starting transfers between devices: 32.8 us -> 35.3 us
    ppermute x18, waiting for transfers between devices: 24.2 us -> 21.8 us  [exchanged_both(): return lax.ppermute(shard, ('rack', 'expert'), pairs)]
    ppermute x18, starting transfers between devices: 23.3 us -> 25.5 us  [exchanged_both(): return lax.ppermute(shard, ('rack', 'expert'), pairs)]
where the time goes in v9:
time: 105 us; the launch traced here: 104 us
  waiting for transfers between devices  40 us (38%)
  starting transfers between devices  35.3 us (34%)
  Pallas kernels  16.3 us (16%)
  blocking collectives  12.3 us (12%)
    ppermute x18, starting transfers between devices, exchanged_both(): return lax.ppermute(shard, ('rack', 'expert'), pairs)  25.5 us
    ppermute x18, waiting for transfers between devices, exchanged_both(): return lax.ppermute(shard, ('rack', 'expert'), pairs)  21.8 us
    ppermute x16, waiting for transfers between devices, exchanged(): lax.ppermute(shard, axis, [(i, i ^ mask) for i in range(lax.axis_size(axi...  18.2 us
    pallas_call x22, Pallas kernels, kernel_call(): pl.pallas_call(body, out_shape=out_shape, in_specs=[WHOLE] * len(operands...  16.3 us
    all_to_all x1, blocking collectives, dense_steps(): lax.all_to_all(updates[0], ('rack', 'expert'), split_axis=0, concat_axis=...  12.3 us
    ppermute x16, starting transfers between devices, exchanged(): lax.ppermute(shard, axis, [(i, i ^ mask) for i in range(lax.axis_size(axi...  9.78 us
  transfers between devices with their start and end apart: 34, of which 27 were waited for; matrix products, arithmetic and copies ran while one was open for 0% of the time, Pallas kernels for 10%

profile of v9, /device:TPU:0, one launch (start us, length us, event | category | flops | bytes accessed | tf_op | source)
XLA Modules:
  0.0 104.4 jit_solution(1222454822386945901)
XLA Ops:
  0.0 0.9 shard_map.64
  0.9 2.4 %collective-permute-start = (bf16[16,128]{1,0:T(8,128)(2,1)S(1)}, bf16[16,128]{1,0:T(8,128)(2,1)S(1)}, u32[]{:S(2)}, u32[]{:S(2)}) collective-permute-start(bf16[16,128]{1,0:T(8,128)(2,1)S(1)} %get-tuple-element.42.refs_0_), channel_id=1, source_target_pairs={{0,12},{1,13},{2,14},{3,15},{4,8},{5,9},{6,10},{7,11},{8,4},{9,5},... | collective-permute-start | bytes 12296 | tf_op jit(solution)/shard_map/ppermute | solution.py:37
  3.3 1.7 %collective-permute-start.2 = (bf16[16,128]{1,0:T(8,128)(2,1)S(1)}, bf16[16,128]{1,0:T(8,128)(2,1)S(1)}, u32[]{:S(2)}, u32[]{:S(2)}) collective-permute-start(bf16[16,128]{1,0:T(8,128)(2,1)S(1)} %get-tuple-element.43), channel_id=1, source_target_pairs={{0,9},{1,8},{2,11},{3,10},{4,13},{5,12},{6,15},{7,14},{8,1},{9,0},... | collective-permute-start | bytes 12296 | tf_op jit(solution)/shard_map/ppermute | solution.py:37
  5.2 2.3 %shard_map.65.refs_4_.refs_3_.upper_ref = bf16[1024,2048]{1,0:T(8,128)(2,1)S(1)} custom-call(bf16[1792,2,1024]{2,1,0:T(2,128)(2,1)} %bitcast.11), custom_call_target="tpu_custom_call" | custom-call | bytes 7340032 | tf_op jit(solution)/shard_map/pallas_call | solution.py:69
  8.0 3.4 %collective-permute-start.5 = (bf16[4,16,128]{2,1,0:T(8,128)(2,1)S(1)}, bf16[4,16,128]{2,1,0:T(8,128)(2,1)S(1)}, u32[]{:S(2)}, u32[]{:S(2)}) collective-permute-start(bf16[4,16,128]{2,1,0:T(8,128)(2,1)S(1)} %shard_map.66.refs_0_), channel_id=1, source_target_pairs={{0,22},{1,23},{2,20},{3,21},{4,18},{5,19},{6,16},{7,17},{8,30},{9,... | collective-permute-start | bytes 49160 | tf_op jit(solution)/shard_map/ppermute | solution.py:37
  11.6 0.5 collective-permute-start.3
  12.1 2.0 %shard_map.67.refs_4_.lower_ref.refs_5_ = bf16[768,2048]{1,0:T(8,128)(2,1)S(1)} custom-call(bf16[4,16,128]{2,1,0:T(8,128)(2,1)S(1)} %shard_map.66.refs_0_, bf16[1792,2,1024]{2,1,0:T(2,128)(2,1)} %bitcast.12), custom_call_target="tpu_custom_call" | custom-call | bytes 7356416 | tf_op jit(solution)/shard_map/pallas_call | solution.py:69
  14.1 1.4 %collective-permute-done.4.refs_2_ = bf16[4,16,128]{2,1,0:T(8,128)(2,1)S(1)} collective-permute-done((bf16[4,16,128]{2,1,0:T(8,128)(2,1)S(1)}, bf16[4,16,128]{2,1,0:T(8,128)(2,1)S(1)}, u32[]{:S(2)}, u32[]{:S(2)}) %collective-permute-start.4) | collective-permute-done | bytes 16416 | tf_op jit(solution)/shard_map/ppermute | solution.py:37
  15.8 1.0 collective-permute-done.6.refs_1_
  16.9 0.9 shard_map.69
  17.7 1.4 %collective-permute-start.7 = (bf16[32,1152]{1,0:T(8,128)(2,1)S(1)}, bf16[32,1152]{1,0:T(8,128)(2,1)S(1)}, u32[]{:S(2)}, u32[]{:S(2)}) collective-permute-start(bf16[32,1152]{1,0:T(8,128)(2,1)S(1)} %get-tuple-element.46.tail_ref), channel_id=1, source_target_pairs={{0,1},{1,0},{2,3},{3,2},{4,5},{5,4},{6,7},{7,6},{8,9},{9,8},{10,11... | collective-permute-start | bytes 221192 | tf_op jit(solution)/shard_map/ppermute | solution.py:19
  19.1 0.7 shard_map.70
  19.8 0.7 collective-permute-start.8
  20.6 1.6 %collective-permute-done.7.other_tail_ref.swapped_ref = bf16[32,1152]{1,0:T(8,128)(2,1)S(1)} collective-permute-done((bf16[32,1152]{1,0:T(8,128)(2,1)S(1)}, bf16[32,1152]{1,0:T(8,128)(2,1)S(1)}, u32[]{:S(2)}, u32[]{:S(2)}) %collective-permute-start.7) | collective-permute-done | bytes 73760 | tf_op jit(solution)/shard_map/ppermute | solution.py:19
  22.2 0.5 shard_map.71.refs_0_
  22.8 1.4 %collective-permute-done.8.swapped_ref = bf16[32,1024]{1,0:T(8,128)(2,1)S(1)} collective-permute-done((bf16[32,1024]{1,0:T(8,128)(2,1)S(1)}, bf16[32,1024]{1,0:T(8,128)(2,1)S(1)}, u32[]{:S(2)}, u32[]{:S(2)}) %collective-permute-start.8) | collective-permute-done | bytes 65568 | tf_op jit(solution)/shard_map/ppermute | solution.py:19
  24.1 0.6 shard_map.72
  24.8 1.2 %collective-permute-done.9 = bf16[16,1792]{1,0:T(8,128)(2,1)S(1)} collective-permute-done((bf16[16,1792]{1,0:T(8,128)(2,1)S(1)}, bf16[16,1792]{1,0:T(8,128)(2,1)S(1)}, u32[]{:S(2)}, u32[]{:S(2)}) %collective-permute-start.9) | collective-permute-done | bytes 57376 | tf_op jit(solution)/shard_map/ppermute | solution.py:19
  26.0 1.5 %collective-permute-start.12 = (bf16[16,1792]{1,0:T(8,128)(2,1)S(1)}, bf16[16,1792]{1,0:T(8,128)(2,1)S(1)}, u32[]{:S(2)}, u32[]{:S(2)}) collective-permute-start(bf16[16,1792]{1,0:T(8,128)(2,1)S(1)} %fusion), channel_id=1, source_target_pairs={{0,24},{1,25},{2,26},{3,27},{4,28},{5,29},{6,30},{7,31},{8,16},{9,... | collective-permute-start | bytes 172040 | tf_op jit(solution)/shard_map/ppermute | solution.py:37
  27.5 1.0 collective-permute-start.11
  28.5 0.8 collective-permute-start.10
  29.3 2.0 %collective-permute-done.12 = bf16[16,1792]{1,0:T(8,128)(2,1)S(1)} collective-permute-done((bf16[16,1792]{1,0:T(8,128)(2,1)S(1)}, bf16[16,1792]{1,0:T(8,128)(2,1)S(1)}, u32[]{:S(2)}, u32[]{:S(2)}) %collective-permute-start.12) | collective-permute-done | bytes 57376 | tf_op jit(solution)/shard_map/ppermute | solution.py:37
  31.3 1.0 collective-permute-done.11
  32.3 2.6 %collective-permute-start.13 = (bf16[16,1792]{1,0:T(8,128)(2,1)S(1)}, bf16[16,1792]{1,0:T(8,128)(2,1)S(1)}, u32[]{:S(2)}, u32[]{:S(2)}) collective-permute-start(bf16[16,1792]{1,0:T(8,128)(2,1)S(1)} %fusion.3), channel_id=1, source_target_pairs={{0,6},{1,7},{2,4},{3,5},{4,2},{5,3},{6,0},{7,1},{8,14},{9,15},{10,... | collective-permute-start | bytes 172040 | tf_op jit(solution)/shard_map/ppermute | solution.py:37
  34.9 3.4 %collective-permute-done.13 = bf16[16,1792]{1,0:T(8,128)(2,1)S(1)} collective-permute-done((bf16[16,1792]{1,0:T(8,128)(2,1)S(1)}, bf16[16,1792]{1,0:T(8,128)(2,1)S(1)}, u32[]{:S(2)}, u32[]{:S(2)}) %collective-permute-start.13) | collective-permute-done | bytes 57376 | tf_op jit(solution)/shard_map/ppermute | solution.py:37
  38.6 1.0 collective-permute-done.14.refs_2_
  39.6 0.7 shard_map.73
  40.8 0.7 shard_map.74
  41.5 1.7 %collective-permute-start.16 = (bf16[32,1024]{1,0:T(8,128)(2,1)S(1)}, bf16[32,1024]{1,0:T(8,128)(2,1)S(1)}, u32[]{:S(2)}, u32[]{:S(2)}) collective-permute-start(bf16[32,1024]{1,0:T(8,128)(2,1)S(1)} %get-tuple-element.58), channel_id=1, source_target_pairs={{0,1},{1,0},{2,3},{3,2},{4,5},{5,4},{6,7},{7,6},{8,9},{9,8},{10,11... | collective-permute-start | bytes 196616 | tf_op jit(solution)/shard_map/ppermute | solution.py:19
  43.2 2.3 %collective-permute-done.15.other_tail_ref.swapped_ref = bf16[32,1152]{1,0:T(8,128)(2,1)S(1)} collective-permute-done((bf16[32,1152]{1,0:T(8,128)(2,1)S(1)}, bf16[32,1152]{1,0:T(8,128)(2,1)S(1)}, u32[]{:S(2)}, u32[]{:S(2)}) %collective-permute-start.15) | collective-permute-done | bytes 73760 | tf_op jit(solution)/shard_map/ppermute | solution.py:19
  45.5 0.5 shard_map.75.refs_0_
  46.2 0.6 shard_map.76
  46.9 1.2 %collective-permute-done.17 = bf16[16,1792]{1,0:T(8,128)(2,1)S(1)} collective-permute-done((bf16[16,1792]{1,0:T(8,128)(2,1)S(1)}, bf16[16,1792]{1,0:T(8,128)(2,1)S(1)}, u32[]{:S(2)}, u32[]{:S(2)}) %collective-permute-start.17) | collective-permute-done | bytes 57376 | tf_op jit(solution)/shard_map/ppermute | solution.py:19
  48.1 1.6 %collective-permute-start.20 = (bf16[16,1792]{1,0:T(8,128)(2,1)S(1)}, bf16[16,1792]{1,0:T(8,128)(2,1)S(1)}, u32[]{:S(2)}, u32[]{:S(2)}) collective-permute-start(bf16[16,1792]{1,0:T(8,128)(2,1)S(1)} %fusion.1), channel_id=1, source_target_pairs={{0,24},{1,25},{2,26},{3,27},{4,28},{5,29},{6,30},{7,31},{8,16},{9,... | collective-permute-start | bytes 172040 | tf_op jit(solution)/shard_map/ppermute | solution.py:37
  49.8 0.6 collective-permute-start.19
  50.4 1.0 collective-permute-start.18
  51.4 1.9 %collective-permute-done.20 = bf16[16,1792]{1,0:T(8,128)(2,1)S(1)} collective-permute-done((bf16[16,1792]{1,0:T(8,128)(2,1)S(1)}, bf16[16,1792]{1,0:T(8,128)(2,1)S(1)}, u32[]{:S(2)}, u32[]{:S(2)}) %collective-permute-start.20) | collective-permute-done | bytes 57376 | tf_op jit(solution)/shard_map/ppermute | solution.py:37
  53.3 1.2 %collective-permute-done.19 = bf16[16,1792]{1,0:T(8,128)(2,1)S(1)} collective-permute-done((bf16[16,1792]{1,0:T(8,128)(2,1)S(1)}, bf16[16,1792]{1,0:T(8,128)(2,1)S(1)}, u32[]{:S(2)}, u32[]{:S(2)}) %collective-permute-start.19) | collective-permute-done | bytes 57376 | tf_op jit(solution)/shard_map/ppermute | solution.py:37
  54.5 2.3 %collective-permute-start.21 = (bf16[16,1792]{1,0:T(8,128)(2,1)S(1)}, bf16[16,1792]{1,0:T(8,128)(2,1)S(1)}, u32[]{:S(2)}, u32[]{:S(2)}) collective-permute-start(bf16[16,1792]{1,0:T(8,128)(2,1)S(1)} %fusion.4), channel_id=1, source_target_pairs={{0,6},{1,7},{2,4},{3,5},{4,2},{5,3},{6,0},{7,1},{8,14},{9,15},{10,... | collective-permute-start | bytes 172040 | tf_op jit(solution)/shard_map/ppermute | solution.py:37
  56.8 3.8 %collective-permute-done.21 = bf16[16,1792]{1,0:T(8,128)(2,1)S(1)} collective-permute-done((bf16[16,1792]{1,0:T(8,128)(2,1)S(1)}, bf16[16,1792]{1,0:T(8,128)(2,1)S(1)}, u32[]{:S(2)}, u32[]{:S(2)}) %collective-permute-start.21) | collective-permute-done | bytes 57376 | tf_op jit(solution)/shard_map/ppermute | solution.py:37
  60.9 1.1 %collective-permute-done.22.refs_2_ = bf16[16,1792]{1,0:T(8,128)(2,1)S(1)} collective-permute-done((bf16[16,1792]{1,0:T(8,128)(2,1)S(1)}, bf16[16,1792]{1,0:T(8,128)(2,1)S(1)}, u32[]{:S(2)}, u32[]{:S(2)}) %collective-permute-start.22) | collective-permute-done | bytes 57376 | tf_op jit(solution)/shard_map/ppermute | solution.py:19
  62.0 0.7 shard_map.77
  63.0 0.7 shard_map.78
  63.7 1.8 %collective-permute-start.24 = (bf16[32,1024]{1,0:T(8,128)(2,1)S(1)}, bf16[32,1024]{1,0:T(8,128)(2,1)S(1)}, u32[]{:S(2)}, u32[]{:S(2)}) collective-permute-start(bf16[32,1024]{1,0:T(8,128)(2,1)S(1)} %get-tuple-element.66), channel_id=1, source_target_pairs={{0,1},{1,0},{2,3},{3,2},{4,5},{5,4},{6,7},{7,6},{8,9},{9,8},{10,11... | collective-permute-start | bytes 196616 | tf_op jit(solution)/shard_map/ppermute | solution.py:19
  65.6 2.3 %collective-permute-done.23.other_tail_ref.swapped_ref = bf16[32,1152]{1,0:T(8,128)(2,1)S(1)} collective-permute-done((bf16[32,1152]{1,0:T(8,128)(2,1)S(1)}, bf16[32,1152]{1,0:T(8,128)(2,1)S(1)}, u32[]{:S(2)}, u32[]{:S(2)}) %collective-permute-start.23) | collective-permute-done | bytes 73760 | tf_op jit(solution)/shard_map/ppermute | solution.py:19
  67.8 0.5 shard_map.79.refs_0_
  68.5 0.6 shard_map.80
  69.2 1.2 %collective-permute-done.25 = bf16[16,1792]{1,0:T(8,128)(2,1)S(1)} collective-permute-done((bf16[16,1792]{1,0:T(8,128)(2,1)S(1)}, bf16[16,1792]{1,0:T(8,128)(2,1)S(1)}, u32[]{:S(2)}, u32[]{:S(2)}) %collective-permute-start.25) | collective-permute-done | bytes 57376 | tf_op jit(solution)/shard_map/ppermute | solution.py:19
  70.4 1.5 %collective-permute-start.28 = (bf16[16,1792]{1,0:T(8,128)(2,1)S(1)}, bf16[16,1792]{1,0:T(8,128)(2,1)S(1)}, u32[]{:S(2)}, u32[]{:S(2)}) collective-permute-start(bf16[16,1792]{1,0:T(8,128)(2,1)S(1)} %fusion.2), channel_id=1, source_target_pairs={{0,24},{1,25},{2,26},{3,27},{4,28},{5,29},{6,30},{7,31},{8,16},{9,... | collective-permute-start | bytes 172040 | tf_op jit(solution)/shard_map/ppermute | solution.py:37
  71.9 0.6 collective-permute-start.27
  72.5 1.2 %collective-permute-start.26 = (bf16[16,1792]{1,0:T(8,128)(2,1)S(1)}, bf16[16,1792]{1,0:T(8,128)(2,1)S(1)}, u32[]{:S(2)}, u32[]{:S(2)}) collective-permute-start(bf16[16,1792]{1,0:T(8,128)(2,1)S(1)} %fusion.2), channel_id=1, source_target_pairs={{0,12},{1,13},{2,14},{3,15},{4,8},{5,9},{6,10},{7,11},{8,4},{9,5},... | collective-permute-start | bytes 172040 | tf_op jit(solution)/shard_map/ppermute | solution.py:37
  73.7 2.0 %collective-permute-done.28 = bf16[16,1792]{1,0:T(8,128)(2,1)S(1)} collective-permute-done((bf16[16,1792]{1,0:T(8,128)(2,1)S(1)}, bf16[16,1792]{1,0:T(8,128)(2,1)S(1)}, u32[]{:S(2)}, u32[]{:S(2)}) %collective-permute-start.28) | collective-permute-done | bytes 57376 | tf_op jit(solution)/shard_map/ppermute | solution.py:37
  75.7 1.0 collective-permute-done.27
  76.7 2.3 %collective-permute-start.29 = (bf16[16,1792]{1,0:T(8,128)(2,1)S(1)}, bf16[16,1792]{1,0:T(8,128)(2,1)S(1)}, u32[]{:S(2)}, u32[]{:S(2)}) collective-permute-start(bf16[16,1792]{1,0:T(8,128)(2,1)S(1)} %fusion.5), channel_id=1, source_target_pairs={{0,6},{1,7},{2,4},{3,5},{4,2},{5,3},{6,0},{7,1},{8,14},{9,15},{10,... | collective-permute-start | bytes 172040 | tf_op jit(solution)/shard_map/ppermute | solution.py:37
  79.0 3.8 %collective-permute-done.29 = bf16[16,1792]{1,0:T(8,128)(2,1)S(1)} collective-permute-done((bf16[16,1792]{1,0:T(8,128)(2,1)S(1)}, bf16[16,1792]{1,0:T(8,128)(2,1)S(1)}, u32[]{:S(2)}, u32[]{:S(2)}) %collective-permute-start.29) | collective-permute-done | bytes 57376 | tf_op jit(solution)/shard_map/ppermute | solution.py:37
  83.0 1.1 %collective-permute-done.30.refs_2_ = bf16[16,1792]{1,0:T(8,128)(2,1)S(1)} collective-permute-done((bf16[16,1792]{1,0:T(8,128)(2,1)S(1)}, bf16[16,1792]{1,0:T(8,128)(2,1)S(1)}, u32[]{:S(2)}, u32[]{:S(2)}) %collective-permute-start.30) | collective-permute-done | bytes 57376 | tf_op jit(solution)/shard_map/ppermute | solution.py:19
  84.2 0.7 shard_map.81
  85.2 0.7 shard_map.82
  85.9 1.8 %collective-permute-start.32 = (bf16[32,1024]{1,0:T(8,128)(2,1)S(1)}, bf16[32,1024]{1,0:T(8,128)(2,1)S(1)}, u32[]{:S(2)}, u32[]{:S(2)}) collective-permute-start(bf16[32,1024]{1,0:T(8,128)(2,1)S(1)} %get-tuple-element.73), channel_id=1, source_target_pairs={{0,1},{1,0},{2,3},{3,2},{4,5},{5,4},{6,7},{7,6},{8,9},{9,8},{10,11... | collective-permute-start | bytes 196616 | tf_op jit(solution)/shard_map/ppermute | solution.py:19
  88.0 2.1 %collective-permute-done.31.other_tail_ref.swapped_ref = bf16[32,1152]{1,0:T(8,128)(2,1)S(1)} collective-permute-done((bf16[32,1152]{1,0:T(8,128)(2,1)S(1)}, bf16[32,1152]{1,0:T(8,128)(2,1)S(1)}, u32[]{:S(2)}, u32[]{:S(2)}) %collective-permute-start.31) | collective-permute-done | bytes 73760 | tf_op jit(solution)/shard_map/ppermute | solution.py:19
  90.0 0.5 shard_map.83.refs_0_
  90.8 0.6 shard_map.84
  91.4 12.3 %all_to_all.5.arrived_ref = bf16[32,14,128]{2,1,0:T(8,128)(2,1)S(1)} all-to-all(bf16[32,14,128]{2,1,0:T(8,128)(2,1)S(1)} %shard_map.84), channel_id=1, replica_groups=mesh['rack'=8,'expert'=4] {'rack','expert'}, dimensions={0} | all-to-all | bytes 229376 | tf_op jit(solution)/shard_map/all_to_all | solution.py:408
  103.6 0.7 shard_map.85
  (38 shorter events, 4.1 us)
Async XLA Ops:
  0.9 6.7 %collective-permute-start = (bf16[16,128]{1,0:T(8,128)(2,1)S(1)}, bf16[16,128]{1,0:T(8,128)(2,1)S(1)}, u32[]{:S(2)}, u32[]{:S(2)}) collective-permute-start(bf16[16,128]{1,0:T(8,128)(2,1)S(1)} %get-tuple-element.42.refs_0_), channel_id=1, source_target_pairs={{0,12},{1,13},{2,14},{3,15},{4,8},{5,9},{6,10},{7,11},{8,4},{9,5},... | collective-permute-start | bytes 12296 | tf_op jit(solution)/shard_map/ppermute | solution.py:37
  3.3 4.5 %collective-permute-start.2 = (bf16[16,128]{1,0:T(8,128)(2,1)S(1)}, bf16[16,128]{1,0:T(8,128)(2,1)S(1)}, u32[]{:S(2)}, u32[]{:S(2)}) collective-permute-start(bf16[16,128]{1,0:T(8,128)(2,1)S(1)} %get-tuple-element.43), channel_id=1, source_target_pairs={{0,9},{1,8},{2,11},{3,10},{4,13},{5,12},{6,15},{7,14},{8,1},{9,0},... | collective-permute-start | bytes 12296 | tf_op jit(solution)/shard_map/ppermute | solution.py:37
  5.0 3.0 %collective-permute-start.1 = (bf16[16,128]{1,0:T(8,128)(2,1)S(1)}, bf16[16,128]{1,0:T(8,128)(2,1)S(1)}, u32[]{:S(2)}, u32[]{:S(2)}) collective-permute-start(bf16[16,128]{1,0:T(8,128)(2,1)S(1)} %get-tuple-element.43), channel_id=1, source_target_pairs={{0,5},{1,4},{2,7},{3,6},{4,1},{5,0},{6,3},{7,2},{8,13},{9,12},{10,... | collective-permute-start | bytes 12296 | tf_op jit(solution)/shard_map/ppermute | solution.py:37
  8.0 6.1 %collective-permute-start.5 = (bf16[4,16,128]{2,1,0:T(8,128)(2,1)S(1)}, bf16[4,16,128]{2,1,0:T(8,128)(2,1)S(1)}, u32[]{:S(2)}, u32[]{:S(2)}) collective-permute-start(bf16[4,16,128]{2,1,0:T(8,128)(2,1)S(1)} %shard_map.66.refs_0_), channel_id=1, source_target_pairs={{0,22},{1,23},{2,20},{3,21},{4,18},{5,19},{6,16},{7,17},{8,30},{9,... | collective-permute-start | bytes 49160 | tf_op jit(solution)/shard_map/ppermute | solution.py:37
  11.5 4.1 %collective-permute-start.4 = (bf16[4,16,128]{2,1,0:T(8,128)(2,1)S(1)}, bf16[4,16,128]{2,1,0:T(8,128)(2,1)S(1)}, u32[]{:S(2)}, u32[]{:S(2)}) collective-permute-start(bf16[4,16,128]{2,1,0:T(8,128)(2,1)S(1)} %shard_map.66.refs_0_), channel_id=1, source_target_pairs={{0,6},{1,7},{2,4},{3,5},{4,2},{5,3},{6,0},{7,1},{8,14},{9,15},{10,... | collective-permute-start | bytes 49160 | tf_op jit(solution)/shard_map/ppermute | solution.py:37
  11.6 3.9 %collective-permute-start.3 = (bf16[4,16,128]{2,1,0:T(8,128)(2,1)S(1)}, bf16[4,16,128]{2,1,0:T(8,128)(2,1)S(1)}, u32[]{:S(2)}, u32[]{:S(2)}) collective-permute-start(bf16[4,16,128]{2,1,0:T(8,128)(2,1)S(1)} %shard_map.66.refs_0_), channel_id=1, source_target_pairs={{0,16},{1,17},{2,18},{3,19},{4,20},{5,21},{6,22},{7,23},{8,24},{9,... | collective-permute-start | bytes 49160 | tf_op jit(solution)/shard_map/ppermute | solution.py:37
  15.5 1.3 %collective-permute-start.6 = (bf16[16,16,128]{2,1,0:T(8,128)(2,1)S(1)}, bf16[16,16,128]{2,1,0:T(8,128)(2,1)S(1)}, u32[]{:S(2)}, u32[]{:S(2)}) collective-permute-start(bf16[16,16,128]{2,1,0:T(8,128)(2,1)S(1)} %shard_map.68.refs_0_), channel_id=1, source_target_pairs={{0,4},{4,0},{8,12},{12,8},{16,20},{20,16},{24,28},{28,24},{1,5},{5... | collective-permute-start | bytes 196616 | tf_op jit(solution)/shard_map/ppermute | solution.py:19
  17.7 4.5 %copy-start = (bf16[1,1,1024,1792]{3,2,1,0:T(8,128)(2,1)S(1)}, bf16[1,1,1024,1792]{3,2,1,0:T(8,128)(2,1)}, u32[]{:S(2)}) copy-start(bf16[1,1,1024,1792]{3,2,1,0:T(8,128)(2,1)} %param.11) | copy-start | bytes 11010052
  17.7 4.5 %collective-permute-start.7 = (bf16[32,1152]{1,0:T(8,128)(2,1)S(1)}, bf16[32,1152]{1,0:T(8,128)(2,1)S(1)}, u32[]{:S(2)}, u32[]{:S(2)}) collective-permute-start(bf16[32,1152]{1,0:T(8,128)(2,1)S(1)} %get-tuple-element.46.tail_ref), channel_id=1, source_target_pairs={{0,1},{1,0},{2,3},{3,2},{4,5},{5,4},{6,7},{7,6},{8,9},{9,8},{10,11... | collective-permute-start | bytes 221192 | tf_op jit(solution)/shard_map/ppermute | solution.py:19
  19.8 4.3 %collective-permute-start.8 = (bf16[32,1024]{1,0:T(8,128)(2,1)S(1)}, bf16[32,1024]{1,0:T(8,128)(2,1)S(1)}, u32[]{:S(2)}, u32[]{:S(2)}) collective-permute-start(bf16[32,1024]{1,0:T(8,128)(2,1)S(1)} %get-tuple-element.49), channel_id=1, source_target_pairs={{0,1},{1,0},{2,3},{3,2},{4,5},{5,4},{6,7},{7,6},{8,9},{9,8},{10,11... | collective-permute-start | bytes 196616 | tf_op jit(solution)/shard_map/ppermute | solution.py:19
  24.7 1.3 %collective-permute-start.9 = (bf16[16,1792]{1,0:T(8,128)(2,1)S(1)}, bf16[16,1792]{1,0:T(8,128)(2,1)S(1)}, u32[]{:S(2)}, u32[]{:S(2)}) collective-permute-start(bf16[16,1792]{1,0:T(8,128)(2,1)S(1)} %get-tuple-element.53), channel_id=1, source_target_pairs={{0,4},{4,0},{8,12},{12,8},{16,20},{20,16},{24,28},{28,24},{1,5},{5... | collective-permute-start | bytes 172040 | tf_op jit(solution)/shard_map/ppermute | solution.py:19
  26.0 5.2 %collective-permute-start.12 = (bf16[16,1792]{1,0:T(8,128)(2,1)S(1)}, bf16[16,1792]{1,0:T(8,128)(2,1)S(1)}, u32[]{:S(2)}, u32[]{:S(2)}) collective-permute-start(bf16[16,1792]{1,0:T(8,128)(2,1)S(1)} %fusion), channel_id=1, source_target_pairs={{0,24},{1,25},{2,26},{3,27},{4,28},{5,29},{6,30},{7,31},{8,16},{9,... | collective-permute-start | bytes 172040 | tf_op jit(solution)/shard_map/ppermute | solution.py:37
  27.5 4.8 %collective-permute-start.11 = (bf16[16,1792]{1,0:T(8,128)(2,1)S(1)}, bf16[16,1792]{1,0:T(8,128)(2,1)S(1)}, u32[]{:S(2)}, u32[]{:S(2)}) collective-permute-start(bf16[16,1792]{1,0:T(8,128)(2,1)S(1)} %fusion), channel_id=1, source_target_pairs={{0,20},{1,21},{2,22},{3,23},{4,16},{5,17},{6,18},{7,19},{8,28},{9,... | collective-permute-start | bytes 172040 | tf_op jit(solution)/shard_map/ppermute | solution.py:37
  28.5 3.8 %collective-permute-start.10 = (bf16[16,1792]{1,0:T(8,128)(2,1)S(1)}, bf16[16,1792]{1,0:T(8,128)(2,1)S(1)}, u32[]{:S(2)}, u32[]{:S(2)}) collective-permute-start(bf16[16,1792]{1,0:T(8,128)(2,1)S(1)} %fusion), channel_id=1, source_target_pairs={{0,12},{1,13},{2,14},{3,15},{4,8},{5,9},{6,10},{7,11},{8,4},{9,5},... | collective-permute-start | bytes 172040 | tf_op jit(solution)/shard_map/ppermute | solution.py:37
  32.3 6.0 %collective-permute-start.13 = (bf16[16,1792]{1,0:T(8,128)(2,1)S(1)}, bf16[16,1792]{1,0:T(8,128)(2,1)S(1)}, u32[]{:S(2)}, u32[]{:S(2)}) collective-permute-start(bf16[16,1792]{1,0:T(8,128)(2,1)S(1)} %fusion.3), channel_id=1, source_target_pairs={{0,6},{1,7},{2,4},{3,5},{4,2},{5,3},{6,0},{7,1},{8,14},{9,15},{10,... | collective-permute-start | bytes 172040 | tf_op jit(solution)/shard_map/ppermute | solution.py:37
  38.3 1.3 %collective-permute-start.14 = (bf16[16,1792]{1,0:T(8,128)(2,1)S(1)}, bf16[16,1792]{1,0:T(8,128)(2,1)S(1)}, u32[]{:S(2)}, u32[]{:S(2)}) collective-permute-start(bf16[16,1792]{1,0:T(8,128)(2,1)S(1)} %get-tuple-element.83), channel_id=1, source_target_pairs={{0,4},{4,0},{8,12},{12,8},{16,20},{20,16},{24,28},{28,24},{1,5},{5... | collective-permute-start | bytes 172040 | tf_op jit(solution)/shard_map/ppermute | solution.py:19
  40.4 5.2 %collective-permute-start.15 = (bf16[32,1152]{1,0:T(8,128)(2,1)S(1)}, bf16[32,1152]{1,0:T(8,128)(2,1)S(1)}, u32[]{:S(2)}, u32[]{:S(2)}) collective-permute-start(bf16[32,1152]{1,0:T(8,128)(2,1)S(1)} %get-tuple-element.55.tail_ref), channel_id=1, source_target_pairs={{0,1},{1,0},{2,3},{3,2},{4,5},{5,4},{6,7},{7,6},{8,9},{9,8},{10,11... | collective-permute-start | bytes 221192 | tf_op jit(solution)/shard_map/ppermute | solution.py:19
  41.5 4.7 %collective-permute-start.16 = (bf16[32,1024]{1,0:T(8,128)(2,1)S(1)}, bf16[32,1024]{1,0:T(8,128)(2,1)S(1)}, u32[]{:S(2)}, u32[]{:S(2)}) collective-permute-start(bf16[32,1024]{1,0:T(8,128)(2,1)S(1)} %get-tuple-element.58), channel_id=1, source_target_pairs={{0,1},{1,0},{2,3},{3,2},{4,5},{5,4},{6,7},{7,6},{8,9},{9,8},{10,11... | collective-permute-start | bytes 196616 | tf_op jit(solution)/shard_map/ppermute | solution.py:19
  46.8 1.3 %collective-permute-start.17 = (bf16[16,1792]{1,0:T(8,128)(2,1)S(1)}, bf16[16,1792]{1,0:T(8,128)(2,1)S(1)}, u32[]{:S(2)}, u32[]{:S(2)}) collective-permute-start(bf16[16,1792]{1,0:T(8,128)(2,1)S(1)} %get-tuple-element.61), channel_id=1, source_target_pairs={{0,4},{4,0},{8,12},{12,8},{16,20},{20,16},{24,28},{28,24},{1,5},{5... | collective-permute-start | bytes 172040 | tf_op jit(solution)/shard_map/ppermute | solution.py:19
  48.1 5.2 %collective-permute-start.20 = (bf16[16,1792]{1,0:T(8,128)(2,1)S(1)}, bf16[16,1792]{1,0:T(8,128)(2,1)S(1)}, u32[]{:S(2)}, u32[]{:S(2)}) collective-permute-start(bf16[16,1792]{1,0:T(8,128)(2,1)S(1)} %fusion.1), channel_id=1, source_target_pairs={{0,24},{1,25},{2,26},{3,27},{4,28},{5,29},{6,30},{7,31},{8,16},{9,... | collective-permute-start | bytes 172040 | tf_op jit(solution)/shard_map/ppermute | solution.py:37
  49.8 4.7 %collective-permute-start.19 = (bf16[16,1792]{1,0:T(8,128)(2,1)S(1)}, bf16[16,1792]{1,0:T(8,128)(2,1)S(1)}, u32[]{:S(2)}, u32[]{:S(2)}) collective-permute-start(bf16[16,1792]{1,0:T(8,128)(2,1)S(1)} %fusion.1), channel_id=1, source_target_pairs={{0,20},{1,21},{2,22},{3,23},{4,16},{5,17},{6,18},{7,19},{8,28},{9,... | collective-permute-start | bytes 172040 | tf_op jit(solution)/shard_map/ppermute | solution.py:37
  50.4 4.1 %collective-permute-start.18 = (bf16[16,1792]{1,0:T(8,128)(2,1)S(1)}, bf16[16,1792]{1,0:T(8,128)(2,1)S(1)}, u32[]{:S(2)}, u32[]{:S(2)}) collective-permute-start(bf16[16,1792]{1,0:T(8,128)(2,1)S(1)} %fusion.1), channel_id=1, source_target_pairs={{0,12},{1,13},{2,14},{3,15},{4,8},{5,9},{6,10},{7,11},{8,4},{9,5},... | collective-permute-start | bytes 172040 | tf_op jit(solution)/shard_map/ppermute | solution.py:37
  54.5 6.1 %collective-permute-start.21 = (bf16[16,1792]{1,0:T(8,128)(2,1)S(1)}, bf16[16,1792]{1,0:T(8,128)(2,1)S(1)}, u32[]{:S(2)}, u32[]{:S(2)}) collective-permute-start(bf16[16,1792]{1,0:T(8,128)(2,1)S(1)} %fusion.4), channel_id=1, source_target_pairs={{0,6},{1,7},{2,4},{3,5},{4,2},{5,3},{6,0},{7,1},{8,14},{9,15},{10,... | collective-permute-start | bytes 172040 | tf_op jit(solution)/shard_map/ppermute | solution.py:37
  60.7 1.3 %collective-permute-start.22 = (bf16[16,1792]{1,0:T(8,128)(2,1)S(1)}, bf16[16,1792]{1,0:T(8,128)(2,1)S(1)}, u32[]{:S(2)}, u32[]{:S(2)}) collective-permute-start(bf16[16,1792]{1,0:T(8,128)(2,1)S(1)} %get-tuple-element.81), channel_id=1, source_target_pairs={{0,4},{4,0},{8,12},{12,8},{16,20},{20,16},{24,28},{28,24},{1,5},{5... | collective-permute-start | bytes 172040 | tf_op jit(solution)/shard_map/ppermute | solution.py:19
  62.7 5.1 %collective-permute-start.23 = (bf16[32,1152]{1,0:T(8,128)(2,1)S(1)}, bf16[32,1152]{1,0:T(8,128)(2,1)S(1)}, u32[]{:S(2)}, u32[]{:S(2)}) collective-permute-start(bf16[32,1152]{1,0:T(8,128)(2,1)S(1)} %get-tuple-element.63.tail_ref), channel_id=1, source_target_pairs={{0,1},{1,0},{2,3},{3,2},{4,5},{5,4},{6,7},{7,6},{8,9},{9,8},{10,11... | collective-permute-start | bytes 221192 | tf_op jit(solution)/shard_map/ppermute | solution.py:19
  63.7 4.8 %collective-permute-start.24 = (bf16[32,1024]{1,0:T(8,128)(2,1)S(1)}, bf16[32,1024]{1,0:T(8,128)(2,1)S(1)}, u32[]{:S(2)}, u32[]{:S(2)}) collective-permute-start(bf16[32,1024]{1,0:T(8,128)(2,1)S(1)} %get-tuple-element.66), channel_id=1, source_target_pairs={{0,1},{1,0},{2,3},{3,2},{4,5},{5,4},{6,7},{7,6},{8,9},{9,8},{10,11... | collective-permute-start | bytes 196616 | tf_op jit(solution)/shard_map/ppermute | solution.py:19
  69.1 1.3 %collective-permute-start.25 = (bf16[16,1792]{1,0:T(8,128)(2,1)S(1)}, bf16[16,1792]{1,0:T(8,128)(2,1)S(1)}, u32[]{:S(2)}, u32[]{:S(2)}) collective-permute-start(bf16[16,1792]{1,0:T(8,128)(2,1)S(1)} %get-tuple-element.69), channel_id=1, source_target_pairs={{0,4},{4,0},{8,12},{12,8},{16,20},{20,16},{24,28},{28,24},{1,5},{5... | collective-permute-start | bytes 172040 | tf_op jit(solution)/shard_map/ppermute | solution.py:19
  70.4 5.2 %collective-permute-start.28 = (bf16[16,1792]{1,0:T(8,128)(2,1)S(1)}, bf16[16,1792]{1,0:T(8,128)(2,1)S(1)}, u32[]{:S(2)}, u32[]{:S(2)}) collective-permute-start(bf16[16,1792]{1,0:T(8,128)(2,1)S(1)} %fusion.2), channel_id=1, source_target_pairs={{0,24},{1,25},{2,26},{3,27},{4,28},{5,29},{6,30},{7,31},{8,16},{9,... | collective-permute-start | bytes 172040 | tf_op jit(solution)/shard_map/ppermute | solution.py:37
  71.9 4.8 %collective-permute-start.27 = (bf16[16,1792]{1,0:T(8,128)(2,1)S(1)}, bf16[16,1792]{1,0:T(8,128)(2,1)S(1)}, u32[]{:S(2)}, u32[]{:S(2)}) collective-permute-start(bf16[16,1792]{1,0:T(8,128)(2,1)S(1)} %fusion.2), channel_id=1, source_target_pairs={{0,20},{1,21},{2,22},{3,23},{4,16},{5,17},{6,18},{7,19},{8,28},{9,... | collective-permute-start | bytes 172040 | tf_op jit(solution)/shard_map/ppermute | solution.py:37
  72.5 4.2 %collective-permute-start.26 = (bf16[16,1792]{1,0:T(8,128)(2,1)S(1)}, bf16[16,1792]{1,0:T(8,128)(2,1)S(1)}, u32[]{:S(2)}, u32[]{:S(2)}) collective-permute-start(bf16[16,1792]{1,0:T(8,128)(2,1)S(1)} %fusion.2), channel_id=1, source_target_pairs={{0,12},{1,13},{2,14},{3,15},{4,8},{5,9},{6,10},{7,11},{8,4},{9,5},... | collective-permute-start | bytes 172040 | tf_op jit(solution)/shard_map/ppermute | solution.py:37
  76.7 6.1 %collective-permute-start.29 = (bf16[16,1792]{1,0:T(8,128)(2,1)S(1)}, bf16[16,1792]{1,0:T(8,128)(2,1)S(1)}, u32[]{:S(2)}, u32[]{:S(2)}) collective-permute-start(bf16[16,1792]{1,0:T(8,128)(2,1)S(1)} %fusion.5), channel_id=1, source_target_pairs={{0,6},{1,7},{2,4},{3,5},{4,2},{5,3},{6,0},{7,1},{8,14},{9,15},{10,... | collective-permute-start | bytes 172040 | tf_op jit(solution)/shard_map/ppermute | solution.py:37
  82.9 1.3 %collective-permute-start.30 = (bf16[16,1792]{1,0:T(8,128)(2,1)S(1)}, bf16[16,1792]{1,0:T(8,128)(2,1)S(1)}, u32[]{:S(2)}, u32[]{:S(2)}) collective-permute-start(bf16[16,1792]{1,0:T(8,128)(2,1)S(1)} %get-tuple-element.79), channel_id=1, source_target_pairs={{0,4},{4,0},{8,12},{12,8},{16,20},{20,16},{24,28},{28,24},{1,5},{5... | collective-permute-start | bytes 172040 | tf_op jit(solution)/shard_map/ppermute | solution.py:19
  84.9 5.1 %collective-permute-start.31 = (bf16[32,1152]{1,0:T(8,128)(2,1)S(1)}, bf16[32,1152]{1,0:T(8,128)(2,1)S(1)}, u32[]{:S(2)}, u32[]{:S(2)}) collective-permute-start(bf16[32,1152]{1,0:T(8,128)(2,1)S(1)} %get-tuple-element.70.tail_ref), channel_id=1, source_target_pairs={{0,1},{1,0},{2,3},{3,2},{4,5},{5,4},{6,7},{7,6},{8,9},{9,8},{10,11... | collective-permute-start | bytes 221192 | tf_op jit(solution)/shard_map/ppermute | solution.py:19
  85.9 4.9 %collective-permute-start.32 = (bf16[32,1024]{1,0:T(8,128)(2,1)S(1)}, bf16[32,1024]{1,0:T(8,128)(2,1)S(1)}, u32[]{:S(2)}, u32[]{:S(2)}) collective-permute-start(bf16[32,1024]{1,0:T(8,128)(2,1)S(1)} %get-tuple-element.73), channel_id=1, source_target_pairs={{0,1},{1,0},{2,3},{3,2},{4,5},{5,4},{6,7},{7,6},{8,9},{9,8},{10,11... | collective-permute-start | bytes 196616 | tf_op jit(solution)/shard_map/ppermute | solution.py:19
  87.7 3.6 %collective-permute-start.33 = (f32[1,1792]{1,0:T(1,128)S(1)}, f32[1,1792]{1,0:T(1,128)S(1)}, u32[]{:S(2)}, u32[]{:S(2)}) collective-permute-start(f32[1,1792]{1,0:T(1,128)S(1)} %get-tuple-element.75), channel_id=1, source_target_pairs={{0,1},{1,0},{2,3},{3,2},{4,5},{5,4},{6,7},{7,6},{8,9},{9,8},{10,11... | collective-permute-start | bytes 21512 | tf_op jit(solution)/shard_map/ppermute | solution.py:19
